TPU v7x, 32 devices: a whole 2x2x4 slice. The times are simulated.
32 devices in a mesh: lat: 4 (over z), lon: 4 (over y, core), tm: 2 (over x).
Axes of the slice: x: 2, y: 2, z: 4, core: 2. Of those that a mesh axis runs over, the one named last changes fastest.
Arguments:
- gradient: float32 [56, 64, 1024], P('tm', 'lat', 'lon'), may hold values from -6 to 6
- control: float32 [56, 64, 1024], P('tm', 'lat', 'lon'), may hold values from -6 to 6
- diffusivity: float32 [64, 1024], P('lat', 'lon'), may hold values from 0.03 to 0.24
- land_mask: int32 [64, 1024], P('lat', 'lon'), may hold values 0 or 1
- time_corr: float32 [56, 56], replicated, may hold values from -0.35 to 1.35
- pair_steps: bfloat16 [8, 56, 64, 1024], P(None, 'tm', 'lat', 'lon'), may hold values from -12 to 12
- pair_grads: bfloat16 [8, 56, 64, 1024], P(None, 'tm', 'lat', 'lon'), may hold values from -24 to 24
Outputs:
- next_control: float32 [56, 64, 1024], P('tm', 'lat', 'lon')
All inputs are finite; a program needn't handle non-finite values. No bound on the sum of `land_mask` on one device may be relied on, other than what follows from the above.
Results may differ from a plain program's by a relative error of at most 0.0003.
Values sent between devices are 32-bit elements; how exact they have to be, the bound alone decides.
No kernel may reach another device: no remote copies, remote signals or barrier semaphores. Data moves between devices by JAX's collectives and lax.ppermute only.
A program may use at most 64 MiB of HBM per device.

v0:
```python
import jax
import jax.numpy as jnp
from jax import lax
from jax.sharding import PartitionSpec as P

PAIRS = 8
SWEEPS = 6


def with_halo(block, sides, width):
    for axis, dim in sides:
        count = lax.axis_size(axis)
        forward = [(i, i + 1) for i in range(count - 1)]
        forward.append((count - 1, 0))
        backward = [(target, source) for source, target in forward]
        low = lax.ppermute(
            lax.slice_in_dim(block, block.shape[dim] - width, None, axis=dim), axis, forward
        )
        high = lax.ppermute(lax.slice_in_dim(block, 0, width, axis=dim), axis, backward)
        block = jnp.concatenate([low, block, high], axis=dim)
    return block


def stencil(padded, kappa_pad):
    centre = padded[..., 1:-1, 1:-1]
    kc = kappa_pad[1:-1, 1:-1]
    north = 0.5 * (kc + kappa_pad[:-2, 1:-1]) * (padded[..., :-2, 1:-1] - centre)
    south = 0.5 * (kc + kappa_pad[2:, 1:-1]) * (padded[..., 2:, 1:-1] - centre)
    west = 0.5 * (kc + kappa_pad[1:-1, :-2]) * (padded[..., 1:-1, :-2] - centre)
    east = 0.5 * (kc + kappa_pad[1:-1, 2:]) * (padded[..., 1:-1, 2:] - centre)
    return centre + north + south + west + east


def clear_rows(values, margin, at_top, at_bottom):
    height = values.shape[-2]
    index = jnp.arange(height, dtype=jnp.int32)[:, None]
    outside = at_top & (index < margin) | at_bottom & (index >= height - margin)
    return jnp.where(outside, jnp.zeros((), values.dtype), values)


def solve_upper(upper, target):
    result = jnp.zeros_like(target)
    for position in reversed(range(PAIRS)):
        remainder = target[position] - jnp.sum(upper[position] * result)
        result = result.at[position].set(remainder / upper[position, position])
    return result


def solve_upper_transposed(upper, target):
    result = jnp.zeros_like(target)
    for position in range(PAIRS):
        remainder = target[position] - jnp.sum(upper[:, position] * result)
        result = result.at[position].set(remainder / upper[position, position])
    return result


def compact(cross, square, proj_s, proj_y, count):
    index = jnp.arange(PAIRS, dtype=jnp.int32)
    valid = (index < count).astype(jnp.float32)
    last = (index == count - 1).astype(jnp.float32)
    curve = jnp.diagonal(cross)
    gamma = jnp.sum(last * curve) / jnp.sum(last * jnp.diagonal(square))
    pair_mask = valid[:, None] * valid[None, :]
    upper = jnp.triu(cross) * pair_mask + jnp.diag(1.0 - valid)
    first = solve_upper(upper, proj_s * valid)
    middle = jnp.diag(curve * valid) + gamma * square * pair_mask
    target = jnp.dot(middle, first, precision=lax.Precision.HIGHEST) - gamma * proj_y * valid
    second = solve_upper_transposed(upper, target)
    return (gamma, first, second)


def local(gradient, control, diffusivity, land_mask, time_corr, pair_steps, pair_grads):
    at_top = lax.axis_index("lat") == 0
    at_bottom = lax.axis_index("lat") == lax.axis_size("lat") - 1
    flat_steps = pair_steps.reshape(PAIRS, -1)
    flat_grads = pair_grads.reshape(PAIRS, -1)
    dims = (((1,), (1,)), ((), ()))
    masked = gradient * land_mask.astype(jnp.float32)[None]
    margin = 1
    kappa_pad = with_halo(diffusivity, (("lat", 0), ("lon", 1)), margin)
    kappa_pad = clear_rows(kappa_pad, margin, at_top, at_bottom)
    field = masked
    for sweep in range(SWEEPS):
        padded = with_halo(field, (("lat", 1), ("lon", 2)), 1)
        padded = clear_rows(padded, 1, at_top, at_bottom)
        field = stencil(padded, kappa_pad)
    regrouped = lax.all_to_all(field, "tm", split_axis=1, concat_axis=0, tiled=True)
    mixed = jnp.einsum("st,sab->tab", time_corr, regrouped, precision=lax.Precision.HIGHEST)
    control_grad = lax.all_to_all(mixed, "tm", split_axis=0, concat_axis=1, tiled=True)
    grad_half = control_grad.astype(jnp.bfloat16).reshape(-1)
    proj_s = jnp.dot(flat_steps, grad_half, preferred_element_type=jnp.float32)
    proj_y = jnp.dot(flat_grads, grad_half, preferred_element_type=jnp.float32)
    cross, square, proj_s, proj_y = lax.psum(
        (
            lax.dot_general(flat_steps, flat_grads, dims, preferred_element_type=jnp.float32),
            lax.dot_general(flat_grads, flat_grads, dims, preferred_element_type=jnp.float32),
            proj_s,
            proj_y,
        ),
        ("lat", "lon", "tm"),
    )
    gamma, first, second = compact(cross, square, proj_s, proj_y, PAIRS)
    update = gamma * control_grad
    for index in range(PAIRS):
        update = update + second[index] * pair_steps[index].astype(jnp.float32)
        update = update - gamma * first[index] * pair_grads[index].astype(jnp.float32)
    return control - update


def solution(mesh):
    placed = (
        P("tm", "lat", "lon"),
        P("tm", "lat", "lon"),
        P("lat", "lon"),
        P("lat", "lon"),
        P(),
        P(None, "tm", "lat", "lon"),
        P(None, "tm", "lat", "lon"),
    )
    return jax.shard_map(
        local, mesh=mesh, in_specs=placed, out_specs=P("tm", "lat", "lon"), check_vma=False
    )
```

profile of v0, /device:TPU:0, one launch (start us, length us, event | category | flops | bytes accessed | tf_op | source)
XLA Modules:
  0.0 237.1 jit_solution(9576315491271568459)
XLA Ops:
  2.0 3.1 %collective-permute-start = (f32[28,1,256]{2,0,1:T(8,128)S(1)}, f32[28,1,256]{2,0,1:T(8,128)S(1)}, u32[]{:S(2)}, u32[]{:S(2)}) collective-permute-start(f32[28,1,256]{2,0,1:T(8,128)S(1)} %get-tuple-element.231), channel_id=1, source_target_pairs={{0,8},{8,16},{16,24},{24,0},{1,9},{9,17},{17,25},{25,1},{2,10},{10... | collective-permute-start | bytes 86024 | tf_op jit(solution)/shard_map/ppermute | solution.py:16
  7.9 3.8 %collective-permute-start.5 = (f32[1,256]{1,0:T(1,128)S(1)}, f32[1,256]{1,0:T(1,128)S(1)}, u32[]{:S(2)}, u32[]{:S(2)}) collective-permute-start(f32[1,256]{1,0:T(1,128)S(1)} %get-tuple-element.240), channel_id=1, source_target_pairs={{8,0},{16,8},{24,16},{0,24},{9,1},{17,9},{25,17},{1,25},{10,2},{18... | collective-permute-start | bytes 3080 | tf_op jit(solution)/shard_map/ppermute | solution.py:19
  20.2 5.4 %collective-permute-done.2 = f32[28,18,1]{2,0,1:T(8,128)S(1)} collective-permute-done((f32[28,18,1]{2,0,1:T(8,128)S(1)}, f32[28,18,1]{2,0,1:T(8,128)S(1)}, u32[]{:S(2)}, u32[]{:S(2)}) %collective-permute-start.2) | collective-permute-done | bytes 2048 | tf_op jit(solution)/shard_map/ppermute | solution.py:16
  28.0 3.9 %collective-permute-start.9 = (f32[28,1,256]{2,0,1:T(8,128)S(1)}, f32[28,1,256]{2,0,1:T(8,128)S(1)}, u32[]{:S(2)}, u32[]{:S(2)}) collective-permute-start(f32[28,1,256]{2,0,1:T(8,128)S(1)} %get-tuple-element.230), channel_id=1, source_target_pairs={{8,0},{16,8},{24,16},{0,24},{9,1},{17,9},{25,17},{1,25},{10,2},{18... | collective-permute-start | bytes 86024 | tf_op jit(solution)/shard_map/ppermute | solution.py:19
  31.8 2.2 collective-permute-done.8
  36.0 5.5 %collective-permute-done.10 = f32[28,18,1]{2,0,1:T(8,128)S(1)} collective-permute-done((f32[28,18,1]{2,0,1:T(8,128)S(1)}, f32[28,18,1]{2,0,1:T(8,128)S(1)}, u32[]{:S(2)}, u32[]{:S(2)}) %collective-permute-start.10) | collective-permute-done | bytes 2048 | tf_op jit(solution)/shard_map/ppermute | solution.py:16
  45.1 2.6 %collective-permute-start.13 = (f32[28,1,256]{2,0,1:T(8,128)S(1)}, f32[28,1,256]{2,0,1:T(8,128)S(1)}, u32[]{:S(2)}, u32[]{:S(2)}) collective-permute-start(f32[28,1,256]{2,0,1:T(8,128)S(1)} %get-tuple-element.228), channel_id=1, source_target_pairs={{8,0},{16,8},{24,16},{0,24},{9,1},{17,9},{25,17},{1,25},{10,2},{18... | collective-permute-start | bytes 86024 | tf_op jit(solution)/shard_map/ppermute | solution.py:19
  51.7 5.3 %collective-permute-done.14 = f32[28,18,1]{2,0,1:T(8,128)S(1)} collective-permute-done((f32[28,18,1]{2,0,1:T(8,128)S(1)}, f32[28,18,1]{2,0,1:T(8,128)S(1)}, u32[]{:S(2)}, u32[]{:S(2)}) %collective-permute-start.14) | collective-permute-done | bytes 2048 | tf_op jit(solution)/shard_map/ppermute | solution.py:16
  61.0 2.7 %collective-permute-start.17 = (f32[28,1,256]{2,0,1:T(8,128)S(1)}, f32[28,1,256]{2,0,1:T(8,128)S(1)}, u32[]{:S(2)}, u32[]{:S(2)}) collective-permute-start(f32[28,1,256]{2,0,1:T(8,128)S(1)} %get-tuple-element.226), channel_id=1, source_target_pairs={{8,0},{16,8},{24,16},{0,24},{9,1},{17,9},{25,17},{1,25},{10,2},{18... | collective-permute-start | bytes 86024 | tf_op jit(solution)/shard_map/ppermute | solution.py:19
  67.6 5.0 %collective-permute-done.18 = f32[28,18,1]{2,0,1:T(8,128)S(1)} collective-permute-done((f32[28,18,1]{2,0,1:T(8,128)S(1)}, f32[28,18,1]{2,0,1:T(8,128)S(1)}, u32[]{:S(2)}, u32[]{:S(2)}) %collective-permute-start.18) | collective-permute-done | bytes 2048 | tf_op jit(solution)/shard_map/ppermute | solution.py:16
  72.7 2.2 collective-permute-done.19
  77.2 2.6 %collective-permute-start.21 = (f32[28,1,256]{2,0,1:T(8,128)S(1)}, f32[28,1,256]{2,0,1:T(8,128)S(1)}, u32[]{:S(2)}, u32[]{:S(2)}) collective-permute-start(f32[28,1,256]{2,0,1:T(8,128)S(1)} %get-tuple-element.224), channel_id=1, source_target_pairs={{8,0},{16,8},{24,16},{0,24},{9,1},{17,9},{25,17},{1,25},{10,2},{18... | collective-permute-start | bytes 86024 | tf_op jit(solution)/shard_map/ppermute | solution.py:19
  83.8 4.8 %collective-permute-done.22 = f32[28,18,1]{2,0,1:T(8,128)S(1)} collective-permute-done((f32[28,18,1]{2,0,1:T(8,128)S(1)}, f32[28,18,1]{2,0,1:T(8,128)S(1)}, u32[]{:S(2)}, u32[]{:S(2)}) %collective-permute-start.22) | collective-permute-done | bytes 2048 | tf_op jit(solution)/shard_map/ppermute | solution.py:16
  88.6 2.5 %collective-permute-done.23 = f32[28,18,1]{2,0,1:T(8,128)S(1)} collective-permute-done((f32[28,18,1]{2,0,1:T(8,128)S(1)}, f32[28,18,1]{2,0,1:T(8,128)S(1)}, u32[]{:S(2)}, u32[]{:S(2)}) %collective-permute-start.23) | collective-permute-done | bytes 2048 | tf_op jit(solution)/shard_map/ppermute | solution.py:19
  93.4 2.7 %collective-permute-start.25 = (f32[28,1,256]{2,0,1:T(8,128)S(1)}, f32[28,1,256]{2,0,1:T(8,128)S(1)}, u32[]{:S(2)}, u32[]{:S(2)}) collective-permute-start(f32[28,1,256]{2,0,1:T(8,128)S(1)} %get-tuple-element.222), channel_id=1, source_target_pairs={{8,0},{16,8},{24,16},{0,24},{9,1},{17,9},{25,17},{1,25},{10,2},{18... | collective-permute-start | bytes 86024 | tf_op jit(solution)/shard_map/ppermute | solution.py:19
  100.0 4.7 %collective-permute-done.26 = f32[28,18,1]{2,0,1:T(8,128)S(1)} collective-permute-done((f32[28,18,1]{2,0,1:T(8,128)S(1)}, f32[28,18,1]{2,0,1:T(8,128)S(1)}, u32[]{:S(2)}, u32[]{:S(2)}) %collective-permute-start.26) | collective-permute-done | bytes 2048 | tf_op jit(solution)/shard_map/ppermute | solution.py:16
  104.7 2.5 %collective-permute-done.27 = f32[28,18,1]{2,0,1:T(8,128)S(1)} collective-permute-done((f32[28,18,1]{2,0,1:T(8,128)S(1)}, f32[28,18,1]{2,0,1:T(8,128)S(1)}, u32[]{:S(2)}, u32[]{:S(2)}) %collective-permute-start.27) | collective-permute-done | bytes 2048 | tf_op jit(solution)/shard_map/ppermute | solution.py:19
  109.0 3.7 %all-to-all-start = ((f32[28,16,256]{2,0,1:T(8,128)}), f32[28,16,256]{2,0,1:T(8,128)S(1)}, u32[]{:S(2)}, u32[]{:S(2)}) async-start(f32[28,16,256]{2,0,1:T(8,128)} %fusion.25), calls=%async_computation | async-start | bytes 1048576 | tf_op jit(solution)/shard_map/all_to_all | solution.py:87
  112.7 3.8 %fusion.12 = f32[8,8]{1,0:T(8,128)S(1)} fusion(bf16[8,28,16,256]{3,2,1,0:T(8,128)(2,1)S(1)} %copy-done.1, bf16[8,28,16,256]{3,2,1,0:T(8,128)(2,1)} %param.44), kind=kOutput, calls=%fused_computation.13 | convolution fusion | flops 14680064 | bytes 3670272 | tf_op jit(solution)/shard_map/dot_general | solution.py:95
  116.5 4.7 %all-to-all-done = f32[28,16,256]{2,0,1:T(8,128)S(1)} async-done(((f32[28,16,256]{2,0,1:T(8,128)}), f32[28,16,256]{2,0,1:T(8,128)S(1)}, u32[]{:S(2)}, u32[]{:S(2)}) %all-to-all-start) | async-done | bytes 458784 | tf_op jit(solution)/shard_map/all_to_all | solution.py:87
  123.1 3.5 %all-to-all-start.1 = ((f32[56,8,256]{2,1,0:T(8,128)}), f32[56,8,256]{2,1,0:T(8,128)S(1)}, u32[]{:S(2)}, u32[]{:S(2)}) async-start(f32[56,8,256]{2,1,0:T(8,128)} %copy.44), calls=%async_computation.1 | async-start | bytes 917504 | tf_op jit(solution)/shard_map/all_to_all | solution.py:89
  128.3 5.5 %all-to-all-done.1 = f32[56,8,256]{2,1,0:T(8,128)S(1)} async-done(((f32[56,8,256]{2,1,0:T(8,128)}), f32[56,8,256]{2,1,0:T(8,128)S(1)}, u32[]{:S(2)}, u32[]{:S(2)}) %all-to-all-start.1) | async-done | bytes 458784 | tf_op jit(solution)/shard_map/all_to_all | solution.py:89
  137.9 39.6 %all-reduce.2 = (f32[8,8]{1,0:T(8,128)S(1)}, f32[8,8]{1,0:T(8,128)S(1)}, f32[8]{0:T(128)S(1)}, f32[8]{0:T(128)S(1)}) all-reduce(f32[8,8]{1,0:T(8,128)S(1)} %fusion.12, f32[8,8]{1,0:T(8,128)S(1)} %fusion.9, f32[8]{0:T(128)S(1)} %fusion.20, f32[8]{0:T(128)S(1)} %fusion.17), channel_id=1, replica_groups=mesh['lat'=4,'lon'=4,'tm'=2] {'lat','lon','tm'}, use_global_device_ids=true, to_apply=%region_0.1 | all-reduce | flops 144 | bytes 1152 | tf_op jit(solution)/shard_map/psum | solution.py:93
  230.2 6.8 %fusion.72 = f32[28,16,256]{2,1,0:T(8,128)} fusion(f32[28,16,256]{2,1,0:T(8,128)S(1)} %copy-done.3, f32[28,2,8,256]{3,2,0,1:T(8,128)S(1)} %bitcast.192, bf16[8,28,16,256]{3,2,1,0:T(8,128)(2,1)S(1)} %copy-done.1, f32[]{:T(128)S(6)} %mul.598, bf16[8,28,16,256]{3,2,1,0:T(8,128)(2,1)} %param.44, f32[]{:T(128)S(6)} %div.67, f32[]{:T(128)S(6)} %mul.590, f32[]{:T(128)} %div.66, ...), kind=kLoop, calls=%fused_computation.104 | loop fusion | flops 5619712 | bytes 5046336 | tf_op jit(solution)/shard_map/sub | solution.py:107
  (140 shorter events, 71.2 us)
Async XLA Ops:
  2.0 16.0 %collective-permute-start = (f32[28,1,256]{2,0,1:T(8,128)S(1)}, f32[28,1,256]{2,0,1:T(8,128)S(1)}, u32[]{:S(2)}, u32[]{:S(2)}) collective-permute-start(f32[28,1,256]{2,0,1:T(8,128)S(1)} %get-tuple-element.231), channel_id=1, source_target_pairs={{0,8},{8,16},{16,24},{24,0},{1,9},{9,17},{17,25},{25,1},{2,10},{10... | collective-permute-start | bytes 86024 | tf_op jit(solution)/shard_map/ppermute | solution.py:16
  5.1 13.0 %collective-permute-start.1 = (f32[28,1,256]{2,0,1:T(8,128)S(1)}, f32[28,1,256]{2,0,1:T(8,128)S(1)}, u32[]{:S(2)}, u32[]{:S(2)}) collective-permute-start(f32[28,1,256]{2,0,1:T(8,128)S(1)} %get-tuple-element.232), channel_id=1, source_target_pairs={{8,0},{16,8},{24,16},{0,24},{9,1},{17,9},{25,17},{1,25},{10,2},{18... | collective-permute-start | bytes 86024 | tf_op jit(solution)/shard_map/ppermute | solution.py:19
  7.9 5.4 %collective-permute-start.4 = (f32[1,256]{1,0:T(1,128)S(1)}, f32[1,256]{1,0:T(1,128)S(1)}, u32[]{:S(2)}, u32[]{:S(2)}) collective-permute-start(f32[1,256]{1,0:T(1,128)S(1)} %get-tuple-element.239), channel_id=1, source_target_pairs={{0,8},{8,16},{16,24},{24,0},{1,9},{9,17},{17,25},{25,1},{2,10},{10... | collective-permute-start | bytes 3080 | tf_op jit(solution)/shard_map/ppermute | solution.py:16
  7.9 5.4 %collective-permute-start.5 = (f32[1,256]{1,0:T(1,128)S(1)}, f32[1,256]{1,0:T(1,128)S(1)}, u32[]{:S(2)}, u32[]{:S(2)}) collective-permute-start(f32[1,256]{1,0:T(1,128)S(1)} %get-tuple-element.240), channel_id=1, source_target_pairs={{8,0},{16,8},{24,16},{0,24},{9,1},{17,9},{25,17},{1,25},{10,2},{18... | collective-permute-start | bytes 3080 | tf_op jit(solution)/shard_map/ppermute | solution.py:19
  18.3 7.3 %collective-permute-start.2 = (f32[28,18,1]{2,0,1:T(8,128)S(1)}, f32[28,18,1]{2,0,1:T(8,128)S(1)}, u32[]{:S(2)}, u32[]{:S(2)}) collective-permute-start(f32[28,18,1]{2,0,1:T(8,128)S(1)} %get-tuple-element.219), channel_id=1, source_target_pairs={{0,2},{2,4},{4,6},{6,0},{1,3},{3,5},{5,7},{7,1},{8,10},{10,12},{12... | collective-permute-start | bytes 6056 | tf_op jit(solution)/shard_map/ppermute | solution.py:16
  20.1 6.7 %collective-permute-start.3 = (f32[28,18,1]{2,0,1:T(8,128)S(1)}, f32[28,18,1]{2,0,1:T(8,128)S(1)}, u32[]{:S(2)}, u32[]{:S(2)}) collective-permute-start(f32[28,18,1]{2,0,1:T(8,128)S(1)} %get-tuple-element.220), channel_id=1, source_target_pairs={{2,0},{4,2},{6,4},{0,6},{3,1},{5,3},{7,5},{1,7},{10,8},{12,10},{14... | collective-permute-start | bytes 6056 | tf_op jit(solution)/shard_map/ppermute | solution.py:19
  27.9 6.1 %collective-permute-start.8 = (f32[28,1,256]{2,0,1:T(8,128)S(1)}, f32[28,1,256]{2,0,1:T(8,128)S(1)}, u32[]{:S(2)}, u32[]{:S(2)}) collective-permute-start(f32[28,1,256]{2,0,1:T(8,128)S(1)} %get-tuple-element.229), channel_id=1, source_target_pairs={{0,8},{8,16},{16,24},{24,0},{1,9},{9,17},{17,25},{25,1},{2,10},{10... | collective-permute-start | bytes 86024 | tf_op jit(solution)/shard_map/ppermute | solution.py:16
  28.0 6.0 %collective-permute-start.9 = (f32[28,1,256]{2,0,1:T(8,128)S(1)}, f32[28,1,256]{2,0,1:T(8,128)S(1)}, u32[]{:S(2)}, u32[]{:S(2)}) collective-permute-start(f32[28,1,256]{2,0,1:T(8,128)S(1)} %get-tuple-element.230), channel_id=1, source_target_pairs={{8,0},{16,8},{24,16},{0,24},{9,1},{17,9},{25,17},{1,25},{10,2},{18... | collective-permute-start | bytes 86024 | tf_op jit(solution)/shard_map/ppermute | solution.py:19
  34.2 7.3 %collective-permute-start.10 = (f32[28,18,1]{2,0,1:T(8,128)S(1)}, f32[28,18,1]{2,0,1:T(8,128)S(1)}, u32[]{:S(2)}, u32[]{:S(2)}) collective-permute-start(f32[28,18,1]{2,0,1:T(8,128)S(1)} %get-tuple-element.217), channel_id=1, source_target_pairs={{0,2},{2,4},{4,6},{6,0},{1,3},{3,5},{5,7},{7,1},{8,10},{10,12},{12... | collective-permute-start | bytes 6056 | tf_op jit(solution)/shard_map/ppermute | solution.py:16
  34.3 8.5 %collective-permute-start.11 = (f32[28,18,1]{2,0,1:T(8,128)S(1)}, f32[28,18,1]{2,0,1:T(8,128)S(1)}, u32[]{:S(2)}, u32[]{:S(2)}) collective-permute-start(f32[28,18,1]{2,0,1:T(8,128)S(1)} %get-tuple-element.218), channel_id=1, source_target_pairs={{2,0},{4,2},{6,4},{0,6},{3,1},{5,3},{7,5},{1,7},{10,8},{12,10},{14... | collective-permute-start | bytes 6056 | tf_op jit(solution)/shard_map/ppermute | solution.py:19
  43.8 5.9 %collective-permute-start.12 = (f32[28,1,256]{2,0,1:T(8,128)S(1)}, f32[28,1,256]{2,0,1:T(8,128)S(1)}, u32[]{:S(2)}, u32[]{:S(2)}) collective-permute-start(f32[28,1,256]{2,0,1:T(8,128)S(1)} %get-tuple-element.227), channel_id=1, source_target_pairs={{0,8},{8,16},{16,24},{24,0},{1,9},{9,17},{17,25},{25,1},{2,10},{10... | collective-permute-start | bytes 86024 | tf_op jit(solution)/shard_map/ppermute | solution.py:16
  49.9 7.1 %collective-permute-start.14 = (f32[28,18,1]{2,0,1:T(8,128)S(1)}, f32[28,18,1]{2,0,1:T(8,128)S(1)}, u32[]{:S(2)}, u32[]{:S(2)}) collective-permute-start(f32[28,18,1]{2,0,1:T(8,128)S(1)} %get-tuple-element.215), channel_id=1, source_target_pairs={{0,2},{2,4},{4,6},{6,0},{1,3},{3,5},{5,7},{7,1},{8,10},{10,12},{12... | collective-permute-start | bytes 6056 | tf_op jit(solution)/shard_map/ppermute | solution.py:16
  50.0 8.7 %collective-permute-start.15 = (f32[28,18,1]{2,0,1:T(8,128)S(1)}, f32[28,18,1]{2,0,1:T(8,128)S(1)}, u32[]{:S(2)}, u32[]{:S(2)}) collective-permute-start(f32[28,18,1]{2,0,1:T(8,128)S(1)} %get-tuple-element.216), channel_id=1, source_target_pairs={{2,0},{4,2},{6,4},{0,6},{3,1},{5,3},{7,5},{1,7},{10,8},{12,10},{14... | collective-permute-start | bytes 6056 | tf_op jit(solution)/shard_map/ppermute | solution.py:19
  59.7 5.8 %collective-permute-start.16 = (f32[28,1,256]{2,0,1:T(8,128)S(1)}, f32[28,1,256]{2,0,1:T(8,128)S(1)}, u32[]{:S(2)}, u32[]{:S(2)}) collective-permute-start(f32[28,1,256]{2,0,1:T(8,128)S(1)} %get-tuple-element.225), channel_id=1, source_target_pairs={{0,8},{8,16},{16,24},{24,0},{1,9},{9,17},{17,25},{25,1},{2,10},{10... | collective-permute-start | bytes 86024 | tf_op jit(solution)/shard_map/ppermute | solution.py:16
  65.8 6.8 %collective-permute-start.18 = (f32[28,18,1]{2,0,1:T(8,128)S(1)}, f32[28,18,1]{2,0,1:T(8,128)S(1)}, u32[]{:S(2)}, u32[]{:S(2)}) collective-permute-start(f32[28,18,1]{2,0,1:T(8,128)S(1)} %get-tuple-element.213), channel_id=1, source_target_pairs={{0,2},{2,4},{4,6},{6,0},{1,3},{3,5},{5,7},{7,1},{8,10},{10,12},{12... | collective-permute-start | bytes 6056 | tf_op jit(solution)/shard_map/ppermute | solution.py:16
  65.9 9.0 %collective-permute-start.19 = (f32[28,18,1]{2,0,1:T(8,128)S(1)}, f32[28,18,1]{2,0,1:T(8,128)S(1)}, u32[]{:S(2)}, u32[]{:S(2)}) collective-permute-start(f32[28,18,1]{2,0,1:T(8,128)S(1)} %get-tuple-element.214), channel_id=1, source_target_pairs={{2,0},{4,2},{6,4},{0,6},{3,1},{5,3},{7,5},{1,7},{10,8},{12,10},{14... | collective-permute-start | bytes 6056 | tf_op jit(solution)/shard_map/ppermute | solution.py:19
  75.9 5.8 %collective-permute-start.20 = (f32[28,1,256]{2,0,1:T(8,128)S(1)}, f32[28,1,256]{2,0,1:T(8,128)S(1)}, u32[]{:S(2)}, u32[]{:S(2)}) collective-permute-start(f32[28,1,256]{2,0,1:T(8,128)S(1)} %get-tuple-element.223), channel_id=1, source_target_pairs={{0,8},{8,16},{16,24},{24,0},{1,9},{9,17},{17,25},{25,1},{2,10},{10... | collective-permute-start | bytes 86024 | tf_op jit(solution)/shard_map/ppermute | solution.py:16
  82.0 6.6 %collective-permute-start.22 = (f32[28,18,1]{2,0,1:T(8,128)S(1)}, f32[28,18,1]{2,0,1:T(8,128)S(1)}, u32[]{:S(2)}, u32[]{:S(2)}) collective-permute-start(f32[28,18,1]{2,0,1:T(8,128)S(1)} %get-tuple-element.211), channel_id=1, source_target_pairs={{0,2},{2,4},{4,6},{6,0},{1,3},{3,5},{5,7},{7,1},{8,10},{10,12},{12... | collective-permute-start | bytes 6056 | tf_op jit(solution)/shard_map/ppermute | solution.py:16
  82.0 9.1 %collective-permute-start.23 = (f32[28,18,1]{2,0,1:T(8,128)S(1)}, f32[28,18,1]{2,0,1:T(8,128)S(1)}, u32[]{:S(2)}, u32[]{:S(2)}) collective-permute-start(f32[28,18,1]{2,0,1:T(8,128)S(1)} %get-tuple-element.212), channel_id=1, source_target_pairs={{2,0},{4,2},{6,4},{0,6},{3,1},{5,3},{7,5},{1,7},{10,8},{12,10},{14... | collective-permute-start | bytes 6056 | tf_op jit(solution)/shard_map/ppermute | solution.py:19
  92.1 5.8 %collective-permute-start.24 = (f32[28,1,256]{2,0,1:T(8,128)S(1)}, f32[28,1,256]{2,0,1:T(8,128)S(1)}, u32[]{:S(2)}, u32[]{:S(2)}) collective-permute-start(f32[28,1,256]{2,0,1:T(8,128)S(1)} %get-tuple-element.221), channel_id=1, source_target_pairs={{0,8},{8,16},{16,24},{24,0},{1,9},{9,17},{17,25},{25,1},{2,10},{10... | collective-permute-start | bytes 86024 | tf_op jit(solution)/shard_map/ppermute | solution.py:16
  98.2 6.5 %collective-permute-start.26 = (f32[28,18,1]{2,0,1:T(8,128)S(1)}, f32[28,18,1]{2,0,1:T(8,128)S(1)}, u32[]{:S(2)}, u32[]{:S(2)}) collective-permute-start(f32[28,18,1]{2,0,1:T(8,128)S(1)} %get-tuple-element.209), channel_id=1, source_target_pairs={{0,2},{2,4},{4,6},{6,0},{1,3},{3,5},{5,7},{7,1},{8,10},{10,12},{12... | collective-permute-start | bytes 6056 | tf_op jit(solution)/shard_map/ppermute | solution.py:16
  98.3 9.0 %collective-permute-start.27 = (f32[28,18,1]{2,0,1:T(8,128)S(1)}, f32[28,18,1]{2,0,1:T(8,128)S(1)}, u32[]{:S(2)}, u32[]{:S(2)}) collective-permute-start(f32[28,18,1]{2,0,1:T(8,128)S(1)} %get-tuple-element.210), channel_id=1, source_target_pairs={{2,0},{4,2},{6,4},{0,6},{3,1},{5,3},{7,5},{1,7},{10,8},{12,10},{14... | collective-permute-start | bytes 6056 | tf_op jit(solution)/shard_map/ppermute | solution.py:19
  109.0 12.2 %all-to-all-start = ((f32[28,16,256]{2,0,1:T(8,128)}), f32[28,16,256]{2,0,1:T(8,128)S(1)}, u32[]{:S(2)}, u32[]{:S(2)}) async-start(f32[28,16,256]{2,0,1:T(8,128)} %fusion.25), calls=%async_computation | async-start | bytes 1048576 | tf_op jit(solution)/shard_map/all_to_all | solution.py:87
  123.1 10.7 %all-to-all-start.1 = ((f32[56,8,256]{2,1,0:T(8,128)}), f32[56,8,256]{2,1,0:T(8,128)S(1)}, u32[]{:S(2)}, u32[]{:S(2)}) async-start(f32[56,8,256]{2,1,0:T(8,128)} %copy.44), calls=%async_computation.1 | async-start | bytes 917504 | tf_op jit(solution)/shard_map/all_to_all | solution.py:89
  (10 other events, 245.6 us)
where the time goes:
time: 238 us; the launch traced here: 237 us
  waiting for transfers between devices  65.4 us (27%)
  starting transfers between devices  48.3 us (20%)
  blocking collectives  39.6 us (17%)
  between operations  36.8 us (15%)
  other arithmetic  28.8 us (12%)
  matrix products  10.4 us (4%)
  local copies, waits for them, and re-layouts  7.86 us (3%)
    ppermute x14, waiting for transfers between devices, with_halo(): lax.ppermute(lax.slice_in_dim(block, block.shape[dim] - width, None, axis...  43.5 us
    psum x1, blocking collectives, local(): lax.psum((lax.dot_general(flat_steps, flat_grads, dims, preferred_element...  39.6 us
    ppermute x14, starting transfers between devices, with_halo(): lax.ppermute(lax.slice_in_dim(block, 0, width, axis=dim), axis, backward)  30.8 us
    ppermute x14, waiting for transfers between devices, with_halo(): lax.ppermute(lax.slice_in_dim(block, 0, width, axis=dim), axis, backward)  11.6 us
    ppermute x14, starting transfers between devices, with_halo(): lax.ppermute(lax.slice_in_dim(block, block.shape[dim] - width, None, axis...  10.4 us
    sub x1, other arithmetic, local(): return control - update  6.83 us
    all_to_all x1, waiting for transfers between devices, local(): lax.all_to_all(mixed, 'tm', split_axis=0, concat_axis=1, tiled=True)  5.53 us
    reduce_sum x8, other arithmetic, solve_upper(): remainder = target[position] - jnp.sum(upper[position] * result)  5.2 us
  transfers between devices with their start and end apart: 30, of which 23 were waited for; matrix products, arithmetic and copies ran while one was open for 3% of the time, Pallas kernels for 0%

commit v1 on v0

v1 whole, which is shorter than its diff:
```python
import jax
import jax.numpy as jnp
from jax import lax
from jax.experimental import pallas as pl
from jax.experimental.pallas import tpu as pltpu
from jax.sharding import PartitionSpec as P

PAIRS = 8
SWEEPS = 6
SUB = 8
LANE = 128
GROUP = 8
PER = LANE // GROUP
CROSS = [(i, j) for i in range(PAIRS) for j in range(i, PAIRS)]
NSYM = len(CROSS)
WHERE = {pair: k for k, pair in enumerate(CROSS)}
NGRAM = 2 * NSYM
NPROJ = 2 * PAIRS
NROW = NGRAM + NPROJ
CHUNKS = 2

VMEM = pl.BlockSpec(memory_space=pltpu.VMEM)
SMEM = pl.BlockSpec(memory_space=pltpu.SMEM)
PARAMS = pltpu.CompilerParams(vmem_limit_bytes=48 * 1024 * 1024)


def f32(*shape):
    return jax.ShapeDtypeStruct(shape, jnp.float32)


def call(kernel, outs, args, specs=None, scratch=(), name=None):
    single = not isinstance(outs, (tuple, list))
    return pl.pallas_call(
        kernel,
        out_shape=outs,
        in_specs=specs or [VMEM] * len(args),
        out_specs=VMEM if single else [VMEM] * len(outs),
        scratch_shapes=list(scratch),
        compiler_params=PARAMS,
        name=name,
    )(*args)


def lane_index():
    return lax.broadcasted_iota(jnp.int32, (SUB, LANE), 1)


def row_index():
    return lax.broadcasted_iota(jnp.int32, (SUB, LANE), 0)


def pack_kernel(grad_ref, mask_ref, diff_ref, masked_ref, first_ref, last_ref, west_ref, east_ref):
    steps, rows, cols = grad_ref.shape
    mask = mask_ref[...].astype(jnp.float32)
    lane = lane_index()
    zero = jnp.zeros((SUB, LANE), jnp.float32)
    tiles = rows // SUB
    for base in range(0, steps + 1, PER):
        west = [zero] * tiles
        east = [zero] * tiles
        for step in range(base, min(base + PER, steps + 1)):
            value = grad_ref[step] * mask if step < steps else diff_ref[...]
            if step < steps:
                masked_ref[step] = value
            first_ref[step] = value[:SUB]
            last_ref[step] = value[rows - SUB:]
            start = (step - base) * GROUP
            here = (lane >= start) & (lane < start + GROUP)
            for r in range(tiles):
                left = value[r * SUB:(r + 1) * SUB, :LANE]
                right = value[r * SUB:(r + 1) * SUB, cols - LANE:]
                west[r] = jnp.where(here, pltpu.roll(left, start, 1) if start else left, west[r])
                turn = (start + GROUP) % LANE
                east[r] = jnp.where(here, pltpu.roll(right, turn, 1) if turn else right, east[r])
        place = base // PER * LANE
        for r in range(tiles):
            west_ref[r * SUB:(r + 1) * SUB, place:place + LANE] = west[r]
            east_ref[r * SUB:(r + 1) * SUB, place:place + LANE] = east[r]


def load_tiles(step, slot, own, above, below, left_ref, right_ref, up_ref, down_ref, lane):
    rows, cols = own.shape
    tiles = [above, *(own[r * SUB:(r + 1) * SUB] for r in range(rows // SUB)), below]
    group = lax.rem(step, PER) if not isinstance(step, int) else step % PER
    block = lax.div(step, PER) if not isinstance(step, int) else step // PER
    place = pl.multiple_of(block * LANE, LANE) if not isinstance(step, int) else block * LANE
    to_left = lax.rem(LANE - group * GROUP, LANE) if not isinstance(step, int) else (LANE - group * GROUP) % LANE
    to_right = lax.rem(2 * LANE - GROUP - group * GROUP, LANE) if not isinstance(step, int) else (2 * LANE - GROUP - group * GROUP) % LANE
    sides = [(up_ref, 0, up_ref, SUB)]
    sides += [(left_ref, r * SUB, right_ref, r * SUB) for r in range(rows // SUB)]
    sides += [(down_ref, 0, down_ref, SUB)]
    result = []
    for tile, (lref, lrow, rref, rrow) in zip(tiles, sides):
        west = pltpu.roll(lref[lrow:lrow + SUB, pl.ds(place, LANE)], to_right, 1)
        east = pltpu.roll(rref[rrow:rrow + SUB, pl.ds(place, LANE)], to_left, 1)
        extra = jnp.where(lane < LANE // 2, east, west)
        result.append([tile[:, c * LANE:(c + 1) * LANE] for c in range(cols // LANE)] + [extra])
    return result


def shifted(tiles, r, c, kind, masks):
    height, width = len(tiles), len(tiles[0])
    if kind == "w":
        return jnp.where(masks[0], pltpu.roll(tiles[r][(c - 1) % width], 1, 1), pltpu.roll(tiles[r][c], 1, 1))
    if kind == "e":
        return jnp.where(masks[1], pltpu.roll(tiles[r][(c + 1) % width], LANE - 1, 1), pltpu.roll(tiles[r][c], LANE - 1, 1))
    if kind == "n":
        return jnp.where(masks[2], pltpu.roll(tiles[(r - 1) % height][c], 1, 0), pltpu.roll(tiles[r][c], 1, 0))
    return jnp.where(masks[3], pltpu.roll(tiles[(r + 1) % height][c], SUB - 1, 0), pltpu.roll(tiles[r][c], SUB - 1, 0))


def make_sweep_kernel(begin, count):
    def kernel(masked_ref, diff_ref, above_ref, below_ref, left_ref, right_ref, up_ref, down_ref, out_ref, coef_ref):
        steps, rows, cols = masked_ref.shape
        lane, row = lane_index(), row_index()
        masks = (lane == 0, lane == LANE - 1, row == 0, row == SUB - 1)
        height, width = rows // SUB + 2, cols // LANE + 1
        packed = (left_ref, right_ref, up_ref, down_ref, lane)
        kappa = load_tiles(steps, 0, diff_ref[...], above_ref[steps], below_ref[steps], *packed)
        for r in range(height):
            for c in range(width):
                centre = kappa[r][c]
                inside = centre > 0.0
                total = jnp.ones((SUB, LANE), jnp.float32)
                for n, kind in enumerate("nswe"):
                    part = jnp.where(inside, 0.5 * (centre + shifted(kappa, r, c, kind, masks)), 0.0)
                    total = total - part
                    coef_ref[(r * width + c) * 5 + 1 + n] = part
                coef_ref[(r * width + c) * 5] = total

        def body(offset, carry):
            step = begin + offset
            tiles = load_tiles(step, 0, masked_ref[step], above_ref[step], below_ref[step], *packed)
            for sweep in range(SWEEPS):
                fresh = [list(line) for line in tiles]
                for r in range(height):
                    for c in range(width):
                        if sweep == SWEEPS - 1 and (r in (0, height - 1) or c == width - 1):
                            continue
                        at = (r * width + c) * 5
                        total = coef_ref[at] * tiles[r][c]
                        for n, kind in enumerate("nswe"):
                            total = total + coef_ref[at + 1 + n] * shifted(tiles, r, c, kind, masks)
                        fresh[r][c] = total
                tiles = fresh
            for r in range(1, height - 1):
                for c in range(width - 1):
                    out_ref[offset, (r - 1) * SUB:r * SUB, c * LANE:(c + 1) * LANE] = tiles[r][c]
            return carry

        lax.fori_loop(0, count, body, 0)

    return kernel


def gram_kernel(steps_ref, grads_ref, out_ref):
    _, steps, rows, cols = steps_ref.shape
    for half, left_ref in enumerate((steps_ref, grads_ref)):
        def body(step, sums):
            sums = list(sums)
            for c in range(0, cols, LANE):
                for r in range(0, rows, 2 * SUB):
                    where = (step, pl.ds(r, 2 * SUB), pl.ds(c, LANE))
                    right = [grads_ref[(i, *where)].astype(jnp.float32) for i in range(PAIRS)]
                    left = right if half else [left_ref[(i, *where)].astype(jnp.float32) for i in range(PAIRS)]
                    for part in range(2):
                        cut = slice(part * SUB, (part + 1) * SUB)
                        for k, (i, j) in enumerate(CROSS):
                            sums[k] = sums[k] + left[i][cut] * right[j][cut]
            return tuple(sums)

        zero = jnp.zeros((SUB, LANE), jnp.float32)
        sums = lax.fori_loop(0, steps, body, (zero,) * NSYM)
        for k in range(NSYM):
            out_ref[half * NSYM + k:half * NSYM + k + 1, :] = jnp.sum(sums[k], axis=0, keepdims=True)


def mix_into(corr_ref, row0, col0, field_ref, acc_ref, fresh):
    count, rows, cols = field_ref.shape
    steps = acc_ref.shape[0]
    block = 7
    for begin in range(0, steps, block):
        size = min(block, steps - begin)
        for c in range(0, cols, 2 * LANE):
            for r in range(0, rows, 2 * SUB):
                where = (pl.ds(r, 2 * SUB), pl.ds(c, 2 * LANE))

                def body(s, sums):
                    value = field_ref[(s, *where)]
                    return tuple(
                        sums[k] + corr_ref[row0 + s, col0 + begin + k] * value for k in range(size)
                    )

                start = tuple(
                    jnp.zeros((2 * SUB, 2 * LANE), jnp.float32) if fresh else acc_ref[(begin + k, *where)]
                    for k in range(size)
                )
                sums = lax.fori_loop(0, count, body, start, unroll=2)
                for k in range(size):
                    acc_ref[(begin + k, *where)] = sums[k]


def make_mix_own(parts):
    def kernel(corr_ref, base_ref, *refs):
        out_ref = refs[-1]
        row = base_ref[0]
        for n in range(parts):
            mix_into(corr_ref, row, base_ref[0], refs[n], out_ref, n == 0)
            row = row + refs[n].shape[0]

    return kernel


def make_mix_rest(sources, final):
    parts = len(sources)

    def kernel(corr_ref, base_ref, origin_ref, acc_ref, *refs):
        field_refs = refs[:parts]
        if final:
            gram_ref, steps_ref, grads_ref, out_ref, message_ref, rows_ref = refs[parts:]
        else:
            (out_ref,) = refs[parts:]
        out_ref[...] = acc_ref[...]
        for (shift, offset), field_ref in zip(sources, field_refs):
            mix_into(corr_ref, origin_ref[shift] + offset, base_ref[0], field_ref, out_ref, False)
        if not final:
            return
        _, steps, rows, cols = steps_ref.shape

        def body(step, sums):
            sums = list(sums)
            for c in range(0, cols, LANE):
                for r in range(0, rows, 2 * SUB):
                    where = (step, pl.ds(r, 2 * SUB), pl.ds(c, LANE))
                    half = out_ref[where].astype(jnp.bfloat16).astype(jnp.float32)
                    for n in range(NPROJ):
                        source = steps_ref if n < PAIRS else grads_ref
                        product = source[(n % PAIRS, *where)].astype(jnp.float32) * half
                        sums[n] = sums[n] + (product[:SUB] + product[SUB:])
            return tuple(sums)

        zero = jnp.zeros((SUB, LANE), jnp.float32)
        sums = lax.fori_loop(0, steps, body, (zero,) * NPROJ)
        rows_ref[0:NGRAM, :] = gram_ref[...]
        for n in range(NPROJ):
            rows_ref[NGRAM + n:NGRAM + n + 1, :] = jnp.sum(sums[n], axis=0, keepdims=True)
        lane, row = lane_index(), row_index()
        total = zero
        for first in range(0, NROW, SUB):
            summed = jnp.sum(rows_ref[first:first + SUB, :], axis=1, keepdims=True)
            total = total + jnp.where(lane == row + first, summed, 0.0)
        message = jnp.sum(total, axis=0, keepdims=True)
        message_ref[...] = jnp.broadcast_to(message[None], message_ref.shape)

    return kernel


def final_kernel(inbox_ref, mixed_ref, control_ref, steps_ref, grads_ref, out_ref, rows_ref):
    totals = jnp.sum(inbox_ref[...], axis=0)
    lane, row = lane_index(), row_index()
    spread = jnp.broadcast_to(totals, (SUB, LANE))
    for first in range(0, NROW, SUB):
        picked = jnp.where(lane == row + first, spread, 0.0)
        rows_ref[first:first + SUB, :] = jnp.broadcast_to(jnp.sum(picked, axis=1, keepdims=True), (SUB, LANE))

    def entry(k):
        return jnp.broadcast_to(rows_ref[k:k + 1, :], (SUB, LANE))

    cross = {pair: entry(k) for pair, k in WHERE.items()}

    def square(i, j):
        return entry(NSYM + WHERE[(min(i, j), max(i, j))])

    gamma = cross[(PAIRS - 1, PAIRS - 1)] / square(PAIRS - 1, PAIRS - 1)
    first = [None] * PAIRS
    for i in reversed(range(PAIRS)):
        rest = entry(NGRAM + i)
        for j in reversed(range(i + 1, PAIRS)):
            rest = rest - cross[(i, j)] * first[j]
        first[i] = rest / cross[(i, i)]
    second = [None] * PAIRS
    for i in range(PAIRS):
        inner = -entry(NGRAM + PAIRS + i)
        for j in range(PAIRS):
            inner = inner + square(i, j) * first[j]
        rest = cross[(i, i)] * first[i] + gamma * inner
        for j in range(i):
            rest = rest - cross[(j, i)] * second[j]
        second[i] = rest / cross[(i, i)]
    scaled = [gamma * value for value in first]

    _, steps, rows, cols = steps_ref.shape

    def body(step, carry):
        for c in range(0, cols, LANE):
            for r in range(0, rows, 2 * SUB):
                where = (step, pl.ds(r, 2 * SUB), pl.ds(c, LANE))
                mixed = mixed_ref[where]
                control = control_ref[where]
                update = [gamma * mixed[:SUB], gamma * mixed[SUB:]]
                for i in range(PAIRS):
                    s = steps_ref[(i, *where)].astype(jnp.float32)
                    y = grads_ref[(i, *where)].astype(jnp.float32)
                    for part, cut in enumerate((slice(0, SUB), slice(SUB, 2 * SUB))):
                        update[part] = update[part] + (second[i] * s[cut] - scaled[i] * y[cut])
                out_ref[step, pl.ds(r, SUB), pl.ds(c, LANE)] = control[:SUB] - update[0]
                out_ref[step, pl.ds(r + SUB, SUB), pl.ds(c, LANE)] = control[SUB:] - update[1]
        return carry

    lax.fori_loop(0, steps, body, 0)


def local(gradient, control, diffusivity, land_mask, time_corr, pair_steps, pair_grads):
    steps, rows, cols = gradient.shape
    height, breadth, groups = (lax.axis_size(axis) for axis in ("lat", "lon", "tm"))
    mine = lax.axis_index("tm")
    base = (mine * steps).reshape(1).astype(jnp.int32)
    origin = (lax.rem(mine - jnp.arange(groups, dtype=jnp.int32) + groups, groups) * steps).astype(jnp.int32)
    down = [(i, i + 1) for i in range(height - 1)]
    up = [(i + 1, i) for i in range(height - 1)]
    right = [(i, (i + 1) % breadth) for i in range(breadth)]
    left = [(j, i) for i, j in right]

    packed_width = -(-(steps + 1) // PER) * LANE
    masked, first, last, west, east = call(
        pack_kernel,
        (f32(steps, rows, cols), f32(steps + 1, SUB, cols), f32(steps + 1, SUB, cols), f32(rows, packed_width), f32(rows, packed_width)),
        (gradient, land_mask, diffusivity),
        name="pack",
    )
    from_left = lax.ppermute(east, "lon", right)
    from_right = lax.ppermute(west, "lon", left)
    above = lax.ppermute(last, "lat", down)
    below = lax.ppermute(first, "lat", up)
    corners_up = jnp.concatenate([from_left[:SUB], from_right[:SUB]], axis=0)
    corners_down = jnp.concatenate([from_left[rows - SUB:], from_right[rows - SUB:]], axis=0)
    above_sides = lax.ppermute(corners_down, "lat", down)
    below_sides = lax.ppermute(corners_up, "lat", up)

    gram = call(gram_kernel, f32(NGRAM, LANE), (pair_steps, pair_grads), name="gram")

    chunk = steps // CHUNKS
    own, other = [], []
    for n in range(CHUNKS):
        width = cols // LANE + 1
        field = call(
            make_sweep_kernel(n * chunk, chunk),
            f32(chunk, rows, cols),
            (masked, diffusivity, above, below, from_left, from_right, above_sides, below_sides),
            scratch=[pltpu.VMEM(((rows // SUB + 2) * width * 5, SUB, LANE), jnp.float32)],
            name="sweeps",
        )
        own.append(field)
        for shift in range(1, groups):
            pairs = [(i, (i + shift) % groups) for i in range(groups)]
            other.append((shift, n * chunk, lax.ppermute(field, "tm", pairs)))
    mixed = call(
        make_mix_own(CHUNKS), f32(steps, rows, cols), (time_corr, base, *own),
        specs=[SMEM, SMEM] + [VMEM] * CHUNKS, name="mix_own",
    )
    early, late = other[:-1], other[-1:]
    if early:
        mixed = call(
            make_mix_rest([(s, o) for s, o, _ in early], False), f32(steps, rows, cols),
            (time_corr, base, origin, mixed, *(v for _, _, v in early)),
            specs=[SMEM, SMEM, SMEM] + [VMEM] * (1 + len(early)), name="mix_early",
        )
    devices = height * breadth * groups
    mixed, message = call(
        make_mix_rest([(s, o) for s, o, _ in late], True), (f32(steps, rows, cols), f32(devices, 1, LANE)),
        (time_corr, base, origin, mixed, *(v for _, _, v in late), gram, pair_steps, pair_grads),
        specs=[SMEM, SMEM, SMEM] + [VMEM] * (4 + len(late)),
        scratch=[pltpu.VMEM((NROW, LANE), jnp.float32)], name="mix_late",
    )
    inbox = lax.all_to_all(message, ("lat", "lon", "tm"), split_axis=0, concat_axis=0, tiled=True)
    return call(
        final_kernel, f32(steps, rows, cols), (inbox, mixed, control, pair_steps, pair_grads),
        scratch=[pltpu.VMEM((NROW, LANE), jnp.float32)], name="final",
    )


def solution(mesh):
    placed = (
        P("tm", "lat", "lon"),
        P("tm", "lat", "lon"),
        P("lat", "lon"),
        P("lat", "lon"),
        P(),
        P(None, "tm", "lat", "lon"),
        P(None, "tm", "lat", "lon"),
    )
    return jax.shard_map(
        local, mesh=mesh, in_specs=placed, out_specs=P("tm", "lat", "lon"), check_vma=False
    )
```

time: 238 us -> 66.7 us (0.28)
  waiting for transfers between devices: 65.4 us -> 1.71 us
  between operations: 36.8 us -> 0.2 us
  starting transfers between devices: 48.3 us -> 16.6 us
  Pallas kernels: 0 us -> 29.1 us
  other arithmetic: 28.8 us -> 0.02 us
  blocking collectives: 39.6 us -> 13.7 us
  matrix products: 10.4 us -> 0 us
  local copies, waits for them, and re-layouts: 7.86 us -> 4.83 us
    ppermute x28 -> x8, waiting for transfers between devices: 55.1 us -> 1.71 us  [the longest x1 1.69 us: local(): below_sides = lax.ppermute(corners_up, 'lat', up)]
    psum x1 -> x0, blocking collectives: 39.6 us -> none  [local(): lax.psum((lax.dot_general(flat_steps, flat_grads, dims, preferred_element...]
    pallas_call x0 -> x8, Pallas kernels: none -> 29.1 us  [call(): pl.pallas_call(kernel, out_shape=outs, in_specs=specs or [VMEM] * len(arg...]
    ppermute x28 -> x8, starting transfers between devices: 41.1 us -> 16.6 us  [the longest x1 5.18 us: local(): above_sides = lax.ppermute(corners_down, 'lat', down)]
    all_to_all x0 -> x1, blocking collectives: none -> 13.7 us  [local(): lax.all_to_all(message, ('lat', 'lon', 'tm'), split_axis=0, concat_axis=0...]
    dot_general x6 -> x0, matrix products: 10.4 us -> none  [the longest x1 3.79 us: local(): lax.dot_general(flat_steps, flat_grads, dims, preferred_element_type=jnp....]
    all_to_all x2 -> x0, waiting for transfers between devices: 10.2 us -> none  [the longest x1 5.53 us: local(): lax.all_to_all(mixed, 'tm', split_axis=0, concat_axis=1, tiled=True)]
    reduce_sum x15 -> x0, other arithmetic: 9.62 us -> none  [the longest x8 5.2 us: solve_upper(): remainder = target[position] - jnp.sum(upper[position] * result)]
  transfers between devices with their start and end apart: 30 -> 8, of which waited for: 23 -> 1; matrix products, arithmetic and copies ran while one was open for 3% -> 0% of each run, Pallas kernels for 0% -> 24%
where the time goes in v1:
time: 66.7 us; the launch traced here: 66.2 us
  Pallas kernels  29.1 us (44%)
  starting transfers between devices  16.6 us (25%)
  blocking collectives  13.7 us (21%)
  local copies, waits for them, and re-layouts  4.83 us (7%)
  waiting for transfers between devices  1.71 us (3%)
    pallas_call x8, Pallas kernels, call(): pl.pallas_call(kernel, out_shape=outs, in_specs=specs or [VMEM] * len(arg...  29.1 us
    all_to_all x1, blocking collectives, local(): lax.all_to_all(message, ('lat', 'lon', 'tm'), split_axis=0, concat_axis=0...  13.7 us
    ppermute x1, starting transfers between devices, local(): above_sides = lax.ppermute(corners_down, 'lat', down)  5.18 us
    unnamed x18, local copies, waits for them, and re-layouts  4.82 us
    ppermute x1, starting transfers between devices, local(): above = lax.ppermute(last, 'lat', down)  4.2 us
    ppermute x2, starting transfers between devices, local(): other.append((shift, n * chunk, lax.ppermute(field, 'tm', pairs)))  2.16 us
    ppermute x1, starting transfers between devices, local(): from_right = lax.ppermute(west, 'lon', left)  2.02 us
    ppermute x1, waiting for transfers between devices, local(): below_sides = lax.ppermute(corners_up, 'lat', up)  1.69 us
  transfers between devices with their start and end apart: 8, of which 1 were waited for; matrix products, arithmetic and copies ran while one was open for 0% of the time, Pallas kernels for 24%

profile of v1, /device:TPU:0, one launch (start us, length us, event | category | flops | bytes accessed | tf_op | source)
XLA Modules:
  0.0 66.2 jit_solution(12089018569364111954)
XLA Ops:
  0.0 1.2 %copy-done.4 = f32[28,16,256]{2,1,0:T(8,128)S(1)} copy-done((f32[28,16,256]{2,1,0:T(8,128)S(1)}, f32[28,16,256]{2,1,0:T(8,128)}, u32[]{:S(2)}) %copy-start.4) | copy-done | bytes 458776
  1.2 0.7 %copy-done.6 = f32[16,256]{1,0:T(8,128)S(1)} copy-done((f32[16,256]{1,0:T(8,128)S(1)}, f32[16,256]{1,0:T(8,128)}, u32[]{:S(2)}) %copy-start.6) | copy-done | bytes 16408
  1.9 0.7 %copy-done.8 = s32[16,256]{1,0:T(8,128)S(1)} copy-done((s32[16,256]{1,0:T(8,128)S(1)}, s32[16,256]{1,0:T(8,128)}, u32[]{:S(2)}) %copy-start.8) | copy-done | bytes 16408
  2.6 0.2 pack.1
  2.8 0.5 collective-permute-start.2
  3.3 2.0 %collective-permute-start.3 = (f32[16,256]{1,0:T(8,128)S(1)}, f32[16,256]{1,0:T(8,128)S(1)}, u32[]{:S(2)}, u32[]{:S(2)}) collective-permute-start(f32[16,256]{1,0:T(8,128)S(1)} %get-tuple-element.16), channel_id=1, source_target_pairs={{2,0},{4,2},{6,4},{0,6},{3,1},{5,3},{7,5},{1,7},{10,8},{12,10},{14... | collective-permute-start | bytes 49160 | tf_op jit(solution)/shard_map/ppermute | solution.py:332
  5.3 4.2 %collective-permute-start = (f32[29,8,256]{2,1,0:T(8,128)S(1)}, f32[29,8,256]{2,1,0:T(8,128)S(1)}, u32[]{:S(2)}, u32[]{:S(2)}) collective-permute-start(f32[29,8,256]{2,1,0:T(8,128)S(1)} %get-tuple-element.13), channel_id=1, source_target_pairs={{0,8},{8,16},{16,24},{1,9},{9,17},{17,25},{2,10},{10,18},{18,26},{... | collective-permute-start | bytes 712712 | tf_op jit(solution)/shard_map/ppermute | solution.py:333
  9.5 1.3 %collective-permute-start.1 = (f32[29,8,256]{2,1,0:T(8,128)S(1)}, f32[29,8,256]{2,1,0:T(8,128)S(1)}, u32[]{:S(2)}, u32[]{:S(2)}) collective-permute-start(f32[29,8,256]{2,1,0:T(8,128)S(1)} %get-tuple-element.14), channel_id=1, source_target_pairs={{8,0},{16,8},{24,16},{9,1},{17,9},{25,17},{10,2},{18,10},{26,18},{... | collective-permute-start | bytes 712712 | tf_op jit(solution)/shard_map/ppermute | solution.py:334
  10.9 1.3 %collective-permute-start.5 = (f32[16,256]{1,0:T(8,128)S(1)}, f32[16,256]{1,0:T(8,128)S(1)}, u32[]{:S(2)}, u32[]{:S(2)}) collective-permute-start(f32[16,256]{1,0:T(8,128)S(1)} %pad_maximum_fusion.1), channel_id=1, source_target_pairs={{8,0},{16,8},{24,16},{9,1},{17,9},{25,17},{10,2},{18,10},{26,18},{... | collective-permute-start | bytes 49160 | tf_op jit(solution)/shard_map/ppermute | solution.py:338
  12.2 5.2 %collective-permute-start.4 = (f32[16,256]{1,0:T(8,128)S(1)}, f32[16,256]{1,0:T(8,128)S(1)}, u32[]{:S(2)}, u32[]{:S(2)}) collective-permute-start(f32[16,256]{1,0:T(8,128)S(1)} %pad_maximum_fusion), channel_id=1, source_target_pairs={{0,8},{8,16},{16,24},{1,9},{9,17},{17,25},{2,10},{10,18},{18,26},{... | collective-permute-start | bytes 49160 | tf_op jit(solution)/shard_map/ppermute | solution.py:337
  17.4 1.7 %collective-permute-done.5.down_ref = f32[16,256]{1,0:T(8,128)S(1)} collective-permute-done((f32[16,256]{1,0:T(8,128)S(1)}, f32[16,256]{1,0:T(8,128)S(1)}, u32[]{:S(2)}, u32[]{:S(2)}) %collective-permute-start.5) | collective-permute-done | bytes 16416 | tf_op jit(solution)/shard_map/ppermute | solution.py:338
  19.1 0.0 copy-start.7
  19.1 0.7 %copy-done.7 = f32[16,256]{1,0:T(8,128)S(1)} copy-done((f32[16,256]{1,0:T(8,128)S(1)}, f32[16,256]{1,0:T(8,128)}, u32[]{:S(2)}) %copy-start.7) | copy-done | bytes 16408
  19.8 7.7 %sweeps.2.refs_0_ = f32[14,16,256]{2,1,0:T(8,128)S(1)} custom-call(f32[28,16,256]{2,1,0:T(8,128)S(1)} %get-tuple-element.12.masked_ref, f32[16,256]{1,0:T(8,128)S(1)} %copy-done.7, f32[29,8,256]{2,1,0:T(8,128)S(1)} %collective-permute-done.above_ref, f32[29,8,256]{2,1,0:T(8,128)S(1)} %collective-permute-done.1.below_ref, ...), custom_call_target="tpu_custom_call" | custom-call | tf_op jit(solution)/shard_map/sweeps/pallas_call | solution.py:33
  27.5 1.6 %collective-permute-start.6 = (f32[14,16,256]{2,1,0:T(8,128)S(1)}, f32[14,16,256]{2,1,0:T(8,128)S(1)}, u32[]{:S(2)}, u32[]{:S(2)}) collective-permute-start(f32[14,16,256]{2,1,0:T(8,128)S(1)} %sweeps.2.refs_0_), channel_id=1, source_target_pairs={{0,1},{1,0},{2,3},{3,2},{4,5},{5,4},{6,7},{7,6},{8,9},{9,8},{10,11... | collective-permute-start | bytes 688136 | tf_op jit(solution)/shard_map/ppermute | solution.py:356
  29.1 7.7 %sweeps.3.refs_1_ = f32[14,16,256]{2,1,0:T(8,128)S(1)} custom-call(f32[28,16,256]{2,1,0:T(8,128)S(1)} %get-tuple-element.12.masked_ref, f32[16,256]{1,0:T(8,128)S(1)} %copy-done.7, f32[29,8,256]{2,1,0:T(8,128)S(1)} %collective-permute-done.above_ref, f32[29,8,256]{2,1,0:T(8,128)S(1)} %collective-permute-done.1.below_ref, ...), custom_call_target="tpu_custom_call" | custom-call | tf_op jit(solution)/shard_map/sweeps/pallas_call | solution.py:33
  36.8 0.6 collective-permute-start.7
  37.4 1.5 %copy-done.1 = bf16[8,28,16,256]{3,2,1,0:T(8,128)(2,1)S(1)} copy-done((bf16[8,28,16,256]{3,2,1,0:T(8,128)(2,1)S(1)}, bf16[8,28,16,256]{3,2,1,0:T(8,128)(2,1)}, u32[]{:S(2)}) %copy-start.1) | copy-done | bytes 1835032
  38.9 3.4 %gram.1.refs_1_ = f32[72,128]{1,0:T(8,128)S(1)} custom-call(bf16[8,28,16,256]{3,2,1,0:T(8,128)(2,1)S(1)} %copy-done, bf16[8,28,16,256]{3,2,1,0:T(8,128)(2,1)S(1)} %copy-done.1), custom_call_target="tpu_custom_call" | custom-call | tf_op jit(solution)/shard_map/gram/pallas_call | solution.py:33
  42.4 3.0 %mix_own.1.acc_ref = f32[28,16,256]{2,1,0:T(8,128)S(1)} custom-call(f32[56,56]{1,0:T(8,128)S(1)} %copy-done.5, s32[1]{0:T(128)} %bitcast.base_ref, f32[14,16,256]{2,1,0:T(8,128)S(1)} %sweeps.2.refs_0_, f32[14,16,256]{2,1,0:T(8,128)S(1)} %sweeps.3.refs_1_), custom_call_target="tpu_custom_call" | custom-call | tf_op jit(solution)/shard_map/mix_own/pallas_call | solution.py:33
  45.4 2.0 %mix_early.1.acc_ref = f32[28,16,256]{2,1,0:T(8,128)S(1)} custom-call(f32[56,56]{1,0:T(8,128)S(1)} %copy-done.5, s32[1]{0:T(128)} %bitcast.base_ref, s32[2]{0:T(128)S(1)} %fusion.1.origin_ref, f32[28,16,256]{2,1,0:T(8,128)S(1)} %mix_own.1.acc_ref, f32[14,16,256]{2,1,0:T(8,128)S(1)} %collective-permute-done.6.refs_0_), custom_call_target="tpu_custom_call" | custom-call | tf_op jit(solution)/shard_map/mix_early/pallas_call | solution.py:33
  47.4 3.1 %mix_late.1 = (f32[28,16,256]{2,1,0:T(8,128)S(1)}, f32[32,1,128]{2,1,0:T(1,128)S(1)}) custom-call(f32[56,56]{1,0:T(8,128)S(1)} %copy-done.5, s32[1]{0:T(128)} %bitcast.base_ref, s32[2]{0:T(128)S(1)} %fusion.1.origin_ref, f32[28,16,256]{2,1,0:T(8,128)S(1)} %mix_early.1.acc_ref, f32[14,16,256]{2,1,0:T(8,128)S(1)} %collective-permute-done.7.refs_0_, ...), custom_call_target="tpu_custom_call" | custom-call | tf_op jit(solution)/shard_map/mix_late/pallas_call | solution.py:33
  50.6 13.7 %all_to_all.5.inbox_ref = f32[32,1,128]{2,1,0:T(1,128)S(1)} all-to-all(f32[32,1,128]{2,1,0:T(1,128)S(1)} %get-tuple-element.17), channel_id=1, replica_groups=mesh['lat'=4,'lon'=4,'tm'=2] {'lat','lon','tm'}, dimensions={0} | all-to-all | bytes 32768 | tf_op jit(solution)/shard_map/all_to_all | solution.py:375
  64.3 1.9 %final.1 = f32[28,16,256]{2,1,0:T(8,128)} custom-call(f32[32,1,128]{2,1,0:T(1,128)S(1)} %all_to_all.5.inbox_ref, f32[28,16,256]{2,1,0:T(8,128)S(1)} %get-tuple-element.18.mixed_ref, f32[28,16,256]{2,1,0:T(8,128)S(1)} %copy-done.3, bf16[8,28,16,256]{3,2,1,0:T(8,128)(2,1)S(1)} %copy-done, bf16[8,28,16,256]{3,2,1,0:T(8,128)(2,1)S(1)} %copy-done.2), custom_call_target="tpu_custom_call" | custom-call | tf_op jit(solution)/shard_map/final/pallas_call | solution.py:33
  (24 shorter events, 0.1 us)
Async XLA Ops:
  0.0 37.4 %copy-start = (bf16[8,28,16,256]{3,2,1,0:T(8,128)(2,1)S(1)}, bf16[8,28,16,256]{3,2,1,0:T(8,128)(2,1)}, u32[]{:S(2)}) copy-start(bf16[8,28,16,256]{3,2,1,0:T(8,128)(2,1)} %steps_ref.3) | copy-start | bytes 5505028
  0.0 1.2 %copy-start.4 = (f32[28,16,256]{2,1,0:T(8,128)S(1)}, f32[28,16,256]{2,1,0:T(8,128)}, u32[]{:S(2)}) copy-start(f32[28,16,256]{2,1,0:T(8,128)} %grad_ref.1) | copy-start | bytes 1376260
  1.2 0.7 %copy-start.6 = (f32[16,256]{1,0:T(8,128)S(1)}, f32[16,256]{1,0:T(8,128)}, u32[]{:S(2)}) copy-start(f32[16,256]{1,0:T(8,128)} %diff_ref.5) | copy-start | bytes 49156
  1.9 0.7 %copy-start.8 = (s32[16,256]{1,0:T(8,128)S(1)}, s32[16,256]{1,0:T(8,128)}, u32[]{:S(2)}) copy-start(s32[16,256]{1,0:T(8,128)} %mask_ref.1) | copy-start | bytes 49156
  2.8 8.0 %collective-permute-start.2 = (f32[16,256]{1,0:T(8,128)S(1)}, f32[16,256]{1,0:T(8,128)S(1)}, u32[]{:S(2)}, u32[]{:S(2)}) collective-permute-start(f32[16,256]{1,0:T(8,128)S(1)} %get-tuple-element.15), channel_id=1, source_target_pairs={{0,2},{2,4},{4,6},{6,0},{1,3},{3,5},{5,7},{7,1},{8,10},{10,12},{12... | collective-permute-start | bytes 49160 | tf_op jit(solution)/shard_map/ppermute | solution.py:331
  3.3 7.6 %collective-permute-start.3 = (f32[16,256]{1,0:T(8,128)S(1)}, f32[16,256]{1,0:T(8,128)S(1)}, u32[]{:S(2)}, u32[]{:S(2)}) collective-permute-start(f32[16,256]{1,0:T(8,128)S(1)} %get-tuple-element.16), channel_id=1, source_target_pairs={{2,0},{4,2},{6,4},{0,6},{3,1},{5,3},{7,5},{1,7},{10,8},{12,10},{14... | collective-permute-start | bytes 49160 | tf_op jit(solution)/shard_map/ppermute | solution.py:332
  5.3 13.8 %collective-permute-start = (f32[29,8,256]{2,1,0:T(8,128)S(1)}, f32[29,8,256]{2,1,0:T(8,128)S(1)}, u32[]{:S(2)}, u32[]{:S(2)}) collective-permute-start(f32[29,8,256]{2,1,0:T(8,128)S(1)} %get-tuple-element.13), channel_id=1, source_target_pairs={{0,8},{8,16},{16,24},{1,9},{9,17},{17,25},{2,10},{10,18},{18,26},{... | collective-permute-start | bytes 712712 | tf_op jit(solution)/shard_map/ppermute | solution.py:333
  9.5 9.6 %collective-permute-start.1 = (f32[29,8,256]{2,1,0:T(8,128)S(1)}, f32[29,8,256]{2,1,0:T(8,128)S(1)}, u32[]{:S(2)}, u32[]{:S(2)}) collective-permute-start(f32[29,8,256]{2,1,0:T(8,128)S(1)} %get-tuple-element.14), channel_id=1, source_target_pairs={{8,0},{16,8},{24,16},{9,1},{17,9},{25,17},{10,2},{18,10},{26,18},{... | collective-permute-start | bytes 712712 | tf_op jit(solution)/shard_map/ppermute | solution.py:334
  10.9 8.2 %collective-permute-start.5 = (f32[16,256]{1,0:T(8,128)S(1)}, f32[16,256]{1,0:T(8,128)S(1)}, u32[]{:S(2)}, u32[]{:S(2)}) collective-permute-start(f32[16,256]{1,0:T(8,128)S(1)} %pad_maximum_fusion.1), channel_id=1, source_target_pairs={{8,0},{16,8},{24,16},{9,1},{17,9},{25,17},{10,2},{18,10},{26,18},{... | collective-permute-start | bytes 49160 | tf_op jit(solution)/shard_map/ppermute | solution.py:338
  12.2 6.9 %collective-permute-start.4 = (f32[16,256]{1,0:T(8,128)S(1)}, f32[16,256]{1,0:T(8,128)S(1)}, u32[]{:S(2)}, u32[]{:S(2)}) collective-permute-start(f32[16,256]{1,0:T(8,128)S(1)} %pad_maximum_fusion), channel_id=1, source_target_pairs={{0,8},{8,16},{16,24},{1,9},{9,17},{17,25},{2,10},{10,18},{18,26},{... | collective-permute-start | bytes 49160 | tf_op jit(solution)/shard_map/ppermute | solution.py:337
  19.1 0.7 %copy-start.7 = (f32[16,256]{1,0:T(8,128)S(1)}, f32[16,256]{1,0:T(8,128)}, u32[]{:S(2)}) copy-start(f32[16,256]{1,0:T(8,128)} %diff_ref.5) | copy-start | bytes 49156
  27.5 17.8 %collective-permute-start.6 = (f32[14,16,256]{2,1,0:T(8,128)S(1)}, f32[14,16,256]{2,1,0:T(8,128)S(1)}, u32[]{:S(2)}, u32[]{:S(2)}) collective-permute-start(f32[14,16,256]{2,1,0:T(8,128)S(1)} %sweeps.2.refs_0_), channel_id=1, source_target_pairs={{0,1},{1,0},{2,3},{3,2},{4,5},{5,4},{6,7},{7,6},{8,9},{9,8},{10,11... | collective-permute-start | bytes 688136 | tf_op jit(solution)/shard_map/ppermute | solution.py:356
  36.8 10.6 %collective-permute-start.7 = (f32[14,16,256]{2,1,0:T(8,128)S(1)}, f32[14,16,256]{2,1,0:T(8,128)S(1)}, u32[]{:S(2)}, u32[]{:S(2)}) collective-permute-start(f32[14,16,256]{2,1,0:T(8,128)S(1)} %sweeps.3.refs_1_), channel_id=1, source_target_pairs={{0,1},{1,0},{2,3},{3,2},{4,5},{5,4},{6,7},{7,6},{8,9},{9,8},{10,11... | collective-permute-start | bytes 688136 | tf_op jit(solution)/shard_map/ppermute | solution.py:356
  37.4 1.5 %copy-start.1 = (bf16[8,28,16,256]{3,2,1,0:T(8,128)(2,1)S(1)}, bf16[8,28,16,256]{3,2,1,0:T(8,128)(2,1)}, u32[]{:S(2)}) copy-start(bf16[8,28,16,256]{3,2,1,0:T(8,128)(2,1)} %grads_ref.3) | copy-start | bytes 5505028
  38.9 3.5 %copy-start.5 = (f32[56,56]{1,0:T(8,128)S(1)}, f32[56,56]{1,0:T(8,128)}, u32[]{:S(2)}) copy-start(f32[56,56]{1,0:T(8,128)} %corr_ref.5) | copy-start | bytes 37636
  42.3 5.1 %copy-start.2 = (bf16[8,28,16,256]{3,2,1,0:T(8,128)(2,1)S(1)}, bf16[8,28,16,256]{3,2,1,0:T(8,128)(2,1)}, u32[]{:S(2)}) copy-start(bf16[8,28,16,256]{3,2,1,0:T(8,128)(2,1)} %grads_ref.3) | copy-start | bytes 5505028
  47.4 16.9 %copy-start.3 = (f32[28,16,256]{2,1,0:T(8,128)S(1)}, f32[28,16,256]{2,1,0:T(8,128)}, u32[]{:S(2)}) copy-start(f32[28,16,256]{2,1,0:T(8,128)} %control_ref.1) | copy-start | bytes 1376260

commit v2 on v1

v2 whole, which is shorter than its diff:
```python
import functools
import jax
import jax.numpy as jnp
from jax import lax
from jax.experimental import pallas as pl
from jax.experimental.pallas import tpu as pltpu
from jax.sharding import PartitionSpec as P

PAIRS = 8
SWEEPS = 6
SUB = 8
LANE = 128
HALO = SWEEPS
GROUP = 8
PER = LANE // GROUP
CROSS = [(i, j) for i in range(PAIRS) for j in range(i, PAIRS)]
NSYM = len(CROSS)
WHERE = {pair: k for k, pair in enumerate(CROSS)}
NGRAM = 2 * NSYM
NPROJ = 2 * PAIRS
NROW = NGRAM + NPROJ

VMEM = pl.BlockSpec(memory_space=pltpu.VMEM)
HBM = pl.BlockSpec(memory_space=pl.ANY)
PARAMS = pltpu.CompilerParams(vmem_limit_bytes=48 * 1024 * 1024)


def f32(*shape):
    return jax.ShapeDtypeStruct(shape, jnp.float32)


def call(kernel, outs, args, specs=None, scratch=(), name=None):
    single = not isinstance(outs, (tuple, list))
    return pl.pallas_call(
        kernel,
        out_shape=outs,
        in_specs=specs or [VMEM] * len(args),
        out_specs=VMEM if single else [VMEM] * len(outs),
        scratch_shapes=list(scratch),
        compiler_params=PARAMS,
        name=name,
    )(*args)


def lane_index():
    return lax.broadcasted_iota(jnp.int32, (SUB, LANE), 1)


def row_index():
    return lax.broadcasted_iota(jnp.int32, (SUB, LANE), 0)


def gram_kernel(steps_ref, grads_ref, out_ref):
    _, steps, rows, cols = steps_ref.shape
    for half, left_ref in enumerate((steps_ref, grads_ref)):
        def body(step, sums):
            sums = list(sums)
            for c in range(0, cols, LANE):
                for r in range(0, rows, 2 * SUB):
                    where = (step, pl.ds(r, 2 * SUB), pl.ds(c, LANE))
                    right = [grads_ref[(i, *where)].astype(jnp.float32) for i in range(PAIRS)]
                    left = right if half else [left_ref[(i, *where)].astype(jnp.float32) for i in range(PAIRS)]
                    for part in range(2):
                        cut = slice(part * SUB, (part + 1) * SUB)
                        for k, (i, j) in enumerate(CROSS):
                            sums[k] = sums[k] + left[i][cut] * right[j][cut]
            return tuple(sums)

        zero = jnp.zeros((SUB, LANE), jnp.float32)
        sums = lax.fori_loop(0, steps, body, (zero,) * NSYM)
        for k in range(NSYM):
            out_ref[half * NSYM + k:half * NSYM + k + 1, :] = jnp.sum(sums[k], axis=0, keepdims=True)


def groups_of(steps):
    return [(begin, min(SUB, steps - begin)) for begin in range(0, steps, SUB)]


def slots_of(steps):
    return -(-(steps + 1) // SUB) * SUB


def pack_kernel(grad_hbm, mask_hbm, diff_hbm, field_ref, first_ref, last_ref, grad_ref, mask_ref, diff_ref, turn_ref, sems):
    steps, rows, cols = grad_ref.shape
    slots = field_ref.shape[1]
    copies = [
        pltpu.make_async_copy(mask_hbm, mask_ref, sems.at[0]),
        pltpu.make_async_copy(diff_hbm, diff_ref, sems.at[1]),
        pltpu.make_async_copy(grad_hbm, grad_ref, sems.at[2]),
    ]
    for copy in copies:
        copy.start()
    for copy in copies:
        copy.wait()
    zero = jnp.zeros((SUB, LANE), jnp.float32)
    for c in range(cols // LANE):
        across = slice(c * LANE, (c + 1) * LANE)
        for r in range(rows // SUB):
            down = slice(r * SUB, (r + 1) * SUB)
            base = (c * (rows // SUB) + r) * slots * SUB
            mask = mask_ref[down, across].astype(jnp.float32)
            for slot in range(slots):
                if slot < steps:
                    value = grad_ref[slot, down, across] * mask
                else:
                    value = diff_ref[down, across] if slot == steps else zero
                turn_ref[base + slot * SUB:base + (slot + 1) * SUB, :] = value
    for c in range(cols // LANE):
        across = slice(c * LANE, (c + 1) * LANE)
        for row in range(rows):
            base = (c * (rows // SUB) + row // SUB) * slots * SUB + row % SUB
            for slot in range(0, slots, SUB):
                value = turn_ref[pl.ds(base + slot * SUB, SUB, stride=SUB), :]
                field_ref[row, slot:slot + SUB, across] = value
                if row < HALO:
                    first_ref[row, slot:slot + SUB, across] = value
                if row >= rows - HALO:
                    last_ref[row - (rows - HALO), slot:slot + SUB, across] = value


def extended(row, above_ref, field_ref, below_ref):
    rows = field_ref.shape[0]
    if row < HALO:
        return above_ref, row
    if row < HALO + rows:
        return field_ref, row - HALO
    return below_ref, row - HALO - rows


def side_kernel(above_ref, field_ref, below_ref, order_ref, west_ref, east_ref):
    rows, slots, cols = field_ref.shape
    lane = lane_index()
    for slot in range(0, slots, SUB):
        down = slice(slot, slot + SUB)
        for base in range(0, rows + 2 * HALO, PER):
            west = east = jnp.zeros((SUB, LANE), jnp.float32)
            for row in range(base, min(base + PER, rows + 2 * HALO)):
                ref, at = extended(row, above_ref, field_ref, below_ref)
                begin = (row - base) * GROUP
                here = (lane >= begin) & (lane < begin + GROUP)
                left = ref[at, down, 0:LANE]
                right = ref[at, down, cols - LANE:cols]
                west = jnp.where(here, pltpu.roll(left, begin, 1) if begin else left, west)
                turn = (begin + GROUP) % LANE
                east = jnp.where(here, pltpu.roll(right, turn, 1) if turn else right, east)
            place = slice(base // PER * LANE, (base // PER + 1) * LANE)
            west_ref[down, place] = west
            east_ref[down, place] = east


def make_row_loader(above_ref, field_ref, below_ref, left_ref, right_ref):
    cols = field_ref.shape[2]
    lane = lane_index()

    def load(row, down, size):
        ref, at = extended(row, above_ref, field_ref, below_ref)
        place = slice(row // PER * LANE, (row // PER + 1) * LANE)
        begin = row % PER * GROUP
        tiles = [ref[at, down, c * LANE:(c + 1) * LANE] for c in range(cols // LANE)]
        east, west = right_ref[down, place], left_ref[down, place]
        if size == 1:
            tiles = [jnp.broadcast_to(tile, (SUB, LANE)) for tile in tiles]
            east, west = (jnp.broadcast_to(tile, (SUB, LANE)) for tile in (east, west))
        east = pltpu.roll(east, LANE - begin, 1) if begin else east
        turn = (2 * LANE - GROUP - begin) % LANE
        west = pltpu.roll(west, turn, 1) if turn else west
        return tiles + [jnp.where(lane < LANE // 2, east, west)]

    return load


def from_east(tiles, at_end):
    turned = [pltpu.roll(tile, LANE - 1, 1) for tile in tiles]
    return [jnp.where(at_end, turned[(c + 1) % len(tiles)], turned[c]) for c in range(len(tiles))]


def from_west(tiles, at_start):
    turned = [pltpu.roll(tile, 1, 1) for tile in tiles]
    return [jnp.where(at_start, turned[c - 1], turned[c]) for c in range(len(tiles))]


def weight_kernel(above_ref, field_ref, below_ref, left_ref, right_ref, south_ref, east_ref, *, steps):
    rows, _, cols = field_ref.shape
    load = make_row_loader(above_ref, field_ref, below_ref, left_ref, right_ref)
    at_end = lane_index() == LANE - 1
    height = rows + 2 * HALO
    above = None
    for row in range(height):
        kappa = load(row, slice(steps, steps + 1), 1)
        beside = from_east(kappa, at_end)
        for c in range(len(kappa)):
            east_ref[row, :, c * LANE:(c + 1) * LANE] = 0.5 * (kappa[c] + beside[c])
            if above is not None:
                south_ref[row - 1, :, c * LANE:(c + 1) * LANE] = 0.5 * (above[c] + kappa[c])
        above = kappa
    for side, row in enumerate((HALO - 1, HALO + rows)):
        kappa = load(row, slice(steps, steps + 1), 1)
        for c in range(len(kappa)):
            south_ref[height - 1 + side, :, c * LANE:(c + 1) * LANE] = jnp.where(kappa[c] > 0.0, 1.0, 0.0)


def sweep_kernel(above_ref, field_ref, below_ref, left_ref, right_ref, south_ref, east_ref, out_ref, *, begin):
    rows, _, cols = field_ref.shape
    height, width = rows + 2 * HALO, cols // LANE + 1
    count = out_ref.shape[1]
    lane = lane_index()
    at_start, at_end = lane == 0, lane == LANE - 1
    load = make_row_loader(above_ref, field_ref, below_ref, left_ref, right_ref)
    state = [None] * (SWEEPS + 1)

    def at(ref, row, c):
        return ref[row, :, c * LANE:(c + 1) * LANE]

    def feed(sweep, row, tiles):
        if sweep > SWEEPS:
            for c in range(width - 1):
                out_ref[row - HALO, :, c * LANE:(c + 1) * LANE] = tiles[c][:count]
            return
        before = state[sweep]
        if before is None:
            state[sweep] = (tiles, None)
            return
        centre, north = before
        south = [at(south_ref, row - 1, c) * (tiles[c] - centre[c]) for c in range(width)]
        state[sweep] = (tiles, south)
        if north is None:
            return
        ahead = from_east(centre, at_end)
        flux = [at(east_ref, row - 1, c) * (ahead[c] - centre[c]) for c in range(width)]
        behind = from_west(flux, at_start)
        fresh = []
        for c in range(width):
            change = (south[c] - north[c]) + (flux[c] - behind[c])
            if row - 1 < HALO:
                change = change * at(south_ref, height - 1, c)
            if row - 1 >= HALO + rows:
                change = change * at(south_ref, height, c)
            fresh.append(centre[c] + change)
        feed(sweep + 1, row - 1, fresh)

    for row in range(height):
        feed(1, row, load(row, slice(begin, begin + SUB), SUB))


def split_stack(value):
    high = value.astype(jnp.bfloat16).astype(jnp.float32)
    rest = value - high
    middle = rest.astype(jnp.bfloat16).astype(jnp.float32)
    low = rest - middle
    return jnp.concatenate([high, middle, high, low, middle, high], axis=0).astype(jnp.bfloat16)


def corr_stack(time_corr, source, target, count, steps):
    block = lax.dynamic_slice(time_corr, (source, target), (count, steps))
    block = jnp.pad(block, ((0, -count % SUB), (0, 0))).T
    high = lax.reduce_precision(block, 8, 7)
    rest = block - high
    middle = lax.reduce_precision(rest, 8, 7)
    low = rest - middle
    return jnp.concatenate([high, high, middle, high, middle, low], axis=1).astype(jnp.bfloat16)


def mixed_row(row, corr_ref, field_refs):
    parts = []
    for ref in field_refs:
        part = ref[row]
        parts.append(part)
        if -part.shape[0] % SUB:
            parts.append(jnp.zeros((-part.shape[0] % SUB, part.shape[1]), jnp.float32))
    stacked = split_stack(jnp.concatenate(parts, axis=0) if len(parts) > 1 else parts[0])
    return jnp.dot(corr_ref[...], stacked, preferred_element_type=jnp.float32)


def make_mix(first):
    def kernel(*refs):
        *refs, out_ref = refs
        if first:
            corr_ref, *field_refs = refs
        else:
            acc_ref, corr_ref, *field_refs = refs
        for row in range(out_ref.shape[0]):
            total = mixed_row(row, corr_ref, field_refs)
            out_ref[row] = total if first else acc_ref[row] + total

    return kernel


def last_mix_kernel(acc_ref, corr_ref, field_ref, gram_ref, steps_ref, grads_ref, out_ref, message_ref, turn_ref, rows_ref):
    _, steps, rows, cols = steps_ref.shape
    slots = turn_ref.shape[0] // (rows * (cols // LANE))
    for row in range(rows):
        total = acc_ref[row] + mixed_row(row, corr_ref, [field_ref])
        for c in range(cols // LANE):
            base = (c * (rows // SUB) + row // SUB) * slots * SUB + row % SUB
            for begin, count in groups_of(steps):
                turn_ref[pl.ds(base + begin * SUB, count, stride=SUB), :] = total[begin:begin + count, c * LANE:(c + 1) * LANE]

    zero = jnp.zeros((SUB, LANE), jnp.float32)

    def body(step, sums):
        sums = list(sums)
        for c in range(cols // LANE):
            for r in range(0, rows, 2 * SUB):
                where = (step, pl.ds(r, 2 * SUB), pl.ds(c * LANE, LANE))
                halves = []
                for part in range(2):
                    base = (c * (rows // SUB) + r // SUB + part) * slots * SUB
                    halves.append(turn_ref[pl.ds(pl.multiple_of(base + step * SUB, SUB), SUB), :])
                mixed = jnp.concatenate(halves, axis=0)
                out_ref[where] = mixed
                half = mixed.astype(jnp.bfloat16).astype(jnp.float32)
                for n in range(NPROJ):
                    source = steps_ref if n < PAIRS else grads_ref
                    product = source[(n % PAIRS, *where)].astype(jnp.float32) * half
                    sums[n] = sums[n] + (product[:SUB] + product[SUB:])
        return tuple(sums)

    sums = lax.fori_loop(0, steps, body, (zero,) * NPROJ)
    rows_ref[0:NGRAM, :] = gram_ref[...]
    for n in range(NPROJ):
        rows_ref[NGRAM + n:NGRAM + n + 1, :] = jnp.sum(sums[n], axis=0, keepdims=True)
    lane, row = lane_index(), row_index()
    total = zero
    for first in range(0, NROW, SUB):
        summed = jnp.sum(rows_ref[first:first + SUB, :], axis=1, keepdims=True)
        total = total + jnp.where(lane == row + first, summed, 0.0)
    message = jnp.sum(total, axis=0, keepdims=True)
    message_ref[...] = jnp.broadcast_to(message[None], message_ref.shape)


def final_kernel(inbox_ref, mixed_ref, control_ref, steps_ref, grads_ref, out_ref, rows_ref):
    totals = jnp.sum(inbox_ref[...], axis=0)
    lane, row = lane_index(), row_index()
    spread = jnp.broadcast_to(totals, (SUB, LANE))
    for first in range(0, NROW, SUB):
        picked = jnp.where(lane == row + first, spread, 0.0)
        rows_ref[first:first + SUB, :] = jnp.broadcast_to(jnp.sum(picked, axis=1, keepdims=True), (SUB, LANE))

    def entry(k):
        return jnp.broadcast_to(rows_ref[k:k + 1, :], (SUB, LANE))

    cross = {pair: entry(k) for pair, k in WHERE.items()}

    def square(i, j):
        return entry(NSYM + WHERE[(min(i, j), max(i, j))])

    gamma = cross[(PAIRS - 1, PAIRS - 1)] / square(PAIRS - 1, PAIRS - 1)
    first = [None] * PAIRS
    for i in reversed(range(PAIRS)):
        rest = entry(NGRAM + i)
        for j in reversed(range(i + 1, PAIRS)):
            rest = rest - cross[(i, j)] * first[j]
        first[i] = rest / cross[(i, i)]
    second = [None] * PAIRS
    for i in range(PAIRS):
        inner = -entry(NGRAM + PAIRS + i)
        for j in range(PAIRS):
            inner = inner + square(i, j) * first[j]
        rest = cross[(i, i)] * first[i] + gamma * inner
        for j in range(i):
            rest = rest - cross[(j, i)] * second[j]
        second[i] = rest / cross[(i, i)]
    scaled = [gamma * value for value in first]

    _, steps, rows, cols = steps_ref.shape

    def body(step, carry):
        for c in range(0, cols, LANE):
            for r in range(0, rows, 2 * SUB):
                where = (step, pl.ds(r, 2 * SUB), pl.ds(c, LANE))
                mixed = mixed_ref[where]
                control = control_ref[where]
                update = [gamma * mixed[:SUB], gamma * mixed[SUB:]]
                for i in range(PAIRS):
                    s = steps_ref[(i, *where)].astype(jnp.float32)
                    y = grads_ref[(i, *where)].astype(jnp.float32)
                    for part, cut in enumerate((slice(0, SUB), slice(SUB, 2 * SUB))):
                        update[part] = update[part] + (second[i] * s[cut] - scaled[i] * y[cut])
                out_ref[step, pl.ds(r, SUB), pl.ds(c, LANE)] = control[:SUB] - update[0]
                out_ref[step, pl.ds(r + SUB, SUB), pl.ds(c, LANE)] = control[SUB:] - update[1]
        return carry

    lax.fori_loop(0, steps, body, 0)


def local(gradient, control, diffusivity, land_mask, time_corr, pair_steps, pair_grads):
    steps, rows, cols = gradient.shape
    height, breadth, groups = (lax.axis_size(axis) for axis in ("lat", "lon", "tm"))
    mine = lax.axis_index("tm")
    down = [(i, i + 1) for i in range(height - 1)]
    up = [(i + 1, i) for i in range(height - 1)]
    right = [(i, (i + 1) % breadth) for i in range(breadth)]
    left = [(j, i) for i, j in right]
    slots = slots_of(steps)
    turn = pltpu.VMEM((rows * (cols // LANE) * slots, LANE), jnp.float32)

    field, first, last = call(
        pack_kernel,
        (f32(rows, slots, cols), f32(HALO, slots, cols), f32(HALO, slots, cols)),
        (gradient, land_mask, diffusivity),
        specs=[HBM] * 3,
        scratch=[
            pltpu.VMEM((steps, rows, cols), jnp.float32), pltpu.VMEM((rows, cols), jnp.int32),
            pltpu.VMEM((rows, cols), jnp.float32), turn, pltpu.SemaphoreType.DMA((3,)),
        ],
        name="pack",
    )
    above = lax.ppermute(last, "lat", down)
    below = lax.ppermute(first, "lat", up)
    gram = call(gram_kernel, f32(NGRAM, LANE), (pair_steps, pair_grads), name="gram")
    side_shape = f32(slots, -(-(rows + 2 * HALO) // PER) * LANE)
    west, east = call(side_kernel, (side_shape, side_shape), (above, field, below, gram), name="sides")
    from_left = lax.ppermute(east, "lon", right)
    from_right = lax.ppermute(west, "lon", left)
    whole = (above, field, below, from_left, from_right)
    tall, wide = rows + 2 * HALO, cols + LANE
    south, beside = call(
        functools.partial(weight_kernel, steps=steps), (f32(tall + 1, SUB, wide), f32(tall, SUB, wide)), whole, name="weights"
    )
    own, other = [], []
    for begin, count in groups_of(steps):
        part = call(
            functools.partial(sweep_kernel, begin=begin), f32(rows, count, cols), (*whole, south, beside), name="sweeps"
        )
        own.append(part)
        for shift in range(1, groups):
            pairs = [(i, (i + shift) % groups) for i in range(groups)]
            source = lax.rem(mine - shift + groups, groups) * steps + begin
            other.append((corr_stack(time_corr, source, mine * steps, count, steps), lax.ppermute(part, "tm", pairs)))
    mixed = call(
        make_mix(True), f32(rows, steps, cols),
        (corr_stack(time_corr, mine * steps, mine * steps, steps, steps), *own), name="mix_own",
    )
    for corr, part in other[:-1]:
        mixed = call(make_mix(False), f32(rows, steps, cols), (mixed, corr, part), name="mix_more")
    devices = height * breadth * groups
    mixed, message = call(
        last_mix_kernel, (f32(steps, rows, cols), f32(devices, 1, LANE)),
        (mixed, *other[-1], gram, pair_steps, pair_grads),
        scratch=[turn, pltpu.VMEM((NROW, LANE), jnp.float32)], name="mix_last",
    )
    inbox = lax.all_to_all(message, ("lat", "lon", "tm"), split_axis=0, concat_axis=0, tiled=True)
    return call(
        final_kernel, f32(steps, rows, cols), (inbox, mixed, control, pair_steps, pair_grads),
        scratch=[pltpu.VMEM((NROW, LANE), jnp.float32)], name="final",
    )


def solution(mesh):
    placed = (
        P("tm", "lat", "lon"),
        P("tm", "lat", "lon"),
        P("lat", "lon"),
        P("lat", "lon"),
        P(),
        P(None, "tm", "lat", "lon"),
        P(None, "tm", "lat", "lon"),
    )
    return jax.shard_map(
        local, mesh=mesh, in_specs=placed, out_specs=P("tm", "lat", "lon"), check_vma=False
    )
```

time: 66.7 us -> 53.1 us (0.80)
  Pallas kernels: 29.1 us -> 14.8 us
  starting transfers between devices: 16.6 us -> 12.3 us
  waiting for transfers between devices: 1.71 us -> 4.46 us
  local copies, waits for them, and re-layouts: 4.83 us -> 7.44 us
    pallas_call x8 -> x14, Pallas kernels: 29.1 us -> 14.8 us  [call(): pl.pallas_call(kernel, out_shape=outs, in_specs=specs or [VMEM] * len(arg...]
    ppermute x4, starting transfers between devices: 8.62 us -> 4.31 us  [local(): lax.ppermute(part, 'tm', pairs)]
    ppermute x1, waiting for transfers between devices: 0.01 us -> 1.39 us  [local(): from_left = lax.ppermute(east, 'lon', right)]
    ppermute x4, waiting for transfers between devices: 1.7 us -> 3.06 us  [local(): lax.ppermute(part, 'tm', pairs)]
    unnamed x18 -> x23, local copies, waits for them, and re-layouts: 4.82 us -> 5.93 us
    dynamic_slice x0 -> x3, local copies, waits for them, and re-layouts: none -> 1.03 us  [corr_stack(): block = lax.dynamic_slice(time_corr, (source, target), (count, steps))]
    ppermute x1, starting transfers between devices: 4.2 us -> 4.94 us  [local(): above = lax.ppermute(last, 'lat', down)]
  transfers between devices with their start and end apart: 8 -> 8, of which waited for: 1 -> 3; matrix products, arithmetic and copies ran while one was open for 0% -> 4% of each run, Pallas kernels for 24% -> 17%
where the time goes in v2:
time: 53.1 us; the launch traced here: 52.6 us
  Pallas kernels  14.8 us (28%)
  blocking collectives  13.3 us (25%)
  starting transfers between devices  12.3 us (23%)
  local copies, waits for them, and re-layouts  7.44 us (14%)
  waiting for transfers between devices  4.46 us (8%)
    pallas_call x14, Pallas kernels, call(): pl.pallas_call(kernel, out_shape=outs, in_specs=specs or [VMEM] * len(arg...  14.8 us
    all_to_all x1, blocking collectives, local(): lax.all_to_all(message, ('lat', 'lon', 'tm'), split_axis=0, concat_axis=0...  13.3 us
    unnamed x23, local copies, waits for them, and re-layouts  5.93 us
    ppermute x1, starting transfers between devices, local(): above = lax.ppermute(last, 'lat', down)  4.94 us
    ppermute x4, starting transfers between devices, local(): lax.ppermute(part, 'tm', pairs)  4.31 us
    ppermute x4, waiting for transfers between devices, local(): lax.ppermute(part, 'tm', pairs)  3.06 us
    ppermute x1, starting transfers between devices, local(): from_right = lax.ppermute(west, 'lon', left)  1.73 us
    ppermute x1, waiting for transfers between devices, local(): from_left = lax.ppermute(east, 'lon', right)  1.39 us
  transfers between devices with their start and end apart: 8, of which 3 were waited for; matrix products, arithmetic and copies ran while one was open for 4% of the time, Pallas kernels for 17%

profile of v2, /device:TPU:0, one launch (start us, length us, event | category | flops | bytes accessed | tf_op | source)
XLA Modules:
  0.0 52.6 jit_solution(5178638724210152339)
XLA Ops:
  0.0 1.0 %copy-done.5 = f32[28,16,256]{2,1,0:T(8,128)S(1)} copy-done((f32[28,16,256]{2,1,0:T(8,128)S(1)}, f32[28,16,256]{2,1,0:T(8,128)}, u32[]{:S(2)}) %copy-start.5) | copy-done | bytes 458776
  1.0 0.7 %copy-done.6 = s32[16,256]{1,0:T(8,128)S(1)} copy-done((s32[16,256]{1,0:T(8,128)S(1)}, s32[16,256]{1,0:T(8,128)}, u32[]{:S(2)}) %copy-start.6) | copy-done | bytes 16408
  1.7 0.7 %copy-done.7 = f32[16,256]{1,0:T(8,128)S(1)} copy-done((f32[16,256]{1,0:T(8,128)S(1)}, f32[16,256]{1,0:T(8,128)}, u32[]{:S(2)}) %copy-start.7) | copy-done | bytes 16408
  2.9 4.9 %collective-permute-start = (f32[6,32,256]{2,1,0:T(8,128)S(1)}, f32[6,32,256]{2,1,0:T(8,128)S(1)}, u32[]{:S(2)}, u32[]{:S(2)}) collective-permute-start(f32[6,32,256]{2,1,0:T(8,128)S(1)} %get-tuple-element.14), channel_id=1, source_target_pairs={{0,8},{8,16},{16,24},{1,9},{9,17},{17,25},{2,10},{10,18},{18,26},{... | collective-permute-start | bytes 589832 | tf_op jit(solution)/shard_map/ppermute | solution.py:408
  7.9 1.3 %collective-permute-start.1 = (f32[6,32,256]{2,1,0:T(8,128)S(1)}, f32[6,32,256]{2,1,0:T(8,128)S(1)}, u32[]{:S(2)}, u32[]{:S(2)}) collective-permute-start(f32[6,32,256]{2,1,0:T(8,128)S(1)} %get-tuple-element.16), channel_id=1, source_target_pairs={{8,0},{16,8},{24,16},{9,1},{17,9},{25,17},{10,2},{18,10},{26,18},{... | collective-permute-start | bytes 589832 | tf_op jit(solution)/shard_map/ppermute | solution.py:409
  9.2 0.9 %fusion.5 = (f32[8,28]{1,0:T(8,128)S(1)}, f32[8,28]{1,0:T(8,128)S(1)}, f32[8,28]{1,0:T(8,128)S(1)}) fusion(f32[56,56]{1,0:T(8,128)} %param.11, s32[]{:T(128)S(6)} %select_n.23, s32[]{:T(128)S(6)} %select_n.20, s32[]{:T(128)S(6)} %select_n.22, s32[]{:T(128)S(6)} %select_n.21), kind=kLoop, calls=%fused_computation.25 | loop fusion | bytes 5392 | tf_op jit(solution)/shard_map/dynamic_slice | solution.py:254
  10.3 1.5 %copy-done = bf16[8,28,16,256]{3,2,1,0:T(8,128)(2,1)S(1)} copy-done((bf16[8,28,16,256]{3,2,1,0:T(8,128)(2,1)S(1)}, bf16[8,28,16,256]{3,2,1,0:T(8,128)(2,1)}, u32[]{:S(2)}) %copy-start) | copy-done | bytes 1835032
  11.8 1.5 %copy-done.2 = bf16[8,28,16,256]{3,2,1,0:T(8,128)(2,1)S(1)} copy-done((bf16[8,28,16,256]{3,2,1,0:T(8,128)(2,1)S(1)}, bf16[8,28,16,256]{3,2,1,0:T(8,128)(2,1)}, u32[]{:S(2)}) %copy-start.2) | copy-done | bytes 1835032
  13.3 3.4 %gram.1.order_ref.gram_ref = f32[72,128]{1,0:T(8,128)S(1)} custom-call(bf16[8,28,16,256]{3,2,1,0:T(8,128)(2,1)S(1)} %copy-done, bf16[8,28,16,256]{3,2,1,0:T(8,128)(2,1)S(1)} %copy-done.2), custom_call_target="tpu_custom_call" | custom-call | tf_op jit(solution)/shard_map/gram/pallas_call | solution.py:34
  17.1 1.7 %collective-permute-start.3 = (f32[32,256]{1,0:T(8,128)S(1)}, f32[32,256]{1,0:T(8,128)S(1)}, u32[]{:S(2)}, u32[]{:S(2)}) collective-permute-start(f32[32,256]{1,0:T(8,128)S(1)} %get-tuple-element.18), channel_id=1, source_target_pairs={{2,0},{4,2},{6,4},{0,6},{3,1},{5,3},{7,5},{1,7},{10,8},{12,10},{14... | collective-permute-start | bytes 98312 | tf_op jit(solution)/shard_map/ppermute | solution.py:414
  19.1 1.4 %collective-permute-done.2.left_ref = f32[32,256]{1,0:T(8,128)S(1)} collective-permute-done((f32[32,256]{1,0:T(8,128)S(1)}, f32[32,256]{1,0:T(8,128)S(1)}, u32[]{:S(2)}, u32[]{:S(2)}) %collective-permute-start.2) | collective-permute-done | bytes 32800 | tf_op jit(solution)/shard_map/ppermute | solution.py:413
  20.8 1.5 %sweeps.4.refs_1_ = f32[16,8,256]{2,1,0:T(8,128)S(1)} custom-call(f32[6,32,256]{2,1,0:T(8,128)S(1)} %collective-permute-done.above_ref, f32[16,32,256]{2,1,0:T(8,128)S(1)} %get-tuple-element.15.field_ref, f32[6,32,256]{2,1,0:T(8,128)S(1)} %collective-permute-done.1.below_ref, f32[32,256]{1,0:T(8,128)S(1)} %collective-permute-done.2.left_ref, ...), custom_call_target="tpu_custom_call" | custom-call | tf_op jit(solution)/shard_map/sweeps/pallas_call | solution.py:34
  22.3 1.6 %collective-permute-start.4 = (f32[16,8,256]{2,1,0:T(8,128)S(1)}, f32[16,8,256]{2,1,0:T(8,128)S(1)}, u32[]{:S(2)}, u32[]{:S(2)}) collective-permute-start(f32[16,8,256]{2,1,0:T(8,128)S(1)} %sweeps.4.refs_1_), channel_id=1, source_target_pairs={{0,1},{1,0},{2,3},{3,2},{4,5},{5,4},{6,7},{7,6},{8,9},{9,8},{10,11... | collective-permute-start | bytes 393224 | tf_op jit(solution)/shard_map/ppermute | solution.py:429
  23.9 1.5 %sweeps.5.refs_2_ = f32[16,8,256]{2,1,0:T(8,128)S(1)} custom-call(f32[6,32,256]{2,1,0:T(8,128)S(1)} %collective-permute-done.above_ref, f32[16,32,256]{2,1,0:T(8,128)S(1)} %get-tuple-element.15.field_ref, f32[6,32,256]{2,1,0:T(8,128)S(1)} %collective-permute-done.1.below_ref, f32[32,256]{1,0:T(8,128)S(1)} %collective-permute-done.2.left_ref, ...), custom_call_target="tpu_custom_call" | custom-call | tf_op jit(solution)/shard_map/sweeps/pallas_call | solution.py:34
  25.4 0.6 %collective-permute-start.5 = (f32[16,8,256]{2,1,0:T(8,128)S(1)}, f32[16,8,256]{2,1,0:T(8,128)S(1)}, u32[]{:S(2)}, u32[]{:S(2)}) collective-permute-start(f32[16,8,256]{2,1,0:T(8,128)S(1)} %sweeps.5.refs_2_), channel_id=1, source_target_pairs={{0,1},{1,0},{2,3},{3,2},{4,5},{5,4},{6,7},{7,6},{8,9},{9,8},{10,11... | collective-permute-start | bytes 393224 | tf_op jit(solution)/shard_map/ppermute | solution.py:429
  26.0 1.5 %sweeps.6.refs_3_ = f32[16,8,256]{2,1,0:T(8,128)S(1)} custom-call(f32[6,32,256]{2,1,0:T(8,128)S(1)} %collective-permute-done.above_ref, f32[16,32,256]{2,1,0:T(8,128)S(1)} %get-tuple-element.15.field_ref, f32[6,32,256]{2,1,0:T(8,128)S(1)} %collective-permute-done.1.below_ref, f32[32,256]{1,0:T(8,128)S(1)} %collective-permute-done.2.left_ref, ...), custom_call_target="tpu_custom_call" | custom-call | tf_op jit(solution)/shard_map/sweeps/pallas_call | solution.py:34
  27.5 1.6 %collective-permute-start.6 = (f32[16,8,256]{2,1,0:T(8,128)S(1)}, f32[16,8,256]{2,1,0:T(8,128)S(1)}, u32[]{:S(2)}, u32[]{:S(2)}) collective-permute-start(f32[16,8,256]{2,1,0:T(8,128)S(1)} %sweeps.6.refs_3_), channel_id=1, source_target_pairs={{0,1},{1,0},{2,3},{3,2},{4,5},{5,4},{6,7},{7,6},{8,9},{9,8},{10,11... | collective-permute-start | bytes 393224 | tf_op jit(solution)/shard_map/ppermute | solution.py:429
  29.6 1.5 %sweeps.7.refs_4_ = f32[16,4,256]{2,1,0:T(4,128)S(1)} custom-call(f32[6,32,256]{2,1,0:T(8,128)S(1)} %collective-permute-done.above_ref, f32[16,32,256]{2,1,0:T(8,128)S(1)} %get-tuple-element.15.field_ref, f32[6,32,256]{2,1,0:T(8,128)S(1)} %collective-permute-done.1.below_ref, f32[32,256]{1,0:T(8,128)S(1)} %collective-permute-done.2.left_ref, ...), custom_call_target="tpu_custom_call" | custom-call | tf_op jit(solution)/shard_map/sweeps/pallas_call | solution.py:34
  31.2 0.6 %collective-permute-start.7 = (f32[16,4,256]{2,1,0:T(4,128)S(1)}, f32[16,4,256]{2,1,0:T(4,128)S(1)}, u32[]{:S(2)}, u32[]{:S(2)}) collective-permute-start(f32[16,4,256]{2,1,0:T(4,128)S(1)} %sweeps.7.refs_4_), channel_id=1, source_target_pairs={{0,1},{1,0},{2,3},{3,2},{4,5},{5,4},{6,7},{7,6},{8,9},{9,8},{10,11... | collective-permute-start | bytes 196616 | tf_op jit(solution)/shard_map/ppermute | solution.py:429
  32.7 1.6 %collective-permute-done.6.refs_2_ = f32[16,8,256]{2,1,0:T(8,128)S(1)} collective-permute-done((f32[16,8,256]{2,1,0:T(8,128)S(1)}, f32[16,8,256]{2,1,0:T(8,128)S(1)}, u32[]{:S(2)}, u32[]{:S(2)}) %collective-permute-start.6) | collective-permute-done | bytes 131104 | tf_op jit(solution)/shard_map/ppermute | solution.py:429
  34.5 1.5 %collective-permute-done.7.field_ref = f32[16,4,256]{2,1,0:T(4,128)S(1)} collective-permute-done((f32[16,4,256]{2,1,0:T(4,128)S(1)}, f32[16,4,256]{2,1,0:T(4,128)S(1)}, u32[]{:S(2)}, u32[]{:S(2)}) %collective-permute-start.7) | collective-permute-done | bytes 65568 | tf_op jit(solution)/shard_map/ppermute | solution.py:429
  36.0 1.3 %mix_last.1 = (f32[28,16,256]{2,1,0:T(8,128)S(1)}, f32[32,1,128]{2,1,0:T(1,128)S(1)}) custom-call(f32[16,28,256]{2,1,0:T(8,128)S(1)} %mix_more.5.acc_ref, bf16[28,48]{1,0:T(8,128)(2,1)S(1)} %concatenate.24.corr_ref, f32[16,4,256]{2,1,0:T(4,128)S(1)} %collective-permute-done.7.field_ref, f32[72,128]{1,0:T(8,128)S(1)} %gram.1.order_ref.gram_ref, ...), custom_call_target="tpu_custom_call" | custom-call | tf_op jit(solution)/shard_map/mix_last/pallas_call | solution.py:34
  37.3 13.3 %all_to_all.5.inbox_ref = f32[32,1,128]{2,1,0:T(1,128)S(1)} all-to-all(f32[32,1,128]{2,1,0:T(1,128)S(1)} %get-tuple-element.21), channel_id=1, replica_groups=mesh['lat'=4,'lon'=4,'tm'=2] {'lat','lon','tm'}, dimensions={0} | all-to-all | bytes 32768 | tf_op jit(solution)/shard_map/all_to_all | solution.py:442
  50.6 2.0 %final.1 = f32[28,16,256]{2,1,0:T(8,128)} custom-call(f32[32,1,128]{2,1,0:T(1,128)S(1)} %all_to_all.5.inbox_ref, f32[28,16,256]{2,1,0:T(8,128)S(1)} %get-tuple-element.22.mixed_ref, f32[28,16,256]{2,1,0:T(8,128)S(1)} %copy-done.4, bf16[8,28,16,256]{3,2,1,0:T(8,128)(2,1)S(1)} %copy-done.1, bf16[8,28,16,256]{3,2,1,0:T(8,128)(2,1)S(1)} %copy-done.3), custom_call_target="tpu_custom_call" | custom-call | tf_op jit(solution)/shard_map/final/pallas_call | solution.py:34
  (43 shorter events, 3.3 us)
Async XLA Ops:
  0.0 1.0 %copy-start.5 = (f32[28,16,256]{2,1,0:T(8,128)S(1)}, f32[28,16,256]{2,1,0:T(8,128)}, u32[]{:S(2)}) copy-start(f32[28,16,256]{2,1,0:T(8,128)} %grad_hbm.1) | copy-start | bytes 1376260
  1.0 0.7 %copy-start.6 = (s32[16,256]{1,0:T(8,128)S(1)}, s32[16,256]{1,0:T(8,128)}, u32[]{:S(2)}) copy-start(s32[16,256]{1,0:T(8,128)} %mask_hbm.1) | copy-start | bytes 49156
  1.7 0.7 %copy-start.7 = (f32[16,256]{1,0:T(8,128)S(1)}, f32[16,256]{1,0:T(8,128)}, u32[]{:S(2)}) copy-start(f32[16,256]{1,0:T(8,128)} %diff_hbm.1) | copy-start | bytes 49156
  2.9 13.9 %collective-permute-start = (f32[6,32,256]{2,1,0:T(8,128)S(1)}, f32[6,32,256]{2,1,0:T(8,128)S(1)}, u32[]{:S(2)}, u32[]{:S(2)}) collective-permute-start(f32[6,32,256]{2,1,0:T(8,128)S(1)} %get-tuple-element.14), channel_id=1, source_target_pairs={{0,8},{8,16},{16,24},{1,9},{9,17},{17,25},{2,10},{10,18},{18,26},{... | collective-permute-start | bytes 589832 | tf_op jit(solution)/shard_map/ppermute | solution.py:408
  7.9 8.9 %collective-permute-start.1 = (f32[6,32,256]{2,1,0:T(8,128)S(1)}, f32[6,32,256]{2,1,0:T(8,128)S(1)}, u32[]{:S(2)}, u32[]{:S(2)}) collective-permute-start(f32[6,32,256]{2,1,0:T(8,128)S(1)} %get-tuple-element.16), channel_id=1, source_target_pairs={{8,0},{16,8},{24,16},{9,1},{17,9},{25,17},{10,2},{18,10},{26,18},{... | collective-permute-start | bytes 589832 | tf_op jit(solution)/shard_map/ppermute | solution.py:409
  10.3 1.5 %copy-start = (bf16[8,28,16,256]{3,2,1,0:T(8,128)(2,1)S(1)}, bf16[8,28,16,256]{3,2,1,0:T(8,128)(2,1)}, u32[]{:S(2)}) copy-start(bf16[8,28,16,256]{3,2,1,0:T(8,128)(2,1)} %steps_ref.5) | copy-start | bytes 5505028
  11.8 1.5 %copy-start.2 = (bf16[8,28,16,256]{3,2,1,0:T(8,128)(2,1)S(1)}, bf16[8,28,16,256]{3,2,1,0:T(8,128)(2,1)}, u32[]{:S(2)}) copy-start(bf16[8,28,16,256]{3,2,1,0:T(8,128)(2,1)} %grads_ref.5) | copy-start | bytes 5505028
  13.3 5.6 %copy-start.8 = (f32[56,56]{1,0:T(8,128)S(1)}, f32[56,56]{1,0:T(8,128)}, u32[]{:S(2)}) copy-start(f32[56,56]{1,0:T(8,128)} %param.11) | copy-start | bytes 37636
  17.1 3.4 %collective-permute-start.2 = (f32[32,256]{1,0:T(8,128)S(1)}, f32[32,256]{1,0:T(8,128)S(1)}, u32[]{:S(2)}, u32[]{:S(2)}) collective-permute-start(f32[32,256]{1,0:T(8,128)S(1)} %get-tuple-element.17), channel_id=1, source_target_pairs={{0,2},{2,4},{4,6},{6,0},{1,3},{3,5},{5,7},{7,1},{8,10},{10,12},{12... | collective-permute-start | bytes 98312 | tf_op jit(solution)/shard_map/ppermute | solution.py:413
  17.1 3.3 %collective-permute-start.3 = (f32[32,256]{1,0:T(8,128)S(1)}, f32[32,256]{1,0:T(8,128)S(1)}, u32[]{:S(2)}, u32[]{:S(2)}) collective-permute-start(f32[32,256]{1,0:T(8,128)S(1)} %get-tuple-element.18), channel_id=1, source_target_pairs={{2,0},{4,2},{6,4},{0,6},{3,1},{5,3},{7,5},{1,7},{10,8},{12,10},{14... | collective-permute-start | bytes 98312 | tf_op jit(solution)/shard_map/ppermute | solution.py:414
  22.3 10.0 %collective-permute-start.4 = (f32[16,8,256]{2,1,0:T(8,128)S(1)}, f32[16,8,256]{2,1,0:T(8,128)S(1)}, u32[]{:S(2)}, u32[]{:S(2)}) collective-permute-start(f32[16,8,256]{2,1,0:T(8,128)S(1)} %sweeps.4.refs_1_), channel_id=1, source_target_pairs={{0,1},{1,0},{2,3},{3,2},{4,5},{5,4},{6,7},{7,6},{8,9},{9,8},{10,11... | collective-permute-start | bytes 393224 | tf_op jit(solution)/shard_map/ppermute | solution.py:429
  25.4 7.1 %collective-permute-start.5 = (f32[16,8,256]{2,1,0:T(8,128)S(1)}, f32[16,8,256]{2,1,0:T(8,128)S(1)}, u32[]{:S(2)}, u32[]{:S(2)}) collective-permute-start(f32[16,8,256]{2,1,0:T(8,128)S(1)} %sweeps.5.refs_2_), channel_id=1, source_target_pairs={{0,1},{1,0},{2,3},{3,2},{4,5},{5,4},{6,7},{7,6},{8,9},{9,8},{10,11... | collective-permute-start | bytes 393224 | tf_op jit(solution)/shard_map/ppermute | solution.py:429
  27.5 6.8 %collective-permute-start.6 = (f32[16,8,256]{2,1,0:T(8,128)S(1)}, f32[16,8,256]{2,1,0:T(8,128)S(1)}, u32[]{:S(2)}, u32[]{:S(2)}) collective-permute-start(f32[16,8,256]{2,1,0:T(8,128)S(1)} %sweeps.6.refs_3_), channel_id=1, source_target_pairs={{0,1},{1,0},{2,3},{3,2},{4,5},{5,4},{6,7},{7,6},{8,9},{9,8},{10,11... | collective-permute-start | bytes 393224 | tf_op jit(solution)/shard_map/ppermute | solution.py:429
  31.2 4.9 %collective-permute-start.7 = (f32[16,4,256]{2,1,0:T(4,128)S(1)}, f32[16,4,256]{2,1,0:T(4,128)S(1)}, u32[]{:S(2)}, u32[]{:S(2)}) collective-permute-start(f32[16,4,256]{2,1,0:T(4,128)S(1)} %sweeps.7.refs_4_), channel_id=1, source_target_pairs={{0,1},{1,0},{2,3},{3,2},{4,5},{5,4},{6,7},{7,6},{8,9},{9,8},{10,11... | collective-permute-start | bytes 196616 | tf_op jit(solution)/shard_map/ppermute | solution.py:429
  31.9 4.2 %copy-start.3 = (bf16[8,28,16,256]{3,2,1,0:T(8,128)(2,1)S(1)}, bf16[8,28,16,256]{3,2,1,0:T(8,128)(2,1)}, u32[]{:S(2)}) copy-start(bf16[8,28,16,256]{3,2,1,0:T(8,128)(2,1)} %grads_ref.5) | copy-start | bytes 5505028
  32.3 3.8 %copy-start.1 = (bf16[8,28,16,256]{3,2,1,0:T(8,128)(2,1)S(1)}, bf16[8,28,16,256]{3,2,1,0:T(8,128)(2,1)}, u32[]{:S(2)}) copy-start(bf16[8,28,16,256]{3,2,1,0:T(8,128)(2,1)} %steps_ref.5) | copy-start | bytes 5505028
  34.5 16.1 %copy-start.4 = (f32[28,16,256]{2,1,0:T(8,128)S(1)}, f32[28,16,256]{2,1,0:T(8,128)}, u32[]{:S(2)}) copy-start(f32[28,16,256]{2,1,0:T(8,128)} %control_ref.1) | copy-start | bytes 1376260

commit v3 on v2

--- a/solution.py
+++ b/solution.py
@@ -21,7 +21,7 @@
 NROW = NGRAM + NPROJ
 
 VMEM = pl.BlockSpec(memory_space=pltpu.VMEM)
-HBM = pl.BlockSpec(memory_space=pl.ANY)
+HBM = pl.BlockSpec(memory_space=pltpu.HBM)
 PARAMS = pltpu.CompilerParams(vmem_limit_bytes=48 * 1024 * 1024)
 
 
@@ -50,26 +50,50 @@
     return lax.broadcasted_iota(jnp.int32, (SUB, LANE), 0)
 
 
-def gram_kernel(steps_ref, grads_ref, out_ref):
+def gram_kernel(steps_hbm, grads_hbm, out_ref, steps_ref, grads_ref, sems):
     _, steps, rows, cols = steps_ref.shape
-    for half, left_ref in enumerate((steps_ref, grads_ref)):
+    pieces = 4
+    while steps % pieces:
+        pieces -= 1
+    count = steps // pieces
+    copies = []
+    for n in range(pieces):
+        part = (slice(None), pl.ds(n * count, count))
+        copies.append((
+            pltpu.make_async_copy(steps_hbm.at[part], steps_ref.at[part], sems.at[0, n]),
+            pltpu.make_async_copy(grads_hbm.at[part], grads_ref.at[part], sems.at[1, n]),
+        ))
+    for pair in copies:
+        for copy in pair:
+            copy.start()
+
+    def make_body(half):
         def body(step, sums):
             sums = list(sums)
             for c in range(0, cols, LANE):
                 for r in range(0, rows, 2 * SUB):
                     where = (step, pl.ds(r, 2 * SUB), pl.ds(c, LANE))
                     right = [grads_ref[(i, *where)].astype(jnp.float32) for i in range(PAIRS)]
-                    left = right if half else [left_ref[(i, *where)].astype(jnp.float32) for i in range(PAIRS)]
+                    left = right if half else [steps_ref[(i, *where)].astype(jnp.float32) for i in range(PAIRS)]
                     for part in range(2):
                         cut = slice(part * SUB, (part + 1) * SUB)
                         for k, (i, j) in enumerate(CROSS):
                             sums[k] = sums[k] + left[i][cut] * right[j][cut]
             return tuple(sums)
 
-        zero = jnp.zeros((SUB, LANE), jnp.float32)
-        sums = lax.fori_loop(0, steps, body, (zero,) * NSYM)
-        for k in range(NSYM):
-            out_ref[half * NSYM + k:half * NSYM + k + 1, :] = jnp.sum(sums[k], axis=0, keepdims=True)
+        return body
+
+    zero = jnp.zeros((SUB, LANE), jnp.float32)
+    sums = (zero,) * NSYM
+    for n in range(pieces):
+        for copy in copies[n]:
+            copy.wait()
+        sums = lax.fori_loop(n * count, (n + 1) * count, make_body(0), sums)
+    for k in range(NSYM):
+        out_ref[k:k + 1, :] = jnp.sum(sums[k], axis=0, keepdims=True)
+    sums = lax.fori_loop(0, steps, make_body(1), (zero,) * NSYM)
+    for k in range(NSYM):
+        out_ref[NSYM + k:NSYM + k + 1, :] = jnp.sum(sums[k], axis=0, keepdims=True)
 
 
 def groups_of(steps):
@@ -83,28 +107,30 @@
 def pack_kernel(grad_hbm, mask_hbm, diff_hbm, field_ref, first_ref, last_ref, grad_ref, mask_ref, diff_ref, turn_ref, sems):
     steps, rows, cols = grad_ref.shape
     slots = field_ref.shape[1]
-    copies = [
-        pltpu.make_async_copy(mask_hbm, mask_ref, sems.at[0]),
-        pltpu.make_async_copy(diff_hbm, diff_ref, sems.at[1]),
-        pltpu.make_async_copy(grad_hbm, grad_ref, sems.at[2]),
-    ]
+    pieces = [(begin, min(SUB, steps - begin)) for begin in range(0, steps, SUB)]
+    copies = [pltpu.make_async_copy(mask_hbm, mask_ref, sems.at[0]), pltpu.make_async_copy(diff_hbm, diff_ref, sems.at[1])]
+    for n, (begin, count) in enumerate(pieces):
+        part = pl.ds(begin, count)
+        copies.append(pltpu.make_async_copy(grad_hbm.at[part], grad_ref.at[part], sems.at[2 + n]))
     for copy in copies:
         copy.start()
-    for copy in copies:
-        copy.wait()
+    copies[0].wait()
+    copies[1].wait()
     zero = jnp.zeros((SUB, LANE), jnp.float32)
-    for c in range(cols // LANE):
-        across = slice(c * LANE, (c + 1) * LANE)
-        for r in range(rows // SUB):
-            down = slice(r * SUB, (r + 1) * SUB)
-            base = (c * (rows // SUB) + r) * slots * SUB
-            mask = mask_ref[down, across].astype(jnp.float32)
-            for slot in range(slots):
-                if slot < steps:
-                    value = grad_ref[slot, down, across] * mask
-                else:
-                    value = diff_ref[down, across] if slot == steps else zero
-                turn_ref[base + slot * SUB:base + (slot + 1) * SUB, :] = value
+    tiles = [
+        (slice(r * SUB, (r + 1) * SUB), slice(c * LANE, (c + 1) * LANE), (c * (rows // SUB) + r) * slots * SUB)
+        for c in range(cols // LANE) for r in range(rows // SUB)
+    ]
+    mask = [mask_ref[down, across].astype(jnp.float32) for down, across, _ in tiles]
+    for slot in range(steps, slots):
+        for down, across, base in tiles:
+            value = diff_ref[down, across] if slot == steps else zero
+            turn_ref[base + slot * SUB:base + (slot + 1) * SUB, :] = value
+    for n, (begin, count) in enumerate(pieces):
+        copies[2 + n].wait()
+        for slot in range(begin, begin + count):
+            for (down, across, base), keep in zip(tiles, mask):
+                turn_ref[base + slot * SUB:base + (slot + 1) * SUB, :] = grad_ref[slot, down, across] * keep
     for c in range(cols // LANE):
         across = slice(c * LANE, (c + 1) * LANE)
         for row in range(rows):
@@ -179,67 +205,82 @@
     return [jnp.where(at_start, turned[c - 1], turned[c]) for c in range(len(tiles))]
 
 
-def weight_kernel(above_ref, field_ref, below_ref, left_ref, right_ref, south_ref, east_ref, *, steps):
+def weight_kernel(above_ref, field_ref, below_ref, left_ref, right_ref, south_ref, east_ref, west_ref, keep_ref, *, steps):
     rows, _, cols = field_ref.shape
     load = make_row_loader(above_ref, field_ref, below_ref, left_ref, right_ref)
-    at_end = lane_index() == LANE - 1
+    lane = lane_index()
+    at_start, at_end = lane == 0, lane == LANE - 1
     height = rows + 2 * HALO
     above = None
     for row in range(height):
         kappa = load(row, slice(steps, steps + 1), 1)
         beside = from_east(kappa, at_end)
+        east = [0.5 * (kappa[c] + beside[c]) for c in range(len(kappa))]
+        west = from_west(east, at_start)
         for c in range(len(kappa)):
-            east_ref[row, :, c * LANE:(c + 1) * LANE] = 0.5 * (kappa[c] + beside[c])
+            across = slice(c * LANE, (c + 1) * LANE)
+            east_ref[row, :, across] = east[c]
+            west_ref[row, :, across] = west[c]
+            keep_ref[row, :, across] = 1.0 - east[c] - west[c]
             if above is not None:
-                south_ref[row - 1, :, c * LANE:(c + 1) * LANE] = 0.5 * (above[c] + kappa[c])
+                south_ref[row - 1, :, across] = 0.5 * (above[c] + kappa[c])
+            if row in (HALO - 1, HALO + rows):
+                south_ref[height - 1 + (row >= HALO), :, across] = jnp.where(kappa[c] > 0.0, 1.0, 0.0)
         above = kappa
-    for side, row in enumerate((HALO - 1, HALO + rows)):
-        kappa = load(row, slice(steps, steps + 1), 1)
-        for c in range(len(kappa)):
-            south_ref[height - 1 + side, :, c * LANE:(c + 1) * LANE] = jnp.where(kappa[c] > 0.0, 1.0, 0.0)
-
-
-def sweep_kernel(above_ref, field_ref, below_ref, left_ref, right_ref, south_ref, east_ref, out_ref, *, begin):
+
+
+def sweep_kernel(
+    above_ref, field_ref, below_ref, left_ref, right_ref, south_ref, east_ref, west_ref, keep_ref, out_ref, *, begin
+):
     rows, _, cols = field_ref.shape
     height, width = rows + 2 * HALO, cols // LANE + 1
     count = out_ref.shape[1]
     lane = lane_index()
     at_start, at_end = lane == 0, lane == LANE - 1
     load = make_row_loader(above_ref, field_ref, below_ref, left_ref, right_ref)
-    state = [None] * (SWEEPS + 1)
+    state = [None] * SWEEPS
 
     def at(ref, row, c):
         return ref[row, :, c * LANE:(c + 1) * LANE]
 
-    def feed(sweep, row, tiles):
-        if sweep > SWEEPS:
-            for c in range(width - 1):
-                out_ref[row - HALO, :, c * LANE:(c + 1) * LANE] = tiles[c][:count]
-            return
+    def advance(sweep, row, tiles):
         before = state[sweep]
         if before is None:
             state[sweep] = (tiles, None)
-            return
+            return None
         centre, north = before
         south = [at(south_ref, row - 1, c) * (tiles[c] - centre[c]) for c in range(width)]
         state[sweep] = (tiles, south)
         if north is None:
-            return
-        ahead = from_east(centre, at_end)
-        flux = [at(east_ref, row - 1, c) * (ahead[c] - centre[c]) for c in range(width)]
-        behind = from_west(flux, at_start)
+            return None
+        ahead, behind = from_east(centre, at_end), from_west(centre, at_start)
         fresh = []
         for c in range(width):
-            change = (south[c] - north[c]) + (flux[c] - behind[c])
+            change = south[c] - north[c]
             if row - 1 < HALO:
                 change = change * at(south_ref, height - 1, c)
             if row - 1 >= HALO + rows:
                 change = change * at(south_ref, height, c)
-            fresh.append(centre[c] + change)
-        feed(sweep + 1, row - 1, fresh)
-
-    for row in range(height):
-        feed(1, row, load(row, slice(begin, begin + SUB), SUB))
+            across = at(east_ref, row - 1, c) * ahead[c] + at(west_ref, row - 1, c) * behind[c]
+            fresh.append(at(keep_ref, row - 1, c) * centre[c] + across + change)
+        return fresh
+
+    waiting = [None] * (SWEEPS + 1)
+    for tick in range(height + SWEEPS + 1):
+        if waiting[SWEEPS] is not None:
+            row, tiles = waiting[SWEEPS]
+            for c in range(width - 1):
+                out_ref[row - HALO, :, c * LANE:(c + 1) * LANE] = tiles[c][:count]
+        for sweep in reversed(range(SWEEPS)):
+            if sweep == 0:
+                entry = (tick, load(tick, slice(begin, begin + SUB), SUB)) if tick < height else None
+            else:
+                entry = waiting[sweep]
+            waiting[sweep + 1] = None
+            if entry is not None:
+                fresh = advance(sweep, *entry)
+                if fresh is not None:
+                    waiting[sweep + 1] = (entry[0] - 1, fresh)
 
 
 def split_stack(value):
@@ -401,27 +442,37 @@
         specs=[HBM] * 3,
         scratch=[
             pltpu.VMEM((steps, rows, cols), jnp.float32), pltpu.VMEM((rows, cols), jnp.int32),
-            pltpu.VMEM((rows, cols), jnp.float32), turn, pltpu.SemaphoreType.DMA((3,)),
+            pltpu.VMEM((rows, cols), jnp.float32), turn, pltpu.SemaphoreType.DMA((2 + len(groups_of(steps)),)),
         ],
         name="pack",
     )
     above = lax.ppermute(last, "lat", down)
     below = lax.ppermute(first, "lat", up)
-    gram = call(gram_kernel, f32(NGRAM, LANE), (pair_steps, pair_grads), name="gram")
+    gram = call(
+        gram_kernel, f32(NGRAM, LANE), (pair_steps, pair_grads), specs=[HBM] * 2,
+        scratch=[
+            pltpu.VMEM(pair_steps.shape, jnp.bfloat16), pltpu.VMEM(pair_grads.shape, jnp.bfloat16),
+            pltpu.SemaphoreType.DMA((2, 4)),
+        ],
+        name="gram",
+    )
     side_shape = f32(slots, -(-(rows + 2 * HALO) // PER) * LANE)
     west, east = call(side_kernel, (side_shape, side_shape), (above, field, below, gram), name="sides")
     from_left = lax.ppermute(east, "lon", right)
     from_right = lax.ppermute(west, "lon", left)
     whole = (above, field, below, from_left, from_right)
     tall, wide = rows + 2 * HALO, cols + LANE
-    south, beside = call(
-        functools.partial(weight_kernel, steps=steps), (f32(tall + 1, SUB, wide), f32(tall, SUB, wide)), whole, name="weights"
+    weights = call(
+        functools.partial(weight_kernel, steps=steps),
+        (f32(tall + 1, SUB, wide), f32(tall, SUB, wide), f32(tall, SUB, wide), f32(tall, SUB, wide)), whole, name="weights",
     )
     own, other = [], []
     for begin, count in groups_of(steps):
         part = call(
-            functools.partial(sweep_kernel, begin=begin), f32(rows, count, cols), (*whole, south, beside), name="sweeps"
+            functools.partial(sweep_kernel, begin=begin), f32(rows, count, cols), (*whole, *weights), name="sweeps"
         )
+        if not own:
+            time_corr, part = lax.optimization_barrier((time_corr, part))
         own.append(part)
         for shift in range(1, groups):
             pairs = [(i, (i + shift) % groups) for i in range(groups)]

time: 53.1 us -> 54.4 us (1.024)
  Pallas kernels: 14.8 us -> 15.4 us
    unnamed x23 -> x18, local copies, waits for them, and re-layouts: 5.93 us -> 6.96 us
    dynamic_slice x3 -> x2, local copies, waits for them, and re-layouts: 1.03 us -> 0.16 us  [corr_stack(): block = lax.dynamic_slice(time_corr, (source, target), (count, steps))]
    pallas_call x14, Pallas kernels: 14.8 us -> 15.4 us  [call(): pl.pallas_call(kernel, out_shape=outs, in_specs=specs or [VMEM] * len(arg...]
  transfers between devices with their start and end apart: 8 -> 8, of which waited for: 3 -> 4; matrix products, arithmetic and copies ran while one was open for 4% -> 1% of each run, Pallas kernels for 17% -> 17%
where the time goes in v3:
time: 54.4 us; the launch traced here: 54 us
  Pallas kernels  15.4 us (28%)
  blocking collectives  13.6 us (25%)
  starting transfers between devices  12.3 us (23%)
  local copies, waits for them, and re-layouts  7.68 us (14%)
  waiting for transfers between devices  4.73 us (9%)
    pallas_call x14, Pallas kernels, call(): pl.pallas_call(kernel, out_shape=outs, in_specs=specs or [VMEM] * len(arg...  15.4 us
    all_to_all x1, blocking collectives, local(): lax.all_to_all(message, ('lat', 'lon', 'tm'), split_axis=0, concat_axis=0...  13.6 us
    unnamed x18, local copies, waits for them, and re-layouts  6.96 us
    ppermute x1, starting transfers between devices, local(): above = lax.ppermute(last, 'lat', down)  4.94 us
    ppermute x4, starting transfers between devices, local(): lax.ppermute(part, 'tm', pairs)  4.26 us
    ppermute x4, waiting for transfers between devices, local(): lax.ppermute(part, 'tm', pairs)  2.97 us
    ppermute x1, starting transfers between devices, local(): from_right = lax.ppermute(west, 'lon', left)  1.73 us
    ppermute x1, waiting for transfers between devices, local(): from_left = lax.ppermute(east, 'lon', right)  1.59 us
  transfers between devices with their start and end apart: 8, of which 4 were waited for; matrix products, arithmetic and copies ran while one was open for 1% of the time, Pallas kernels for 17%

profile of v3, /device:TPU:0, one launch (start us, length us, event | category | flops | bytes accessed | tf_op | source)
XLA Modules:
  0.0 54.0 jit_solution(16750660780487942006)
XLA Ops:
  0.0 1.0 %copy-done.5 = f32[28,16,256]{2,1,0:T(8,128)S(1)} copy-done((f32[28,16,256]{2,1,0:T(8,128)S(1)}, f32[28,16,256]{2,1,0:T(8,128)}, u32[]{:S(2)}) %copy-start.5) | copy-done | bytes 458776
  1.0 0.7 %copy-done.6 = s32[16,256]{1,0:T(8,128)S(1)} copy-done((s32[16,256]{1,0:T(8,128)S(1)}, s32[16,256]{1,0:T(8,128)}, u32[]{:S(2)}) %copy-start.6) | copy-done | bytes 16408
  1.7 0.7 %copy-done.7 = f32[16,256]{1,0:T(8,128)S(1)} copy-done((f32[16,256]{1,0:T(8,128)S(1)}, f32[16,256]{1,0:T(8,128)}, u32[]{:S(2)}) %copy-start.7) | copy-done | bytes 16408
  2.5 0.8 %pack.1 = (f32[16,32,256]{2,1,0:T(8,128)S(1)}, f32[6,32,256]{2,1,0:T(8,128)S(1)}, f32[6,32,256]{2,1,0:T(8,128)S(1)}) custom-call(f32[28,16,256]{2,1,0:T(8,128)S(1)} %copy-done.5, s32[16,256]{1,0:T(8,128)S(1)} %copy-done.6, f32[16,256]{1,0:T(8,128)S(1)} %copy-done.7), custom_call_target="tpu_custom_call" | custom-call | tf_op jit(solution)/shard_map/pack/pallas_call | solution.py:34
  3.3 4.9 %collective-permute-start = (f32[6,32,256]{2,1,0:T(8,128)S(1)}, f32[6,32,256]{2,1,0:T(8,128)S(1)}, u32[]{:S(2)}, u32[]{:S(2)}) collective-permute-start(f32[6,32,256]{2,1,0:T(8,128)S(1)} %get-tuple-element.18), channel_id=1, source_target_pairs={{0,8},{8,16},{16,24},{1,9},{9,17},{17,25},{2,10},{10,18},{18,26},{... | collective-permute-start | bytes 589832 | tf_op jit(solution)/shard_map/ppermute | solution.py:449
  8.2 1.3 %collective-permute-start.1 = (f32[6,32,256]{2,1,0:T(8,128)S(1)}, f32[6,32,256]{2,1,0:T(8,128)S(1)}, u32[]{:S(2)}, u32[]{:S(2)}) collective-permute-start(f32[6,32,256]{2,1,0:T(8,128)S(1)} %get-tuple-element.20), channel_id=1, source_target_pairs={{8,0},{16,8},{24,16},{9,1},{17,9},{25,17},{10,2},{18,10},{26,18},{... | collective-permute-start | bytes 589832 | tf_op jit(solution)/shard_map/ppermute | solution.py:450
  9.5 1.5 %copy-done = bf16[8,28,16,256]{3,2,1,0:T(8,128)(2,1)S(1)} copy-done((bf16[8,28,16,256]{3,2,1,0:T(8,128)(2,1)S(1)}, bf16[8,28,16,256]{3,2,1,0:T(8,128)(2,1)}, u32[]{:S(2)}) %copy-start) | copy-done | bytes 1835032
  11.0 1.5 %copy-done.2 = bf16[8,28,16,256]{3,2,1,0:T(8,128)(2,1)S(1)} copy-done((bf16[8,28,16,256]{3,2,1,0:T(8,128)(2,1)S(1)}, bf16[8,28,16,256]{3,2,1,0:T(8,128)(2,1)}, u32[]{:S(2)}) %copy-start.2) | copy-done | bytes 1835032
  12.5 3.8 %gram.1.order_ref.gram_ref = f32[72,128]{1,0:T(8,128)S(1)} custom-call(bf16[8,28,16,256]{3,2,1,0:T(8,128)(2,1)S(1)} %copy-done, bf16[8,28,16,256]{3,2,1,0:T(8,128)(2,1)S(1)} %copy-done.2), custom_call_target="tpu_custom_call" | custom-call | tf_op jit(solution)/shard_map/gram/pallas_call | solution.py:34
  16.8 1.7 %collective-permute-start.3 = (f32[32,256]{1,0:T(8,128)S(1)}, f32[32,256]{1,0:T(8,128)S(1)}, u32[]{:S(2)}, u32[]{:S(2)}) collective-permute-start(f32[32,256]{1,0:T(8,128)S(1)} %get-tuple-element.22), channel_id=1, source_target_pairs={{2,0},{4,2},{6,4},{0,6},{3,1},{5,3},{7,5},{1,7},{10,8},{12,10},{14... | collective-permute-start | bytes 98312 | tf_op jit(solution)/shard_map/ppermute | solution.py:462
  18.6 1.6 %collective-permute-done.2.left_ref = f32[32,256]{1,0:T(8,128)S(1)} collective-permute-done((f32[32,256]{1,0:T(8,128)S(1)}, f32[32,256]{1,0:T(8,128)S(1)}, u32[]{:S(2)}, u32[]{:S(2)}) %collective-permute-start.2) | collective-permute-done | bytes 32800 | tf_op jit(solution)/shard_map/ppermute | solution.py:461
  20.2 0.7 %weights.1 = (f32[29,8,384]{2,1,0:T(8,128)S(1)}, f32[28,8,384]{2,1,0:T(8,128)S(1)}, f32[28,8,384]{2,1,0:T(8,128)S(1)}, f32[28,8,384]{2,1,0:T(8,128)S(1)}) custom-call(f32[6,32,256]{2,1,0:T(8,128)S(1)} %collective-permute-done.above_ref, f32[16,32,256]{2,1,0:T(8,128)S(1)} %get-tuple-element.19.field_ref, f32[6,32,256]{2,1,0:T(8,128)S(1)} %collective-permute-done.1.below_ref, ...), custom_call_target="tpu_custom_call" | custom-call | tf_op jit(solution)/shard_map/weights/pallas_call | solution.py:34
  20.9 1.4 %sweeps.4.refs_1_ = f32[16,8,256]{2,1,0:T(8,128)S(1)} custom-call(f32[6,32,256]{2,1,0:T(8,128)S(1)} %collective-permute-done.above_ref, f32[16,32,256]{2,1,0:T(8,128)S(1)} %get-tuple-element.19.field_ref, f32[6,32,256]{2,1,0:T(8,128)S(1)} %collective-permute-done.1.below_ref, f32[32,256]{1,0:T(8,128)S(1)} %collective-permute-done.2.left_ref, ...), custom_call_target="tpu_custom_call" | custom-call | tf_op jit(solution)/shard_map/sweeps/pallas_call | solution.py:34
  22.4 1.5 %collective-permute-start.4 = (f32[16,8,256]{2,1,0:T(8,128)S(1)}, f32[16,8,256]{2,1,0:T(8,128)S(1)}, u32[]{:S(2)}, u32[]{:S(2)}) collective-permute-start(f32[16,8,256]{2,1,0:T(8,128)S(1)} %sweeps.4.refs_1_), channel_id=1, source_target_pairs={{0,1},{1,0},{2,3},{3,2},{4,5},{5,4},{6,7},{7,6},{8,9},{9,8},{10,11... | collective-permute-start | bytes 393224 | tf_op jit(solution)/shard_map/ppermute | solution.py:480
  23.9 1.4 %sweeps.5.refs_2_ = f32[16,8,256]{2,1,0:T(8,128)S(1)} custom-call(f32[6,32,256]{2,1,0:T(8,128)S(1)} %collective-permute-done.above_ref, f32[16,32,256]{2,1,0:T(8,128)S(1)} %get-tuple-element.19.field_ref, f32[6,32,256]{2,1,0:T(8,128)S(1)} %collective-permute-done.1.below_ref, f32[32,256]{1,0:T(8,128)S(1)} %collective-permute-done.2.left_ref, ...), custom_call_target="tpu_custom_call" | custom-call | tf_op jit(solution)/shard_map/sweeps/pallas_call | solution.py:34
  25.9 1.4 %sweeps.6.refs_3_ = f32[16,8,256]{2,1,0:T(8,128)S(1)} custom-call(f32[6,32,256]{2,1,0:T(8,128)S(1)} %collective-permute-done.above_ref, f32[16,32,256]{2,1,0:T(8,128)S(1)} %get-tuple-element.19.field_ref, f32[6,32,256]{2,1,0:T(8,128)S(1)} %collective-permute-done.1.below_ref, f32[32,256]{1,0:T(8,128)S(1)} %collective-permute-done.2.left_ref, ...), custom_call_target="tpu_custom_call" | custom-call | tf_op jit(solution)/shard_map/sweeps/pallas_call | solution.py:34
  27.2 1.6 %collective-permute-start.6 = (f32[16,8,256]{2,1,0:T(8,128)S(1)}, f32[16,8,256]{2,1,0:T(8,128)S(1)}, u32[]{:S(2)}, u32[]{:S(2)}) collective-permute-start(f32[16,8,256]{2,1,0:T(8,128)S(1)} %sweeps.6.refs_3_), channel_id=1, source_target_pairs={{0,1},{1,0},{2,3},{3,2},{4,5},{5,4},{6,7},{7,6},{8,9},{9,8},{10,11... | collective-permute-start | bytes 393224 | tf_op jit(solution)/shard_map/ppermute | solution.py:480
  28.8 1.4 %sweeps.7.refs_4_ = f32[16,4,256]{2,1,0:T(4,128)S(1)} custom-call(f32[6,32,256]{2,1,0:T(8,128)S(1)} %collective-permute-done.above_ref, f32[16,32,256]{2,1,0:T(8,128)S(1)} %get-tuple-element.19.field_ref, f32[6,32,256]{2,1,0:T(8,128)S(1)} %collective-permute-done.1.below_ref, f32[32,256]{1,0:T(8,128)S(1)} %collective-permute-done.2.left_ref, ...), custom_call_target="tpu_custom_call" | custom-call | tf_op jit(solution)/shard_map/sweeps/pallas_call | solution.py:34
  32.4 1.8 %collective-permute-done.6.refs_2_ = f32[16,8,256]{2,1,0:T(8,128)S(1)} collective-permute-done((f32[16,8,256]{2,1,0:T(8,128)S(1)}, f32[16,8,256]{2,1,0:T(8,128)S(1)}, u32[]{:S(2)}, u32[]{:S(2)}) %collective-permute-start.6) | collective-permute-done | bytes 131104 | tf_op jit(solution)/shard_map/ppermute | solution.py:480
  34.4 1.2 %collective-permute-done.7.field_ref = f32[16,4,256]{2,1,0:T(4,128)S(1)} collective-permute-done((f32[16,4,256]{2,1,0:T(4,128)S(1)}, f32[16,4,256]{2,1,0:T(4,128)S(1)}, u32[]{:S(2)}, u32[]{:S(2)}) %collective-permute-start.7) | collective-permute-done | bytes 65568 | tf_op jit(solution)/shard_map/ppermute | solution.py:480
  35.6 1.5 %copy-done.3 = bf16[8,28,16,256]{3,2,1,0:T(8,128)(2,1)S(1)} copy-done((bf16[8,28,16,256]{3,2,1,0:T(8,128)(2,1)S(1)}, bf16[8,28,16,256]{3,2,1,0:T(8,128)(2,1)}, u32[]{:S(2)}) %copy-start.3) | copy-done | bytes 1835032
  37.1 1.3 %mix_last.1 = (f32[28,16,256]{2,1,0:T(8,128)S(1)}, f32[32,1,128]{2,1,0:T(1,128)S(1)}) custom-call(f32[16,28,256]{2,1,0:T(8,128)S(1)} %mix_more.5.acc_ref, bf16[28,48]{1,0:T(8,128)(2,1)S(1)} %concatenate.24.corr_ref, f32[16,4,256]{2,1,0:T(4,128)S(1)} %collective-permute-done.7.field_ref, f32[72,128]{1,0:T(8,128)S(1)} %gram.1.order_ref.gram_ref, ...), custom_call_target="tpu_custom_call" | custom-call | tf_op jit(solution)/shard_map/mix_last/pallas_call | solution.py:34
  38.4 13.6 %all_to_all.5.inbox_ref = f32[32,1,128]{2,1,0:T(1,128)S(1)} all-to-all(f32[32,1,128]{2,1,0:T(1,128)S(1)} %get-tuple-element.29), channel_id=1, replica_groups=mesh['lat'=4,'lon'=4,'tm'=2] {'lat','lon','tm'}, dimensions={0} | all-to-all | bytes 32768 | tf_op jit(solution)/shard_map/all_to_all | solution.py:493
  52.0 2.0 %final.1 = f32[28,16,256]{2,1,0:T(8,128)} custom-call(f32[32,1,128]{2,1,0:T(1,128)S(1)} %all_to_all.5.inbox_ref, f32[28,16,256]{2,1,0:T(8,128)S(1)} %get-tuple-element.30.mixed_ref, f32[28,16,256]{2,1,0:T(8,128)S(1)} %copy-done.4, bf16[8,28,16,256]{3,2,1,0:T(8,128)(2,1)S(1)} %copy-done.1, bf16[8,28,16,256]{3,2,1,0:T(8,128)(2,1)S(1)} %copy-done.3), custom_call_target="tpu_custom_call" | custom-call | tf_op jit(solution)/shard_map/final/pallas_call | solution.py:34
  (36 shorter events, 3.6 us)
Async XLA Ops:
  0.0 1.0 %copy-start.5 = (f32[28,16,256]{2,1,0:T(8,128)S(1)}, f32[28,16,256]{2,1,0:T(8,128)}, u32[]{:S(2)}) copy-start(f32[28,16,256]{2,1,0:T(8,128)} %grad_hbm.1) | copy-start | bytes 1376260
  1.0 0.7 %copy-start.6 = (s32[16,256]{1,0:T(8,128)S(1)}, s32[16,256]{1,0:T(8,128)}, u32[]{:S(2)}) copy-start(s32[16,256]{1,0:T(8,128)} %mask_hbm.1) | copy-start | bytes 49156
  1.7 0.7 %copy-start.7 = (f32[16,256]{1,0:T(8,128)S(1)}, f32[16,256]{1,0:T(8,128)}, u32[]{:S(2)}) copy-start(f32[16,256]{1,0:T(8,128)} %diff_hbm.1) | copy-start | bytes 49156
  3.3 13.0 %collective-permute-start = (f32[6,32,256]{2,1,0:T(8,128)S(1)}, f32[6,32,256]{2,1,0:T(8,128)S(1)}, u32[]{:S(2)}, u32[]{:S(2)}) collective-permute-start(f32[6,32,256]{2,1,0:T(8,128)S(1)} %get-tuple-element.18), channel_id=1, source_target_pairs={{0,8},{8,16},{16,24},{1,9},{9,17},{17,25},{2,10},{10,18},{18,26},{... | collective-permute-start | bytes 589832 | tf_op jit(solution)/shard_map/ppermute | solution.py:449
  8.2 8.3 %collective-permute-start.1 = (f32[6,32,256]{2,1,0:T(8,128)S(1)}, f32[6,32,256]{2,1,0:T(8,128)S(1)}, u32[]{:S(2)}, u32[]{:S(2)}) collective-permute-start(f32[6,32,256]{2,1,0:T(8,128)S(1)} %get-tuple-element.20), channel_id=1, source_target_pairs={{8,0},{16,8},{24,16},{9,1},{17,9},{25,17},{10,2},{18,10},{26,18},{... | collective-permute-start | bytes 589832 | tf_op jit(solution)/shard_map/ppermute | solution.py:450
  9.5 1.5 %copy-start = (bf16[8,28,16,256]{3,2,1,0:T(8,128)(2,1)S(1)}, bf16[8,28,16,256]{3,2,1,0:T(8,128)(2,1)}, u32[]{:S(2)}) copy-start(bf16[8,28,16,256]{3,2,1,0:T(8,128)(2,1)} %steps_ref.3) | copy-start | bytes 5505028
  11.0 1.5 %copy-start.2 = (bf16[8,28,16,256]{3,2,1,0:T(8,128)(2,1)S(1)}, bf16[8,28,16,256]{3,2,1,0:T(8,128)(2,1)}, u32[]{:S(2)}) copy-start(bf16[8,28,16,256]{3,2,1,0:T(8,128)(2,1)} %grads_ref.3) | copy-start | bytes 5505028
  16.8 5.5 %copy-start.8 = (f32[56,56]{1,0:T(8,128)S(1)}, f32[56,56]{1,0:T(8,128)}, u32[]{:S(2)}) copy-start(f32[56,56]{1,0:T(8,128)} %param.11) | copy-start | bytes 37636
  16.8 3.4 %collective-permute-start.2 = (f32[32,256]{1,0:T(8,128)S(1)}, f32[32,256]{1,0:T(8,128)S(1)}, u32[]{:S(2)}, u32[]{:S(2)}) collective-permute-start(f32[32,256]{1,0:T(8,128)S(1)} %get-tuple-element.21), channel_id=1, source_target_pairs={{0,2},{2,4},{4,6},{6,0},{1,3},{3,5},{5,7},{7,1},{8,10},{10,12},{12... | collective-permute-start | bytes 98312 | tf_op jit(solution)/shard_map/ppermute | solution.py:461
  16.8 3.3 %collective-permute-start.3 = (f32[32,256]{1,0:T(8,128)S(1)}, f32[32,256]{1,0:T(8,128)S(1)}, u32[]{:S(2)}, u32[]{:S(2)}) collective-permute-start(f32[32,256]{1,0:T(8,128)S(1)} %get-tuple-element.22), channel_id=1, source_target_pairs={{2,0},{4,2},{6,4},{0,6},{3,1},{5,3},{7,5},{1,7},{10,8},{12,10},{14... | collective-permute-start | bytes 98312 | tf_op jit(solution)/shard_map/ppermute | solution.py:462
  22.4 9.6 %collective-permute-start.4 = (f32[16,8,256]{2,1,0:T(8,128)S(1)}, f32[16,8,256]{2,1,0:T(8,128)S(1)}, u32[]{:S(2)}, u32[]{:S(2)}) collective-permute-start(f32[16,8,256]{2,1,0:T(8,128)S(1)} %sweeps.4.refs_1_), channel_id=1, source_target_pairs={{0,1},{1,0},{2,3},{3,2},{4,5},{5,4},{6,7},{7,6},{8,9},{9,8},{10,11... | collective-permute-start | bytes 393224 | tf_op jit(solution)/shard_map/ppermute | solution.py:480
  25.3 6.9 %collective-permute-start.5 = (f32[16,8,256]{2,1,0:T(8,128)S(1)}, f32[16,8,256]{2,1,0:T(8,128)S(1)}, u32[]{:S(2)}, u32[]{:S(2)}) collective-permute-start(f32[16,8,256]{2,1,0:T(8,128)S(1)} %sweeps.5.refs_2_), channel_id=1, source_target_pairs={{0,1},{1,0},{2,3},{3,2},{4,5},{5,4},{6,7},{7,6},{8,9},{9,8},{10,11... | collective-permute-start | bytes 393224 | tf_op jit(solution)/shard_map/ppermute | solution.py:480
  27.2 7.0 %collective-permute-start.6 = (f32[16,8,256]{2,1,0:T(8,128)S(1)}, f32[16,8,256]{2,1,0:T(8,128)S(1)}, u32[]{:S(2)}, u32[]{:S(2)}) collective-permute-start(f32[16,8,256]{2,1,0:T(8,128)S(1)} %sweeps.6.refs_3_), channel_id=1, source_target_pairs={{0,1},{1,0},{2,3},{3,2},{4,5},{5,4},{6,7},{7,6},{8,9},{9,8},{10,11... | collective-permute-start | bytes 393224 | tf_op jit(solution)/shard_map/ppermute | solution.py:480
  30.2 5.4 %collective-permute-start.7 = (f32[16,4,256]{2,1,0:T(4,128)S(1)}, f32[16,4,256]{2,1,0:T(4,128)S(1)}, u32[]{:S(2)}, u32[]{:S(2)}) collective-permute-start(f32[16,4,256]{2,1,0:T(4,128)S(1)} %sweeps.7.refs_4_), channel_id=1, source_target_pairs={{0,1},{1,0},{2,3},{3,2},{4,5},{5,4},{6,7},{7,6},{8,9},{9,8},{10,11... | collective-permute-start | bytes 196616 | tf_op jit(solution)/shard_map/ppermute | solution.py:480
  31.9 3.8 %copy-start.1 = (bf16[8,28,16,256]{3,2,1,0:T(8,128)(2,1)S(1)}, bf16[8,28,16,256]{3,2,1,0:T(8,128)(2,1)}, u32[]{:S(2)}) copy-start(bf16[8,28,16,256]{3,2,1,0:T(8,128)(2,1)} %steps_ref.3) | copy-start | bytes 5505028
  35.6 1.5 %copy-start.3 = (bf16[8,28,16,256]{3,2,1,0:T(8,128)(2,1)S(1)}, bf16[8,28,16,256]{3,2,1,0:T(8,128)(2,1)}, u32[]{:S(2)}) copy-start(bf16[8,28,16,256]{3,2,1,0:T(8,128)(2,1)} %grads_ref.3) | copy-start | bytes 5505028
  37.1 14.9 %copy-start.4 = (f32[28,16,256]{2,1,0:T(8,128)S(1)}, f32[28,16,256]{2,1,0:T(8,128)}, u32[]{:S(2)}) copy-start(f32[28,16,256]{2,1,0:T(8,128)} %control_ref.1) | copy-start | bytes 1376260

commit v4 on v3

--- a/solution.py
+++ b/solution.py
@@ -438,7 +438,7 @@
     field, first, last = call(
         pack_kernel,
         (f32(rows, slots, cols), f32(HALO, slots, cols), f32(HALO, slots, cols)),
-        (gradient, land_mask, diffusivity),
+        [pltpu.with_memory_space_constraint(v, pltpu.HBM) for v in (gradient, land_mask, diffusivity)],
         specs=[HBM] * 3,
         scratch=[
             pltpu.VMEM((steps, rows, cols), jnp.float32), pltpu.VMEM((rows, cols), jnp.int32),
@@ -448,12 +448,11 @@
     )
     above = lax.ppermute(last, "lat", down)
     below = lax.ppermute(first, "lat", up)
-    gram = call(
-        gram_kernel, f32(NGRAM, LANE), (pair_steps, pair_grads), specs=[HBM] * 2,
-        scratch=[
-            pltpu.VMEM(pair_steps.shape, jnp.bfloat16), pltpu.VMEM(pair_grads.shape, jnp.bfloat16),
-            pltpu.SemaphoreType.DMA((2, 4)),
-        ],
+    pair_shape = jax.ShapeDtypeStruct(pair_steps.shape, jnp.bfloat16)
+    gram, pair_steps, pair_grads = call(
+        gram_kernel, (f32(NGRAM, LANE), pair_shape, pair_shape),
+        [pltpu.with_memory_space_constraint(v, pltpu.HBM) for v in (pair_steps, pair_grads)], specs=[HBM] * 2,
+        scratch=[pltpu.SemaphoreType.DMA((2, 4))],
         name="gram",
     )
     side_shape = f32(slots, -(-(rows + 2 * HALO) // PER) * LANE)
@@ -484,13 +483,12 @@
     )
     for corr, part in other[:-1]:
         mixed = call(make_mix(False), f32(rows, steps, cols), (mixed, corr, part), name="mix_more")
-    devices = height * breadth * groups
     mixed, message = call(
-        last_mix_kernel, (f32(steps, rows, cols), f32(devices, 1, LANE)),
+        last_mix_kernel, (f32(steps, rows, cols), f32(1, 1, LANE)),
         (mixed, *other[-1], gram, pair_steps, pair_grads),
         scratch=[turn, pltpu.VMEM((NROW, LANE), jnp.float32)], name="mix_last",
     )
-    inbox = lax.all_to_all(message, ("lat", "lon", "tm"), split_axis=0, concat_axis=0, tiled=True)
+    inbox = lax.all_gather(message, ("lat", "lon", "tm"), axis=0, tiled=True)
     return call(
         final_kernel, f32(steps, rows, cols), (inbox, mixed, control, pair_steps, pair_grads),
         scratch=[pltpu.VMEM((NROW, LANE), jnp.float32)], name="final",

time: 54.4 us -> 114 us (2.10)
  blocking collectives: 13.6 us -> 67.5 us
  Pallas kernels: 15.4 us -> 22.4 us
  waiting for transfers between devices: 4.73 us -> 2.66 us
  local copies, waits for them, and re-layouts: 7.68 us -> 9.04 us
    all_gather x0 -> x1, blocking collectives: none -> 67.5 us  [local(): inbox = lax.all_gather(message, ('lat', 'lon', 'tm'), axis=0, tiled=True)]
    all_to_all x1 -> x0, blocking collectives: 13.6 us -> none  [local(): lax.all_to_all(message, ('lat', 'lon', 'tm'), split_axis=0, concat_axis=0...]
    pallas_call x14, Pallas kernels: 15.4 us -> 22.4 us  [call(): pl.pallas_call(kernel, out_shape=outs, in_specs=specs or [VMEM] * len(arg...]
    ppermute x4, waiting for transfers between devices: 2.97 us -> 0.01 us  [local(): lax.ppermute(part, 'tm', pairs)]
    optimization_barrier x1, local copies, waits for them, and re-layouts: 0.07 us -> 1.43 us  [local(): time_corr, part = lax.optimization_barrier((time_corr, part))]
    unnamed x18 -> x20, local copies, waits for them, and re-layouts: 6.96 us -> 6.23 us
  transfers between devices with their start and end apart: 8 -> 8, of which waited for: 4 -> 2; matrix products, arithmetic and copies ran while one was open for 1% -> 1% of each run, Pallas kernels for 17% -> 14%
where the time goes in v4:
time: 114 us
  blocking collectives  67.5 us (59%)
  Pallas kernels  22.4 us (20%)
  starting transfers between devices  12.1 us (11%)
  local copies, waits for them, and re-layouts  9.04 us (8%)
  waiting for transfers between devices  2.66 us (2%)
    all_gather x1, blocking collectives, local(): inbox = lax.all_gather(message, ('lat', 'lon', 'tm'), axis=0, tiled=True)  67.5 us
    pallas_call x14, Pallas kernels, call(): pl.pallas_call(kernel, out_shape=outs, in_specs=specs or [VMEM] * len(arg...  22.4 us
    unnamed x20, local copies, waits for them, and re-layouts  6.23 us
    ppermute x1, starting transfers between devices, local(): above = lax.ppermute(last, 'lat', down)  4.94 us
    ppermute x4, starting transfers between devices, local(): lax.ppermute(part, 'tm', pairs)  4.05 us
  transfers between devices with their start and end apart: 8, of which 2 were waited for; matrix products, arithmetic and copies ran while one was open for 1% of the time, Pallas kernels for 14%

profile of v4, /device:TPU:0, one launch (start us, length us, event | category | flops | bytes accessed | tf_op | source)
XLA Modules:
  0.0 114.0 jit_solution(6478147349845683373)
XLA Ops:
  0.0 1.2 %pack.1 = (f32[16,32,256]{2,1,0:T(8,128)S(1)}, f32[6,32,256]{2,1,0:T(8,128)S(1)}, f32[6,32,256]{2,1,0:T(8,128)S(1)}) custom-call(f32[28,16,256]{2,1,0:T(8,128)} %grad_hbm.1, s32[16,256]{1,0:T(8,128)} %mask_hbm.1, f32[16,256]{1,0:T(8,128)} %diff_hbm.1), custom_call_target="tpu_custom_call" | custom-call | tf_op jit(solution)/shard_map/pack/pallas_call | solution.py:34
  1.2 4.9 %collective-permute-start = (f32[6,32,256]{2,1,0:T(8,128)S(1)}, f32[6,32,256]{2,1,0:T(8,128)S(1)}, u32[]{:S(2)}, u32[]{:S(2)}) collective-permute-start(f32[6,32,256]{2,1,0:T(8,128)S(1)} %get-tuple-element.21), channel_id=1, source_target_pairs={{0,8},{8,16},{16,24},{1,9},{9,17},{17,25},{2,10},{10,18},{18,26},{... | collective-permute-start | bytes 589832 | tf_op jit(solution)/shard_map/ppermute | solution.py:449
  6.2 1.3 %collective-permute-start.1 = (f32[6,32,256]{2,1,0:T(8,128)S(1)}, f32[6,32,256]{2,1,0:T(8,128)S(1)}, u32[]{:S(2)}, u32[]{:S(2)}) collective-permute-start(f32[6,32,256]{2,1,0:T(8,128)S(1)} %get-tuple-element.23), channel_id=1, source_target_pairs={{8,0},{16,8},{24,16},{9,1},{17,9},{25,17},{10,2},{18,10},{26,18},{... | collective-permute-start | bytes 589832 | tf_op jit(solution)/shard_map/ppermute | solution.py:450
  7.5 4.6 %gram.1 = (f32[72,128]{1,0:T(8,128)S(1)}, bf16[8,28,16,256]{3,2,1,0:T(8,128)(2,1)S(1)}, bf16[8,28,16,256]{3,2,1,0:T(8,128)(2,1)S(1)}) custom-call(bf16[8,28,16,256]{3,2,1,0:T(8,128)(2,1)} %steps_hbm.1, bf16[8,28,16,256]{3,2,1,0:T(8,128)(2,1)} %grads_hbm.1), custom_call_target="tpu_custom_call" | custom-call | tf_op jit(solution)/shard_map/gram/pallas_call | solution.py:34
  12.1 1.3 %copy-done = bf16[8,28,16,256]{3,2,1,0:T(8,128)(2,1)} copy-done((bf16[8,28,16,256]{3,2,1,0:T(8,128)(2,1)}, bf16[8,28,16,256]{3,2,1,0:T(8,128)(2,1)S(1)}, u32[]{:S(2)}) %copy-start) | copy-done | bytes 1835032
  13.4 1.0 collective-permute-done.1.below_ref
  14.8 1.7 %collective-permute-start.3 = (f32[32,256]{1,0:T(8,128)S(1)}, f32[32,256]{1,0:T(8,128)S(1)}, u32[]{:S(2)}, u32[]{:S(2)}) collective-permute-start(f32[32,256]{1,0:T(8,128)S(1)} %get-tuple-element.26), channel_id=1, source_target_pairs={{2,0},{4,2},{6,4},{0,6},{3,1},{5,3},{7,5},{1,7},{10,8},{12,10},{14... | collective-permute-start | bytes 98312 | tf_op jit(solution)/shard_map/ppermute | solution.py:461
  16.5 1.6 %collective-permute-done.2.left_ref = f32[32,256]{1,0:T(8,128)S(1)} collective-permute-done((f32[32,256]{1,0:T(8,128)S(1)}, f32[32,256]{1,0:T(8,128)S(1)}, u32[]{:S(2)}, u32[]{:S(2)}) %collective-permute-start.2) | collective-permute-done | bytes 32800 | tf_op jit(solution)/shard_map/ppermute | solution.py:460
  18.9 1.4 %sweeps.4.refs_1_ = f32[16,8,256]{2,1,0:T(8,128)S(1)} custom-call(f32[6,32,256]{2,1,0:T(8,128)S(1)} %collective-permute-done.above_ref, f32[16,32,256]{2,1,0:T(8,128)S(1)} %get-tuple-element.22.field_ref, f32[6,32,256]{2,1,0:T(8,128)S(1)} %collective-permute-done.1.below_ref, f32[32,256]{1,0:T(8,128)S(1)} %collective-permute-done.2.left_ref, ...), custom_call_target="tpu_custom_call" | custom-call | tf_op jit(solution)/shard_map/sweeps/pallas_call | solution.py:34
  22.4 1.4 %copy.18 = f32[56,56]{0,1:T(8,128)} copy(f32[56,56]{1,0:T(8,128)} %param.11) | data formatting | bytes 25088 | tf_op jit(solution)/shard_map/optimization_barrier | solution.py:474
  23.8 1.5 %collective-permute-start.4 = (f32[16,8,256]{2,1,0:T(8,128)}, f32[16,8,256]{2,1,0:T(8,128)}, u32[]{:S(2)}, u32[]{:S(2)}) collective-permute-start(f32[16,8,256]{2,1,0:T(8,128)} %copy-done.6), channel_id=1, source_target_pairs={{0,1},{1,0},{2,3},{3,2},{4,5},{5,4},{6,7},{7,6},{8,9},{9,8},{10,11... | collective-permute-start | bytes 393224 | tf_op jit(solution)/shard_map/ppermute | solution.py:479
  25.3 1.0 copy-done.3
  26.3 1.0 copy-done.5
  27.2 2.0 %sweeps.5.refs_2_ = f32[16,8,256]{2,1,0:T(8,128)} custom-call(f32[6,32,256]{2,1,0:T(8,128)S(1)} %collective-permute-done.above_ref, f32[16,32,256]{2,1,0:T(8,128)S(1)} %get-tuple-element.22.field_ref, f32[6,32,256]{2,1,0:T(8,128)S(1)} %collective-permute-done.1.below_ref, f32[32,256]{1,0:T(8,128)S(1)} %collective-permute-done.2.left_ref, ...), custom_call_target="tpu_custom_call" | custom-call | tf_op jit(solution)/shard_map/sweeps/pallas_call | solution.py:34
  29.8 2.0 %sweeps.6.refs_3_ = f32[16,8,256]{2,1,0:T(8,128)} custom-call(f32[6,32,256]{2,1,0:T(8,128)S(1)} %collective-permute-done.above_ref, f32[16,32,256]{2,1,0:T(8,128)S(1)} %get-tuple-element.22.field_ref, f32[6,32,256]{2,1,0:T(8,128)S(1)} %collective-permute-done.1.below_ref, f32[32,256]{1,0:T(8,128)S(1)} %collective-permute-done.2.left_ref, ...), custom_call_target="tpu_custom_call" | custom-call | tf_op jit(solution)/shard_map/sweeps/pallas_call | solution.py:34
  31.8 1.5 %collective-permute-start.6 = (f32[16,8,256]{2,1,0:T(8,128)}, f32[16,8,256]{2,1,0:T(8,128)}, u32[]{:S(2)}, u32[]{:S(2)}) collective-permute-start(f32[16,8,256]{2,1,0:T(8,128)} %sweeps.6.refs_3_), channel_id=1, source_target_pairs={{0,1},{1,0},{2,3},{3,2},{4,5},{5,4},{6,7},{7,6},{8,9},{9,8},{10,11... | collective-permute-start | bytes 393224 | tf_op jit(solution)/shard_map/ppermute | solution.py:479
  33.3 2.0 %sweeps.7.refs_4_ = f32[16,4,256]{2,1,0:T(4,128)} custom-call(f32[6,32,256]{2,1,0:T(8,128)S(1)} %collective-permute-done.above_ref, f32[16,32,256]{2,1,0:T(8,128)S(1)} %get-tuple-element.22.field_ref, f32[6,32,256]{2,1,0:T(8,128)S(1)} %collective-permute-done.1.below_ref, f32[32,256]{1,0:T(8,128)S(1)} %collective-permute-done.2.left_ref, ...), custom_call_target="tpu_custom_call" | custom-call | tf_op jit(solution)/shard_map/sweeps/pallas_call | solution.py:34
  37.1 1.4 %mix_own.1.refs_0_ = f32[16,28,256]{2,1,0:T(8,128)S(1)} custom-call(bf16[28,192]{1,0:T(8,128)(2,1)S(1)} %concatenate.20.refs_0_, f32[16,8,256]{2,1,0:T(8,128)S(1)} %copy-done.7, f32[16,8,256]{2,1,0:T(8,128)} %sweeps.5.refs_2_, f32[16,8,256]{2,1,0:T(8,128)} %sweeps.6.refs_3_, f32[16,4,256]{2,1,0:T(4,128)} %sweeps.7.refs_4_), custom_call_target="tpu_custom_call" | custom-call | tf_op jit(solution)/shard_map/mix_own/pallas_call | solution.py:34
  39.7 1.2 %mix_more.3.refs_0_ = f32[16,28,256]{2,1,0:T(8,128)S(1)} custom-call(f32[16,28,256]{2,1,0:T(8,128)S(1)} %mix_own.1.refs_0_, bf16[28,48]{1,0:T(8,128)(2,1)S(1)} %concatenate.21.refs_1_, f32[16,8,256]{2,1,0:T(8,128)} %collective-permute-done.4.refs_2_), custom_call_target="tpu_custom_call" | custom-call | tf_op jit(solution)/shard_map/mix_more/pallas_call | solution.py:34
  40.9 1.1 mix_more.4.refs_0_
  42.1 1.1 mix_more.5.acc_ref
  43.2 1.3 %mix_last.1 = (f32[28,16,256]{2,1,0:T(8,128)S(1)}, f32[1,1,128]{2,1,0:T(1,128)S(1)}) custom-call(f32[16,28,256]{2,1,0:T(8,128)S(1)} %mix_more.5.acc_ref, bf16[28,48]{1,0:T(8,128)(2,1)S(1)} %concatenate.24.corr_ref, f32[16,4,256]{2,1,0:T(4,128)S(1)} %collective-permute-done.7.field_ref, f32[72,128]{1,0:T(8,128)S(1)} %get-tuple-element.24.order_ref.gram_ref, ...), custom_call_target="tpu_custom_call" | custom-call | tf_op jit(solution)/shard_map/mix_last/pallas_call | solution.py:34
  44.5 67.5 %all_gather.3.inbox_ref = f32[32,1,128]{2,1,0:T(1,128)S(1)} all-gather(f32[1,1,128]{2,1,0:T(1,128)S(1)} %get-tuple-element.35), channel_id=1, replica_groups=mesh['lat'=4,'lon'=4,'tm'=2] {'lat','lon','tm'}, dimensions={0}, use_global_device_ids=true | all-gather | bytes 16896 | tf_op jit(solution)/shard_map/all_gather | solution.py:491
  112.0 2.0 %final.1 = f32[28,16,256]{2,1,0:T(8,128)} custom-call(f32[32,1,128]{2,1,0:T(1,128)S(1)} %all_gather.3.inbox_ref, f32[28,16,256]{2,1,0:T(8,128)S(1)} %get-tuple-element.36.mixed_ref, f32[28,16,256]{2,1,0:T(8,128)S(1)} %copy-done.8, bf16[8,28,16,256]{3,2,1,0:T(8,128)(2,1)S(1)} %get-tuple-element.33.steps_ref, bf16[8,28,16,256]{3,2,1,0:T(8,128)(2,1)S(1)} %copy-done.1), custom_call_target="tpu_custom_call" | custom-call | tf_op jit(solution)/shard_map/final/pallas_call | solution.py:34
  (38 shorter events, 6.7 us)
Async XLA Ops:
  1.2 12.2 %collective-permute-start = (f32[6,32,256]{2,1,0:T(8,128)S(1)}, f32[6,32,256]{2,1,0:T(8,128)S(1)}, u32[]{:S(2)}, u32[]{:S(2)}) collective-permute-start(f32[6,32,256]{2,1,0:T(8,128)S(1)} %get-tuple-element.21), channel_id=1, source_target_pairs={{0,8},{8,16},{16,24},{1,9},{9,17},{17,25},{2,10},{10,18},{18,26},{... | collective-permute-start | bytes 589832 | tf_op jit(solution)/shard_map/ppermute | solution.py:449
  6.2 8.3 %collective-permute-start.1 = (f32[6,32,256]{2,1,0:T(8,128)S(1)}, f32[6,32,256]{2,1,0:T(8,128)S(1)}, u32[]{:S(2)}, u32[]{:S(2)}) collective-permute-start(f32[6,32,256]{2,1,0:T(8,128)S(1)} %get-tuple-element.23), channel_id=1, source_target_pairs={{8,0},{16,8},{24,16},{9,1},{17,9},{25,17},{10,2},{18,10},{26,18},{... | collective-permute-start | bytes 589832 | tf_op jit(solution)/shard_map/ppermute | solution.py:450
  12.1 1.3 %copy-start = (bf16[8,28,16,256]{3,2,1,0:T(8,128)(2,1)}, bf16[8,28,16,256]{3,2,1,0:T(8,128)(2,1)S(1)}, u32[]{:S(2)}) copy-start(bf16[8,28,16,256]{3,2,1,0:T(8,128)(2,1)S(1)} %get-tuple-element.34.grads_ref) | copy-start | bytes 5505028
  14.7 3.4 %collective-permute-start.2 = (f32[32,256]{1,0:T(8,128)S(1)}, f32[32,256]{1,0:T(8,128)S(1)}, u32[]{:S(2)}, u32[]{:S(2)}) collective-permute-start(f32[32,256]{1,0:T(8,128)S(1)} %get-tuple-element.25), channel_id=1, source_target_pairs={{0,2},{2,4},{4,6},{6,0},{1,3},{3,5},{5,7},{7,1},{8,10},{10,12},{12... | collective-permute-start | bytes 98312 | tf_op jit(solution)/shard_map/ppermute | solution.py:460
  14.8 3.3 %collective-permute-start.3 = (f32[32,256]{1,0:T(8,128)S(1)}, f32[32,256]{1,0:T(8,128)S(1)}, u32[]{:S(2)}, u32[]{:S(2)}) collective-permute-start(f32[32,256]{1,0:T(8,128)S(1)} %get-tuple-element.26), channel_id=1, source_target_pairs={{2,0},{4,2},{6,4},{0,6},{3,1},{5,3},{7,5},{1,7},{10,8},{12,10},{14... | collective-permute-start | bytes 98312 | tf_op jit(solution)/shard_map/ppermute | solution.py:461
  20.2 0.7 copy-start.2
  21.0 0.7 copy-start.4
  21.7 0.7 copy-start.6
  23.8 15.9 %collective-permute-start.4 = (f32[16,8,256]{2,1,0:T(8,128)}, f32[16,8,256]{2,1,0:T(8,128)}, u32[]{:S(2)}, u32[]{:S(2)}) collective-permute-start(f32[16,8,256]{2,1,0:T(8,128)} %copy-done.6), channel_id=1, source_target_pairs={{0,1},{1,0},{2,3},{3,2},{4,5},{5,4},{6,7},{7,6},{8,9},{9,8},{10,11... | collective-permute-start | bytes 393224 | tf_op jit(solution)/shard_map/ppermute | solution.py:479
  25.3 1.0 copy-start.3
  26.3 1.0 copy-start.5
  29.3 11.6 %collective-permute-start.5 = (f32[16,8,256]{2,1,0:T(8,128)}, f32[16,8,256]{2,1,0:T(8,128)}, u32[]{:S(2)}, u32[]{:S(2)}) collective-permute-start(f32[16,8,256]{2,1,0:T(8,128)} %sweeps.5.refs_2_), channel_id=1, source_target_pairs={{0,1},{1,0},{2,3},{3,2},{4,5},{5,4},{6,7},{7,6},{8,9},{9,8},{10,11... | collective-permute-start | bytes 393224 | tf_op jit(solution)/shard_map/ppermute | solution.py:479
  31.8 4.0 %copy-start.9 = (f32[56,56]{0,1:T(8,128)S(1)}, f32[56,56]{0,1:T(8,128)}, u32[]{:S(2)}) copy-start(f32[56,56]{0,1:T(8,128)} %copy.18) | copy-start | bytes 37636
  31.8 10.2 %collective-permute-start.6 = (f32[16,8,256]{2,1,0:T(8,128)}, f32[16,8,256]{2,1,0:T(8,128)}, u32[]{:S(2)}, u32[]{:S(2)}) collective-permute-start(f32[16,8,256]{2,1,0:T(8,128)} %sweeps.6.refs_3_), channel_id=1, source_target_pairs={{0,1},{1,0},{2,3},{3,2},{4,5},{5,4},{6,7},{7,6},{8,9},{9,8},{10,11... | collective-permute-start | bytes 393224 | tf_op jit(solution)/shard_map/ppermute | solution.py:479
  35.3 7.9 %collective-permute-start.7 = (f32[16,4,256]{2,1,0:T(4,128)}, f32[16,4,256]{2,1,0:T(4,128)S(1)}, u32[]{:S(2)}, u32[]{:S(2)}) collective-permute-start(f32[16,4,256]{2,1,0:T(4,128)} %sweeps.7.refs_4_), channel_id=1, source_target_pairs={{0,1},{1,0},{2,3},{3,2},{4,5},{5,4},{6,7},{7,6},{8,9},{9,8},{10,11... | collective-permute-start | bytes 196616 | tf_op jit(solution)/shard_map/ppermute | solution.py:479
  36.1 0.9 copy-start.7
  39.6 3.5 %copy-start.1 = (bf16[8,28,16,256]{3,2,1,0:T(8,128)(2,1)S(1)}, bf16[8,28,16,256]{3,2,1,0:T(8,128)(2,1)}, u32[]{:S(2)}) copy-start(bf16[8,28,16,256]{3,2,1,0:T(8,128)(2,1)} %copy-done) | copy-start | bytes 5505028
  43.2 68.8 %copy-start.8 = (f32[28,16,256]{2,1,0:T(8,128)S(1)}, f32[28,16,256]{2,1,0:T(8,128)}, u32[]{:S(2)}) copy-start(f32[28,16,256]{2,1,0:T(8,128)} %control_ref.1) | copy-start | bytes 1376260

commit v5 on v4

--- a/solution.py
+++ b/solution.py
@@ -22,7 +22,7 @@
 
 VMEM = pl.BlockSpec(memory_space=pltpu.VMEM)
 HBM = pl.BlockSpec(memory_space=pltpu.HBM)
-PARAMS = pltpu.CompilerParams(vmem_limit_bytes=48 * 1024 * 1024)
+PARAMS = pltpu.CompilerParams(vmem_limit_bytes=12 * 1024 * 1024)
 
 
 def f32(*shape):
@@ -483,12 +483,13 @@
     )
     for corr, part in other[:-1]:
         mixed = call(make_mix(False), f32(rows, steps, cols), (mixed, corr, part), name="mix_more")
+    devices = height * breadth * groups
     mixed, message = call(
-        last_mix_kernel, (f32(steps, rows, cols), f32(1, 1, LANE)),
+        last_mix_kernel, (f32(steps, rows, cols), f32(devices, 1, LANE)),
         (mixed, *other[-1], gram, pair_steps, pair_grads),
         scratch=[turn, pltpu.VMEM((NROW, LANE), jnp.float32)], name="mix_last",
     )
-    inbox = lax.all_gather(message, ("lat", "lon", "tm"), axis=0, tiled=True)
+    inbox = lax.all_to_all(message, ("lat", "lon", "tm"), split_axis=0, concat_axis=0, tiled=True)
     return call(
         final_kernel, f32(steps, rows, cols), (inbox, mixed, control, pair_steps, pair_grads),
         scratch=[pltpu.VMEM((NROW, LANE), jnp.float32)], name="final",

time: 114 us -> 59.9 us (0.53)
  blocking collectives: 67.5 us -> 12.9 us
    all_gather x1 -> x0, blocking collectives: 67.5 us -> none  [local(): inbox = lax.all_gather(message, ('lat', 'lon', 'tm'), axis=0, tiled=True)]
    all_to_all x0 -> x1, blocking collectives: none -> 12.9 us  [local(): lax.all_to_all(message, ('lat', 'lon', 'tm'), split_axis=0, concat_axis=0...]
  transfers between devices with their start and end apart: 8 -> 8, of which waited for: 2 -> 2; matrix products, arithmetic and copies ran while one was open for 1% -> 3% of each run, Pallas kernels for 14% -> 26%
where the time goes in v5:
time: 59.9 us; the launch traced here: 59.4 us
  Pallas kernels  22.4 us (37%)
  blocking collectives  12.9 us (22%)
  starting transfers between devices  12.1 us (20%)
  local copies, waits for them, and re-layouts  9.04 us (15%)
  waiting for transfers between devices  2.66 us (4%)
    pallas_call x14, Pallas kernels, call(): pl.pallas_call(kernel, out_shape=outs, in_specs=specs or [VMEM] * len(arg...  22.4 us
    all_to_all x1, blocking collectives, local(): lax.all_to_all(message, ('lat', 'lon', 'tm'), split_axis=0, concat_axis=0...  12.9 us
    unnamed x20, local copies, waits for them, and re-layouts  6.23 us
    ppermute x1, starting transfers between devices, local(): above = lax.ppermute(last, 'lat', down)  4.94 us
    ppermute x4, starting transfers between devices, local(): lax.ppermute(part, 'tm', pairs)  4.05 us
    ppermute x1, starting transfers between devices, local(): from_right = lax.ppermute(west, 'lon', left)  1.73 us
    ppermute x1, waiting for transfers between devices, local(): from_left = lax.ppermute(east, 'lon', right)  1.59 us
    optimization_barrier x1, local copies, waits for them, and re-layouts, local(): time_corr, part = lax.optimization_barrier((time_corr, part))  1.43 us
  transfers between devices with their start and end apart: 8, of which 2 were waited for; matrix products, arithmetic and copies ran while one was open for 3% of the time, Pallas kernels for 26%

profile of v5, /device:TPU:0, one launch (start us, length us, event | category | flops | bytes accessed | tf_op | source)
XLA Modules:
  0.0 59.4 jit_solution(16370472876277001120)
XLA Ops:
  0.0 1.2 %pack.1 = (f32[16,32,256]{2,1,0:T(8,128)S(1)}, f32[6,32,256]{2,1,0:T(8,128)S(1)}, f32[6,32,256]{2,1,0:T(8,128)S(1)}) custom-call(f32[28,16,256]{2,1,0:T(8,128)} %grad_hbm.1, s32[16,256]{1,0:T(8,128)} %mask_hbm.1, f32[16,256]{1,0:T(8,128)} %diff_hbm.1), custom_call_target="tpu_custom_call" | custom-call | tf_op jit(solution)/shard_map/pack/pallas_call | solution.py:34
  1.2 4.9 %collective-permute-start = (f32[6,32,256]{2,1,0:T(8,128)S(1)}, f32[6,32,256]{2,1,0:T(8,128)S(1)}, u32[]{:S(2)}, u32[]{:S(2)}) collective-permute-start(f32[6,32,256]{2,1,0:T(8,128)S(1)} %get-tuple-element.21), channel_id=1, source_target_pairs={{0,8},{8,16},{16,24},{1,9},{9,17},{17,25},{2,10},{10,18},{18,26},{... | collective-permute-start | bytes 589832 | tf_op jit(solution)/shard_map/ppermute | solution.py:449
  6.2 1.3 %collective-permute-start.1 = (f32[6,32,256]{2,1,0:T(8,128)S(1)}, f32[6,32,256]{2,1,0:T(8,128)S(1)}, u32[]{:S(2)}, u32[]{:S(2)}) collective-permute-start(f32[6,32,256]{2,1,0:T(8,128)S(1)} %get-tuple-element.23), channel_id=1, source_target_pairs={{8,0},{16,8},{24,16},{9,1},{17,9},{25,17},{10,2},{18,10},{26,18},{... | collective-permute-start | bytes 589832 | tf_op jit(solution)/shard_map/ppermute | solution.py:450
  7.5 4.6 %gram.1 = (f32[72,128]{1,0:T(8,128)S(1)}, bf16[8,28,16,256]{3,2,1,0:T(8,128)(2,1)S(1)}, bf16[8,28,16,256]{3,2,1,0:T(8,128)(2,1)S(1)}) custom-call(bf16[8,28,16,256]{3,2,1,0:T(8,128)(2,1)} %steps_hbm.1, bf16[8,28,16,256]{3,2,1,0:T(8,128)(2,1)} %grads_hbm.1), custom_call_target="tpu_custom_call" | custom-call | tf_op jit(solution)/shard_map/gram/pallas_call | solution.py:34
  12.1 1.3 %copy-done = bf16[8,28,16,256]{3,2,1,0:T(8,128)(2,1)} copy-done((bf16[8,28,16,256]{3,2,1,0:T(8,128)(2,1)}, bf16[8,28,16,256]{3,2,1,0:T(8,128)(2,1)S(1)}, u32[]{:S(2)}) %copy-start) | copy-done | bytes 1835032
  13.4 1.0 %collective-permute-done.1.below_ref = f32[6,32,256]{2,1,0:T(8,128)S(1)} collective-permute-done((f32[6,32,256]{2,1,0:T(8,128)S(1)}, f32[6,32,256]{2,1,0:T(8,128)S(1)}, u32[]{:S(2)}, u32[]{:S(2)}) %collective-permute-start.1) | collective-permute-done | bytes 196640 | tf_op jit(solution)/shard_map/ppermute | solution.py:450
  14.8 1.7 %collective-permute-start.3 = (f32[32,256]{1,0:T(8,128)S(1)}, f32[32,256]{1,0:T(8,128)S(1)}, u32[]{:S(2)}, u32[]{:S(2)}) collective-permute-start(f32[32,256]{1,0:T(8,128)S(1)} %get-tuple-element.26), channel_id=1, source_target_pairs={{2,0},{4,2},{6,4},{0,6},{3,1},{5,3},{7,5},{1,7},{10,8},{12,10},{14... | collective-permute-start | bytes 98312 | tf_op jit(solution)/shard_map/ppermute | solution.py:461
  16.5 1.6 %collective-permute-done.2.left_ref = f32[32,256]{1,0:T(8,128)S(1)} collective-permute-done((f32[32,256]{1,0:T(8,128)S(1)}, f32[32,256]{1,0:T(8,128)S(1)}, u32[]{:S(2)}, u32[]{:S(2)}) %collective-permute-start.2) | collective-permute-done | bytes 32800 | tf_op jit(solution)/shard_map/ppermute | solution.py:460
  18.9 1.4 %sweeps.4.refs_1_ = f32[16,8,256]{2,1,0:T(8,128)S(1)} custom-call(f32[6,32,256]{2,1,0:T(8,128)S(1)} %collective-permute-done.above_ref, f32[16,32,256]{2,1,0:T(8,128)S(1)} %get-tuple-element.22.field_ref, f32[6,32,256]{2,1,0:T(8,128)S(1)} %collective-permute-done.1.below_ref, f32[32,256]{1,0:T(8,128)S(1)} %collective-permute-done.2.left_ref, ...), custom_call_target="tpu_custom_call" | custom-call | tf_op jit(solution)/shard_map/sweeps/pallas_call | solution.py:34
  22.4 1.4 %copy.13 = f32[56,56]{0,1:T(8,128)} copy(f32[56,56]{1,0:T(8,128)} %param.11) | data formatting | bytes 25088 | tf_op jit(solution)/shard_map/optimization_barrier | solution.py:474
  23.8 1.5 %collective-permute-start.4 = (f32[16,8,256]{2,1,0:T(8,128)}, f32[16,8,256]{2,1,0:T(8,128)}, u32[]{:S(2)}, u32[]{:S(2)}) collective-permute-start(f32[16,8,256]{2,1,0:T(8,128)} %copy-done.6), channel_id=1, source_target_pairs={{0,1},{1,0},{2,3},{3,2},{4,5},{5,4},{6,7},{7,6},{8,9},{9,8},{10,11... | collective-permute-start | bytes 393224 | tf_op jit(solution)/shard_map/ppermute | solution.py:479
  25.3 1.0 %copy-done.3 = f32[28,8,384]{2,1,0:T(8,128)S(1)} copy-done((f32[28,8,384]{2,1,0:T(8,128)S(1)}, f32[28,8,384]{2,1,0:T(8,128)}, u32[]{:S(2)}) %copy-start.3) | copy-done | bytes 344088
  26.3 1.0 %copy-done.5 = f32[28,8,384]{2,1,0:T(8,128)S(1)} copy-done((f32[28,8,384]{2,1,0:T(8,128)S(1)}, f32[28,8,384]{2,1,0:T(8,128)}, u32[]{:S(2)}) %copy-start.5) | copy-done | bytes 344088
  27.2 2.0 %sweeps.5.refs_2_ = f32[16,8,256]{2,1,0:T(8,128)} custom-call(f32[6,32,256]{2,1,0:T(8,128)S(1)} %collective-permute-done.above_ref, f32[16,32,256]{2,1,0:T(8,128)S(1)} %get-tuple-element.22.field_ref, f32[6,32,256]{2,1,0:T(8,128)S(1)} %collective-permute-done.1.below_ref, f32[32,256]{1,0:T(8,128)S(1)} %collective-permute-done.2.left_ref, ...), custom_call_target="tpu_custom_call" | custom-call | tf_op jit(solution)/shard_map/sweeps/pallas_call | solution.py:34
  29.8 2.0 %sweeps.6.refs_3_ = f32[16,8,256]{2,1,0:T(8,128)} custom-call(f32[6,32,256]{2,1,0:T(8,128)S(1)} %collective-permute-done.above_ref, f32[16,32,256]{2,1,0:T(8,128)S(1)} %get-tuple-element.22.field_ref, f32[6,32,256]{2,1,0:T(8,128)S(1)} %collective-permute-done.1.below_ref, f32[32,256]{1,0:T(8,128)S(1)} %collective-permute-done.2.left_ref, ...), custom_call_target="tpu_custom_call" | custom-call | tf_op jit(solution)/shard_map/sweeps/pallas_call | solution.py:34
  31.8 1.5 %collective-permute-start.6 = (f32[16,8,256]{2,1,0:T(8,128)}, f32[16,8,256]{2,1,0:T(8,128)}, u32[]{:S(2)}, u32[]{:S(2)}) collective-permute-start(f32[16,8,256]{2,1,0:T(8,128)} %sweeps.6.refs_3_), channel_id=1, source_target_pairs={{0,1},{1,0},{2,3},{3,2},{4,5},{5,4},{6,7},{7,6},{8,9},{9,8},{10,11... | collective-permute-start | bytes 393224 | tf_op jit(solution)/shard_map/ppermute | solution.py:479
  33.3 2.0 %sweeps.7.refs_4_ = f32[16,4,256]{2,1,0:T(4,128)} custom-call(f32[6,32,256]{2,1,0:T(8,128)S(1)} %collective-permute-done.above_ref, f32[16,32,256]{2,1,0:T(8,128)S(1)} %get-tuple-element.22.field_ref, f32[6,32,256]{2,1,0:T(8,128)S(1)} %collective-permute-done.1.below_ref, f32[32,256]{1,0:T(8,128)S(1)} %collective-permute-done.2.left_ref, ...), custom_call_target="tpu_custom_call" | custom-call | tf_op jit(solution)/shard_map/sweeps/pallas_call | solution.py:34
  37.1 1.4 %mix_own.1.refs_0_ = f32[16,28,256]{2,1,0:T(8,128)S(1)} custom-call(bf16[28,192]{1,0:T(8,128)(2,1)S(1)} %concatenate.20.refs_0_, f32[16,8,256]{2,1,0:T(8,128)S(1)} %copy-done.7, f32[16,8,256]{2,1,0:T(8,128)} %sweeps.5.refs_2_, f32[16,8,256]{2,1,0:T(8,128)} %sweeps.6.refs_3_, f32[16,4,256]{2,1,0:T(4,128)} %sweeps.7.refs_4_), custom_call_target="tpu_custom_call" | custom-call | tf_op jit(solution)/shard_map/mix_own/pallas_call | solution.py:34
  39.7 1.2 %mix_more.3.refs_0_ = f32[16,28,256]{2,1,0:T(8,128)S(1)} custom-call(f32[16,28,256]{2,1,0:T(8,128)S(1)} %mix_own.1.refs_0_, bf16[28,48]{1,0:T(8,128)(2,1)S(1)} %concatenate.21.refs_1_, f32[16,8,256]{2,1,0:T(8,128)} %collective-permute-done.4.refs_2_), custom_call_target="tpu_custom_call" | custom-call | tf_op jit(solution)/shard_map/mix_more/pallas_call | solution.py:34
  40.9 1.1 %mix_more.4.refs_0_ = f32[16,28,256]{2,1,0:T(8,128)S(1)} custom-call(f32[16,28,256]{2,1,0:T(8,128)S(1)} %mix_more.3.refs_0_, bf16[28,48]{1,0:T(8,128)(2,1)S(1)} %concatenate.22.refs_1_, f32[16,8,256]{2,1,0:T(8,128)} %collective-permute-done.5.refs_2_), custom_call_target="tpu_custom_call" | custom-call | tf_op jit(solution)/shard_map/mix_more/pallas_call | solution.py:34
  42.1 1.1 %mix_more.5.acc_ref = f32[16,28,256]{2,1,0:T(8,128)S(1)} custom-call(f32[16,28,256]{2,1,0:T(8,128)S(1)} %mix_more.4.refs_0_, bf16[28,48]{1,0:T(8,128)(2,1)S(1)} %concatenate.23.refs_1_, f32[16,8,256]{2,1,0:T(8,128)} %collective-permute-done.6.refs_2_), custom_call_target="tpu_custom_call" | custom-call | tf_op jit(solution)/shard_map/mix_more/pallas_call | solution.py:34
  43.2 1.3 %mix_last.1 = (f32[28,16,256]{2,1,0:T(8,128)S(1)}, f32[32,1,128]{2,1,0:T(1,128)S(1)}) custom-call(f32[16,28,256]{2,1,0:T(8,128)S(1)} %mix_more.5.acc_ref, bf16[28,48]{1,0:T(8,128)(2,1)S(1)} %concatenate.24.corr_ref, f32[16,4,256]{2,1,0:T(4,128)S(1)} %collective-permute-done.7.field_ref, f32[72,128]{1,0:T(8,128)S(1)} %get-tuple-element.24.order_ref.gram_ref, ...), custom_call_target="tpu_custom_call" | custom-call | tf_op jit(solution)/shard_map/mix_last/pallas_call | solution.py:34
  44.5 12.9 %all_to_all.5.inbox_ref = f32[32,1,128]{2,1,0:T(1,128)S(1)} all-to-all(f32[32,1,128]{2,1,0:T(1,128)S(1)} %get-tuple-element.35), channel_id=1, replica_groups=mesh['lat'=4,'lon'=4,'tm'=2] {'lat','lon','tm'}, dimensions={0} | all-to-all | bytes 32768 | tf_op jit(solution)/shard_map/all_to_all | solution.py:492
  57.4 2.0 %final.1 = f32[28,16,256]{2,1,0:T(8,128)} custom-call(f32[32,1,128]{2,1,0:T(1,128)S(1)} %all_to_all.5.inbox_ref, f32[28,16,256]{2,1,0:T(8,128)S(1)} %get-tuple-element.36.mixed_ref, f32[28,16,256]{2,1,0:T(8,128)S(1)} %copy-done.8, bf16[8,28,16,256]{3,2,1,0:T(8,128)(2,1)S(1)} %get-tuple-element.33.steps_ref, bf16[8,28,16,256]{3,2,1,0:T(8,128)(2,1)S(1)} %copy-done.1), custom_call_target="tpu_custom_call" | custom-call | tf_op jit(solution)/shard_map/final/pallas_call | solution.py:34
  (38 shorter events, 6.7 us)
Async XLA Ops:
  1.2 12.2 %collective-permute-start = (f32[6,32,256]{2,1,0:T(8,128)S(1)}, f32[6,32,256]{2,1,0:T(8,128)S(1)}, u32[]{:S(2)}, u32[]{:S(2)}) collective-permute-start(f32[6,32,256]{2,1,0:T(8,128)S(1)} %get-tuple-element.21), channel_id=1, source_target_pairs={{0,8},{8,16},{16,24},{1,9},{9,17},{17,25},{2,10},{10,18},{18,26},{... | collective-permute-start | bytes 589832 | tf_op jit(solution)/shard_map/ppermute | solution.py:449
  6.2 8.3 %collective-permute-start.1 = (f32[6,32,256]{2,1,0:T(8,128)S(1)}, f32[6,32,256]{2,1,0:T(8,128)S(1)}, u32[]{:S(2)}, u32[]{:S(2)}) collective-permute-start(f32[6,32,256]{2,1,0:T(8,128)S(1)} %get-tuple-element.23), channel_id=1, source_target_pairs={{8,0},{16,8},{24,16},{9,1},{17,9},{25,17},{10,2},{18,10},{26,18},{... | collective-permute-start | bytes 589832 | tf_op jit(solution)/shard_map/ppermute | solution.py:450
  12.1 1.3 %copy-start = (bf16[8,28,16,256]{3,2,1,0:T(8,128)(2,1)}, bf16[8,28,16,256]{3,2,1,0:T(8,128)(2,1)S(1)}, u32[]{:S(2)}) copy-start(bf16[8,28,16,256]{3,2,1,0:T(8,128)(2,1)S(1)} %get-tuple-element.34.grads_ref) | copy-start | bytes 5505028
  14.7 3.4 %collective-permute-start.2 = (f32[32,256]{1,0:T(8,128)S(1)}, f32[32,256]{1,0:T(8,128)S(1)}, u32[]{:S(2)}, u32[]{:S(2)}) collective-permute-start(f32[32,256]{1,0:T(8,128)S(1)} %get-tuple-element.25), channel_id=1, source_target_pairs={{0,2},{2,4},{4,6},{6,0},{1,3},{3,5},{5,7},{7,1},{8,10},{10,12},{12... | collective-permute-start | bytes 98312 | tf_op jit(solution)/shard_map/ppermute | solution.py:460
  14.8 3.3 %collective-permute-start.3 = (f32[32,256]{1,0:T(8,128)S(1)}, f32[32,256]{1,0:T(8,128)S(1)}, u32[]{:S(2)}, u32[]{:S(2)}) collective-permute-start(f32[32,256]{1,0:T(8,128)S(1)} %get-tuple-element.26), channel_id=1, source_target_pairs={{2,0},{4,2},{6,4},{0,6},{3,1},{5,3},{7,5},{1,7},{10,8},{12,10},{14... | collective-permute-start | bytes 98312 | tf_op jit(solution)/shard_map/ppermute | solution.py:461
  20.2 0.7 %copy-start.2 = (f32[28,8,384]{2,1,0:T(8,128)}, f32[28,8,384]{2,1,0:T(8,128)S(1)}, u32[]{:S(2)}) copy-start(f32[28,8,384]{2,1,0:T(8,128)S(1)} %get-tuple-element.29.west_ref) | copy-start | bytes 1032196
  21.0 0.7 %copy-start.4 = (f32[28,8,384]{2,1,0:T(8,128)}, f32[28,8,384]{2,1,0:T(8,128)S(1)}, u32[]{:S(2)}) copy-start(f32[28,8,384]{2,1,0:T(8,128)S(1)} %get-tuple-element.30.keep_ref) | copy-start | bytes 1032196
  21.7 0.7 %copy-start.6 = (f32[16,8,256]{2,1,0:T(8,128)}, f32[16,8,256]{2,1,0:T(8,128)S(1)}, u32[]{:S(2)}) copy-start(f32[16,8,256]{2,1,0:T(8,128)S(1)} %sweeps.4.refs_1_) | copy-start | bytes 393220
  23.8 15.9 %collective-permute-start.4 = (f32[16,8,256]{2,1,0:T(8,128)}, f32[16,8,256]{2,1,0:T(8,128)}, u32[]{:S(2)}, u32[]{:S(2)}) collective-permute-start(f32[16,8,256]{2,1,0:T(8,128)} %copy-done.6), channel_id=1, source_target_pairs={{0,1},{1,0},{2,3},{3,2},{4,5},{5,4},{6,7},{7,6},{8,9},{9,8},{10,11... | collective-permute-start | bytes 393224 | tf_op jit(solution)/shard_map/ppermute | solution.py:479
  25.3 1.0 %copy-start.3 = (f32[28,8,384]{2,1,0:T(8,128)S(1)}, f32[28,8,384]{2,1,0:T(8,128)}, u32[]{:S(2)}) copy-start(f32[28,8,384]{2,1,0:T(8,128)} %copy-done.2) | copy-start | bytes 1032196
  26.3 1.0 %copy-start.5 = (f32[28,8,384]{2,1,0:T(8,128)S(1)}, f32[28,8,384]{2,1,0:T(8,128)}, u32[]{:S(2)}) copy-start(f32[28,8,384]{2,1,0:T(8,128)} %copy-done.4) | copy-start | bytes 1032196
  29.3 11.6 %collective-permute-start.5 = (f32[16,8,256]{2,1,0:T(8,128)}, f32[16,8,256]{2,1,0:T(8,128)}, u32[]{:S(2)}, u32[]{:S(2)}) collective-permute-start(f32[16,8,256]{2,1,0:T(8,128)} %sweeps.5.refs_2_), channel_id=1, source_target_pairs={{0,1},{1,0},{2,3},{3,2},{4,5},{5,4},{6,7},{7,6},{8,9},{9,8},{10,11... | collective-permute-start | bytes 393224 | tf_op jit(solution)/shard_map/ppermute | solution.py:479
  31.8 4.0 %copy-start.9 = (f32[56,56]{0,1:T(8,128)S(1)}, f32[56,56]{0,1:T(8,128)}, u32[]{:S(2)}) copy-start(f32[56,56]{0,1:T(8,128)} %copy.13) | copy-start | bytes 37636
  31.8 10.2 %collective-permute-start.6 = (f32[16,8,256]{2,1,0:T(8,128)}, f32[16,8,256]{2,1,0:T(8,128)}, u32[]{:S(2)}, u32[]{:S(2)}) collective-permute-start(f32[16,8,256]{2,1,0:T(8,128)} %sweeps.6.refs_3_), channel_id=1, source_target_pairs={{0,1},{1,0},{2,3},{3,2},{4,5},{5,4},{6,7},{7,6},{8,9},{9,8},{10,11... | collective-permute-start | bytes 393224 | tf_op jit(solution)/shard_map/ppermute | solution.py:479
  35.3 7.9 %collective-permute-start.7 = (f32[16,4,256]{2,1,0:T(4,128)}, f32[16,4,256]{2,1,0:T(4,128)S(1)}, u32[]{:S(2)}, u32[]{:S(2)}) collective-permute-start(f32[16,4,256]{2,1,0:T(4,128)} %sweeps.7.refs_4_), channel_id=1, source_target_pairs={{0,1},{1,0},{2,3},{3,2},{4,5},{5,4},{6,7},{7,6},{8,9},{9,8},{10,11... | collective-permute-start | bytes 196616 | tf_op jit(solution)/shard_map/ppermute | solution.py:479
  36.1 0.9 %copy-start.7 = (f32[16,8,256]{2,1,0:T(8,128)S(1)}, f32[16,8,256]{2,1,0:T(8,128)}, u32[]{:S(2)}) copy-start(f32[16,8,256]{2,1,0:T(8,128)} %copy-done.6) | copy-start | bytes 393220
  39.6 3.5 %copy-start.1 = (bf16[8,28,16,256]{3,2,1,0:T(8,128)(2,1)S(1)}, bf16[8,28,16,256]{3,2,1,0:T(8,128)(2,1)}, u32[]{:S(2)}) copy-start(bf16[8,28,16,256]{3,2,1,0:T(8,128)(2,1)} %copy-done) | copy-start | bytes 5505028
  43.2 14.2 %copy-start.8 = (f32[28,16,256]{2,1,0:T(8,128)S(1)}, f32[28,16,256]{2,1,0:T(8,128)}, u32[]{:S(2)}) copy-start(f32[28,16,256]{2,1,0:T(8,128)} %control_ref.1) | copy-start | bytes 1376260

commit v6 on v5

--- a/solution.py
+++ b/solution.py
@@ -104,7 +104,7 @@
     return -(-(steps + 1) // SUB) * SUB
 
 
-def pack_kernel(grad_hbm, mask_hbm, diff_hbm, field_ref, first_ref, last_ref, grad_ref, mask_ref, diff_ref, turn_ref, sems):
+def pack_kernel(grad_hbm, mask_hbm, diff_hbm, field_ref, swap_ref, next_ref, grad_ref, mask_ref, diff_ref, turn_ref, sems):
     steps, rows, cols = grad_ref.shape
     slots = field_ref.shape[1]
     pieces = [(begin, min(SUB, steps - begin)) for begin in range(0, steps, SUB)]
@@ -138,34 +138,32 @@
             for slot in range(0, slots, SUB):
                 value = turn_ref[pl.ds(base + slot * SUB, SUB, stride=SUB), :]
                 field_ref[row, slot:slot + SUB, across] = value
-                if row < HALO:
-                    first_ref[row, slot:slot + SUB, across] = value
-                if row >= rows - HALO:
-                    last_ref[row - (rows - HALO), slot:slot + SUB, across] = value
-
-
-def extended(row, above_ref, field_ref, below_ref):
-    rows = field_ref.shape[0]
-    if row < HALO:
-        return above_ref, row
-    if row < HALO + rows:
-        return field_ref, row - HALO
-    return below_ref, row - HALO - rows
-
-
-def side_kernel(above_ref, field_ref, below_ref, order_ref, west_ref, east_ref):
+    odd = lax.rem(lax.axis_index("lat"), 2)
+    near, far = (1 - odd) * (rows - HALO), odd * (rows - HALO)
+    for row in range(HALO):
+        swap_ref[row] = field_ref[near + row]
+        next_ref[row] = field_ref[far + row]
+
+
+def side_kernel(swap_ref, field_ref, next_ref, order_ref, whole_ref, west_ref, east_ref):
     rows, slots, cols = field_ref.shape
+    odd = lax.rem(lax.axis_index("lat"), 2)
+    near, far = (1 - odd) * (HALO + rows), odd * (HALO + rows)
+    for row in range(HALO):
+        whole_ref[near + row] = swap_ref[row]
+        whole_ref[far + row] = next_ref[row]
+    for row in range(rows):
+        whole_ref[HALO + row] = field_ref[row]
     lane = lane_index()
     for slot in range(0, slots, SUB):
         down = slice(slot, slot + SUB)
         for base in range(0, rows + 2 * HALO, PER):
             west = east = jnp.zeros((SUB, LANE), jnp.float32)
             for row in range(base, min(base + PER, rows + 2 * HALO)):
-                ref, at = extended(row, above_ref, field_ref, below_ref)
                 begin = (row - base) * GROUP
                 here = (lane >= begin) & (lane < begin + GROUP)
-                left = ref[at, down, 0:LANE]
-                right = ref[at, down, cols - LANE:cols]
+                left = whole_ref[row, down, 0:LANE]
+                right = whole_ref[row, down, cols - LANE:cols]
                 west = jnp.where(here, pltpu.roll(left, begin, 1) if begin else left, west)
                 turn = (begin + GROUP) % LANE
                 east = jnp.where(here, pltpu.roll(right, turn, 1) if turn else right, east)
@@ -174,19 +172,15 @@
             east_ref[down, place] = east
 
 
-def make_row_loader(above_ref, field_ref, below_ref, left_ref, right_ref):
-    cols = field_ref.shape[2]
-    lane = lane_index()
-
-    def load(row, down, size):
-        ref, at = extended(row, above_ref, field_ref, below_ref)
+def make_row_loader(whole_ref, left_ref, right_ref):
+    cols = whole_ref.shape[2]
+    lane = lax.broadcasted_iota(jnp.int32, (1, LANE), 1)
+
+    def load(row, down):
         place = slice(row // PER * LANE, (row // PER + 1) * LANE)
         begin = row % PER * GROUP
-        tiles = [ref[at, down, c * LANE:(c + 1) * LANE] for c in range(cols // LANE)]
+        tiles = [whole_ref[row, down, c * LANE:(c + 1) * LANE] for c in range(cols // LANE)]
         east, west = right_ref[down, place], left_ref[down, place]
-        if size == 1:
-            tiles = [jnp.broadcast_to(tile, (SUB, LANE)) for tile in tiles]
-            east, west = (jnp.broadcast_to(tile, (SUB, LANE)) for tile in (east, west))
         east = pltpu.roll(east, LANE - begin, 1) if begin else east
         turn = (2 * LANE - GROUP - begin) % LANE
         west = pltpu.roll(west, turn, 1) if turn else west
@@ -205,39 +199,45 @@
     return [jnp.where(at_start, turned[c - 1], turned[c]) for c in range(len(tiles))]
 
 
-def weight_kernel(above_ref, field_ref, below_ref, left_ref, right_ref, south_ref, east_ref, west_ref, keep_ref, *, steps):
-    rows, _, cols = field_ref.shape
-    load = make_row_loader(above_ref, field_ref, below_ref, left_ref, right_ref)
+def weight_kernel(
+    whole_ref, left_ref, right_ref, south_ref, east_ref, west_ref, keep_ref, kappa_ref, packed_ref, *, steps
+):
+    height, _, cols = whole_ref.shape
+    width = cols // LANE + 1
+    load = make_row_loader(whole_ref, left_ref, right_ref)
     lane = lane_index()
     at_start, at_end = lane == 0, lane == LANE - 1
-    height = rows + 2 * HALO
-    above = None
     for row in range(height):
-        kappa = load(row, slice(steps, steps + 1), 1)
+        for c, tile in enumerate(load(row, slice(steps, steps + 1))):
+            kappa_ref[row:row + 1, c * LANE:(c + 1) * LANE] = tile
+    for first in range(0, height, SUB):
+        down = slice(first, first + SUB)
+        kappa = [kappa_ref[down, c * LANE:(c + 1) * LANE] for c in range(width)]
+        below = [kappa_ref[first + 1:first + 1 + SUB, c * LANE:(c + 1) * LANE] for c in range(width)]
         beside = from_east(kappa, at_end)
-        east = [0.5 * (kappa[c] + beside[c]) for c in range(len(kappa))]
+        east = [0.5 * (kappa[c] + beside[c]) for c in range(width)]
         west = from_west(east, at_start)
-        for c in range(len(kappa)):
+        for c in range(width):
             across = slice(c * LANE, (c + 1) * LANE)
-            east_ref[row, :, across] = east[c]
-            west_ref[row, :, across] = west[c]
-            keep_ref[row, :, across] = 1.0 - east[c] - west[c]
-            if above is not None:
-                south_ref[row - 1, :, across] = 0.5 * (above[c] + kappa[c])
-            if row in (HALO - 1, HALO + rows):
-                south_ref[height - 1 + (row >= HALO), :, across] = jnp.where(kappa[c] > 0.0, 1.0, 0.0)
-        above = kappa
-
-
-def sweep_kernel(
-    above_ref, field_ref, below_ref, left_ref, right_ref, south_ref, east_ref, west_ref, keep_ref, out_ref, *, begin
-):
-    rows, _, cols = field_ref.shape
-    height, width = rows + 2 * HALO, cols // LANE + 1
+            packed_ref[0, down, across] = 0.5 * (kappa[c] + below[c])
+            packed_ref[1, down, across] = east[c]
+            packed_ref[2, down, across] = west[c]
+            packed_ref[3, down, across] = 1.0 - east[c] - west[c]
+    for n, ref in enumerate((south_ref, east_ref, west_ref, keep_ref)):
+        for row in range(height - 1):
+            ref[row] = jnp.broadcast_to(packed_ref[n, row:row + 1, :], ref.shape[1:])
+    for side, row in enumerate((HALO - 1, height - HALO)):
+        inside = jnp.where(kappa_ref[row:row + 1, :] > 0.0, 1.0, 0.0)
+        south_ref[height - 1 + side] = jnp.broadcast_to(inside, south_ref.shape[1:])
+
+
+def sweep_kernel(whole_ref, left_ref, right_ref, south_ref, east_ref, west_ref, keep_ref, out_ref, *, begin):
+    height, _, cols = whole_ref.shape
+    rows, width = height - 2 * HALO, cols // LANE + 1
     count = out_ref.shape[1]
     lane = lane_index()
     at_start, at_end = lane == 0, lane == LANE - 1
-    load = make_row_loader(above_ref, field_ref, below_ref, left_ref, right_ref)
+    load = make_row_loader(whole_ref, left_ref, right_ref)
     state = [None] * SWEEPS
 
     def at(ref, row, c):
@@ -273,7 +273,7 @@
                 out_ref[row - HALO, :, c * LANE:(c + 1) * LANE] = tiles[c][:count]
         for sweep in reversed(range(SWEEPS)):
             if sweep == 0:
-                entry = (tick, load(tick, slice(begin, begin + SUB), SUB)) if tick < height else None
+                entry = (tick, load(tick, slice(begin, begin + SUB))) if tick < height else None
             else:
                 entry = waiting[sweep]
             waiting[sweep + 1] = None
@@ -291,14 +291,24 @@
     return jnp.concatenate([high, middle, high, low, middle, high], axis=0).astype(jnp.bfloat16)
 
 
-def corr_stack(time_corr, source, target, count, steps):
-    block = lax.dynamic_slice(time_corr, (source, target), (count, steps))
-    block = jnp.pad(block, ((0, -count % SUB), (0, 0))).T
-    high = lax.reduce_precision(block, 8, 7)
-    rest = block - high
-    middle = lax.reduce_precision(rest, 8, 7)
-    low = rest - middle
-    return jnp.concatenate([high, high, middle, high, middle, low], axis=1).astype(jnp.bfloat16)
+def corr_kernel(corr_ref, *out_refs, groups, steps, sources):
+    mine = lax.axis_index("tm")
+    for at in range(groups):
+        @pl.when(mine == at)
+        def _(at=at):
+            for (shift, begin, count), out_ref in zip(sources, out_refs):
+                source = (at - shift) % groups * steps + begin
+                block = corr_ref[source:source + count, at * steps:(at + 1) * steps]
+                high = block.astype(jnp.bfloat16).astype(jnp.float32)
+                rest = block - high
+                middle = rest.astype(jnp.bfloat16).astype(jnp.float32)
+                low = rest - middle
+                depth = out_ref.shape[1] // 6
+                pad = [jnp.zeros((depth - count, steps), jnp.float32)] if depth > count else []
+                stack = []
+                for part in (high, high, middle, high, middle, low):
+                    stack += [part, *pad]
+                out_ref[...] = jnp.concatenate(stack, axis=0).T.astype(jnp.bfloat16)
 
 
 def mixed_row(row, corr_ref, field_refs):
@@ -427,15 +437,14 @@
 def local(gradient, control, diffusivity, land_mask, time_corr, pair_steps, pair_grads):
     steps, rows, cols = gradient.shape
     height, breadth, groups = (lax.axis_size(axis) for axis in ("lat", "lon", "tm"))
-    mine = lax.axis_index("tm")
-    down = [(i, i + 1) for i in range(height - 1)]
-    up = [(i + 1, i) for i in range(height - 1)]
+    even = [(i, j) for k in range(0, height - 1, 2) for i, j in ((k, k + 1), (k + 1, k))]
+    odd = [(i, j) for k in range(1, height - 1, 2) for i, j in ((k, k + 1), (k + 1, k))]
     right = [(i, (i + 1) % breadth) for i in range(breadth)]
     left = [(j, i) for i, j in right]
     slots = slots_of(steps)
     turn = pltpu.VMEM((rows * (cols // LANE) * slots, LANE), jnp.float32)
 
-    field, first, last = call(
+    field, to_swap, to_next = call(
         pack_kernel,
         (f32(rows, slots, cols), f32(HALO, slots, cols), f32(HALO, slots, cols)),
         [pltpu.with_memory_space_constraint(v, pltpu.HBM) for v in (gradient, land_mask, diffusivity)],
@@ -446,8 +455,8 @@
         ],
         name="pack",
     )
-    above = lax.ppermute(last, "lat", down)
-    below = lax.ppermute(first, "lat", up)
+    from_swap = lax.ppermute(to_swap, "lat", even)
+    from_next = lax.ppermute(to_next, "lat", odd)
     pair_shape = jax.ShapeDtypeStruct(pair_steps.shape, jnp.bfloat16)
     gram, pair_steps, pair_grads = call(
         gram_kernel, (f32(NGRAM, LANE), pair_shape, pair_shape),
@@ -455,38 +464,43 @@
         scratch=[pltpu.SemaphoreType.DMA((2, 4))],
         name="gram",
     )
-    side_shape = f32(slots, -(-(rows + 2 * HALO) // PER) * LANE)
-    west, east = call(side_kernel, (side_shape, side_shape), (above, field, below, gram), name="sides")
+    tall, wide = rows + 2 * HALO, cols + LANE
+    parts = groups_of(steps)
+    sources = [(0, 0, steps)] + [(shift, *part) for part in parts for shift in range(1, groups)]
+    own_corr, *corrs = call(
+        functools.partial(corr_kernel, groups=groups, steps=steps, sources=sources),
+        [jax.ShapeDtypeStruct((steps, 6 * (count + -count % SUB)), jnp.bfloat16) for _, _, count in sources],
+        (time_corr,), name="corr",
+    )
+    side_shape = f32(slots, -(-tall // PER) * LANE)
+    whole, west, east = call(
+        side_kernel, (f32(tall, slots, cols), side_shape, side_shape), (from_swap, field, from_next, gram), name="sides"
+    )
     from_left = lax.ppermute(east, "lon", right)
     from_right = lax.ppermute(west, "lon", left)
-    whole = (above, field, below, from_left, from_right)
-    tall, wide = rows + 2 * HALO, cols + LANE
+    extended = (whole, from_left, from_right)
     weights = call(
         functools.partial(weight_kernel, steps=steps),
-        (f32(tall + 1, SUB, wide), f32(tall, SUB, wide), f32(tall, SUB, wide), f32(tall, SUB, wide)), whole, name="weights",
+        (f32(tall + 1, SUB, wide), f32(tall, SUB, wide), f32(tall, SUB, wide), f32(tall, SUB, wide)), extended,
+        scratch=[pltpu.VMEM((-(-tall // SUB) * SUB + SUB, wide), jnp.float32), pltpu.VMEM((4, -(-tall // SUB) * SUB, wide), jnp.float32)],
+        name="weights",
     )
     own, other = [], []
-    for begin, count in groups_of(steps):
+    for begin, count in parts:
         part = call(
-            functools.partial(sweep_kernel, begin=begin), f32(rows, count, cols), (*whole, *weights), name="sweeps"
+            functools.partial(sweep_kernel, begin=begin), f32(rows, count, cols), (*extended, *weights), name="sweeps"
         )
-        if not own:
-            time_corr, part = lax.optimization_barrier((time_corr, part))
         own.append(part)
         for shift in range(1, groups):
             pairs = [(i, (i + shift) % groups) for i in range(groups)]
-            source = lax.rem(mine - shift + groups, groups) * steps + begin
-            other.append((corr_stack(time_corr, source, mine * steps, count, steps), lax.ppermute(part, "tm", pairs)))
-    mixed = call(
-        make_mix(True), f32(rows, steps, cols),
-        (corr_stack(time_corr, mine * steps, mine * steps, steps, steps), *own), name="mix_own",
-    )
-    for corr, part in other[:-1]:
+            other.append(lax.ppermute(part, "tm", pairs))
+    mixed = call(make_mix(True), f32(rows, steps, cols), (own_corr, *own), name="mix_own")
+    for corr, part in zip(corrs[:-1], other[:-1]):
         mixed = call(make_mix(False), f32(rows, steps, cols), (mixed, corr, part), name="mix_more")
     devices = height * breadth * groups
     mixed, message = call(
         last_mix_kernel, (f32(steps, rows, cols), f32(devices, 1, LANE)),
-        (mixed, *other[-1], gram, pair_steps, pair_grads),
+        (mixed, corrs[-1], other[-1], gram, pair_steps, pair_grads),
         scratch=[turn, pltpu.VMEM((NROW, LANE), jnp.float32)], name="mix_last",
     )
     inbox = lax.all_to_all(message, ("lat", "lon", "tm"), split_axis=0, concat_axis=0, tiled=True)

time: 59.9 us -> 46.4 us (0.77)
  local copies, waits for them, and re-layouts: 9.04 us -> 0.01 us
  Pallas kernels: 22.4 us -> 16.2 us
  waiting for transfers between devices: 2.66 us -> 5.35 us
  starting transfers between devices: 12.1 us -> 9.85 us
  blocking collectives: 12.9 us -> 14.6 us
    unnamed x20 -> x4, local copies, waits for them, and re-layouts: 6.23 us -> 0.01 us
    pallas_call x14 -> x15, Pallas kernels: 22.4 us -> 16.2 us  [call(): pl.pallas_call(kernel, out_shape=outs, in_specs=specs or [VMEM] * len(arg...]
    ppermute x6, waiting for transfers between devices: 1.06 us -> 3.76 us  [the longest x4 3.75 us: local(): other.append(lax.ppermute(part, 'tm', pairs))]
    ppermute x6, starting transfers between devices: 10.3 us -> 8.06 us  [the longest x4 4.31 us: local(): other.append(lax.ppermute(part, 'tm', pairs))]
    all_to_all x1, blocking collectives: 12.9 us -> 14.6 us  [local(): lax.all_to_all(message, ('lat', 'lon', 'tm'), split_axis=0, concat_axis=0...]
    optimization_barrier x1 -> x0, local copies, waits for them, and re-layouts: 1.43 us -> none  [local(): time_corr, part = lax.optimization_barrier((time_corr, part))]
    dynamic_slice x2 -> x0, local copies, waits for them, and re-layouts: 0.89 us -> none  [corr_stack(): block = lax.dynamic_slice(time_corr, (source, target), (count, steps))]
  transfers between devices with their start and end apart: 8 -> 8, of which waited for: 2 -> 3; matrix products, arithmetic and copies ran while one was open for 3% -> 0% of each run, Pallas kernels for 26% -> 21%
where the time goes in v6:
time: 46.4 us; the launch traced here: 46.2 us
  Pallas kernels  16.2 us (35%)
  blocking collectives  14.6 us (31%)
  starting transfers between devices  9.85 us (21%)
  waiting for transfers between devices  5.35 us (12%)
    pallas_call x15, Pallas kernels, call(): pl.pallas_call(kernel, out_shape=outs, in_specs=specs or [VMEM] * len(arg...  16.2 us
    all_to_all x1, blocking collectives, local(): lax.all_to_all(message, ('lat', 'lon', 'tm'), split_axis=0, concat_axis=0...  14.6 us
    ppermute x4, starting transfers between devices, local(): other.append(lax.ppermute(part, 'tm', pairs))  4.31 us
    ppermute x4, waiting for transfers between devices, local(): other.append(lax.ppermute(part, 'tm', pairs))  3.75 us
    ppermute x1, starting transfers between devices, local(): from_swap = lax.ppermute(to_swap, 'lat', even)  3.09 us
    ppermute x1, starting transfers between devices, local(): from_right = lax.ppermute(west, 'lon', left)  1.73 us
    ppermute x1, waiting for transfers between devices, local(): from_left = lax.ppermute(east, 'lon', right)  1.59 us
  transfers between devices with their start and end apart: 8, of which 3 were waited for; matrix products, arithmetic and copies ran while one was open for 0% of the time, Pallas kernels for 21%

profile of v6, /device:TPU:0, one launch (start us, length us, event | category | flops | bytes accessed | tf_op | source)
XLA Modules:
  0.0 46.2 jit_solution(2666073245816890527)
XLA Ops:
  0.0 1.3 %pack.1 = (f32[16,32,256]{2,1,0:T(8,128)S(1)}, f32[6,32,256]{2,1,0:T(8,128)S(1)}, f32[6,32,256]{2,1,0:T(8,128)S(1)}) custom-call(f32[28,16,256]{2,1,0:T(8,128)} %grad_hbm.1, s32[16,256]{1,0:T(8,128)} %mask_hbm.1, f32[16,256]{1,0:T(8,128)} %diff_hbm.1), custom_call_target="tpu_custom_call" | custom-call | tf_op jit(solution)/shard_map/pack/pallas_call | solution.py:34
  1.3 3.1 %collective-permute-start = (f32[6,32,256]{2,1,0:T(8,128)S(1)}, f32[6,32,256]{2,1,0:T(8,128)S(1)}, u32[]{:S(2)}, u32[]{:S(2)}) collective-permute-start(f32[6,32,256]{2,1,0:T(8,128)S(1)} %get-tuple-element.26), channel_id=1, source_target_pairs={{0,8},{8,0},{16,24},{24,16},{1,9},{9,1},{17,25},{25,17},{2,10},{10... | collective-permute-start | bytes 589832 | tf_op jit(solution)/shard_map/ppermute | solution.py:458
  4.3 0.7 %collective-permute-start.1 = (f32[6,32,256]{2,1,0:T(8,128)S(1)}, f32[6,32,256]{2,1,0:T(8,128)S(1)}, u32[]{:S(2)}, u32[]{:S(2)}) collective-permute-start(f32[6,32,256]{2,1,0:T(8,128)S(1)} %get-tuple-element.28), channel_id=1, source_target_pairs={{8,16},{16,8},{9,17},{17,9},{10,18},{18,10},{11,19},{19,11},{12,20... | collective-permute-start | bytes 589832 | tf_op jit(solution)/shard_map/ppermute | solution.py:459
  5.0 4.6 %gram.1 = (f32[72,128]{1,0:T(8,128)S(1)}, bf16[8,28,16,256]{3,2,1,0:T(8,128)(2,1)S(1)}, bf16[8,28,16,256]{3,2,1,0:T(8,128)(2,1)S(1)}) custom-call(bf16[8,28,16,256]{3,2,1,0:T(8,128)(2,1)} %steps_hbm.1, bf16[8,28,16,256]{3,2,1,0:T(8,128)(2,1)} %grads_hbm.1), custom_call_target="tpu_custom_call" | custom-call | tf_op jit(solution)/shard_map/gram/pallas_call | solution.py:34
  9.7 0.3 sides.1
  10.1 1.7 %collective-permute-start.3 = (f32[32,256]{1,0:T(8,128)S(1)}, f32[32,256]{1,0:T(8,128)S(1)}, u32[]{:S(2)}, u32[]{:S(2)}) collective-permute-start(f32[32,256]{1,0:T(8,128)S(1)} %get-tuple-element.32), channel_id=1, source_target_pairs={{2,0},{4,2},{6,4},{0,6},{3,1},{5,3},{7,5},{1,7},{10,8},{12,10},{14... | collective-permute-start | bytes 98312 | tf_op jit(solution)/shard_map/ppermute | solution.py:480
  11.8 1.6 %collective-permute-done.2.left_ref = f32[32,256]{1,0:T(8,128)S(1)} collective-permute-done((f32[32,256]{1,0:T(8,128)S(1)}, f32[32,256]{1,0:T(8,128)S(1)}, u32[]{:S(2)}, u32[]{:S(2)}) %collective-permute-start.2) | collective-permute-done | bytes 32800 | tf_op jit(solution)/shard_map/ppermute | solution.py:479
  13.4 0.3 weights.1
  13.8 1.3 %sweeps.4.refs_1_ = f32[16,8,256]{2,1,0:T(8,128)S(1)} custom-call(f32[28,32,256]{2,1,0:T(8,128)S(1)} %get-tuple-element.30.whole_ref, f32[32,256]{1,0:T(8,128)S(1)} %collective-permute-done.2.left_ref, f32[32,256]{1,0:T(8,128)S(1)} %collective-permute-done.3.right_ref, f32[29,8,384]{2,1,0:T(8,128)S(1)} %get-tuple-element.33.south_ref, ...), custom_call_target="tpu_custom_call" | custom-call | tf_op jit(solution)/shard_map/sweeps/pallas_call | solution.py:34
  15.1 1.6 %collective-permute-start.4 = (f32[16,8,256]{2,1,0:T(8,128)S(1)}, f32[16,8,256]{2,1,0:T(8,128)S(1)}, u32[]{:S(2)}, u32[]{:S(2)}) collective-permute-start(f32[16,8,256]{2,1,0:T(8,128)S(1)} %sweeps.4.refs_1_), channel_id=1, source_target_pairs={{0,1},{1,0},{2,3},{3,2},{4,5},{5,4},{6,7},{7,6},{8,9},{9,8},{10,11... | collective-permute-start | bytes 393224 | tf_op jit(solution)/shard_map/ppermute | solution.py:496
  16.6 1.3 %sweeps.5.refs_2_ = f32[16,8,256]{2,1,0:T(8,128)S(1)} custom-call(f32[28,32,256]{2,1,0:T(8,128)S(1)} %get-tuple-element.30.whole_ref, f32[32,256]{1,0:T(8,128)S(1)} %collective-permute-done.2.left_ref, f32[32,256]{1,0:T(8,128)S(1)} %collective-permute-done.3.right_ref, f32[29,8,384]{2,1,0:T(8,128)S(1)} %get-tuple-element.33.south_ref, ...), custom_call_target="tpu_custom_call" | custom-call | tf_op jit(solution)/shard_map/sweeps/pallas_call | solution.py:34
  18.0 0.6 %collective-permute-start.5 = (f32[16,8,256]{2,1,0:T(8,128)S(1)}, f32[16,8,256]{2,1,0:T(8,128)S(1)}, u32[]{:S(2)}, u32[]{:S(2)}) collective-permute-start(f32[16,8,256]{2,1,0:T(8,128)S(1)} %sweeps.5.refs_2_), channel_id=1, source_target_pairs={{0,1},{1,0},{2,3},{3,2},{4,5},{5,4},{6,7},{7,6},{8,9},{9,8},{10,11... | collective-permute-start | bytes 393224 | tf_op jit(solution)/shard_map/ppermute | solution.py:496
  18.6 1.3 %sweeps.6.refs_3_ = f32[16,8,256]{2,1,0:T(8,128)S(1)} custom-call(f32[28,32,256]{2,1,0:T(8,128)S(1)} %get-tuple-element.30.whole_ref, f32[32,256]{1,0:T(8,128)S(1)} %collective-permute-done.2.left_ref, f32[32,256]{1,0:T(8,128)S(1)} %collective-permute-done.3.right_ref, f32[29,8,384]{2,1,0:T(8,128)S(1)} %get-tuple-element.33.south_ref, ...), custom_call_target="tpu_custom_call" | custom-call | tf_op jit(solution)/shard_map/sweeps/pallas_call | solution.py:34
  19.9 1.6 %collective-permute-start.6 = (f32[16,8,256]{2,1,0:T(8,128)S(1)}, f32[16,8,256]{2,1,0:T(8,128)S(1)}, u32[]{:S(2)}, u32[]{:S(2)}) collective-permute-start(f32[16,8,256]{2,1,0:T(8,128)S(1)} %sweeps.6.refs_3_), channel_id=1, source_target_pairs={{0,1},{1,0},{2,3},{3,2},{4,5},{5,4},{6,7},{7,6},{8,9},{9,8},{10,11... | collective-permute-start | bytes 393224 | tf_op jit(solution)/shard_map/ppermute | solution.py:496
  21.4 1.3 %sweeps.7.refs_4_ = f32[16,4,256]{2,1,0:T(4,128)S(1)} custom-call(f32[28,32,256]{2,1,0:T(8,128)S(1)} %get-tuple-element.30.whole_ref, f32[32,256]{1,0:T(8,128)S(1)} %collective-permute-done.2.left_ref, f32[32,256]{1,0:T(8,128)S(1)} %collective-permute-done.3.right_ref, f32[29,8,384]{2,1,0:T(8,128)S(1)} %get-tuple-element.33.south_ref, ...), custom_call_target="tpu_custom_call" | custom-call | tf_op jit(solution)/shard_map/sweeps/pallas_call | solution.py:34
  22.8 0.6 %collective-permute-start.7 = (f32[16,4,256]{2,1,0:T(4,128)S(1)}, f32[16,4,256]{2,1,0:T(4,128)S(1)}, u32[]{:S(2)}, u32[]{:S(2)}) collective-permute-start(f32[16,4,256]{2,1,0:T(4,128)S(1)} %sweeps.7.refs_4_), channel_id=1, source_target_pairs={{0,1},{1,0},{2,3},{3,2},{4,5},{5,4},{6,7},{7,6},{8,9},{9,8},{10,11... | collective-permute-start | bytes 196616 | tf_op jit(solution)/shard_map/ppermute | solution.py:496
  23.5 0.4 mix_own.1.refs_0_
  23.9 0.2 mix_more.3.refs_0_
  24.1 0.2 mix_more.4.refs_0_
  24.3 2.6 %collective-permute-done.6.refs_2_ = f32[16,8,256]{2,1,0:T(8,128)S(1)} collective-permute-done((f32[16,8,256]{2,1,0:T(8,128)S(1)}, f32[16,8,256]{2,1,0:T(8,128)S(1)}, u32[]{:S(2)}, u32[]{:S(2)}) %collective-permute-start.6) | collective-permute-done | bytes 131104 | tf_op jit(solution)/shard_map/ppermute | solution.py:496
  27.1 1.2 %collective-permute-done.7.field_ref = f32[16,4,256]{2,1,0:T(4,128)S(1)} collective-permute-done((f32[16,4,256]{2,1,0:T(4,128)S(1)}, f32[16,4,256]{2,1,0:T(4,128)S(1)}, u32[]{:S(2)}, u32[]{:S(2)}) %collective-permute-start.7) | collective-permute-done | bytes 65568 | tf_op jit(solution)/shard_map/ppermute | solution.py:496
  28.3 1.3 %mix_last.1 = (f32[28,16,256]{2,1,0:T(8,128)S(1)}, f32[32,1,128]{2,1,0:T(1,128)S(1)}) custom-call(f32[16,28,256]{2,1,0:T(8,128)S(1)} %mix_more.5.acc_ref, bf16[28,48]{1,0:T(8,128)(2,1)S(1)} %get-tuple-element.40.corr_ref, f32[16,4,256]{2,1,0:T(4,128)S(1)} %collective-permute-done.7.field_ref, f32[72,128]{1,0:T(8,128)S(1)} %get-tuple-element.29.order_ref.gram_ref, ...), custom_call_target="tpu_custom_call" | custom-call | tf_op jit(solution)/shard_map/mix_last/pallas_call | solution.py:34
  29.6 14.6 %all_to_all.5.inbox_ref = f32[32,1,128]{2,1,0:T(1,128)S(1)} all-to-all(f32[32,1,128]{2,1,0:T(1,128)S(1)} %get-tuple-element.43), channel_id=1, replica_groups=mesh['lat'=4,'lon'=4,'tm'=2] {'lat','lon','tm'}, dimensions={0} | all-to-all | bytes 32768 | tf_op jit(solution)/shard_map/all_to_all | solution.py:506
  44.2 1.9 %final.1 = f32[28,16,256]{2,1,0:T(8,128)} custom-call(f32[32,1,128]{2,1,0:T(1,128)S(1)} %all_to_all.5.inbox_ref, f32[28,16,256]{2,1,0:T(8,128)S(1)} %get-tuple-element.44.mixed_ref, f32[28,16,256]{2,1,0:T(8,128)S(1)} %copy-done, bf16[8,28,16,256]{3,2,1,0:T(8,128)(2,1)S(1)} %get-tuple-element.41.steps_ref, ...), custom_call_target="tpu_custom_call" | custom-call | tf_op jit(solution)/shard_map/final/pallas_call | solution.py:34
  (12 shorter events, 0.4 us)
Async XLA Ops:
  1.3 8.4 %collective-permute-start = (f32[6,32,256]{2,1,0:T(8,128)S(1)}, f32[6,32,256]{2,1,0:T(8,128)S(1)}, u32[]{:S(2)}, u32[]{:S(2)}) collective-permute-start(f32[6,32,256]{2,1,0:T(8,128)S(1)} %get-tuple-element.26), channel_id=1, source_target_pairs={{0,8},{8,0},{16,24},{24,16},{1,9},{9,1},{17,25},{25,17},{2,10},{10... | collective-permute-start | bytes 589832 | tf_op jit(solution)/shard_map/ppermute | solution.py:458
  4.3 5.3 %collective-permute-start.1 = (f32[6,32,256]{2,1,0:T(8,128)S(1)}, f32[6,32,256]{2,1,0:T(8,128)S(1)}, u32[]{:S(2)}, u32[]{:S(2)}) collective-permute-start(f32[6,32,256]{2,1,0:T(8,128)S(1)} %get-tuple-element.28), channel_id=1, source_target_pairs={{8,16},{16,8},{9,17},{17,9},{10,18},{18,10},{11,19},{19,11},{12,20... | collective-permute-start | bytes 589832 | tf_op jit(solution)/shard_map/ppermute | solution.py:459
  10.0 3.4 %collective-permute-start.2 = (f32[32,256]{1,0:T(8,128)S(1)}, f32[32,256]{1,0:T(8,128)S(1)}, u32[]{:S(2)}, u32[]{:S(2)}) collective-permute-start(f32[32,256]{1,0:T(8,128)S(1)} %get-tuple-element.31), channel_id=1, source_target_pairs={{0,2},{2,4},{4,6},{6,0},{1,3},{3,5},{5,7},{7,1},{8,10},{10,12},{12... | collective-permute-start | bytes 98312 | tf_op jit(solution)/shard_map/ppermute | solution.py:479
  10.1 3.3 %collective-permute-start.3 = (f32[32,256]{1,0:T(8,128)S(1)}, f32[32,256]{1,0:T(8,128)S(1)}, u32[]{:S(2)}, u32[]{:S(2)}) collective-permute-start(f32[32,256]{1,0:T(8,128)S(1)} %get-tuple-element.32), channel_id=1, source_target_pairs={{2,0},{4,2},{6,4},{0,6},{3,1},{5,3},{7,5},{1,7},{10,8},{12,10},{14... | collective-permute-start | bytes 98312 | tf_op jit(solution)/shard_map/ppermute | solution.py:480
  15.1 8.8 %collective-permute-start.4 = (f32[16,8,256]{2,1,0:T(8,128)S(1)}, f32[16,8,256]{2,1,0:T(8,128)S(1)}, u32[]{:S(2)}, u32[]{:S(2)}) collective-permute-start(f32[16,8,256]{2,1,0:T(8,128)S(1)} %sweeps.4.refs_1_), channel_id=1, source_target_pairs={{0,1},{1,0},{2,3},{3,2},{4,5},{5,4},{6,7},{7,6},{8,9},{9,8},{10,11... | collective-permute-start | bytes 393224 | tf_op jit(solution)/shard_map/ppermute | solution.py:496
  18.0 6.2 %collective-permute-start.5 = (f32[16,8,256]{2,1,0:T(8,128)S(1)}, f32[16,8,256]{2,1,0:T(8,128)S(1)}, u32[]{:S(2)}, u32[]{:S(2)}) collective-permute-start(f32[16,8,256]{2,1,0:T(8,128)S(1)} %sweeps.5.refs_2_), channel_id=1, source_target_pairs={{0,1},{1,0},{2,3},{3,2},{4,5},{5,4},{6,7},{7,6},{8,9},{9,8},{10,11... | collective-permute-start | bytes 393224 | tf_op jit(solution)/shard_map/ppermute | solution.py:496
  19.9 3.5 %copy-start.1 = (f32[56,56]{1,0:T(8,128)S(1)}, f32[56,56]{1,0:T(8,128)}, u32[]{:S(2)}) copy-start(f32[56,56]{1,0:T(8,128)} %corr_ref.1) | copy-start | bytes 37636
  19.9 7.0 %collective-permute-start.6 = (f32[16,8,256]{2,1,0:T(8,128)S(1)}, f32[16,8,256]{2,1,0:T(8,128)S(1)}, u32[]{:S(2)}, u32[]{:S(2)}) collective-permute-start(f32[16,8,256]{2,1,0:T(8,128)S(1)} %sweeps.6.refs_3_), channel_id=1, source_target_pairs={{0,1},{1,0},{2,3},{3,2},{4,5},{5,4},{6,7},{7,6},{8,9},{9,8},{10,11... | collective-permute-start | bytes 393224 | tf_op jit(solution)/shard_map/ppermute | solution.py:496
  22.8 5.5 %collective-permute-start.7 = (f32[16,4,256]{2,1,0:T(4,128)S(1)}, f32[16,4,256]{2,1,0:T(4,128)S(1)}, u32[]{:S(2)}, u32[]{:S(2)}) collective-permute-start(f32[16,4,256]{2,1,0:T(4,128)S(1)} %sweeps.7.refs_4_), channel_id=1, source_target_pairs={{0,1},{1,0},{2,3},{3,2},{4,5},{5,4},{6,7},{7,6},{8,9},{9,8},{10,11... | collective-permute-start | bytes 196616 | tf_op jit(solution)/shard_map/ppermute | solution.py:496
  28.3 15.9 %copy-start = (f32[28,16,256]{2,1,0:T(8,128)S(1)}, f32[28,16,256]{2,1,0:T(8,128)}, u32[]{:S(2)}) copy-start(f32[28,16,256]{2,1,0:T(8,128)} %control_ref.1) | copy-start | bytes 1376260

commit v7 on v6

--- a/solution.py
+++ b/solution.py
@@ -29,13 +29,13 @@
     return jax.ShapeDtypeStruct(shape, jnp.float32)
 
 
-def call(kernel, outs, args, specs=None, scratch=(), name=None):
+def call(kernel, outs, args, specs=None, scratch=(), outs_at=VMEM, name=None):
     single = not isinstance(outs, (tuple, list))
     return pl.pallas_call(
         kernel,
         out_shape=outs,
         in_specs=specs or [VMEM] * len(args),
-        out_specs=VMEM if single else [VMEM] * len(outs),
+        out_specs=outs_at if single else [outs_at] * len(outs),
         scratch_shapes=list(scratch),
         compiler_params=PARAMS,
         name=name,
@@ -366,7 +366,7 @@
                     sums[n] = sums[n] + (product[:SUB] + product[SUB:])
         return tuple(sums)
 
-    sums = lax.fori_loop(0, steps, body, (zero,) * NPROJ)
+    sums = lax.fori_loop(0, steps, body, (zero,) * NPROJ, unroll=2)
     rows_ref[0:NGRAM, :] = gram_ref[...]
     for n in range(NPROJ):
         rows_ref[NGRAM + n:NGRAM + n + 1, :] = jnp.sum(sums[n], axis=0, keepdims=True)
@@ -379,7 +379,7 @@
     message_ref[...] = jnp.broadcast_to(message[None], message_ref.shape)
 
 
-def final_kernel(inbox_ref, mixed_ref, control_ref, steps_ref, grads_ref, out_ref, rows_ref):
+def final_kernel(inbox_ref, mixed_ref, control_ref, steps_ref, grads_ref, out_hbm, out_ref, rows_ref, sems):
     totals = jnp.sum(inbox_ref[...], axis=0)
     lane, row = lane_index(), row_index()
     spread = jnp.broadcast_to(totals, (SUB, LANE))
@@ -396,12 +396,13 @@
         return entry(NSYM + WHERE[(min(i, j), max(i, j))])
 
     gamma = cross[(PAIRS - 1, PAIRS - 1)] / square(PAIRS - 1, PAIRS - 1)
+    pivot = [1.0 / cross[(i, i)] for i in range(PAIRS)]
     first = [None] * PAIRS
     for i in reversed(range(PAIRS)):
         rest = entry(NGRAM + i)
         for j in reversed(range(i + 1, PAIRS)):
             rest = rest - cross[(i, j)] * first[j]
-        first[i] = rest / cross[(i, i)]
+        first[i] = rest * pivot[i]
     second = [None] * PAIRS
     for i in range(PAIRS):
         inner = -entry(NGRAM + PAIRS + i)
@@ -410,7 +411,7 @@
         rest = cross[(i, i)] * first[i] + gamma * inner
         for j in range(i):
             rest = rest - cross[(j, i)] * second[j]
-        second[i] = rest / cross[(i, i)]
+        second[i] = rest * pivot[i]
     scaled = [gamma * value for value in first]
 
     _, steps, rows, cols = steps_ref.shape
@@ -431,7 +432,14 @@
                 out_ref[step, pl.ds(r + SUB, SUB), pl.ds(c, LANE)] = control[SUB:] - update[1]
         return carry
 
-    lax.fori_loop(0, steps, body, 0)
+    copies = []
+    for n, (begin, count) in enumerate(groups_of(steps)):
+        lax.fori_loop(begin, begin + count, body, 0, unroll=2)
+        part = pl.ds(begin, count)
+        copies.append(pltpu.make_async_copy(out_ref.at[part], out_hbm.at[part], sems.at[n]))
+        copies[-1].start()
+    for copy in copies:
+        copy.wait()
 
 
 def local(gradient, control, diffusivity, land_mask, time_corr, pair_steps, pair_grads):
@@ -503,10 +511,17 @@
         (mixed, corrs[-1], other[-1], gram, pair_steps, pair_grads),
         scratch=[turn, pltpu.VMEM((NROW, LANE), jnp.float32)], name="mix_last",
     )
-    inbox = lax.all_to_all(message, ("lat", "lon", "tm"), split_axis=0, concat_axis=0, tiled=True)
+    inbox = lax.all_to_all(
+        message, ("lat", "lon", "tm"), split_axis=0, concat_axis=0, tiled=True,
+        axis_index_groups=[list(reversed(range(devices)))],
+    )
     return call(
-        final_kernel, f32(steps, rows, cols), (inbox, mixed, control, pair_steps, pair_grads),
-        scratch=[pltpu.VMEM((NROW, LANE), jnp.float32)], name="final",
+        final_kernel, pltpu.HBM((steps, rows, cols), jnp.float32), (inbox, mixed, control, pair_steps, pair_grads),
+        scratch=[
+            pltpu.VMEM((steps, rows, cols), jnp.float32), pltpu.VMEM((NROW, LANE), jnp.float32),
+            pltpu.SemaphoreType.DMA((len(parts),)),
+        ],
+        outs_at=HBM, name="final",
     )
 
 

time: 46.4 us -> 46 us (level)
  no operation moved by 1% of the time
where the time goes in v7:
time: 46 us; the launch traced here: 45.8 us
  Pallas kernels  15.9 us (35%)
  blocking collectives  14.5 us (32%)
  starting transfers between devices  9.85 us (21%)
  waiting for transfers between devices  5.35 us (12%)
    pallas_call x15, Pallas kernels, call(): pl.pallas_call(kernel, out_shape=outs, in_specs=specs or [VMEM] * len(arg...  15.9 us
    all_to_all x1, blocking collectives, local(): lax.all_to_all(message, ('lat', 'lon', 'tm'), split_axis=0, concat_axis=0...  14.5 us
    ppermute x4, starting transfers between devices, local(): other.append(lax.ppermute(part, 'tm', pairs))  4.31 us
    ppermute x4, waiting for transfers between devices, local(): other.append(lax.ppermute(part, 'tm', pairs))  3.75 us
    ppermute x1, starting transfers between devices, local(): from_swap = lax.ppermute(to_swap, 'lat', even)  3.09 us
    ppermute x1, starting transfers between devices, local(): from_right = lax.ppermute(west, 'lon', left)  1.73 us
    ppermute x1, waiting for transfers between devices, local(): from_left = lax.ppermute(east, 'lon', right)  1.59 us
  transfers between devices with their start and end apart: 8, of which 3 were waited for; matrix products, arithmetic and copies ran while one was open for 0% of the time, Pallas kernels for 21%

profile of v7, /device:TPU:0, one launch (start us, length us, event | category | flops | bytes accessed | tf_op | source)
XLA Modules:
  0.0 45.8 jit_solution(6023061444038365490)
XLA Ops:
  0.0 1.3 %pack.1 = (f32[16,32,256]{2,1,0:T(8,128)S(1)}, f32[6,32,256]{2,1,0:T(8,128)S(1)}, f32[6,32,256]{2,1,0:T(8,128)S(1)}) custom-call(f32[28,16,256]{2,1,0:T(8,128)} %grad_hbm.1, s32[16,256]{1,0:T(8,128)} %mask_hbm.1, f32[16,256]{1,0:T(8,128)} %diff_hbm.1), custom_call_target="tpu_custom_call" | custom-call | tf_op jit(solution)/shard_map/pack/pallas_call | solution.py:34
  1.3 3.1 %collective-permute-start = (f32[6,32,256]{2,1,0:T(8,128)S(1)}, f32[6,32,256]{2,1,0:T(8,128)S(1)}, u32[]{:S(2)}, u32[]{:S(2)}) collective-permute-start(f32[6,32,256]{2,1,0:T(8,128)S(1)} %get-tuple-element.26), channel_id=1, source_target_pairs={{0,8},{8,0},{16,24},{24,16},{1,9},{9,1},{17,25},{25,17},{2,10},{10... | collective-permute-start | bytes 589832 | tf_op jit(solution)/shard_map/ppermute | solution.py:466
  4.3 0.7 %collective-permute-start.1 = (f32[6,32,256]{2,1,0:T(8,128)S(1)}, f32[6,32,256]{2,1,0:T(8,128)S(1)}, u32[]{:S(2)}, u32[]{:S(2)}) collective-permute-start(f32[6,32,256]{2,1,0:T(8,128)S(1)} %get-tuple-element.28), channel_id=1, source_target_pairs={{8,16},{16,8},{9,17},{17,9},{10,18},{18,10},{11,19},{19,11},{12,20... | collective-permute-start | bytes 589832 | tf_op jit(solution)/shard_map/ppermute | solution.py:467
  5.0 4.6 %gram.1 = (f32[72,128]{1,0:T(8,128)S(1)}, bf16[8,28,16,256]{3,2,1,0:T(8,128)(2,1)S(1)}, bf16[8,28,16,256]{3,2,1,0:T(8,128)(2,1)S(1)}) custom-call(bf16[8,28,16,256]{3,2,1,0:T(8,128)(2,1)} %steps_hbm.1, bf16[8,28,16,256]{3,2,1,0:T(8,128)(2,1)} %grads_hbm.1), custom_call_target="tpu_custom_call" | custom-call | tf_op jit(solution)/shard_map/gram/pallas_call | solution.py:34
  9.7 0.3 sides.1
  10.1 1.7 %collective-permute-start.3 = (f32[32,256]{1,0:T(8,128)S(1)}, f32[32,256]{1,0:T(8,128)S(1)}, u32[]{:S(2)}, u32[]{:S(2)}) collective-permute-start(f32[32,256]{1,0:T(8,128)S(1)} %get-tuple-element.32), channel_id=1, source_target_pairs={{2,0},{4,2},{6,4},{0,6},{3,1},{5,3},{7,5},{1,7},{10,8},{12,10},{14... | collective-permute-start | bytes 98312 | tf_op jit(solution)/shard_map/ppermute | solution.py:488
  11.8 1.6 %collective-permute-done.2.left_ref = f32[32,256]{1,0:T(8,128)S(1)} collective-permute-done((f32[32,256]{1,0:T(8,128)S(1)}, f32[32,256]{1,0:T(8,128)S(1)}, u32[]{:S(2)}, u32[]{:S(2)}) %collective-permute-start.2) | collective-permute-done | bytes 32800 | tf_op jit(solution)/shard_map/ppermute | solution.py:487
  13.4 0.3 weights.1
  13.8 1.3 %sweeps.4.refs_1_ = f32[16,8,256]{2,1,0:T(8,128)S(1)} custom-call(f32[28,32,256]{2,1,0:T(8,128)S(1)} %get-tuple-element.30.whole_ref, f32[32,256]{1,0:T(8,128)S(1)} %collective-permute-done.2.left_ref, f32[32,256]{1,0:T(8,128)S(1)} %collective-permute-done.3.right_ref, f32[29,8,384]{2,1,0:T(8,128)S(1)} %get-tuple-element.33.south_ref, ...), custom_call_target="tpu_custom_call" | custom-call | tf_op jit(solution)/shard_map/sweeps/pallas_call | solution.py:34
  15.1 1.6 %collective-permute-start.4 = (f32[16,8,256]{2,1,0:T(8,128)S(1)}, f32[16,8,256]{2,1,0:T(8,128)S(1)}, u32[]{:S(2)}, u32[]{:S(2)}) collective-permute-start(f32[16,8,256]{2,1,0:T(8,128)S(1)} %sweeps.4.refs_1_), channel_id=1, source_target_pairs={{0,1},{1,0},{2,3},{3,2},{4,5},{5,4},{6,7},{7,6},{8,9},{9,8},{10,11... | collective-permute-start | bytes 393224 | tf_op jit(solution)/shard_map/ppermute | solution.py:504
  16.6 1.3 %sweeps.5.refs_2_ = f32[16,8,256]{2,1,0:T(8,128)S(1)} custom-call(f32[28,32,256]{2,1,0:T(8,128)S(1)} %get-tuple-element.30.whole_ref, f32[32,256]{1,0:T(8,128)S(1)} %collective-permute-done.2.left_ref, f32[32,256]{1,0:T(8,128)S(1)} %collective-permute-done.3.right_ref, f32[29,8,384]{2,1,0:T(8,128)S(1)} %get-tuple-element.33.south_ref, ...), custom_call_target="tpu_custom_call" | custom-call | tf_op jit(solution)/shard_map/sweeps/pallas_call | solution.py:34
  18.0 0.6 %collective-permute-start.5 = (f32[16,8,256]{2,1,0:T(8,128)S(1)}, f32[16,8,256]{2,1,0:T(8,128)S(1)}, u32[]{:S(2)}, u32[]{:S(2)}) collective-permute-start(f32[16,8,256]{2,1,0:T(8,128)S(1)} %sweeps.5.refs_2_), channel_id=1, source_target_pairs={{0,1},{1,0},{2,3},{3,2},{4,5},{5,4},{6,7},{7,6},{8,9},{9,8},{10,11... | collective-permute-start | bytes 393224 | tf_op jit(solution)/shard_map/ppermute | solution.py:504
  18.6 1.3 %sweeps.6.refs_3_ = f32[16,8,256]{2,1,0:T(8,128)S(1)} custom-call(f32[28,32,256]{2,1,0:T(8,128)S(1)} %get-tuple-element.30.whole_ref, f32[32,256]{1,0:T(8,128)S(1)} %collective-permute-done.2.left_ref, f32[32,256]{1,0:T(8,128)S(1)} %collective-permute-done.3.right_ref, f32[29,8,384]{2,1,0:T(8,128)S(1)} %get-tuple-element.33.south_ref, ...), custom_call_target="tpu_custom_call" | custom-call | tf_op jit(solution)/shard_map/sweeps/pallas_call | solution.py:34
  19.9 1.6 %collective-permute-start.6 = (f32[16,8,256]{2,1,0:T(8,128)S(1)}, f32[16,8,256]{2,1,0:T(8,128)S(1)}, u32[]{:S(2)}, u32[]{:S(2)}) collective-permute-start(f32[16,8,256]{2,1,0:T(8,128)S(1)} %sweeps.6.refs_3_), channel_id=1, source_target_pairs={{0,1},{1,0},{2,3},{3,2},{4,5},{5,4},{6,7},{7,6},{8,9},{9,8},{10,11... | collective-permute-start | bytes 393224 | tf_op jit(solution)/shard_map/ppermute | solution.py:504
  21.4 1.3 %sweeps.7.refs_4_ = f32[16,4,256]{2,1,0:T(4,128)S(1)} custom-call(f32[28,32,256]{2,1,0:T(8,128)S(1)} %get-tuple-element.30.whole_ref, f32[32,256]{1,0:T(8,128)S(1)} %collective-permute-done.2.left_ref, f32[32,256]{1,0:T(8,128)S(1)} %collective-permute-done.3.right_ref, f32[29,8,384]{2,1,0:T(8,128)S(1)} %get-tuple-element.33.south_ref, ...), custom_call_target="tpu_custom_call" | custom-call | tf_op jit(solution)/shard_map/sweeps/pallas_call | solution.py:34
  22.8 0.6 %collective-permute-start.7 = (f32[16,4,256]{2,1,0:T(4,128)S(1)}, f32[16,4,256]{2,1,0:T(4,128)S(1)}, u32[]{:S(2)}, u32[]{:S(2)}) collective-permute-start(f32[16,4,256]{2,1,0:T(4,128)S(1)} %sweeps.7.refs_4_), channel_id=1, source_target_pairs={{0,1},{1,0},{2,3},{3,2},{4,5},{5,4},{6,7},{7,6},{8,9},{9,8},{10,11... | collective-permute-start | bytes 196616 | tf_op jit(solution)/shard_map/ppermute | solution.py:504
  23.5 0.4 mix_own.1.refs_0_
  23.9 0.2 mix_more.3.refs_0_
  24.1 0.2 mix_more.4.refs_0_
  24.3 2.6 %collective-permute-done.6.refs_2_ = f32[16,8,256]{2,1,0:T(8,128)S(1)} collective-permute-done((f32[16,8,256]{2,1,0:T(8,128)S(1)}, f32[16,8,256]{2,1,0:T(8,128)S(1)}, u32[]{:S(2)}, u32[]{:S(2)}) %collective-permute-start.6) | collective-permute-done | bytes 131104 | tf_op jit(solution)/shard_map/ppermute | solution.py:504
  27.1 1.2 %collective-permute-done.7.field_ref = f32[16,4,256]{2,1,0:T(4,128)S(1)} collective-permute-done((f32[16,4,256]{2,1,0:T(4,128)S(1)}, f32[16,4,256]{2,1,0:T(4,128)S(1)}, u32[]{:S(2)}, u32[]{:S(2)}) %collective-permute-start.7) | collective-permute-done | bytes 65568 | tf_op jit(solution)/shard_map/ppermute | solution.py:504
  28.3 1.2 %mix_last.1 = (f32[28,16,256]{2,1,0:T(8,128)S(1)}, f32[32,1,128]{2,1,0:T(1,128)S(1)}) custom-call(f32[16,28,256]{2,1,0:T(8,128)S(1)} %mix_more.5.acc_ref, bf16[28,48]{1,0:T(8,128)(2,1)S(1)} %get-tuple-element.40.corr_ref, f32[16,4,256]{2,1,0:T(4,128)S(1)} %collective-permute-done.7.field_ref, f32[72,128]{1,0:T(8,128)S(1)} %get-tuple-element.29.order_ref.gram_ref, ...), custom_call_target="tpu_custom_call" | custom-call | tf_op jit(solution)/shard_map/mix_last/pallas_call | solution.py:34
  29.5 14.5 %all_to_all.5.inbox_ref = f32[32,1,128]{2,1,0:T(1,128)S(1)} all-to-all(f32[32,1,128]{2,1,0:T(1,128)S(1)} %get-tuple-element.43), channel_id=1, replica_groups={{31,30,29,28,27,26,25,24,23,22,21,20,19,18,17,16,15,14,13,12,11,10,9,8,..., dimensions={0} | all-to-all | bytes 32768 | tf_op jit(solution)/shard_map/all_to_all | solution.py:514
  44.0 1.7 %final.1 = f32[28,16,256]{2,1,0:T(8,128)} custom-call(f32[32,1,128]{2,1,0:T(1,128)S(1)} %all_to_all.5.inbox_ref, f32[28,16,256]{2,1,0:T(8,128)S(1)} %get-tuple-element.44.mixed_ref, f32[28,16,256]{2,1,0:T(8,128)S(1)} %copy-done, bf16[8,28,16,256]{3,2,1,0:T(8,128)(2,1)S(1)} %get-tuple-element.41.steps_ref, ...), custom_call_target="tpu_custom_call" | custom-call | tf_op jit(solution)/shard_map/final/pallas_call | solution.py:34
  (12 shorter events, 0.4 us)
Async XLA Ops:
  1.3 8.4 %collective-permute-start = (f32[6,32,256]{2,1,0:T(8,128)S(1)}, f32[6,32,256]{2,1,0:T(8,128)S(1)}, u32[]{:S(2)}, u32[]{:S(2)}) collective-permute-start(f32[6,32,256]{2,1,0:T(8,128)S(1)} %get-tuple-element.26), channel_id=1, source_target_pairs={{0,8},{8,0},{16,24},{24,16},{1,9},{9,1},{17,25},{25,17},{2,10},{10... | collective-permute-start | bytes 589832 | tf_op jit(solution)/shard_map/ppermute | solution.py:466
  4.3 5.3 %collective-permute-start.1 = (f32[6,32,256]{2,1,0:T(8,128)S(1)}, f32[6,32,256]{2,1,0:T(8,128)S(1)}, u32[]{:S(2)}, u32[]{:S(2)}) collective-permute-start(f32[6,32,256]{2,1,0:T(8,128)S(1)} %get-tuple-element.28), channel_id=1, source_target_pairs={{8,16},{16,8},{9,17},{17,9},{10,18},{18,10},{11,19},{19,11},{12,20... | collective-permute-start | bytes 589832 | tf_op jit(solution)/shard_map/ppermute | solution.py:467
  10.0 3.4 %collective-permute-start.2 = (f32[32,256]{1,0:T(8,128)S(1)}, f32[32,256]{1,0:T(8,128)S(1)}, u32[]{:S(2)}, u32[]{:S(2)}) collective-permute-start(f32[32,256]{1,0:T(8,128)S(1)} %get-tuple-element.31), channel_id=1, source_target_pairs={{0,2},{2,4},{4,6},{6,0},{1,3},{3,5},{5,7},{7,1},{8,10},{10,12},{12... | collective-permute-start | bytes 98312 | tf_op jit(solution)/shard_map/ppermute | solution.py:487
  10.1 3.3 %collective-permute-start.3 = (f32[32,256]{1,0:T(8,128)S(1)}, f32[32,256]{1,0:T(8,128)S(1)}, u32[]{:S(2)}, u32[]{:S(2)}) collective-permute-start(f32[32,256]{1,0:T(8,128)S(1)} %get-tuple-element.32), channel_id=1, source_target_pairs={{2,0},{4,2},{6,4},{0,6},{3,1},{5,3},{7,5},{1,7},{10,8},{12,10},{14... | collective-permute-start | bytes 98312 | tf_op jit(solution)/shard_map/ppermute | solution.py:488
  15.1 8.8 %collective-permute-start.4 = (f32[16,8,256]{2,1,0:T(8,128)S(1)}, f32[16,8,256]{2,1,0:T(8,128)S(1)}, u32[]{:S(2)}, u32[]{:S(2)}) collective-permute-start(f32[16,8,256]{2,1,0:T(8,128)S(1)} %sweeps.4.refs_1_), channel_id=1, source_target_pairs={{0,1},{1,0},{2,3},{3,2},{4,5},{5,4},{6,7},{7,6},{8,9},{9,8},{10,11... | collective-permute-start | bytes 393224 | tf_op jit(solution)/shard_map/ppermute | solution.py:504
  18.0 6.2 %collective-permute-start.5 = (f32[16,8,256]{2,1,0:T(8,128)S(1)}, f32[16,8,256]{2,1,0:T(8,128)S(1)}, u32[]{:S(2)}, u32[]{:S(2)}) collective-permute-start(f32[16,8,256]{2,1,0:T(8,128)S(1)} %sweeps.5.refs_2_), channel_id=1, source_target_pairs={{0,1},{1,0},{2,3},{3,2},{4,5},{5,4},{6,7},{7,6},{8,9},{9,8},{10,11... | collective-permute-start | bytes 393224 | tf_op jit(solution)/shard_map/ppermute | solution.py:504
  19.9 3.5 %copy-start.1 = (f32[56,56]{1,0:T(8,128)S(1)}, f32[56,56]{1,0:T(8,128)}, u32[]{:S(2)}) copy-start(f32[56,56]{1,0:T(8,128)} %corr_ref.1) | copy-start | bytes 37636
  19.9 7.0 %collective-permute-start.6 = (f32[16,8,256]{2,1,0:T(8,128)S(1)}, f32[16,8,256]{2,1,0:T(8,128)S(1)}, u32[]{:S(2)}, u32[]{:S(2)}) collective-permute-start(f32[16,8,256]{2,1,0:T(8,128)S(1)} %sweeps.6.refs_3_), channel_id=1, source_target_pairs={{0,1},{1,0},{2,3},{3,2},{4,5},{5,4},{6,7},{7,6},{8,9},{9,8},{10,11... | collective-permute-start | bytes 393224 | tf_op jit(solution)/shard_map/ppermute | solution.py:504
  22.8 5.5 %collective-permute-start.7 = (f32[16,4,256]{2,1,0:T(4,128)S(1)}, f32[16,4,256]{2,1,0:T(4,128)S(1)}, u32[]{:S(2)}, u32[]{:S(2)}) collective-permute-start(f32[16,4,256]{2,1,0:T(4,128)S(1)} %sweeps.7.refs_4_), channel_id=1, source_target_pairs={{0,1},{1,0},{2,3},{3,2},{4,5},{5,4},{6,7},{7,6},{8,9},{9,8},{10,11... | collective-permute-start | bytes 196616 | tf_op jit(solution)/shard_map/ppermute | solution.py:504
  28.3 15.7 %copy-start = (f32[28,16,256]{2,1,0:T(8,128)S(1)}, f32[28,16,256]{2,1,0:T(8,128)}, u32[]{:S(2)}) copy-start(f32[28,16,256]{2,1,0:T(8,128)} %control_ref.1) | copy-start | bytes 1376260

commit v8 on v7

--- a/solution.py
+++ b/solution.py
@@ -50,22 +50,8 @@
     return lax.broadcasted_iota(jnp.int32, (SUB, LANE), 0)
 
 
-def gram_kernel(steps_hbm, grads_hbm, out_ref, steps_ref, grads_ref, sems):
+def gram_kernel(steps_ref, grads_ref, order_ref, out_ref):
     _, steps, rows, cols = steps_ref.shape
-    pieces = 4
-    while steps % pieces:
-        pieces -= 1
-    count = steps // pieces
-    copies = []
-    for n in range(pieces):
-        part = (slice(None), pl.ds(n * count, count))
-        copies.append((
-            pltpu.make_async_copy(steps_hbm.at[part], steps_ref.at[part], sems.at[0, n]),
-            pltpu.make_async_copy(grads_hbm.at[part], grads_ref.at[part], sems.at[1, n]),
-        ))
-    for pair in copies:
-        for copy in pair:
-            copy.start()
 
     def make_body(half):
         def body(step, sums):
@@ -84,16 +70,10 @@
         return body
 
     zero = jnp.zeros((SUB, LANE), jnp.float32)
-    sums = (zero,) * NSYM
-    for n in range(pieces):
-        for copy in copies[n]:
-            copy.wait()
-        sums = lax.fori_loop(n * count, (n + 1) * count, make_body(0), sums)
-    for k in range(NSYM):
-        out_ref[k:k + 1, :] = jnp.sum(sums[k], axis=0, keepdims=True)
-    sums = lax.fori_loop(0, steps, make_body(1), (zero,) * NSYM)
-    for k in range(NSYM):
-        out_ref[NSYM + k:NSYM + k + 1, :] = jnp.sum(sums[k], axis=0, keepdims=True)
+    for half in range(2):
+        sums = lax.fori_loop(0, steps, make_body(half), (zero,) * NSYM)
+        for k in range(NSYM):
+            out_ref[half * NSYM + k:half * NSYM + k + 1, :] = jnp.sum(sums[k], axis=0, keepdims=True)
 
 
 def groups_of(steps):
@@ -104,7 +84,15 @@
     return -(-(steps + 1) // SUB) * SUB
 
 
-def pack_kernel(grad_hbm, mask_hbm, diff_hbm, field_ref, swap_ref, next_ref, grad_ref, mask_ref, diff_ref, turn_ref, sems):
+def halves_of(steps):
+    tiles = slots_of(steps) // SUB
+    order = [tiles - 1, *range(tiles - 1)]
+    middle = (tiles + 1) // 2
+    return [half for half in (order[:middle], order[middle:]) if half]
+
+
+def pack_kernel(grad_hbm, mask_hbm, diff_hbm, field_ref, *refs):
+    *message_refs, grad_ref, mask_ref, diff_ref, turn_ref, sems = refs
     steps, rows, cols = grad_ref.shape
     slots = field_ref.shape[1]
     pieces = [(begin, min(SUB, steps - begin)) for begin in range(0, steps, SUB)]
@@ -140,20 +128,25 @@
                 field_ref[row, slot:slot + SUB, across] = value
     odd = lax.rem(lax.axis_index("lat"), 2)
     near, far = (1 - odd) * (rows - HALO), odd * (rows - HALO)
-    for row in range(HALO):
-        swap_ref[row] = field_ref[near + row]
-        next_ref[row] = field_ref[far + row]
-
-
-def side_kernel(swap_ref, field_ref, next_ref, order_ref, whole_ref, west_ref, east_ref):
-    rows, slots, cols = field_ref.shape
+    for n, half in enumerate(halves_of(steps)):
+        for k, tile in enumerate(half):
+            there, here = slice(k * SUB, (k + 1) * SUB), slice(tile * SUB, (tile + 1) * SUB)
+            for row in range(HALO):
+                message_refs[2 * n][row, there] = field_ref[near + row, here]
+                message_refs[2 * n + 1][row, there] = field_ref[far + row, here]
+
+
+def side_kernel(swap_ref, field_ref, next_ref, whole_ref, west_ref, east_ref, *, half):
+    rows, _, cols = field_ref.shape
+    slots = whole_ref.shape[1]
     odd = lax.rem(lax.axis_index("lat"), 2)
     near, far = (1 - odd) * (HALO + rows), odd * (HALO + rows)
     for row in range(HALO):
         whole_ref[near + row] = swap_ref[row]
         whole_ref[far + row] = next_ref[row]
-    for row in range(rows):
-        whole_ref[HALO + row] = field_ref[row]
+    for k, tile in enumerate(half):
+        for row in range(rows):
+            whole_ref[HALO + row, k * SUB:(k + 1) * SUB] = field_ref[row, tile * SUB:(tile + 1) * SUB]
     lane = lane_index()
     for slot in range(0, slots, SUB):
         down = slice(slot, slot + SUB)
@@ -200,7 +193,7 @@
 
 
 def weight_kernel(
-    whole_ref, left_ref, right_ref, south_ref, east_ref, west_ref, keep_ref, kappa_ref, packed_ref, *, steps
+    whole_ref, left_ref, right_ref, south_ref, east_ref, west_ref, keep_ref, kappa_ref, packed_ref, *, slot
 ):
     height, _, cols = whole_ref.shape
     width = cols // LANE + 1
@@ -208,7 +201,7 @@
     lane = lane_index()
     at_start, at_end = lane == 0, lane == LANE - 1
     for row in range(height):
-        for c, tile in enumerate(load(row, slice(steps, steps + 1))):
+        for c, tile in enumerate(load(row, slice(slot, slot + 1))):
             kappa_ref[row:row + 1, c * LANE:(c + 1) * LANE] = tile
     for first in range(0, height, SUB):
         down = slice(first, first + SUB)
@@ -231,7 +224,15 @@
         south_ref[height - 1 + side] = jnp.broadcast_to(inside, south_ref.shape[1:])
 
 
-def sweep_kernel(whole_ref, left_ref, right_ref, south_ref, east_ref, west_ref, keep_ref, out_ref, *, begin):
+def sweep_kernel(whole_ref, left_ref, right_ref, south_ref, east_ref, west_ref, keep_ref, *refs, begin):
+    copies = []
+    _, *refs = refs
+    if len(refs) > 1:
+        source, out_ref, target, sem = refs
+        copies.append(pltpu.make_async_copy(source, target, sem))
+        copies[0].start()
+    else:
+        (out_ref,) = refs
     height, _, cols = whole_ref.shape
     rows, width = height - 2 * HALO, cols // LANE + 1
     count = out_ref.shape[1]
@@ -281,6 +282,8 @@
                 fresh = advance(sweep, *entry)
                 if fresh is not None:
                     waiting[sweep + 1] = (entry[0] - 1, fresh)
+    for copy in copies:
+        copy.wait()
 
 
 def split_stack(value):
@@ -296,19 +299,20 @@
     for at in range(groups):
         @pl.when(mine == at)
         def _(at=at):
-            for (shift, begin, count), out_ref in zip(sources, out_refs):
-                source = (at - shift) % groups * steps + begin
-                block = corr_ref[source:source + count, at * steps:(at + 1) * steps]
+            for pieces, out_ref in zip(sources, out_refs):
+                blocks = []
+                for shift, begin, count in pieces:
+                    source = (at - shift) % groups * steps + begin
+                    blocks.append(corr_ref[source:source + count, at * steps:(at + 1) * steps])
+                    if count % SUB:
+                        blocks.append(jnp.zeros((-count % SUB, steps), jnp.float32))
+                block = jnp.concatenate(blocks, axis=0) if len(blocks) > 1 else blocks[0]
                 high = block.astype(jnp.bfloat16).astype(jnp.float32)
                 rest = block - high
                 middle = rest.astype(jnp.bfloat16).astype(jnp.float32)
                 low = rest - middle
-                depth = out_ref.shape[1] // 6
-                pad = [jnp.zeros((depth - count, steps), jnp.float32)] if depth > count else []
-                stack = []
-                for part in (high, high, middle, high, middle, low):
-                    stack += [part, *pad]
-                out_ref[...] = jnp.concatenate(stack, axis=0).T.astype(jnp.bfloat16)
+                stack = jnp.concatenate([high, high, middle, high, middle, low], axis=0)
+                out_ref[...] = stack.T.astype(jnp.bfloat16)
 
 
 def mixed_row(row, corr_ref, field_refs):
@@ -452,9 +456,10 @@
     slots = slots_of(steps)
     turn = pltpu.VMEM((rows * (cols // LANE) * slots, LANE), jnp.float32)
 
-    field, to_swap, to_next = call(
+    halves = halves_of(steps)
+    field, *messages = call(
         pack_kernel,
-        (f32(rows, slots, cols), f32(HALO, slots, cols), f32(HALO, slots, cols)),
+        [f32(rows, slots, cols)] + [f32(HALO, len(half) * SUB, cols) for half in halves for _ in range(2)],
         [pltpu.with_memory_space_constraint(v, pltpu.HBM) for v in (gradient, land_mask, diffusivity)],
         specs=[HBM] * 3,
         scratch=[
@@ -463,45 +468,56 @@
         ],
         name="pack",
     )
-    from_swap = lax.ppermute(to_swap, "lat", even)
-    from_next = lax.ppermute(to_next, "lat", odd)
-    pair_shape = jax.ShapeDtypeStruct(pair_steps.shape, jnp.bfloat16)
-    gram, pair_steps, pair_grads = call(
-        gram_kernel, (f32(NGRAM, LANE), pair_shape, pair_shape),
-        [pltpu.with_memory_space_constraint(v, pltpu.HBM) for v in (pair_steps, pair_grads)], specs=[HBM] * 2,
-        scratch=[pltpu.SemaphoreType.DMA((2, 4))],
-        name="gram",
-    )
+    arrived = []
+    for n in range(len(halves)):
+        from_next = lax.ppermute(messages[2 * n + 1], "lat", odd)
+        arrived.append((lax.ppermute(messages[2 * n], "lat", even), from_next))
     tall, wide = rows + 2 * HALO, cols + LANE
-    parts = groups_of(steps)
-    sources = [(0, 0, steps)] + [(shift, *part) for part in parts for shift in range(1, groups)]
-    own_corr, *corrs = call(
-        functools.partial(corr_kernel, groups=groups, steps=steps, sources=sources),
-        [jax.ShapeDtypeStruct((steps, 6 * (count + -count % SUB)), jnp.bfloat16) for _, _, count in sources],
-        (time_corr,), name="corr",
-    )
-    side_shape = f32(slots, -(-tall // PER) * LANE)
-    whole, west, east = call(
-        side_kernel, (f32(tall, slots, cols), side_shape, side_shape), (from_swap, field, from_next, gram), name="sides"
-    )
-    from_left = lax.ppermute(east, "lon", right)
-    from_right = lax.ppermute(west, "lon", left)
-    extended = (whole, from_left, from_right)
+    extended = []
+    for half, (from_swap, from_next) in zip(halves, arrived):
+        inner = len(half) * SUB
+        side_shape = f32(inner, -(-tall // PER) * LANE)
+        whole, west, east = call(
+            functools.partial(side_kernel, half=half), (f32(tall, inner, cols), side_shape, side_shape),
+            (from_swap, field, from_next), name="sides",
+        )
+        extended.append((whole, lax.ppermute(east, "lon", right), lax.ppermute(west, "lon", left)))
     weights = call(
-        functools.partial(weight_kernel, steps=steps),
-        (f32(tall + 1, SUB, wide), f32(tall, SUB, wide), f32(tall, SUB, wide), f32(tall, SUB, wide)), extended,
+        functools.partial(weight_kernel, slot=steps % SUB),
+        (f32(tall + 1, SUB, wide), f32(tall, SUB, wide), f32(tall, SUB, wide), f32(tall, SUB, wide)), extended[0],
         scratch=[pltpu.VMEM((-(-tall // SUB) * SUB + SUB, wide), jnp.float32), pltpu.VMEM((4, -(-tall // SUB) * SUB, wide), jnp.float32)],
         name="weights",
     )
-    own, other = [], []
-    for begin, count in parts:
-        part = call(
-            functools.partial(sweep_kernel, begin=begin), f32(rows, count, cols), (*extended, *weights), name="sweeps"
-        )
+    work = [(n, k, tile * SUB, min(SUB, steps - tile * SUB)) for n, half in enumerate(halves) for k, tile in enumerate(half)]
+    work = [item for item in work if item[3] > 0]
+    work.sort(key=lambda item: (item[0], -item[3]))
+    loads = [pltpu.with_memory_space_constraint(v, pltpu.HBM) for v in (pair_steps, pair_grads)]
+    pairs_at = {max(len(work) - 3 + n, 0): load for n, load in enumerate(loads)}
+    own, other, sources, pairs = [], [], [], []
+    for at, (n, k, begin, count) in enumerate(work):
+        kernel = functools.partial(sweep_kernel, begin=k * SUB)
+        order = own[-1] if own else weights[0]
+        if at in pairs_at:
+            load = pairs_at[at]
+            part, loaded = call(
+                kernel, (f32(rows, count, cols), jax.ShapeDtypeStruct(load.shape, load.dtype)), (*extended[n], *weights, order, load),
+                specs=[VMEM] * 8 + [HBM], scratch=[pltpu.SemaphoreType.DMA], name="sweeps",
+            )
+            pairs.append(loaded)
+        else:
+            part = call(kernel, f32(rows, count, cols), (*extended[n], *weights, order), name="sweeps")
         own.append(part)
         for shift in range(1, groups):
-            pairs = [(i, (i + shift) % groups) for i in range(groups)]
-            other.append(lax.ppermute(part, "tm", pairs))
+            sources.append([(shift, begin, count)])
+            other.append(lax.ppermute(part, "tm", [(i, (i + shift) % groups) for i in range(groups)]))
+    pair_steps, pair_grads = pairs if len(pairs) == 2 else (pair_steps, pair_grads)
+    sources.append([(0, begin, count) for _, _, begin, count in work])
+    *corrs, own_corr = call(
+        functools.partial(corr_kernel, groups=groups, steps=steps, sources=sources),
+        [jax.ShapeDtypeStruct((steps, 6 * SUB * len(pieces)), jnp.bfloat16) for pieces in sources],
+        (time_corr,), name="corr",
+    )
+    gram = call(gram_kernel, f32(NGRAM, LANE), (pair_steps, pair_grads, own[-1]), name="gram")
     mixed = call(make_mix(True), f32(rows, steps, cols), (own_corr, *own), name="mix_own")
     for corr, part in zip(corrs[:-1], other[:-1]):
         mixed = call(make_mix(False), f32(rows, steps, cols), (mixed, corr, part), name="mix_more")
@@ -519,7 +535,7 @@
         final_kernel, pltpu.HBM((steps, rows, cols), jnp.float32), (inbox, mixed, control, pair_steps, pair_grads),
         scratch=[
             pltpu.VMEM((steps, rows, cols), jnp.float32), pltpu.VMEM((NROW, LANE), jnp.float32),
-            pltpu.SemaphoreType.DMA((len(parts),)),
+            pltpu.SemaphoreType.DMA((len(groups_of(steps)),)),
         ],
         outs_at=HBM, name="final",
     )

time: 46 us -> 45.7 us (level)
  starting transfers between devices: 9.85 us -> 16.7 us
  blocking collectives: 14.5 us -> 11.1 us
  waiting for transfers between devices: 5.35 us -> 2.23 us
  Pallas kernels: 15.9 us -> 15.3 us
    ppermute x8 -> x12, starting transfers between devices: 9.85 us -> 16.7 us  [the longest x2 7.55 us: local(): arrived.append((lax.ppermute(messages[2 * n], 'lat', even), from_next))]
    all_to_all x1, blocking collectives: 14.5 us -> 11.1 us  [local(): lax.all_to_all(message, ('lat', 'lon', 'tm'), split_axis=0, concat_axis=0...]
    ppermute x8 -> x12, waiting for transfers between devices: 5.35 us -> 2.23 us  [the longest x4 2.2 us: local(): lax.ppermute(part, 'tm', [(i, (i + shift) % groups) for i in range(groups)])]
    pallas_call x15 -> x16, Pallas kernels: 15.9 us -> 15.3 us  [call(): pl.pallas_call(kernel, out_shape=outs, in_specs=specs or [VMEM] * len(arg...]
  transfers between devices with their start and end apart: 8 -> 12, of which waited for: 3 -> 1; matrix products, arithmetic and copies ran while one was open for 0% -> 0% of each run, Pallas kernels for 21% -> 24%
where the time goes in v8:
time: 45.7 us; the launch traced here: 45.4 us
  starting transfers between devices  16.7 us (37%)
  Pallas kernels  15.3 us (33%)
  blocking collectives  11.1 us (24%)
  waiting for transfers between devices  2.23 us (5%)
    pallas_call x16, Pallas kernels, call(): pl.pallas_call(kernel, out_shape=outs, in_specs=specs or [VMEM] * len(arg...  15.3 us
    all_to_all x1, blocking collectives, local(): lax.all_to_all(message, ('lat', 'lon', 'tm'), split_axis=0, concat_axis=0...  11.1 us
    ppermute x2, starting transfers between devices, local(): arrived.append((lax.ppermute(messages[2 * n], 'lat', even), from_next))  7.55 us
    ppermute x4, starting transfers between devices, local(): lax.ppermute(part, 'tm', [(i, (i + shift) % groups) for i in range(groups)])  4.25 us
    ppermute x2, starting transfers between devices, local(): lax.ppermute(west, 'lon', left)  3.47 us
    ppermute x4, waiting for transfers between devices, local(): lax.ppermute(part, 'tm', [(i, (i + shift) % groups) for i in range(groups)])  2.2 us
    ppermute x2, starting transfers between devices, local(): from_next = lax.ppermute(messages[2 * n + 1], 'lat', odd)  1.31 us
  transfers between devices with their start and end apart: 12, of which 1 were waited for; matrix products, arithmetic and copies ran while one was open for 0% of the time, Pallas kernels for 24%

profile of v8, /device:TPU:0, one launch (start us, length us, event | category | flops | bytes accessed | tf_op | source)
XLA Modules:
  0.0 45.4 jit_solution(15565486900145666248)
XLA Ops:
  0.0 1.3 %pack.1 = (f32[16,32,256]{2,1,0:T(8,128)S(1)}, f32[6,16,256]{2,1,0:T(8,128)S(1)}, f32[6,16,256]{2,1,0:T(8,128)S(1)}, f32[6,16,256]{2,1,0:T(8,128)S(1)}, f32[6,16,256]{2,1,0:T(8,128)S(1)}) custom-call(f32[28,16,256]{2,1,0:T(8,128)} %grad_hbm.1, s32[16,256]{1,0:T(8,128)} %mask_hbm.1, f32[16,256]{1,0:T(8,128)} %diff_hbm.1), custom_call_target="tpu_custom_call" | custom-call | tf_op jit(solution)/shard_map/pack/pallas_call | solution.py:34
  1.3 3.1 %collective-permute-start = (f32[6,16,256]{2,1,0:T(8,128)S(1)}, f32[6,16,256]{2,1,0:T(8,128)S(1)}, u32[]{:S(2)}, u32[]{:S(2)}) collective-permute-start(f32[6,16,256]{2,1,0:T(8,128)S(1)} %get-tuple-element.32), channel_id=1, source_target_pairs={{0,8},{8,0},{16,24},{24,16},{1,9},{9,1},{17,25},{25,17},{2,10},{10... | collective-permute-start | bytes 294920 | tf_op jit(solution)/shard_map/ppermute | solution.py:474
  4.4 0.7 %collective-permute-start.1 = (f32[6,16,256]{2,1,0:T(8,128)S(1)}, f32[6,16,256]{2,1,0:T(8,128)S(1)}, u32[]{:S(2)}, u32[]{:S(2)}) collective-permute-start(f32[6,16,256]{2,1,0:T(8,128)S(1)} %get-tuple-element.34), channel_id=1, source_target_pairs={{8,16},{16,8},{9,17},{17,9},{10,18},{18,10},{11,19},{19,11},{12,20... | collective-permute-start | bytes 294920 | tf_op jit(solution)/shard_map/ppermute | solution.py:473
  5.0 4.5 %collective-permute-start.4 = (f32[6,16,256]{2,1,0:T(8,128)S(1)}, f32[6,16,256]{2,1,0:T(8,128)S(1)}, u32[]{:S(2)}, u32[]{:S(2)}) collective-permute-start(f32[6,16,256]{2,1,0:T(8,128)S(1)} %get-tuple-element.43), channel_id=1, source_target_pairs={{0,8},{8,0},{16,24},{24,16},{1,9},{9,1},{17,25},{25,17},{2,10},{10... | collective-permute-start | bytes 294920 | tf_op jit(solution)/shard_map/ppermute | solution.py:474
  9.5 0.7 %collective-permute-start.5 = (f32[6,16,256]{2,1,0:T(8,128)S(1)}, f32[6,16,256]{2,1,0:T(8,128)S(1)}, u32[]{:S(2)}, u32[]{:S(2)}) collective-permute-start(f32[6,16,256]{2,1,0:T(8,128)S(1)} %get-tuple-element.44), channel_id=1, source_target_pairs={{8,16},{16,8},{9,17},{17,9},{10,18},{18,10},{11,19},{19,11},{12,20... | collective-permute-start | bytes 294920 | tf_op jit(solution)/shard_map/ppermute | solution.py:473
  10.4 1.7 %collective-permute-start.3 = (f32[16,256]{1,0:T(8,128)S(1)}, f32[16,256]{1,0:T(8,128)S(1)}, u32[]{:S(2)}, u32[]{:S(2)}) collective-permute-start(f32[16,256]{1,0:T(8,128)S(1)} %get-tuple-element.37), channel_id=1, source_target_pairs={{2,0},{4,2},{6,4},{0,6},{3,1},{5,3},{7,5},{1,7},{10,8},{12,10},{14... | collective-permute-start | bytes 49160 | tf_op jit(solution)/shard_map/ppermute | solution.py:484
  12.4 1.7 %collective-permute-start.7 = (f32[16,256]{1,0:T(8,128)S(1)}, f32[16,256]{1,0:T(8,128)S(1)}, u32[]{:S(2)}, u32[]{:S(2)}) collective-permute-start(f32[16,256]{1,0:T(8,128)S(1)} %get-tuple-element.47), channel_id=1, source_target_pairs={{2,0},{4,2},{6,4},{0,6},{3,1},{5,3},{7,5},{1,7},{10,8},{12,10},{14... | collective-permute-start | bytes 49160 | tf_op jit(solution)/shard_map/ppermute | solution.py:484
  14.2 0.3 weights.1
  14.5 1.4 %sweeps.4.refs_0_.refs_1_ = f32[16,8,256]{2,1,0:T(8,128)S(1)} custom-call(f32[28,16,256]{2,1,0:T(8,128)S(1)} %get-tuple-element.35.whole_ref, f32[16,256]{1,0:T(8,128)S(1)} %collective-permute-done.2.left_ref, f32[16,256]{1,0:T(8,128)S(1)} %collective-permute-done.3.right_ref, f32[29,8,384]{2,1,0:T(8,128)S(1)} %get-tuple-element.38.south_ref.refs_0_, ...), custom_call_target="tpu_custom_call" | custom-call | tf_op jit(solution)/shard_map/sweeps/pallas_call | solution.py:34
  15.9 1.6 %collective-permute-start.8 = (f32[16,8,256]{2,1,0:T(8,128)S(1)}, f32[16,8,256]{2,1,0:T(8,128)S(1)}, u32[]{:S(2)}, u32[]{:S(2)}) collective-permute-start(f32[16,8,256]{2,1,0:T(8,128)S(1)} %sweeps.4.refs_0_.refs_1_), channel_id=1, source_target_pairs={{0,1},{1,0},{2,3},{3,2},{4,5},{5,4},{6,7},{7,6},{8,9},{9,8},{10,11... | collective-permute-start | bytes 393224 | tf_op jit(solution)/shard_map/ppermute | solution.py:512
  17.5 1.5 %sweeps.5 = (f32[16,4,256]{2,1,0:T(4,128)S(1)}, bf16[8,28,16,256]{3,2,1,0:T(8,128)(2,1)S(1)}) custom-call(f32[28,16,256]{2,1,0:T(8,128)S(1)} %get-tuple-element.35.whole_ref, f32[16,256]{1,0:T(8,128)S(1)} %collective-permute-done.2.left_ref, f32[16,256]{1,0:T(8,128)S(1)} %collective-permute-done.3.right_ref, ...), custom_call_target="tpu_custom_call" | custom-call | tf_op jit(solution)/shard_map/sweeps/pallas_call | solution.py:34
  19.0 1.5 %sweeps.6 = (f32[16,8,256]{2,1,0:T(8,128)S(1)}, bf16[8,28,16,256]{3,2,1,0:T(8,128)(2,1)S(1)}) custom-call(f32[28,16,256]{2,1,0:T(8,128)S(1)} %get-tuple-element.45.whole_ref, f32[16,256]{1,0:T(8,128)S(1)} %collective-permute-done.6.left_ref, f32[16,256]{1,0:T(8,128)S(1)} %collective-permute-done.7.right_ref, ...), custom_call_target="tpu_custom_call" | custom-call | tf_op jit(solution)/shard_map/sweeps/pallas_call | solution.py:34
  20.5 0.6 %collective-permute-start.10 = (f32[16,8,256]{2,1,0:T(8,128)S(1)}, f32[16,8,256]{2,1,0:T(8,128)S(1)}, u32[]{:S(2)}, u32[]{:S(2)}) collective-permute-start(f32[16,8,256]{2,1,0:T(8,128)S(1)} %get-tuple-element.48.refs_0_.refs_3_), channel_id=1, source_target_pairs={{0,1},{1,0},{2,3},{3,2},{4,5},{5,4},{6,7},{7,6},{8,9},{9,8},{10,11... | collective-permute-start | bytes 393224 | tf_op jit(solution)/shard_map/ppermute | solution.py:512
  21.1 1.4 %sweeps.7.refs_4_.order_ref = f32[16,8,256]{2,1,0:T(8,128)S(1)} custom-call(f32[28,16,256]{2,1,0:T(8,128)S(1)} %get-tuple-element.45.whole_ref, f32[16,256]{1,0:T(8,128)S(1)} %collective-permute-done.6.left_ref, f32[16,256]{1,0:T(8,128)S(1)} %collective-permute-done.7.right_ref, f32[29,8,384]{2,1,0:T(8,128)S(1)} %get-tuple-element.38.south_ref.refs_0_, ...), custom_call_target="tpu_custom_call" | custom-call | tf_op jit(solution)/shard_map/sweeps/pallas_call | solution.py:34
  22.5 1.6 %collective-permute-start.11 = (f32[16,8,256]{2,1,0:T(8,128)S(1)}, f32[16,8,256]{2,1,0:T(8,128)S(1)}, u32[]{:S(2)}, u32[]{:S(2)}) collective-permute-start(f32[16,8,256]{2,1,0:T(8,128)S(1)} %sweeps.7.refs_4_.order_ref), channel_id=1, source_target_pairs={{0,1},{1,0},{2,3},{3,2},{4,5},{5,4},{6,7},{7,6},{8,9},{9,8},{10,11... | collective-permute-start | bytes 393224 | tf_op jit(solution)/shard_map/ppermute | solution.py:512
  24.1 0.5 %collective-permute-start.9 = (f32[16,4,256]{2,1,0:T(4,128)S(1)}, f32[16,4,256]{2,1,0:T(4,128)S(1)}, u32[]{:S(2)}, u32[]{:S(2)}) collective-permute-start(f32[16,4,256]{2,1,0:T(4,128)S(1)} %get-tuple-element.42.refs_0_.refs_2_), channel_id=1, source_target_pairs={{0,1},{1,0},{2,3},{3,2},{4,5},{5,4},{6,7},{7,6},{8,9},{9,8},{10,11... | collective-permute-start | bytes 196616 | tf_op jit(solution)/shard_map/ppermute | solution.py:512
  24.7 0.4 mix_own.1.refs_0_
  25.1 3.4 %gram.1.gram_ref = f32[72,128]{1,0:T(8,128)S(1)} custom-call(bf16[8,28,16,256]{3,2,1,0:T(8,128)(2,1)S(1)} %get-tuple-element.53.steps_ref, bf16[8,28,16,256]{3,2,1,0:T(8,128)(2,1)S(1)} %get-tuple-element.54.grads_ref, f32[16,8,256]{2,1,0:T(8,128)S(1)} %sweeps.7.refs_4_.order_ref), custom_call_target="tpu_custom_call" | custom-call | tf_op jit(solution)/shard_map/gram/pallas_call | solution.py:34
  28.6 0.2 mix_more.3.refs_0_
  28.8 2.2 %collective-permute-done.9.refs_2_ = f32[16,4,256]{2,1,0:T(4,128)S(1)} collective-permute-done((f32[16,4,256]{2,1,0:T(4,128)S(1)}, f32[16,4,256]{2,1,0:T(4,128)S(1)}, u32[]{:S(2)}, u32[]{:S(2)}) %collective-permute-start.9) | collective-permute-done | bytes 65568 | tf_op jit(solution)/shard_map/ppermute | solution.py:512
  31.2 0.2 mix_more.5.acc_ref
  31.4 1.2 %mix_last.1 = (f32[28,16,256]{2,1,0:T(8,128)S(1)}, f32[32,1,128]{2,1,0:T(1,128)S(1)}) custom-call(f32[16,28,256]{2,1,0:T(8,128)S(1)} %mix_more.5.acc_ref, bf16[28,48]{1,0:T(8,128)(2,1)S(1)} %get-tuple-element.52.corr_ref, f32[16,8,256]{2,1,0:T(8,128)S(1)} %collective-permute-done.11.field_ref, f32[72,128]{1,0:T(8,128)S(1)} %gram.1.gram_ref, ...), custom_call_target="tpu_custom_call" | custom-call | tf_op jit(solution)/shard_map/mix_last/pallas_call | solution.py:34
  32.6 11.1 %all_to_all.5.inbox_ref = f32[32,1,128]{2,1,0:T(1,128)S(1)} all-to-all(f32[32,1,128]{2,1,0:T(1,128)S(1)} %get-tuple-element.55), channel_id=1, replica_groups={{31,30,29,28,27,26,25,24,23,22,21,20,19,18,17,16,15,14,13,12,11,10,9,8,..., dimensions={0} | all-to-all | bytes 32768 | tf_op jit(solution)/shard_map/all_to_all | solution.py:530
  43.7 1.8 %final.1 = f32[28,16,256]{2,1,0:T(8,128)} custom-call(f32[32,1,128]{2,1,0:T(1,128)S(1)} %all_to_all.5.inbox_ref, f32[28,16,256]{2,1,0:T(8,128)S(1)} %get-tuple-element.56.mixed_ref, f32[28,16,256]{2,1,0:T(8,128)S(1)} %copy-done, bf16[8,28,16,256]{3,2,1,0:T(8,128)(2,1)S(1)} %get-tuple-element.53.steps_ref, ...), custom_call_target="tpu_custom_call" | custom-call | tf_op jit(solution)/shard_map/final/pallas_call | solution.py:34
  (21 shorter events, 0.9 us)
Async XLA Ops:
  1.3 8.9 %collective-permute-start = (f32[6,16,256]{2,1,0:T(8,128)S(1)}, f32[6,16,256]{2,1,0:T(8,128)S(1)}, u32[]{:S(2)}, u32[]{:S(2)}) collective-permute-start(f32[6,16,256]{2,1,0:T(8,128)S(1)} %get-tuple-element.32), channel_id=1, source_target_pairs={{0,8},{8,0},{16,24},{24,16},{1,9},{9,1},{17,25},{25,17},{2,10},{10... | collective-permute-start | bytes 294920 | tf_op jit(solution)/shard_map/ppermute | solution.py:474
  4.4 5.8 %collective-permute-start.1 = (f32[6,16,256]{2,1,0:T(8,128)S(1)}, f32[6,16,256]{2,1,0:T(8,128)S(1)}, u32[]{:S(2)}, u32[]{:S(2)}) collective-permute-start(f32[6,16,256]{2,1,0:T(8,128)S(1)} %get-tuple-element.34), channel_id=1, source_target_pairs={{8,16},{16,8},{9,17},{17,9},{10,18},{18,10},{11,19},{19,11},{12,20... | collective-permute-start | bytes 294920 | tf_op jit(solution)/shard_map/ppermute | solution.py:473
  5.0 7.2 %collective-permute-start.4 = (f32[6,16,256]{2,1,0:T(8,128)S(1)}, f32[6,16,256]{2,1,0:T(8,128)S(1)}, u32[]{:S(2)}, u32[]{:S(2)}) collective-permute-start(f32[6,16,256]{2,1,0:T(8,128)S(1)} %get-tuple-element.43), channel_id=1, source_target_pairs={{0,8},{8,0},{16,24},{24,16},{1,9},{9,1},{17,25},{25,17},{2,10},{10... | collective-permute-start | bytes 294920 | tf_op jit(solution)/shard_map/ppermute | solution.py:474
  9.5 2.7 %collective-permute-start.5 = (f32[6,16,256]{2,1,0:T(8,128)S(1)}, f32[6,16,256]{2,1,0:T(8,128)S(1)}, u32[]{:S(2)}, u32[]{:S(2)}) collective-permute-start(f32[6,16,256]{2,1,0:T(8,128)S(1)} %get-tuple-element.44), channel_id=1, source_target_pairs={{8,16},{16,8},{9,17},{17,9},{10,18},{18,10},{11,19},{19,11},{12,20... | collective-permute-start | bytes 294920 | tf_op jit(solution)/shard_map/ppermute | solution.py:473
  10.4 3.8 %collective-permute-start.2 = (f32[16,256]{1,0:T(8,128)S(1)}, f32[16,256]{1,0:T(8,128)S(1)}, u32[]{:S(2)}, u32[]{:S(2)}) collective-permute-start(f32[16,256]{1,0:T(8,128)S(1)} %get-tuple-element.36), channel_id=1, source_target_pairs={{0,2},{2,4},{4,6},{6,0},{1,3},{3,5},{5,7},{7,1},{8,10},{10,12},{12... | collective-permute-start | bytes 49160 | tf_op jit(solution)/shard_map/ppermute | solution.py:484
  10.4 3.8 %collective-permute-start.3 = (f32[16,256]{1,0:T(8,128)S(1)}, f32[16,256]{1,0:T(8,128)S(1)}, u32[]{:S(2)}, u32[]{:S(2)}) collective-permute-start(f32[16,256]{1,0:T(8,128)S(1)} %get-tuple-element.37), channel_id=1, source_target_pairs={{2,0},{4,2},{6,4},{0,6},{3,1},{5,3},{7,5},{1,7},{10,8},{12,10},{14... | collective-permute-start | bytes 49160 | tf_op jit(solution)/shard_map/ppermute | solution.py:484
  12.4 6.6 %collective-permute-start.6 = (f32[16,256]{1,0:T(8,128)S(1)}, f32[16,256]{1,0:T(8,128)S(1)}, u32[]{:S(2)}, u32[]{:S(2)}) collective-permute-start(f32[16,256]{1,0:T(8,128)S(1)} %get-tuple-element.46), channel_id=1, source_target_pairs={{0,2},{2,4},{4,6},{6,0},{1,3},{3,5},{5,7},{7,1},{8,10},{10,12},{12... | collective-permute-start | bytes 49160 | tf_op jit(solution)/shard_map/ppermute | solution.py:484
  12.4 6.5 %collective-permute-start.7 = (f32[16,256]{1,0:T(8,128)S(1)}, f32[16,256]{1,0:T(8,128)S(1)}, u32[]{:S(2)}, u32[]{:S(2)}) collective-permute-start(f32[16,256]{1,0:T(8,128)S(1)} %get-tuple-element.47), channel_id=1, source_target_pairs={{2,0},{4,2},{6,4},{0,6},{3,1},{5,3},{7,5},{1,7},{10,8},{12,10},{14... | collective-permute-start | bytes 49160 | tf_op jit(solution)/shard_map/ppermute | solution.py:484
  15.9 12.6 %collective-permute-start.8 = (f32[16,8,256]{2,1,0:T(8,128)S(1)}, f32[16,8,256]{2,1,0:T(8,128)S(1)}, u32[]{:S(2)}, u32[]{:S(2)}) collective-permute-start(f32[16,8,256]{2,1,0:T(8,128)S(1)} %sweeps.4.refs_0_.refs_1_), channel_id=1, source_target_pairs={{0,1},{1,0},{2,3},{3,2},{4,5},{5,4},{6,7},{7,6},{8,9},{9,8},{10,11... | collective-permute-start | bytes 393224 | tf_op jit(solution)/shard_map/ppermute | solution.py:512
  20.5 4.1 %copy-start.1 = (f32[56,56]{1,0:T(8,128)S(1)}, f32[56,56]{1,0:T(8,128)}, u32[]{:S(2)}) copy-start(f32[56,56]{1,0:T(8,128)} %corr_ref.1) | copy-start | bytes 37636
  20.5 10.7 %collective-permute-start.10 = (f32[16,8,256]{2,1,0:T(8,128)S(1)}, f32[16,8,256]{2,1,0:T(8,128)S(1)}, u32[]{:S(2)}, u32[]{:S(2)}) collective-permute-start(f32[16,8,256]{2,1,0:T(8,128)S(1)} %get-tuple-element.48.refs_0_.refs_3_), channel_id=1, source_target_pairs={{0,1},{1,0},{2,3},{3,2},{4,5},{5,4},{6,7},{7,6},{8,9},{9,8},{10,11... | collective-permute-start | bytes 393224 | tf_op jit(solution)/shard_map/ppermute | solution.py:512
  22.5 8.9 %collective-permute-start.11 = (f32[16,8,256]{2,1,0:T(8,128)S(1)}, f32[16,8,256]{2,1,0:T(8,128)S(1)}, u32[]{:S(2)}, u32[]{:S(2)}) collective-permute-start(f32[16,8,256]{2,1,0:T(8,128)S(1)} %sweeps.7.refs_4_.order_ref), channel_id=1, source_target_pairs={{0,1},{1,0},{2,3},{3,2},{4,5},{5,4},{6,7},{7,6},{8,9},{9,8},{10,11... | collective-permute-start | bytes 393224 | tf_op jit(solution)/shard_map/ppermute | solution.py:512
  24.1 6.9 %collective-permute-start.9 = (f32[16,4,256]{2,1,0:T(4,128)S(1)}, f32[16,4,256]{2,1,0:T(4,128)S(1)}, u32[]{:S(2)}, u32[]{:S(2)}) collective-permute-start(f32[16,4,256]{2,1,0:T(4,128)S(1)} %get-tuple-element.42.refs_0_.refs_2_), channel_id=1, source_target_pairs={{0,1},{1,0},{2,3},{3,2},{4,5},{5,4},{6,7},{7,6},{8,9},{9,8},{10,11... | collective-permute-start | bytes 196616 | tf_op jit(solution)/shard_map/ppermute | solution.py:512
  31.4 12.3 %copy-start = (f32[28,16,256]{2,1,0:T(8,128)S(1)}, f32[28,16,256]{2,1,0:T(8,128)}, u32[]{:S(2)}) copy-start(f32[28,16,256]{2,1,0:T(8,128)} %control_ref.1) | copy-start | bytes 1376260

commit v9 on v7

--- a/solution.py
+++ b/solution.py
@@ -145,16 +145,24 @@
         next_ref[row] = field_ref[far + row]
 
 
-def side_kernel(swap_ref, field_ref, next_ref, order_ref, whole_ref, west_ref, east_ref):
+def side_kernel(swap_ref, field_ref, next_ref, order_ref, whole_ref, pair_ref, beside_ref):
     rows, slots, cols = field_ref.shape
-    odd = lax.rem(lax.axis_index("lat"), 2)
+    place, count = lax.axis_index("lat"), lax.axis_size("lat")
+    odd = lax.rem(place, 2)
     near, far = (1 - odd) * (HALO + rows), odd * (HALO + rows)
+    has_near = jnp.full((SUB, LANE), place + 1 - 2 * odd, jnp.int32) < count
+    after = jnp.full((SUB, LANE), place - 1 + 2 * odd, jnp.int32)
+    has_far = (after >= 0) & (after < count)
     for row in range(HALO):
-        whole_ref[near + row] = swap_ref[row]
-        whole_ref[far + row] = next_ref[row]
+        for slot in range(0, slots, SUB):
+            for c in range(0, cols, LANE):
+                where = (slice(slot, slot + SUB), slice(c, c + LANE))
+                whole_ref[(near + row, *where)] = jnp.where(has_near, swap_ref[(row, *where)], 0.0)
+                whole_ref[(far + row, *where)] = jnp.where(has_far, next_ref[(row, *where)], 0.0)
     for row in range(rows):
         whole_ref[HALO + row] = field_ref[row]
     lane = lane_index()
+    uneven = jnp.full((SUB, LANE), lax.rem(lax.axis_index("lon"), 2), jnp.int32) == 1
     for slot in range(0, slots, SUB):
         down = slice(slot, slot + SUB)
         for base in range(0, rows + 2 * HALO, PER):
@@ -167,9 +175,9 @@
                 west = jnp.where(here, pltpu.roll(left, begin, 1) if begin else left, west)
                 turn = (begin + GROUP) % LANE
                 east = jnp.where(here, pltpu.roll(right, turn, 1) if turn else right, east)
-            place = slice(base // PER * LANE, (base // PER + 1) * LANE)
-            west_ref[down, place] = west
-            east_ref[down, place] = east
+            across = slice(base // PER * LANE, (base // PER + 1) * LANE)
+            pair_ref[down, across] = jnp.where(uneven, west, east)
+            beside_ref[down, across] = jnp.where(uneven, east, west)
 
 
 def make_row_loader(whole_ref, left_ref, right_ref):
@@ -200,9 +208,12 @@
 
 
 def weight_kernel(
-    whole_ref, left_ref, right_ref, south_ref, east_ref, west_ref, keep_ref, kappa_ref, packed_ref, *, steps
+    whole_ref, pair_ref, beside_ref, left_ref, right_ref, south_ref, east_ref, west_ref, keep_ref, kappa_ref, packed_ref, *, steps
 ):
     height, _, cols = whole_ref.shape
+    uneven = jnp.full(pair_ref.shape, lax.rem(lax.axis_index("lon"), 2), jnp.int32) == 1
+    left_ref[...] = jnp.where(uneven, pair_ref[...], beside_ref[...])
+    right_ref[...] = jnp.where(uneven, beside_ref[...], pair_ref[...])
     width = cols // LANE + 1
     load = make_row_loader(whole_ref, left_ref, right_ref)
     lane = lane_index()
@@ -442,13 +453,20 @@
         copy.wait()
 
 
+def matching(firsts, count):
+    partner = list(range(count))
+    for first in firsts:
+        partner[first], partner[(first + 1) % count] = (first + 1) % count, first
+    return list(enumerate(partner))
+
+
 def local(gradient, control, diffusivity, land_mask, time_corr, pair_steps, pair_grads):
     steps, rows, cols = gradient.shape
     height, breadth, groups = (lax.axis_size(axis) for axis in ("lat", "lon", "tm"))
-    even = [(i, j) for k in range(0, height - 1, 2) for i, j in ((k, k + 1), (k + 1, k))]
-    odd = [(i, j) for k in range(1, height - 1, 2) for i, j in ((k, k + 1), (k + 1, k))]
-    right = [(i, (i + 1) % breadth) for i in range(breadth)]
-    left = [(j, i) for i, j in right]
+    even = matching(range(0, height - 1, 2), height)
+    odd = matching(range(1, height - 1, 2), height)
+    evens = matching(range(0, breadth - 1, 2), breadth)
+    odds = matching(range(1, breadth, 2), breadth)
     slots = slots_of(steps)
     turn = pltpu.VMEM((rows * (cols // LANE) * slots, LANE), jnp.float32)
 
@@ -481,18 +499,19 @@
         (time_corr,), name="corr",
     )
     side_shape = f32(slots, -(-tall // PER) * LANE)
-    whole, west, east = call(
+    whole, to_pair, to_beside = call(
         side_kernel, (f32(tall, slots, cols), side_shape, side_shape), (from_swap, field, from_next, gram), name="sides"
     )
-    from_left = lax.ppermute(east, "lon", right)
-    from_right = lax.ppermute(west, "lon", left)
-    extended = (whole, from_left, from_right)
-    weights = call(
+    from_beside = lax.ppermute(to_beside, "lon", odds)
+    from_pair = lax.ppermute(to_pair, "lon", evens)
+    left, right, *weights = call(
         functools.partial(weight_kernel, steps=steps),
-        (f32(tall + 1, SUB, wide), f32(tall, SUB, wide), f32(tall, SUB, wide), f32(tall, SUB, wide)), extended,
+        (side_shape, side_shape, f32(tall + 1, SUB, wide), f32(tall, SUB, wide), f32(tall, SUB, wide), f32(tall, SUB, wide)),
+        (whole, from_pair, from_beside),
         scratch=[pltpu.VMEM((-(-tall // SUB) * SUB + SUB, wide), jnp.float32), pltpu.VMEM((4, -(-tall // SUB) * SUB, wide), jnp.float32)],
         name="weights",
     )
+    extended = (whole, left, right)
     own, other = [], []
     for begin, count in parts:
         part = call(

time: 46 us -> 46 us (level)
  transfers between devices with their start and end apart: 8 -> 8, of which waited for: 3 -> 4; matrix products, arithmetic and copies ran while one was open for 0% -> 0% of each run, Pallas kernels for 21% -> 21%
where the time goes in v9:
time: 46 us; the launch traced here: 45.7 us
  Pallas kernels  16 us (35%)
  blocking collectives  14.6 us (32%)
  starting transfers between devices  9.77 us (21%)
  waiting for transfers between devices  5.16 us (11%)
    pallas_call x15, Pallas kernels, call(): pl.pallas_call(kernel, out_shape=outs, in_specs=specs or [VMEM] * len(arg...  16 us
    all_to_all x1, blocking collectives, local(): lax.all_to_all(message, ('lat', 'lon', 'tm'), split_axis=0, concat_axis=0...  14.6 us
    ppermute x4, starting transfers between devices, local(): other.append(lax.ppermute(part, 'tm', pairs))  4.31 us
    ppermute x4, waiting for transfers between devices, local(): other.append(lax.ppermute(part, 'tm', pairs))  3.38 us
    ppermute x1, starting transfers between devices, local(): from_swap = lax.ppermute(to_swap, 'lat', even)  3.09 us
    ppermute x1, waiting for transfers between devices, local(): from_beside = lax.ppermute(to_beside, 'lon', odds)  1.77 us
    ppermute x1, starting transfers between devices, local(): from_beside = lax.ppermute(to_beside, 'lon', odds)  1.64 us
  transfers between devices with their start and end apart: 8, of which 4 were waited for; matrix products, arithmetic and copies ran while one was open for 0% of the time, Pallas kernels for 21%

profile of v9, /device:TPU:0, one launch (start us, length us, event | category | flops | bytes accessed | tf_op | source)
XLA Modules:
  0.0 45.7 jit_solution(17476633603510413249)
XLA Ops:
  0.0 1.3 %pack.1 = (f32[16,32,256]{2,1,0:T(8,128)S(1)}, f32[6,32,256]{2,1,0:T(8,128)S(1)}, f32[6,32,256]{2,1,0:T(8,128)S(1)}) custom-call(f32[28,16,256]{2,1,0:T(8,128)} %grad_hbm.1, s32[16,256]{1,0:T(8,128)} %mask_hbm.1, f32[16,256]{1,0:T(8,128)} %diff_hbm.1), custom_call_target="tpu_custom_call" | custom-call | tf_op jit(solution)/shard_map/pack/pallas_call | solution.py:34
  1.3 3.1 %collective-permute-start = (f32[6,32,256]{2,1,0:T(8,128)S(1)}, f32[6,32,256]{2,1,0:T(8,128)S(1)}, u32[]{:S(2)}, u32[]{:S(2)}) collective-permute-start(f32[6,32,256]{2,1,0:T(8,128)S(1)} %get-tuple-element.28), channel_id=1, source_target_pairs={{0,8},{8,0},{16,24},{24,16},{1,9},{9,1},{17,25},{25,17},{2,10},{10... | collective-permute-start | bytes 589832 | tf_op jit(solution)/shard_map/ppermute | solution.py:484
  4.3 0.7 %collective-permute-start.1 = (f32[6,32,256]{2,1,0:T(8,128)S(1)}, f32[6,32,256]{2,1,0:T(8,128)S(1)}, u32[]{:S(2)}, u32[]{:S(2)}) collective-permute-start(f32[6,32,256]{2,1,0:T(8,128)S(1)} %get-tuple-element.30), channel_id=1, source_target_pairs={{0,0},{8,16},{16,8},{24,24},{1,1},{9,17},{17,9},{25,25},{2,2},{10,... | collective-permute-start | bytes 589832 | tf_op jit(solution)/shard_map/ppermute | solution.py:485
  5.0 4.6 %gram.1 = (f32[72,128]{1,0:T(8,128)S(1)}, bf16[8,28,16,256]{3,2,1,0:T(8,128)(2,1)S(1)}, bf16[8,28,16,256]{3,2,1,0:T(8,128)(2,1)S(1)}) custom-call(bf16[8,28,16,256]{3,2,1,0:T(8,128)(2,1)} %steps_hbm.1, bf16[8,28,16,256]{3,2,1,0:T(8,128)(2,1)} %grads_hbm.1), custom_call_target="tpu_custom_call" | custom-call | tf_op jit(solution)/shard_map/gram/pallas_call | solution.py:34
  9.7 0.3 sides.1
  10.1 1.6 %collective-permute-start.3 = (f32[32,256]{1,0:T(8,128)S(1)}, f32[32,256]{1,0:T(8,128)S(1)}, u32[]{:S(2)}, u32[]{:S(2)}) collective-permute-start(f32[32,256]{1,0:T(8,128)S(1)} %get-tuple-element.34), channel_id=1, source_target_pairs={{0,6},{2,4},{4,2},{6,0},{1,7},{3,5},{5,3},{7,1},{8,14},{10,12},{12... | collective-permute-start | bytes 98312 | tf_op jit(solution)/shard_map/ppermute | solution.py:505
  11.7 1.8 %collective-permute-done.3.beside_ref = f32[32,256]{1,0:T(8,128)S(1)} collective-permute-done((f32[32,256]{1,0:T(8,128)S(1)}, f32[32,256]{1,0:T(8,128)S(1)}, u32[]{:S(2)}, u32[]{:S(2)}) %collective-permute-start.3) | collective-permute-done | bytes 32800 | tf_op jit(solution)/shard_map/ppermute | solution.py:505
  13.5 0.3 weights.1
  13.9 1.3 %sweeps.4.refs_1_ = f32[16,8,256]{2,1,0:T(8,128)S(1)} custom-call(f32[28,32,256]{2,1,0:T(8,128)S(1)} %get-tuple-element.32.whole_ref, f32[32,256]{1,0:T(8,128)S(1)} %get-tuple-element.35.left_ref, f32[32,256]{1,0:T(8,128)S(1)} %get-tuple-element.36.right_ref, f32[29,8,384]{2,1,0:T(8,128)S(1)} %get-tuple-element.37.south_ref, ...), custom_call_target="tpu_custom_call" | custom-call | tf_op jit(solution)/shard_map/sweeps/pallas_call | solution.py:34
  15.2 1.6 %collective-permute-start.4 = (f32[16,8,256]{2,1,0:T(8,128)S(1)}, f32[16,8,256]{2,1,0:T(8,128)S(1)}, u32[]{:S(2)}, u32[]{:S(2)}) collective-permute-start(f32[16,8,256]{2,1,0:T(8,128)S(1)} %sweeps.4.refs_1_), channel_id=1, source_target_pairs={{0,1},{1,0},{2,3},{3,2},{4,5},{5,4},{6,7},{7,6},{8,9},{9,8},{10,11... | collective-permute-start | bytes 393224 | tf_op jit(solution)/shard_map/ppermute | solution.py:523
  16.8 1.3 %sweeps.5.refs_2_ = f32[16,8,256]{2,1,0:T(8,128)S(1)} custom-call(f32[28,32,256]{2,1,0:T(8,128)S(1)} %get-tuple-element.32.whole_ref, f32[32,256]{1,0:T(8,128)S(1)} %get-tuple-element.35.left_ref, f32[32,256]{1,0:T(8,128)S(1)} %get-tuple-element.36.right_ref, f32[29,8,384]{2,1,0:T(8,128)S(1)} %get-tuple-element.37.south_ref, ...), custom_call_target="tpu_custom_call" | custom-call | tf_op jit(solution)/shard_map/sweeps/pallas_call | solution.py:34
  18.1 0.6 %collective-permute-start.5 = (f32[16,8,256]{2,1,0:T(8,128)S(1)}, f32[16,8,256]{2,1,0:T(8,128)S(1)}, u32[]{:S(2)}, u32[]{:S(2)}) collective-permute-start(f32[16,8,256]{2,1,0:T(8,128)S(1)} %sweeps.5.refs_2_), channel_id=1, source_target_pairs={{0,1},{1,0},{2,3},{3,2},{4,5},{5,4},{6,7},{7,6},{8,9},{9,8},{10,11... | collective-permute-start | bytes 393224 | tf_op jit(solution)/shard_map/ppermute | solution.py:523
  18.7 1.3 %sweeps.6.refs_3_ = f32[16,8,256]{2,1,0:T(8,128)S(1)} custom-call(f32[28,32,256]{2,1,0:T(8,128)S(1)} %get-tuple-element.32.whole_ref, f32[32,256]{1,0:T(8,128)S(1)} %get-tuple-element.35.left_ref, f32[32,256]{1,0:T(8,128)S(1)} %get-tuple-element.36.right_ref, f32[29,8,384]{2,1,0:T(8,128)S(1)} %get-tuple-element.37.south_ref, ...), custom_call_target="tpu_custom_call" | custom-call | tf_op jit(solution)/shard_map/sweeps/pallas_call | solution.py:34
  20.1 1.6 %collective-permute-start.6 = (f32[16,8,256]{2,1,0:T(8,128)S(1)}, f32[16,8,256]{2,1,0:T(8,128)S(1)}, u32[]{:S(2)}, u32[]{:S(2)}) collective-permute-start(f32[16,8,256]{2,1,0:T(8,128)S(1)} %sweeps.6.refs_3_), channel_id=1, source_target_pairs={{0,1},{1,0},{2,3},{3,2},{4,5},{5,4},{6,7},{7,6},{8,9},{9,8},{10,11... | collective-permute-start | bytes 393224 | tf_op jit(solution)/shard_map/ppermute | solution.py:523
  21.6 1.3 %sweeps.7.refs_4_ = f32[16,4,256]{2,1,0:T(4,128)S(1)} custom-call(f32[28,32,256]{2,1,0:T(8,128)S(1)} %get-tuple-element.32.whole_ref, f32[32,256]{1,0:T(8,128)S(1)} %get-tuple-element.35.left_ref, f32[32,256]{1,0:T(8,128)S(1)} %get-tuple-element.36.right_ref, f32[29,8,384]{2,1,0:T(8,128)S(1)} %get-tuple-element.37.south_ref, ...), custom_call_target="tpu_custom_call" | custom-call | tf_op jit(solution)/shard_map/sweeps/pallas_call | solution.py:34
  23.0 0.6 %collective-permute-start.7 = (f32[16,4,256]{2,1,0:T(4,128)S(1)}, f32[16,4,256]{2,1,0:T(4,128)S(1)}, u32[]{:S(2)}, u32[]{:S(2)}) collective-permute-start(f32[16,4,256]{2,1,0:T(4,128)S(1)} %sweeps.7.refs_4_), channel_id=1, source_target_pairs={{0,1},{1,0},{2,3},{3,2},{4,5},{5,4},{6,7},{7,6},{8,9},{9,8},{10,11... | collective-permute-start | bytes 196616 | tf_op jit(solution)/shard_map/ppermute | solution.py:523
  23.7 0.4 mix_own.1.refs_0_
  24.1 0.2 mix_more.3.refs_0_
  24.8 2.6 %collective-permute-done.6.refs_2_ = f32[16,8,256]{2,1,0:T(8,128)S(1)} collective-permute-done((f32[16,8,256]{2,1,0:T(8,128)S(1)}, f32[16,8,256]{2,1,0:T(8,128)S(1)}, u32[]{:S(2)}, u32[]{:S(2)}) %collective-permute-start.6) | collective-permute-done | bytes 131104 | tf_op jit(solution)/shard_map/ppermute | solution.py:523
  27.3 0.2 mix_more.5.acc_ref
  27.6 0.6 %collective-permute-done.7.field_ref = f32[16,4,256]{2,1,0:T(4,128)S(1)} collective-permute-done((f32[16,4,256]{2,1,0:T(4,128)S(1)}, f32[16,4,256]{2,1,0:T(4,128)S(1)}, u32[]{:S(2)}, u32[]{:S(2)}) %collective-permute-start.7) | collective-permute-done | bytes 65568 | tf_op jit(solution)/shard_map/ppermute | solution.py:523
  28.2 1.2 %mix_last.1 = (f32[28,16,256]{2,1,0:T(8,128)S(1)}, f32[32,1,128]{2,1,0:T(1,128)S(1)}) custom-call(f32[16,28,256]{2,1,0:T(8,128)S(1)} %mix_more.5.acc_ref, bf16[28,48]{1,0:T(8,128)(2,1)S(1)} %get-tuple-element.44.corr_ref, f32[16,4,256]{2,1,0:T(4,128)S(1)} %collective-permute-done.7.field_ref, f32[72,128]{1,0:T(8,128)S(1)} %get-tuple-element.31.order_ref.gram_ref, ...), custom_call_target="tpu_custom_call" | custom-call | tf_op jit(solution)/shard_map/mix_last/pallas_call | solution.py:34
  29.4 14.6 %all_to_all.5.inbox_ref = f32[32,1,128]{2,1,0:T(1,128)S(1)} all-to-all(f32[32,1,128]{2,1,0:T(1,128)S(1)} %get-tuple-element.47), channel_id=1, replica_groups={{31,30,29,28,27,26,25,24,23,22,21,20,19,18,17,16,15,14,13,12,11,10,9,8,..., dimensions={0} | all-to-all | bytes 32768 | tf_op jit(solution)/shard_map/all_to_all | solution.py:533
  44.0 1.7 %final.1 = f32[28,16,256]{2,1,0:T(8,128)} custom-call(f32[32,1,128]{2,1,0:T(1,128)S(1)} %all_to_all.5.inbox_ref, f32[28,16,256]{2,1,0:T(8,128)S(1)} %get-tuple-element.48.mixed_ref, f32[28,16,256]{2,1,0:T(8,128)S(1)} %copy-done, bf16[8,28,16,256]{3,2,1,0:T(8,128)(2,1)S(1)} %get-tuple-element.45.steps_ref, ...), custom_call_target="tpu_custom_call" | custom-call | tf_op jit(solution)/shard_map/final/pallas_call | solution.py:34
  (12 shorter events, 0.6 us)
Async XLA Ops:
  1.3 8.4 %collective-permute-start = (f32[6,32,256]{2,1,0:T(8,128)S(1)}, f32[6,32,256]{2,1,0:T(8,128)S(1)}, u32[]{:S(2)}, u32[]{:S(2)}) collective-permute-start(f32[6,32,256]{2,1,0:T(8,128)S(1)} %get-tuple-element.28), channel_id=1, source_target_pairs={{0,8},{8,0},{16,24},{24,16},{1,9},{9,1},{17,25},{25,17},{2,10},{10... | collective-permute-start | bytes 589832 | tf_op jit(solution)/shard_map/ppermute | solution.py:484
  4.3 5.3 %collective-permute-start.1 = (f32[6,32,256]{2,1,0:T(8,128)S(1)}, f32[6,32,256]{2,1,0:T(8,128)S(1)}, u32[]{:S(2)}, u32[]{:S(2)}) collective-permute-start(f32[6,32,256]{2,1,0:T(8,128)S(1)} %get-tuple-element.30), channel_id=1, source_target_pairs={{0,0},{8,16},{16,8},{24,24},{1,1},{9,17},{17,9},{25,25},{2,2},{10,... | collective-permute-start | bytes 589832 | tf_op jit(solution)/shard_map/ppermute | solution.py:485
  10.0 1.7 %collective-permute-start.2 = (f32[32,256]{1,0:T(8,128)S(1)}, f32[32,256]{1,0:T(8,128)S(1)}, u32[]{:S(2)}, u32[]{:S(2)}) collective-permute-start(f32[32,256]{1,0:T(8,128)S(1)} %get-tuple-element.33), channel_id=1, source_target_pairs={{0,2},{2,0},{4,6},{6,4},{1,3},{3,1},{5,7},{7,5},{8,10},{10,8},{12,... | collective-permute-start | bytes 98312 | tf_op jit(solution)/shard_map/ppermute | solution.py:506
  10.1 3.4 %collective-permute-start.3 = (f32[32,256]{1,0:T(8,128)S(1)}, f32[32,256]{1,0:T(8,128)S(1)}, u32[]{:S(2)}, u32[]{:S(2)}) collective-permute-start(f32[32,256]{1,0:T(8,128)S(1)} %get-tuple-element.34), channel_id=1, source_target_pairs={{0,6},{2,4},{4,2},{6,0},{1,7},{3,5},{5,3},{7,1},{8,14},{10,12},{12... | collective-permute-start | bytes 98312 | tf_op jit(solution)/shard_map/ppermute | solution.py:505
  15.2 8.9 %collective-permute-start.4 = (f32[16,8,256]{2,1,0:T(8,128)S(1)}, f32[16,8,256]{2,1,0:T(8,128)S(1)}, u32[]{:S(2)}, u32[]{:S(2)}) collective-permute-start(f32[16,8,256]{2,1,0:T(8,128)S(1)} %sweeps.4.refs_1_), channel_id=1, source_target_pairs={{0,1},{1,0},{2,3},{3,2},{4,5},{5,4},{6,7},{7,6},{8,9},{9,8},{10,11... | collective-permute-start | bytes 393224 | tf_op jit(solution)/shard_map/ppermute | solution.py:523
  18.1 6.4 %collective-permute-start.5 = (f32[16,8,256]{2,1,0:T(8,128)S(1)}, f32[16,8,256]{2,1,0:T(8,128)S(1)}, u32[]{:S(2)}, u32[]{:S(2)}) collective-permute-start(f32[16,8,256]{2,1,0:T(8,128)S(1)} %sweeps.5.refs_2_), channel_id=1, source_target_pairs={{0,1},{1,0},{2,3},{3,2},{4,5},{5,4},{6,7},{7,6},{8,9},{9,8},{10,11... | collective-permute-start | bytes 393224 | tf_op jit(solution)/shard_map/ppermute | solution.py:523
  20.1 3.5 %copy-start.1 = (f32[56,56]{1,0:T(8,128)S(1)}, f32[56,56]{1,0:T(8,128)}, u32[]{:S(2)}) copy-start(f32[56,56]{1,0:T(8,128)} %corr_ref.1) | copy-start | bytes 37636
  20.1 7.3 %collective-permute-start.6 = (f32[16,8,256]{2,1,0:T(8,128)S(1)}, f32[16,8,256]{2,1,0:T(8,128)S(1)}, u32[]{:S(2)}, u32[]{:S(2)}) collective-permute-start(f32[16,8,256]{2,1,0:T(8,128)S(1)} %sweeps.6.refs_3_), channel_id=1, source_target_pairs={{0,1},{1,0},{2,3},{3,2},{4,5},{5,4},{6,7},{7,6},{8,9},{9,8},{10,11... | collective-permute-start | bytes 393224 | tf_op jit(solution)/shard_map/ppermute | solution.py:523
  23.0 5.2 %collective-permute-start.7 = (f32[16,4,256]{2,1,0:T(4,128)S(1)}, f32[16,4,256]{2,1,0:T(4,128)S(1)}, u32[]{:S(2)}, u32[]{:S(2)}) collective-permute-start(f32[16,4,256]{2,1,0:T(4,128)S(1)} %sweeps.7.refs_4_), channel_id=1, source_target_pairs={{0,1},{1,0},{2,3},{3,2},{4,5},{5,4},{6,7},{7,6},{8,9},{9,8},{10,11... | collective-permute-start | bytes 196616 | tf_op jit(solution)/shard_map/ppermute | solution.py:523
  28.2 15.8 %copy-start = (f32[28,16,256]{2,1,0:T(8,128)S(1)}, f32[28,16,256]{2,1,0:T(8,128)}, u32[]{:S(2)}) copy-start(f32[28,16,256]{2,1,0:T(8,128)} %control_ref.1) | copy-start | bytes 1376260

commit v10 on v9

--- a/solution.py
+++ b/solution.py
@@ -50,7 +50,28 @@
     return lax.broadcasted_iota(jnp.int32, (SUB, LANE), 0)
 
 
-def gram_kernel(steps_hbm, grads_hbm, out_ref, steps_ref, grads_ref, sems):
+def product_body(left_ref, right_ref):
+    _, _, rows, cols = left_ref.shape
+
+    def body(step, sums):
+        sums = list(sums)
+        for c in range(0, cols, LANE):
+            for r in range(0, rows, 2 * SUB):
+                where = (step, pl.ds(r, 2 * SUB), pl.ds(c, LANE))
+                right = [right_ref[(i, *where)].astype(jnp.float32) for i in range(PAIRS)]
+                left = right
+                if left_ref is not right_ref:
+                    left = [left_ref[(i, *where)].astype(jnp.float32) for i in range(PAIRS)]
+                for part in range(2):
+                    cut = slice(part * SUB, (part + 1) * SUB)
+                    for k, (i, j) in enumerate(CROSS):
+                        sums[k] = sums[k] + left[i][cut] * right[j][cut]
+        return tuple(sums)
+
+    return body
+
+
+def cross_kernel(steps_hbm, grads_hbm, out_ref, steps_ref, grads_ref, sems):
     _, steps, rows, cols = steps_ref.shape
     pieces = 4
     while steps % pieces:
@@ -67,33 +88,21 @@
         for copy in pair:
             copy.start()
 
-    def make_body(half):
-        def body(step, sums):
-            sums = list(sums)
-            for c in range(0, cols, LANE):
-                for r in range(0, rows, 2 * SUB):
-                    where = (step, pl.ds(r, 2 * SUB), pl.ds(c, LANE))
-                    right = [grads_ref[(i, *where)].astype(jnp.float32) for i in range(PAIRS)]
-                    left = right if half else [steps_ref[(i, *where)].astype(jnp.float32) for i in range(PAIRS)]
-                    for part in range(2):
-                        cut = slice(part * SUB, (part + 1) * SUB)
-                        for k, (i, j) in enumerate(CROSS):
-                            sums[k] = sums[k] + left[i][cut] * right[j][cut]
-            return tuple(sums)
-
-        return body
-
-    zero = jnp.zeros((SUB, LANE), jnp.float32)
-    sums = (zero,) * NSYM
+    sums = (jnp.zeros((SUB, LANE), jnp.float32),) * NSYM
     for n in range(pieces):
         for copy in copies[n]:
             copy.wait()
-        sums = lax.fori_loop(n * count, (n + 1) * count, make_body(0), sums)
+        sums = lax.fori_loop(n * count, (n + 1) * count, product_body(steps_ref, grads_ref), sums)
     for k in range(NSYM):
         out_ref[k:k + 1, :] = jnp.sum(sums[k], axis=0, keepdims=True)
-    sums = lax.fori_loop(0, steps, make_body(1), (zero,) * NSYM)
+
+
+def square_kernel(grads_ref, order_ref, out_ref):
+    steps = grads_ref.shape[1]
+    sums = (jnp.zeros((SUB, LANE), jnp.float32),) * NSYM
+    sums = lax.fori_loop(0, steps, product_body(grads_ref, grads_ref), sums)
     for k in range(NSYM):
-        out_ref[NSYM + k:NSYM + k + 1, :] = jnp.sum(sums[k], axis=0, keepdims=True)
+        out_ref[k:k + 1, :] = jnp.sum(sums[k], axis=0, keepdims=True)
 
 
 def groups_of(steps):
@@ -102,6 +111,20 @@
 
 def slots_of(steps):
     return -(-(steps + 1) // SUB) * SUB
+
+
+def message_rows(steps):
+    return -(-HALO * (steps + 1) // SUB) * SUB
+
+
+def message_parts(row, steps):
+    full = (steps + 1) // SUB * SUB
+    rest = steps + 1 - full
+    parts = [(slice(row * full, (row + 1) * full), slice(0, full))] if full else []
+    if rest:
+        start = HALO * full + row * rest
+        parts.append((slice(start, start + rest), slice(full, steps + 1)))
+    return parts
 
 
 def pack_kernel(grad_hbm, mask_hbm, diff_hbm, field_ref, swap_ref, next_ref, grad_ref, mask_ref, diff_ref, turn_ref, sems):
@@ -141,24 +164,26 @@
     odd = lax.rem(lax.axis_index("lat"), 2)
     near, far = (1 - odd) * (rows - HALO), odd * (rows - HALO)
     for row in range(HALO):
-        swap_ref[row] = field_ref[near + row]
-        next_ref[row] = field_ref[far + row]
-
-
-def side_kernel(swap_ref, field_ref, next_ref, order_ref, whole_ref, pair_ref, beside_ref):
+        for place, there in message_parts(row, steps):
+            swap_ref[place] = field_ref[near + row, there]
+            next_ref[place] = field_ref[far + row, there]
+
+
+def side_kernel(swap_ref, field_ref, next_ref, order_ref, whole_ref, pair_ref, beside_ref, *, steps):
     rows, slots, cols = field_ref.shape
     place, count = lax.axis_index("lat"), lax.axis_size("lat")
     odd = lax.rem(place, 2)
     near, far = (1 - odd) * (HALO + rows), odd * (HALO + rows)
-    has_near = jnp.full((SUB, LANE), place + 1 - 2 * odd, jnp.int32) < count
-    after = jnp.full((SUB, LANE), place - 1 + 2 * odd, jnp.int32)
-    has_far = (after >= 0) & (after < count)
+    after = place - 1 + 2 * odd
+    bounds = jnp.full((1, cols), place + 1 - 2 * odd, jnp.int32) < count, jnp.full((1, cols), after, jnp.int32)
+    inside = bounds[0], (bounds[1] >= 0) & (bounds[1] < count)
     for row in range(HALO):
-        for slot in range(0, slots, SUB):
-            for c in range(0, cols, LANE):
-                where = (slice(slot, slot + SUB), slice(c, c + LANE))
-                whole_ref[(near + row, *where)] = jnp.where(has_near, swap_ref[(row, *where)], 0.0)
-                whole_ref[(far + row, *where)] = jnp.where(has_far, next_ref[(row, *where)], 0.0)
+        for source, target in message_parts(row, steps):
+            whole_ref[near + row, target] = jnp.where(inside[0], swap_ref[source], 0.0)
+            whole_ref[far + row, target] = jnp.where(inside[1], next_ref[source], 0.0)
+        if steps + 1 < slots:
+            whole_ref[near + row, steps + 1:] = jnp.zeros((slots - steps - 1, cols), jnp.float32)
+            whole_ref[far + row, steps + 1:] = jnp.zeros((slots - steps - 1, cols), jnp.float32)
     for row in range(rows):
         whole_ref[HALO + row] = field_ref[row]
     lane = lane_index()
@@ -347,7 +372,7 @@
     return kernel
 
 
-def last_mix_kernel(acc_ref, corr_ref, field_ref, gram_ref, steps_ref, grads_ref, out_ref, message_ref, turn_ref, rows_ref):
+def last_mix_kernel(acc_ref, corr_ref, field_ref, cross_ref, square_ref, steps_ref, grads_ref, out_ref, message_ref, turn_ref, rows_ref):
     _, steps, rows, cols = steps_ref.shape
     slots = turn_ref.shape[0] // (rows * (cols // LANE))
     for row in range(rows):
@@ -378,7 +403,8 @@
         return tuple(sums)
 
     sums = lax.fori_loop(0, steps, body, (zero,) * NPROJ, unroll=2)
-    rows_ref[0:NGRAM, :] = gram_ref[...]
+    rows_ref[0:NSYM, :] = cross_ref[...]
+    rows_ref[NSYM:NGRAM, :] = square_ref[...]
     for n in range(NPROJ):
         rows_ref[NGRAM + n:NGRAM + n + 1, :] = jnp.sum(sums[n], axis=0, keepdims=True)
     lane, row = lane_index(), row_index()
@@ -472,7 +498,7 @@
 
     field, to_swap, to_next = call(
         pack_kernel,
-        (f32(rows, slots, cols), f32(HALO, slots, cols), f32(HALO, slots, cols)),
+        (f32(rows, slots, cols), f32(message_rows(steps), cols), f32(message_rows(steps), cols)),
         [pltpu.with_memory_space_constraint(v, pltpu.HBM) for v in (gradient, land_mask, diffusivity)],
         specs=[HBM] * 3,
         scratch=[
@@ -484,11 +510,11 @@
     from_swap = lax.ppermute(to_swap, "lat", even)
     from_next = lax.ppermute(to_next, "lat", odd)
     pair_shape = jax.ShapeDtypeStruct(pair_steps.shape, jnp.bfloat16)
-    gram, pair_steps, pair_grads = call(
-        gram_kernel, (f32(NGRAM, LANE), pair_shape, pair_shape),
+    cross, pair_steps, pair_grads = call(
+        cross_kernel, (f32(NSYM, LANE), pair_shape, pair_shape),
         [pltpu.with_memory_space_constraint(v, pltpu.HBM) for v in (pair_steps, pair_grads)], specs=[HBM] * 2,
         scratch=[pltpu.SemaphoreType.DMA((2, 4))],
-        name="gram",
+        name="cross",
     )
     tall, wide = rows + 2 * HALO, cols + LANE
     parts = groups_of(steps)
@@ -500,7 +526,7 @@
     )
     side_shape = f32(slots, -(-tall // PER) * LANE)
     whole, to_pair, to_beside = call(
-        side_kernel, (f32(tall, slots, cols), side_shape, side_shape), (from_swap, field, from_next, gram), name="sides"
+        functools.partial(side_kernel, steps=steps), (f32(tall, slots, cols), side_shape, side_shape), (from_swap, field, from_next, cross), name="sides"
     )
     from_beside = lax.ppermute(to_beside, "lon", odds)
     from_pair = lax.ppermute(to_pair, "lon", evens)
@@ -522,12 +548,13 @@
             pairs = [(i, (i + shift) % groups) for i in range(groups)]
             other.append(lax.ppermute(part, "tm", pairs))
     mixed = call(make_mix(True), f32(rows, steps, cols), (own_corr, *own), name="mix_own")
+    square = call(square_kernel, f32(NSYM, LANE), (pair_grads, mixed), name="square")
     for corr, part in zip(corrs[:-1], other[:-1]):
         mixed = call(make_mix(False), f32(rows, steps, cols), (mixed, corr, part), name="mix_more")
     devices = height * breadth * groups
     mixed, message = call(
         last_mix_kernel, (f32(steps, rows, cols), f32(devices, 1, LANE)),
-        (mixed, corrs[-1], other[-1], gram, pair_steps, pair_grads),
+        (mixed, corrs[-1], other[-1], cross, square, pair_steps, pair_grads),
         scratch=[turn, pltpu.VMEM((NROW, LANE), jnp.float32)], name="mix_last",
     )
     inbox = lax.all_to_all(

time: 46 us -> 45.6 us (level)
  waiting for transfers between devices: 5.16 us -> 4.21 us
  blocking collectives: 14.6 us -> 15.1 us
    ppermute x4, waiting for transfers between devices: 3.38 us -> 1.78 us  [local(): other.append(lax.ppermute(part, 'tm', pairs))]
    ppermute x1, waiting for transfers between devices: 0.01 us -> 0.82 us  [local(): from_swap = lax.ppermute(to_swap, 'lat', even)]
    pallas_call x15 -> x16, Pallas kernels: 16 us -> 16.1 us  [call(): pl.pallas_call(kernel, out_shape=outs, in_specs=specs or [VMEM] * len(arg...]
  transfers between devices with their start and end apart: 8 -> 8, of which waited for: 4 -> 4; matrix products, arithmetic and copies ran while one was open for 0% -> 0% of each run, Pallas kernels for 21% -> 22%
where the time goes in v10:
time: 45.6 us; the launch traced here: 45.4 us
  Pallas kernels  16.1 us (35%)
  blocking collectives  15.1 us (33%)
  starting transfers between devices  9.93 us (22%)
  waiting for transfers between devices  4.21 us (9%)
    pallas_call x16, Pallas kernels, call(): pl.pallas_call(kernel, out_shape=outs, in_specs=specs or [VMEM] * len(arg...  16.1 us
    all_to_all x1, blocking collectives, local(): lax.all_to_all(message, ('lat', 'lon', 'tm'), split_axis=0, concat_axis=0...  15.1 us
    ppermute x4, starting transfers between devices, local(): other.append(lax.ppermute(part, 'tm', pairs))  4.31 us
    ppermute x1, starting transfers between devices, local(): from_swap = lax.ppermute(to_swap, 'lat', even)  3.09 us
    ppermute x1, starting transfers between devices, local(): from_beside = lax.ppermute(to_beside, 'lon', odds)  1.8 us
    ppermute x4, waiting for transfers between devices, local(): other.append(lax.ppermute(part, 'tm', pairs))  1.78 us
    ppermute x1, waiting for transfers between devices, local(): from_beside = lax.ppermute(to_beside, 'lon', odds)  1.6 us
  transfers between devices with their start and end apart: 8, of which 4 were waited for; matrix products, arithmetic and copies ran while one was open for 0% of the time, Pallas kernels for 22%

profile of v10, /device:TPU:0, one launch (start us, length us, event | category | flops | bytes accessed | tf_op | source)
XLA Modules:
  0.0 45.4 jit_solution(1093499533562169499)
XLA Ops:
  0.0 1.3 %pack.1 = (f32[16,32,256]{2,1,0:T(8,128)S(1)}, f32[176,256]{1,0:T(8,128)S(1)}, f32[176,256]{1,0:T(8,128)S(1)}) custom-call(f32[28,16,256]{2,1,0:T(8,128)} %grad_hbm.1, s32[16,256]{1,0:T(8,128)} %mask_hbm.1, f32[16,256]{1,0:T(8,128)} %diff_hbm.1), custom_call_target="tpu_custom_call" | custom-call | tf_op jit(solution)/shard_map/pack/pallas_call | solution.py:34
  1.3 3.1 %collective-permute-start = (f32[176,256]{1,0:T(8,128)S(1)}, f32[176,256]{1,0:T(8,128)S(1)}, u32[]{:S(2)}, u32[]{:S(2)}) collective-permute-start(f32[176,256]{1,0:T(8,128)S(1)} %get-tuple-element.28), channel_id=1, source_target_pairs={{0,8},{8,0},{16,24},{24,16},{1,9},{9,1},{17,25},{25,17},{2,10},{10... | collective-permute-start | bytes 540680 | tf_op jit(solution)/shard_map/ppermute | solution.py:510
  4.4 0.7 %collective-permute-start.1 = (f32[176,256]{1,0:T(8,128)S(1)}, f32[176,256]{1,0:T(8,128)S(1)}, u32[]{:S(2)}, u32[]{:S(2)}) collective-permute-start(f32[176,256]{1,0:T(8,128)S(1)} %get-tuple-element.30), channel_id=1, source_target_pairs={{0,0},{8,16},{16,8},{24,24},{1,1},{9,17},{17,9},{25,25},{2,2},{10,... | collective-permute-start | bytes 540680 | tf_op jit(solution)/shard_map/ppermute | solution.py:511
  5.0 3.1 %cross.1 = (f32[36,128]{1,0:T(8,128)S(1)}, bf16[8,28,16,256]{3,2,1,0:T(8,128)(2,1)S(1)}, bf16[8,28,16,256]{3,2,1,0:T(8,128)(2,1)S(1)}) custom-call(bf16[8,28,16,256]{3,2,1,0:T(8,128)(2,1)} %steps_hbm.1, bf16[8,28,16,256]{3,2,1,0:T(8,128)(2,1)} %grads_hbm.1), custom_call_target="tpu_custom_call" | custom-call | tf_op jit(solution)/shard_map/cross/pallas_call | solution.py:34
  8.1 0.8 %collective-permute-done.swap_ref = f32[176,256]{1,0:T(8,128)S(1)} collective-permute-done((f32[176,256]{1,0:T(8,128)S(1)}, f32[176,256]{1,0:T(8,128)S(1)}, u32[]{:S(2)}, u32[]{:S(2)}) %collective-permute-start) | collective-permute-done | bytes 180256 | tf_op jit(solution)/shard_map/ppermute | solution.py:510
  8.9 0.3 sides.1
  9.3 1.8 %collective-permute-start.3 = (f32[32,256]{1,0:T(8,128)S(1)}, f32[32,256]{1,0:T(8,128)S(1)}, u32[]{:S(2)}, u32[]{:S(2)}) collective-permute-start(f32[32,256]{1,0:T(8,128)S(1)} %get-tuple-element.34), channel_id=1, source_target_pairs={{0,6},{2,4},{4,2},{6,0},{1,7},{3,5},{5,3},{7,1},{8,14},{10,12},{12... | collective-permute-start | bytes 98312 | tf_op jit(solution)/shard_map/ppermute | solution.py:531
  11.1 1.6 %collective-permute-done.3.beside_ref = f32[32,256]{1,0:T(8,128)S(1)} collective-permute-done((f32[32,256]{1,0:T(8,128)S(1)}, f32[32,256]{1,0:T(8,128)S(1)}, u32[]{:S(2)}, u32[]{:S(2)}) %collective-permute-start.3) | collective-permute-done | bytes 32800 | tf_op jit(solution)/shard_map/ppermute | solution.py:531
  12.7 0.3 weights.1
  13.1 1.3 %sweeps.4.refs_1_ = f32[16,8,256]{2,1,0:T(8,128)S(1)} custom-call(f32[28,32,256]{2,1,0:T(8,128)S(1)} %get-tuple-element.32.whole_ref, f32[32,256]{1,0:T(8,128)S(1)} %get-tuple-element.35.left_ref, f32[32,256]{1,0:T(8,128)S(1)} %get-tuple-element.36.right_ref, f32[29,8,384]{2,1,0:T(8,128)S(1)} %get-tuple-element.37.south_ref, ...), custom_call_target="tpu_custom_call" | custom-call | tf_op jit(solution)/shard_map/sweeps/pallas_call | solution.py:34
  14.4 1.7 %collective-permute-start.4 = (f32[16,8,256]{2,1,0:T(8,128)S(1)}, f32[16,8,256]{2,1,0:T(8,128)S(1)}, u32[]{:S(2)}, u32[]{:S(2)}) collective-permute-start(f32[16,8,256]{2,1,0:T(8,128)S(1)} %sweeps.4.refs_1_), channel_id=1, source_target_pairs={{0,1},{1,0},{2,3},{3,2},{4,5},{5,4},{6,7},{7,6},{8,9},{9,8},{10,11... | collective-permute-start | bytes 393224 | tf_op jit(solution)/shard_map/ppermute | solution.py:549
  16.2 1.3 %sweeps.5.refs_2_ = f32[16,8,256]{2,1,0:T(8,128)S(1)} custom-call(f32[28,32,256]{2,1,0:T(8,128)S(1)} %get-tuple-element.32.whole_ref, f32[32,256]{1,0:T(8,128)S(1)} %get-tuple-element.35.left_ref, f32[32,256]{1,0:T(8,128)S(1)} %get-tuple-element.36.right_ref, f32[29,8,384]{2,1,0:T(8,128)S(1)} %get-tuple-element.37.south_ref, ...), custom_call_target="tpu_custom_call" | custom-call | tf_op jit(solution)/shard_map/sweeps/pallas_call | solution.py:34
  17.5 0.4 collective-permute-start.5
  18.0 1.3 %sweeps.6.refs_3_ = f32[16,8,256]{2,1,0:T(8,128)S(1)} custom-call(f32[28,32,256]{2,1,0:T(8,128)S(1)} %get-tuple-element.32.whole_ref, f32[32,256]{1,0:T(8,128)S(1)} %get-tuple-element.35.left_ref, f32[32,256]{1,0:T(8,128)S(1)} %get-tuple-element.36.right_ref, f32[29,8,384]{2,1,0:T(8,128)S(1)} %get-tuple-element.37.south_ref, ...), custom_call_target="tpu_custom_call" | custom-call | tf_op jit(solution)/shard_map/sweeps/pallas_call | solution.py:34
  19.3 1.7 %collective-permute-start.6 = (f32[16,8,256]{2,1,0:T(8,128)S(1)}, f32[16,8,256]{2,1,0:T(8,128)S(1)}, u32[]{:S(2)}, u32[]{:S(2)}) collective-permute-start(f32[16,8,256]{2,1,0:T(8,128)S(1)} %sweeps.6.refs_3_), channel_id=1, source_target_pairs={{0,1},{1,0},{2,3},{3,2},{4,5},{5,4},{6,7},{7,6},{8,9},{9,8},{10,11... | collective-permute-start | bytes 393224 | tf_op jit(solution)/shard_map/ppermute | solution.py:549
  21.0 1.3 %sweeps.7.refs_4_ = f32[16,4,256]{2,1,0:T(4,128)S(1)} custom-call(f32[28,32,256]{2,1,0:T(8,128)S(1)} %get-tuple-element.32.whole_ref, f32[32,256]{1,0:T(8,128)S(1)} %get-tuple-element.35.left_ref, f32[32,256]{1,0:T(8,128)S(1)} %get-tuple-element.36.right_ref, f32[29,8,384]{2,1,0:T(8,128)S(1)} %get-tuple-element.37.south_ref, ...), custom_call_target="tpu_custom_call" | custom-call | tf_op jit(solution)/shard_map/sweeps/pallas_call | solution.py:34
  22.4 0.4 collective-permute-start.7
  22.9 0.4 mix_own.1.refs_0_.order_ref
  23.3 1.6 %square.1.square_ref = f32[36,128]{1,0:T(8,128)S(1)} custom-call(bf16[8,28,16,256]{3,2,1,0:T(8,128)(2,1)S(1)} %get-tuple-element.45.grads_ref, f32[16,28,256]{2,1,0:T(8,128)S(1)} %mix_own.1.refs_0_.order_ref), custom_call_target="tpu_custom_call" | custom-call | tf_op jit(solution)/shard_map/square/pallas_call | solution.py:34
  25.4 1.3 %collective-permute-done.6.refs_2_ = f32[16,8,256]{2,1,0:T(8,128)S(1)} collective-permute-done((f32[16,8,256]{2,1,0:T(8,128)S(1)}, f32[16,8,256]{2,1,0:T(8,128)S(1)}, u32[]{:S(2)}, u32[]{:S(2)}) %collective-permute-start.6) | collective-permute-done | bytes 131104 | tf_op jit(solution)/shard_map/ppermute | solution.py:549
  26.9 0.5 %collective-permute-done.7.field_ref = f32[16,4,256]{2,1,0:T(4,128)S(1)} collective-permute-done((f32[16,4,256]{2,1,0:T(4,128)S(1)}, f32[16,4,256]{2,1,0:T(4,128)S(1)}, u32[]{:S(2)}, u32[]{:S(2)}) %collective-permute-start.7) | collective-permute-done | bytes 65568 | tf_op jit(solution)/shard_map/ppermute | solution.py:549
  27.4 1.2 %mix_last.1 = (f32[28,16,256]{2,1,0:T(8,128)S(1)}, f32[32,1,128]{2,1,0:T(1,128)S(1)}) custom-call(f32[16,28,256]{2,1,0:T(8,128)S(1)} %mix_more.5.acc_ref, bf16[28,48]{1,0:T(8,128)(2,1)S(1)} %get-tuple-element.44.corr_ref, f32[16,4,256]{2,1,0:T(4,128)S(1)} %collective-permute-done.7.field_ref, f32[36,128]{1,0:T(8,128)S(1)} %get-tuple-element.31.order_ref.cross_ref, ...), custom_call_target="tpu_custom_call" | custom-call | tf_op jit(solution)/shard_map/mix_last/pallas_call | solution.py:34
  28.6 15.1 %all_to_all.5.inbox_ref = f32[32,1,128]{2,1,0:T(1,128)S(1)} all-to-all(f32[32,1,128]{2,1,0:T(1,128)S(1)} %get-tuple-element.47), channel_id=1, replica_groups={{31,30,29,28,27,26,25,24,23,22,21,20,19,18,17,16,15,14,13,12,11,10,9,8,..., dimensions={0} | all-to-all | bytes 32768 | tf_op jit(solution)/shard_map/all_to_all | solution.py:560
  43.6 1.7 %final.1 = f32[28,16,256]{2,1,0:T(8,128)} custom-call(f32[32,1,128]{2,1,0:T(1,128)S(1)} %all_to_all.5.inbox_ref, f32[28,16,256]{2,1,0:T(8,128)S(1)} %get-tuple-element.48.mixed_ref, f32[28,16,256]{2,1,0:T(8,128)S(1)} %copy-done, bf16[8,28,16,256]{3,2,1,0:T(8,128)(2,1)S(1)} %get-tuple-element.46.steps_ref, ...), custom_call_target="tpu_custom_call" | custom-call | tf_op jit(solution)/shard_map/final/pallas_call | solution.py:34
  (13 shorter events, 0.8 us)
Async XLA Ops:
  1.3 7.6 %collective-permute-start = (f32[176,256]{1,0:T(8,128)S(1)}, f32[176,256]{1,0:T(8,128)S(1)}, u32[]{:S(2)}, u32[]{:S(2)}) collective-permute-start(f32[176,256]{1,0:T(8,128)S(1)} %get-tuple-element.28), channel_id=1, source_target_pairs={{0,8},{8,0},{16,24},{24,16},{1,9},{9,1},{17,25},{25,17},{2,10},{10... | collective-permute-start | bytes 540680 | tf_op jit(solution)/shard_map/ppermute | solution.py:510
  4.4 4.6 %collective-permute-start.1 = (f32[176,256]{1,0:T(8,128)S(1)}, f32[176,256]{1,0:T(8,128)S(1)}, u32[]{:S(2)}, u32[]{:S(2)}) collective-permute-start(f32[176,256]{1,0:T(8,128)S(1)} %get-tuple-element.30), channel_id=1, source_target_pairs={{0,0},{8,16},{16,8},{24,24},{1,1},{9,17},{17,9},{25,25},{2,2},{10,... | collective-permute-start | bytes 540680 | tf_op jit(solution)/shard_map/ppermute | solution.py:511
  9.3 1.9 %collective-permute-start.2 = (f32[32,256]{1,0:T(8,128)S(1)}, f32[32,256]{1,0:T(8,128)S(1)}, u32[]{:S(2)}, u32[]{:S(2)}) collective-permute-start(f32[32,256]{1,0:T(8,128)S(1)} %get-tuple-element.33), channel_id=1, source_target_pairs={{0,2},{2,0},{4,6},{6,4},{1,3},{3,1},{5,7},{7,5},{8,10},{10,8},{12,... | collective-permute-start | bytes 98312 | tf_op jit(solution)/shard_map/ppermute | solution.py:532
  9.3 3.4 %collective-permute-start.3 = (f32[32,256]{1,0:T(8,128)S(1)}, f32[32,256]{1,0:T(8,128)S(1)}, u32[]{:S(2)}, u32[]{:S(2)}) collective-permute-start(f32[32,256]{1,0:T(8,128)S(1)} %get-tuple-element.34), channel_id=1, source_target_pairs={{0,6},{2,4},{4,2},{6,0},{1,7},{3,5},{5,3},{7,1},{8,14},{10,12},{12... | collective-permute-start | bytes 98312 | tf_op jit(solution)/shard_map/ppermute | solution.py:531
  14.4 10.5 %collective-permute-start.4 = (f32[16,8,256]{2,1,0:T(8,128)S(1)}, f32[16,8,256]{2,1,0:T(8,128)S(1)}, u32[]{:S(2)}, u32[]{:S(2)}) collective-permute-start(f32[16,8,256]{2,1,0:T(8,128)S(1)} %sweeps.4.refs_1_), channel_id=1, source_target_pairs={{0,1},{1,0},{2,3},{3,2},{4,5},{5,4},{6,7},{7,6},{8,9},{9,8},{10,11... | collective-permute-start | bytes 393224 | tf_op jit(solution)/shard_map/ppermute | solution.py:549
  17.5 7.6 %collective-permute-start.5 = (f32[16,8,256]{2,1,0:T(8,128)S(1)}, f32[16,8,256]{2,1,0:T(8,128)S(1)}, u32[]{:S(2)}, u32[]{:S(2)}) collective-permute-start(f32[16,8,256]{2,1,0:T(8,128)S(1)} %sweeps.5.refs_2_), channel_id=1, source_target_pairs={{0,1},{1,0},{2,3},{3,2},{4,5},{5,4},{6,7},{7,6},{8,9},{9,8},{10,11... | collective-permute-start | bytes 393224 | tf_op jit(solution)/shard_map/ppermute | solution.py:549
  19.3 3.5 %copy-start.1 = (f32[56,56]{1,0:T(8,128)S(1)}, f32[56,56]{1,0:T(8,128)}, u32[]{:S(2)}) copy-start(f32[56,56]{1,0:T(8,128)} %corr_ref.1) | copy-start | bytes 37636
  19.3 7.4 %collective-permute-start.6 = (f32[16,8,256]{2,1,0:T(8,128)S(1)}, f32[16,8,256]{2,1,0:T(8,128)S(1)}, u32[]{:S(2)}, u32[]{:S(2)}) collective-permute-start(f32[16,8,256]{2,1,0:T(8,128)S(1)} %sweeps.6.refs_3_), channel_id=1, source_target_pairs={{0,1},{1,0},{2,3},{3,2},{4,5},{5,4},{6,7},{7,6},{8,9},{9,8},{10,11... | collective-permute-start | bytes 393224 | tf_op jit(solution)/shard_map/ppermute | solution.py:549
  22.4 5.0 %collective-permute-start.7 = (f32[16,4,256]{2,1,0:T(4,128)S(1)}, f32[16,4,256]{2,1,0:T(4,128)S(1)}, u32[]{:S(2)}, u32[]{:S(2)}) collective-permute-start(f32[16,4,256]{2,1,0:T(4,128)S(1)} %sweeps.7.refs_4_), channel_id=1, source_target_pairs={{0,1},{1,0},{2,3},{3,2},{4,5},{5,4},{6,7},{7,6},{8,9},{9,8},{10,11... | collective-permute-start | bytes 196616 | tf_op jit(solution)/shard_map/ppermute | solution.py:549
  27.4 16.3 %copy-start = (f32[28,16,256]{2,1,0:T(8,128)S(1)}, f32[28,16,256]{2,1,0:T(8,128)}, u32[]{:S(2)}) copy-start(f32[28,16,256]{2,1,0:T(8,128)} %control_ref.1) | copy-start | bytes 1376260

commit v11 on v10

--- a/solution.py
+++ b/solution.py
@@ -127,7 +127,7 @@
     return parts
 
 
-def pack_kernel(grad_hbm, mask_hbm, diff_hbm, field_ref, swap_ref, next_ref, grad_ref, mask_ref, diff_ref, turn_ref, sems):
+def pack_kernel(grad_hbm, mask_hbm, diff_hbm, field_ref, swap_ref, grad_ref, mask_ref, diff_ref, turn_ref, sems):
     steps, rows, cols = grad_ref.shape
     slots = field_ref.shape[1]
     pieces = [(begin, min(SUB, steps - begin)) for begin in range(0, steps, SUB)]
@@ -162,14 +162,20 @@
                 value = turn_ref[pl.ds(base + slot * SUB, SUB, stride=SUB), :]
                 field_ref[row, slot:slot + SUB, across] = value
     odd = lax.rem(lax.axis_index("lat"), 2)
-    near, far = (1 - odd) * (rows - HALO), odd * (rows - HALO)
+    near = (1 - odd) * (rows - HALO)
     for row in range(HALO):
         for place, there in message_parts(row, steps):
             swap_ref[place] = field_ref[near + row, there]
+
+
+def next_kernel(field_ref, next_ref, *, steps):
+    far = lax.rem(lax.axis_index("lat"), 2) * (field_ref.shape[0] - HALO)
+    for row in range(HALO):
+        for place, there in message_parts(row, steps):
             next_ref[place] = field_ref[far + row, there]
 
 
-def side_kernel(swap_ref, field_ref, next_ref, order_ref, whole_ref, pair_ref, beside_ref, *, steps):
+def side_kernel(next_ref, field_ref, swap_ref, order_ref, whole_ref, pair_ref, beside_ref, *, steps):
     rows, slots, cols = field_ref.shape
     place, count = lax.axis_index("lat"), lax.axis_size("lat")
     odd = lax.rem(place, 2)
@@ -267,7 +273,7 @@
         south_ref[height - 1 + side] = jnp.broadcast_to(inside, south_ref.shape[1:])
 
 
-def sweep_kernel(whole_ref, left_ref, right_ref, south_ref, east_ref, west_ref, keep_ref, out_ref, *, begin):
+def sweep_kernel(whole_ref, left_ref, right_ref, south_ref, east_ref, west_ref, keep_ref, out_ref, mid_ref, *, begin):
     height, _, cols = whole_ref.shape
     rows, width = height - 2 * HALO, cols // LANE + 1
     count = out_ref.shape[1]
@@ -301,22 +307,28 @@
             fresh.append(at(keep_ref, row - 1, c) * centre[c] + across + change)
         return fresh
 
-    waiting = [None] * (SWEEPS + 1)
-    for tick in range(height + SWEEPS + 1):
-        if waiting[SWEEPS] is not None:
-            row, tiles = waiting[SWEEPS]
-            for c in range(width - 1):
-                out_ref[row - HALO, :, c * LANE:(c + 1) * LANE] = tiles[c][:count]
-        for sweep in reversed(range(SWEEPS)):
-            if sweep == 0:
-                entry = (tick, load(tick, slice(begin, begin + SUB))) if tick < height else None
-            else:
+    half = SWEEPS // 2
+    for start, stop in ((0, half), (half, SWEEPS)):
+        waiting = [None] * (stop + 1)
+        for tick in range(start, height - start + stop - start + 1):
+            if waiting[stop] is not None:
+                row, tiles = waiting[stop]
+                for c in range(width - 1 if stop == SWEEPS else width):
+                    if stop == SWEEPS:
+                        out_ref[row - HALO, :, c * LANE:(c + 1) * LANE] = tiles[c][:count]
+                    else:
+                        mid_ref[row, :, c * LANE:(c + 1) * LANE] = tiles[c]
+            for sweep in reversed(range(start, stop)):
                 entry = waiting[sweep]
-            waiting[sweep + 1] = None
-            if entry is not None:
-                fresh = advance(sweep, *entry)
-                if fresh is not None:
-                    waiting[sweep + 1] = (entry[0] - 1, fresh)
+                if sweep == start:
+                    entry = None
+                    if tick < height - start:
+                        entry = (tick, [at(mid_ref, tick, c) for c in range(width)] if start else load(tick, slice(begin, begin + SUB)))
+                waiting[sweep + 1] = None
+                if entry is not None:
+                    fresh = advance(sweep, *entry)
+                    if fresh is not None:
+                        waiting[sweep + 1] = (entry[0] - 1, fresh)
 
 
 def split_stack(value):
@@ -496,9 +508,9 @@
     slots = slots_of(steps)
     turn = pltpu.VMEM((rows * (cols // LANE) * slots, LANE), jnp.float32)
 
-    field, to_swap, to_next = call(
+    field, to_swap = call(
         pack_kernel,
-        (f32(rows, slots, cols), f32(message_rows(steps), cols), f32(message_rows(steps), cols)),
+        (f32(rows, slots, cols), f32(message_rows(steps), cols)),
         [pltpu.with_memory_space_constraint(v, pltpu.HBM) for v in (gradient, land_mask, diffusivity)],
         specs=[HBM] * 3,
         scratch=[
@@ -507,8 +519,9 @@
         ],
         name="pack",
     )
+    to_next = call(functools.partial(next_kernel, steps=steps), f32(message_rows(steps), cols), (field,), name="next")
+    from_next = lax.ppermute(to_next, "lat", odd)
     from_swap = lax.ppermute(to_swap, "lat", even)
-    from_next = lax.ppermute(to_next, "lat", odd)
     pair_shape = jax.ShapeDtypeStruct(pair_steps.shape, jnp.bfloat16)
     cross, pair_steps, pair_grads = call(
         cross_kernel, (f32(NSYM, LANE), pair_shape, pair_shape),
@@ -526,7 +539,7 @@
     )
     side_shape = f32(slots, -(-tall // PER) * LANE)
     whole, to_pair, to_beside = call(
-        functools.partial(side_kernel, steps=steps), (f32(tall, slots, cols), side_shape, side_shape), (from_swap, field, from_next, cross), name="sides"
+        functools.partial(side_kernel, steps=steps), (f32(tall, slots, cols), side_shape, side_shape), (from_next, field, from_swap, cross), name="sides"
     )
     from_beside = lax.ppermute(to_beside, "lon", odds)
     from_pair = lax.ppermute(to_pair, "lon", evens)
@@ -541,7 +554,8 @@
     own, other = [], []
     for begin, count in parts:
         part = call(
-            functools.partial(sweep_kernel, begin=begin), f32(rows, count, cols), (*extended, *weights), name="sweeps"
+            functools.partial(sweep_kernel, begin=begin), f32(rows, count, cols), (*extended, *weights),
+            scratch=[pltpu.VMEM((tall, SUB, wide), jnp.float32)], name="sweeps",
         )
         own.append(part)
         for shift in range(1, groups):

time: 45.6 us -> 45.2 us (level)
  blocking collectives: 15.1 us -> 10.2 us
  starting transfers between devices: 9.93 us -> 12.6 us
  Pallas kernels: 16.1 us -> 18.1 us
    all_to_all x1, blocking collectives: 15.1 us -> 10.2 us  [local(): lax.all_to_all(message, ('lat', 'lon', 'tm'), split_axis=0, concat_axis=0...]
    ppermute x1, starting transfers between devices: 3.09 us -> 5.9 us  [local(): from_swap = lax.ppermute(to_swap, 'lat', even)]
    pallas_call x16 -> x17, Pallas kernels: 16.1 us -> 18.1 us  [call(): pl.pallas_call(kernel, out_shape=outs, in_specs=specs or [VMEM] * len(arg...]
    ppermute x4, waiting for transfers between devices: 1.78 us -> 0.94 us  [local(): other.append(lax.ppermute(part, 'tm', pairs))]
  transfers between devices with their start and end apart: 8 -> 8, of which waited for: 4 -> 3; matrix products, arithmetic and copies ran while one was open for 0% -> 0% of each run, Pallas kernels for 22% -> 25%
where the time goes in v11:
time: 45.2 us; the launch traced here: 44.9 us
  Pallas kernels  18.1 us (40%)
  starting transfers between devices  12.6 us (28%)
  blocking collectives  10.2 us (23%)
  waiting for transfers between devices  3.91 us (9%)
    pallas_call x17, Pallas kernels, call(): pl.pallas_call(kernel, out_shape=outs, in_specs=specs or [VMEM] * len(arg...  18.1 us
    all_to_all x1, blocking collectives, local(): lax.all_to_all(message, ('lat', 'lon', 'tm'), split_axis=0, concat_axis=0...  10.2 us
    ppermute x1, starting transfers between devices, local(): from_swap = lax.ppermute(to_swap, 'lat', even)  5.9 us
    ppermute x4, starting transfers between devices, local(): other.append(lax.ppermute(part, 'tm', pairs))  4.31 us
    ppermute x1, waiting for transfers between devices, local(): from_beside = lax.ppermute(to_beside, 'lon', odds)  1.77 us
    ppermute x1, starting transfers between devices, local(): from_beside = lax.ppermute(to_beside, 'lon', odds)  1.64 us
    ppermute x1, waiting for transfers between devices, local(): from_swap = lax.ppermute(to_swap, 'lat', even)  1.2 us
    ppermute x4, waiting for transfers between devices, local(): other.append(lax.ppermute(part, 'tm', pairs))  0.94 us
  transfers between devices with their start and end apart: 8, of which 3 were waited for; matrix products, arithmetic and copies ran while one was open for 0% of the time, Pallas kernels for 25%

profile of v11, /device:TPU:0, one launch (start us, length us, event | category | flops | bytes accessed | tf_op | source)
XLA Modules:
  0.0 44.9 jit_solution(18326136814815632292)
XLA Ops:
  0.0 1.2 %pack.1 = (f32[16,32,256]{2,1,0:T(8,128)S(1)}, f32[176,256]{1,0:T(8,128)S(1)}) custom-call(f32[28,16,256]{2,1,0:T(8,128)} %grad_hbm.1, s32[16,256]{1,0:T(8,128)} %mask_hbm.1, f32[16,256]{1,0:T(8,128)} %diff_hbm.1), custom_call_target="tpu_custom_call" | custom-call | tf_op jit(solution)/shard_map/pack/pallas_call | solution.py:34
  1.3 0.7 %collective-permute-start = (f32[176,256]{1,0:T(8,128)S(1)}, f32[176,256]{1,0:T(8,128)S(1)}, u32[]{:S(2)}, u32[]{:S(2)}) collective-permute-start(f32[176,256]{1,0:T(8,128)S(1)} %next.1), channel_id=1, source_target_pairs={{0,0},{8,16},{16,8},{24,24},{1,1},{9,17},{17,9},{25,25},{2,2},{10,... | collective-permute-start | bytes 540680 | tf_op jit(solution)/shard_map/ppermute | solution.py:523
  2.0 5.9 %collective-permute-start.1 = (f32[176,256]{1,0:T(8,128)S(1)}, f32[176,256]{1,0:T(8,128)S(1)}, u32[]{:S(2)}, u32[]{:S(2)}) collective-permute-start(f32[176,256]{1,0:T(8,128)S(1)} %get-tuple-element.28), channel_id=1, source_target_pairs={{0,8},{8,0},{16,24},{24,16},{1,9},{9,1},{17,25},{25,17},{2,10},{10... | collective-permute-start | bytes 540680 | tf_op jit(solution)/shard_map/ppermute | solution.py:524
  7.9 3.0 %cross.1 = (f32[36,128]{1,0:T(8,128)S(1)}, bf16[8,28,16,256]{3,2,1,0:T(8,128)(2,1)S(1)}, bf16[8,28,16,256]{3,2,1,0:T(8,128)(2,1)S(1)}) custom-call(bf16[8,28,16,256]{3,2,1,0:T(8,128)(2,1)} %steps_hbm.1, bf16[8,28,16,256]{3,2,1,0:T(8,128)(2,1)} %grads_hbm.1), custom_call_target="tpu_custom_call" | custom-call | tf_op jit(solution)/shard_map/cross/pallas_call | solution.py:34
  10.9 1.2 %collective-permute-done.1.swap_ref = f32[176,256]{1,0:T(8,128)S(1)} collective-permute-done((f32[176,256]{1,0:T(8,128)S(1)}, f32[176,256]{1,0:T(8,128)S(1)}, u32[]{:S(2)}, u32[]{:S(2)}) %collective-permute-start.1) | collective-permute-done | bytes 180256 | tf_op jit(solution)/shard_map/ppermute | solution.py:524
  12.1 0.3 sides.1
  12.6 1.6 %collective-permute-start.3 = (f32[32,256]{1,0:T(8,128)S(1)}, f32[32,256]{1,0:T(8,128)S(1)}, u32[]{:S(2)}, u32[]{:S(2)}) collective-permute-start(f32[32,256]{1,0:T(8,128)S(1)} %get-tuple-element.32), channel_id=1, source_target_pairs={{0,6},{2,4},{4,2},{6,0},{1,7},{3,5},{5,3},{7,1},{8,14},{10,12},{12... | collective-permute-start | bytes 98312 | tf_op jit(solution)/shard_map/ppermute | solution.py:544
  14.2 1.8 %collective-permute-done.3.beside_ref = f32[32,256]{1,0:T(8,128)S(1)} collective-permute-done((f32[32,256]{1,0:T(8,128)S(1)}, f32[32,256]{1,0:T(8,128)S(1)}, u32[]{:S(2)}, u32[]{:S(2)}) %collective-permute-start.3) | collective-permute-done | bytes 32800 | tf_op jit(solution)/shard_map/ppermute | solution.py:544
  16.0 0.3 weights.1
  16.3 1.9 %sweeps.4.refs_1_ = f32[16,8,256]{2,1,0:T(8,128)S(1)} custom-call(f32[28,32,256]{2,1,0:T(8,128)S(1)} %get-tuple-element.30.whole_ref, f32[32,256]{1,0:T(8,128)S(1)} %get-tuple-element.33.left_ref, f32[32,256]{1,0:T(8,128)S(1)} %get-tuple-element.34.right_ref, f32[29,8,384]{2,1,0:T(8,128)S(1)} %get-tuple-element.35.south_ref, ...), custom_call_target="tpu_custom_call" | custom-call | tf_op jit(solution)/shard_map/sweeps/pallas_call | solution.py:34
  18.2 1.6 %collective-permute-start.4 = (f32[16,8,256]{2,1,0:T(8,128)S(1)}, f32[16,8,256]{2,1,0:T(8,128)S(1)}, u32[]{:S(2)}, u32[]{:S(2)}) collective-permute-start(f32[16,8,256]{2,1,0:T(8,128)S(1)} %sweeps.4.refs_1_), channel_id=1, source_target_pairs={{0,1},{1,0},{2,3},{3,2},{4,5},{5,4},{6,7},{7,6},{8,9},{9,8},{10,11... | collective-permute-start | bytes 393224 | tf_op jit(solution)/shard_map/ppermute | solution.py:563
  19.7 1.9 %sweeps.5.refs_2_ = f32[16,8,256]{2,1,0:T(8,128)S(1)} custom-call(f32[28,32,256]{2,1,0:T(8,128)S(1)} %get-tuple-element.30.whole_ref, f32[32,256]{1,0:T(8,128)S(1)} %get-tuple-element.33.left_ref, f32[32,256]{1,0:T(8,128)S(1)} %get-tuple-element.34.right_ref, f32[29,8,384]{2,1,0:T(8,128)S(1)} %get-tuple-element.35.south_ref, ...), custom_call_target="tpu_custom_call" | custom-call | tf_op jit(solution)/shard_map/sweeps/pallas_call | solution.py:34
  21.6 0.6 %collective-permute-start.5 = (f32[16,8,256]{2,1,0:T(8,128)S(1)}, f32[16,8,256]{2,1,0:T(8,128)S(1)}, u32[]{:S(2)}, u32[]{:S(2)}) collective-permute-start(f32[16,8,256]{2,1,0:T(8,128)S(1)} %sweeps.5.refs_2_), channel_id=1, source_target_pairs={{0,1},{1,0},{2,3},{3,2},{4,5},{5,4},{6,7},{7,6},{8,9},{9,8},{10,11... | collective-permute-start | bytes 393224 | tf_op jit(solution)/shard_map/ppermute | solution.py:563
  22.2 1.8 %sweeps.6.refs_3_ = f32[16,8,256]{2,1,0:T(8,128)S(1)} custom-call(f32[28,32,256]{2,1,0:T(8,128)S(1)} %get-tuple-element.30.whole_ref, f32[32,256]{1,0:T(8,128)S(1)} %get-tuple-element.33.left_ref, f32[32,256]{1,0:T(8,128)S(1)} %get-tuple-element.34.right_ref, f32[29,8,384]{2,1,0:T(8,128)S(1)} %get-tuple-element.35.south_ref, ...), custom_call_target="tpu_custom_call" | custom-call | tf_op jit(solution)/shard_map/sweeps/pallas_call | solution.py:34
  24.1 1.6 %collective-permute-start.6 = (f32[16,8,256]{2,1,0:T(8,128)S(1)}, f32[16,8,256]{2,1,0:T(8,128)S(1)}, u32[]{:S(2)}, u32[]{:S(2)}) collective-permute-start(f32[16,8,256]{2,1,0:T(8,128)S(1)} %sweeps.6.refs_3_), channel_id=1, source_target_pairs={{0,1},{1,0},{2,3},{3,2},{4,5},{5,4},{6,7},{7,6},{8,9},{9,8},{10,11... | collective-permute-start | bytes 393224 | tf_op jit(solution)/shard_map/ppermute | solution.py:563
  25.6 1.9 %sweeps.7.refs_4_ = f32[16,4,256]{2,1,0:T(4,128)S(1)} custom-call(f32[28,32,256]{2,1,0:T(8,128)S(1)} %get-tuple-element.30.whole_ref, f32[32,256]{1,0:T(8,128)S(1)} %get-tuple-element.33.left_ref, f32[32,256]{1,0:T(8,128)S(1)} %get-tuple-element.34.right_ref, f32[29,8,384]{2,1,0:T(8,128)S(1)} %get-tuple-element.35.south_ref, ...), custom_call_target="tpu_custom_call" | custom-call | tf_op jit(solution)/shard_map/sweeps/pallas_call | solution.py:34
  27.5 0.6 %collective-permute-start.7 = (f32[16,4,256]{2,1,0:T(4,128)S(1)}, f32[16,4,256]{2,1,0:T(4,128)S(1)}, u32[]{:S(2)}, u32[]{:S(2)}) collective-permute-start(f32[16,4,256]{2,1,0:T(4,128)S(1)} %sweeps.7.refs_4_), channel_id=1, source_target_pairs={{0,1},{1,0},{2,3},{3,2},{4,5},{5,4},{6,7},{7,6},{8,9},{9,8},{10,11... | collective-permute-start | bytes 196616 | tf_op jit(solution)/shard_map/ppermute | solution.py:563
  28.2 0.4 mix_own.1.refs_0_.order_ref
  28.6 1.6 %square.1.square_ref = f32[36,128]{1,0:T(8,128)S(1)} custom-call(bf16[8,28,16,256]{3,2,1,0:T(8,128)(2,1)S(1)} %get-tuple-element.43.grads_ref, f32[16,28,256]{2,1,0:T(8,128)S(1)} %mix_own.1.refs_0_.order_ref), custom_call_target="tpu_custom_call" | custom-call | tf_op jit(solution)/shard_map/square/pallas_call | solution.py:34
  30.2 0.2 mix_more.3.refs_0_
  30.9 0.9 %collective-permute-done.7.field_ref = f32[16,4,256]{2,1,0:T(4,128)S(1)} collective-permute-done((f32[16,4,256]{2,1,0:T(4,128)S(1)}, f32[16,4,256]{2,1,0:T(4,128)S(1)}, u32[]{:S(2)}, u32[]{:S(2)}) %collective-permute-start.7) | collective-permute-done | bytes 65568 | tf_op jit(solution)/shard_map/ppermute | solution.py:563
  31.8 1.2 %mix_last.1 = (f32[28,16,256]{2,1,0:T(8,128)S(1)}, f32[32,1,128]{2,1,0:T(1,128)S(1)}) custom-call(f32[16,28,256]{2,1,0:T(8,128)S(1)} %mix_more.5.acc_ref, bf16[28,48]{1,0:T(8,128)(2,1)S(1)} %get-tuple-element.42.corr_ref, f32[16,4,256]{2,1,0:T(4,128)S(1)} %collective-permute-done.7.field_ref, f32[36,128]{1,0:T(8,128)S(1)} %get-tuple-element.29.order_ref.cross_ref, ...), custom_call_target="tpu_custom_call" | custom-call | tf_op jit(solution)/shard_map/mix_last/pallas_call | solution.py:34
  33.0 10.2 %all_to_all.5.inbox_ref = f32[32,1,128]{2,1,0:T(1,128)S(1)} all-to-all(f32[32,1,128]{2,1,0:T(1,128)S(1)} %get-tuple-element.45), channel_id=1, replica_groups={{31,30,29,28,27,26,25,24,23,22,21,20,19,18,17,16,15,14,13,12,11,10,9,8,..., dimensions={0} | all-to-all | bytes 32768 | tf_op jit(solution)/shard_map/all_to_all | solution.py:574
  43.2 1.7 %final.1 = f32[28,16,256]{2,1,0:T(8,128)} custom-call(f32[32,1,128]{2,1,0:T(1,128)S(1)} %all_to_all.5.inbox_ref, f32[28,16,256]{2,1,0:T(8,128)S(1)} %get-tuple-element.46.mixed_ref, f32[28,16,256]{2,1,0:T(8,128)S(1)} %copy-done, bf16[8,28,16,256]{3,2,1,0:T(8,128)(2,1)S(1)} %get-tuple-element.44.steps_ref, ...), custom_call_target="tpu_custom_call" | custom-call | tf_op jit(solution)/shard_map/final/pallas_call | solution.py:34
  (14 shorter events, 0.7 us)
Async XLA Ops:
  1.3 9.6 %collective-permute-start = (f32[176,256]{1,0:T(8,128)S(1)}, f32[176,256]{1,0:T(8,128)S(1)}, u32[]{:S(2)}, u32[]{:S(2)}) collective-permute-start(f32[176,256]{1,0:T(8,128)S(1)} %next.1), channel_id=1, source_target_pairs={{0,0},{8,16},{16,8},{24,24},{1,1},{9,17},{17,9},{25,25},{2,2},{10,... | collective-permute-start | bytes 540680 | tf_op jit(solution)/shard_map/ppermute | solution.py:523
  2.0 10.2 %collective-permute-start.1 = (f32[176,256]{1,0:T(8,128)S(1)}, f32[176,256]{1,0:T(8,128)S(1)}, u32[]{:S(2)}, u32[]{:S(2)}) collective-permute-start(f32[176,256]{1,0:T(8,128)S(1)} %get-tuple-element.28), channel_id=1, source_target_pairs={{0,8},{8,0},{16,24},{24,16},{1,9},{9,1},{17,25},{25,17},{2,10},{10... | collective-permute-start | bytes 540680 | tf_op jit(solution)/shard_map/ppermute | solution.py:524
  12.5 1.7 %collective-permute-start.2 = (f32[32,256]{1,0:T(8,128)S(1)}, f32[32,256]{1,0:T(8,128)S(1)}, u32[]{:S(2)}, u32[]{:S(2)}) collective-permute-start(f32[32,256]{1,0:T(8,128)S(1)} %get-tuple-element.31), channel_id=1, source_target_pairs={{0,2},{2,0},{4,6},{6,4},{1,3},{3,1},{5,7},{7,5},{8,10},{10,8},{12,... | collective-permute-start | bytes 98312 | tf_op jit(solution)/shard_map/ppermute | solution.py:545
  12.6 3.4 %collective-permute-start.3 = (f32[32,256]{1,0:T(8,128)S(1)}, f32[32,256]{1,0:T(8,128)S(1)}, u32[]{:S(2)}, u32[]{:S(2)}) collective-permute-start(f32[32,256]{1,0:T(8,128)S(1)} %get-tuple-element.32), channel_id=1, source_target_pairs={{0,6},{2,4},{4,2},{6,0},{1,7},{3,5},{5,3},{7,1},{8,14},{10,12},{12... | collective-permute-start | bytes 98312 | tf_op jit(solution)/shard_map/ppermute | solution.py:544
  18.2 12.0 %collective-permute-start.4 = (f32[16,8,256]{2,1,0:T(8,128)S(1)}, f32[16,8,256]{2,1,0:T(8,128)S(1)}, u32[]{:S(2)}, u32[]{:S(2)}) collective-permute-start(f32[16,8,256]{2,1,0:T(8,128)S(1)} %sweeps.4.refs_1_), channel_id=1, source_target_pairs={{0,1},{1,0},{2,3},{3,2},{4,5},{5,4},{6,7},{7,6},{8,9},{9,8},{10,11... | collective-permute-start | bytes 393224 | tf_op jit(solution)/shard_map/ppermute | solution.py:563
  21.6 8.8 %collective-permute-start.5 = (f32[16,8,256]{2,1,0:T(8,128)S(1)}, f32[16,8,256]{2,1,0:T(8,128)S(1)}, u32[]{:S(2)}, u32[]{:S(2)}) collective-permute-start(f32[16,8,256]{2,1,0:T(8,128)S(1)} %sweeps.5.refs_2_), channel_id=1, source_target_pairs={{0,1},{1,0},{2,3},{3,2},{4,5},{5,4},{6,7},{7,6},{8,9},{9,8},{10,11... | collective-permute-start | bytes 393224 | tf_op jit(solution)/shard_map/ppermute | solution.py:563
  24.1 4.0 %copy-start.1 = (f32[56,56]{1,0:T(8,128)S(1)}, f32[56,56]{1,0:T(8,128)}, u32[]{:S(2)}) copy-start(f32[56,56]{1,0:T(8,128)} %corr_ref.1) | copy-start | bytes 37636
  24.1 6.6 %collective-permute-start.6 = (f32[16,8,256]{2,1,0:T(8,128)S(1)}, f32[16,8,256]{2,1,0:T(8,128)S(1)}, u32[]{:S(2)}, u32[]{:S(2)}) collective-permute-start(f32[16,8,256]{2,1,0:T(8,128)S(1)} %sweeps.6.refs_3_), channel_id=1, source_target_pairs={{0,1},{1,0},{2,3},{3,2},{4,5},{5,4},{6,7},{7,6},{8,9},{9,8},{10,11... | collective-permute-start | bytes 393224 | tf_op jit(solution)/shard_map/ppermute | solution.py:563
  27.5 4.3 %collective-permute-start.7 = (f32[16,4,256]{2,1,0:T(4,128)S(1)}, f32[16,4,256]{2,1,0:T(4,128)S(1)}, u32[]{:S(2)}, u32[]{:S(2)}) collective-permute-start(f32[16,4,256]{2,1,0:T(4,128)S(1)} %sweeps.7.refs_4_), channel_id=1, source_target_pairs={{0,1},{1,0},{2,3},{3,2},{4,5},{5,4},{6,7},{7,6},{8,9},{9,8},{10,11... | collective-permute-start | bytes 196616 | tf_op jit(solution)/shard_map/ppermute | solution.py:563
  31.8 11.4 %copy-start = (f32[28,16,256]{2,1,0:T(8,128)S(1)}, f32[28,16,256]{2,1,0:T(8,128)}, u32[]{:S(2)}) copy-start(f32[28,16,256]{2,1,0:T(8,128)} %control_ref.1) | copy-start | bytes 1376260

commit v12 on v10

--- a/solution.py
+++ b/solution.py
@@ -127,7 +127,7 @@
     return parts
 
 
-def pack_kernel(grad_hbm, mask_hbm, diff_hbm, field_ref, swap_ref, next_ref, grad_ref, mask_ref, diff_ref, turn_ref, sems):
+def pack_kernel(grad_hbm, mask_hbm, diff_hbm, field_ref, swap_ref, grad_ref, mask_ref, diff_ref, turn_ref, sems):
     steps, rows, cols = grad_ref.shape
     slots = field_ref.shape[1]
     pieces = [(begin, min(SUB, steps - begin)) for begin in range(0, steps, SUB)]
@@ -162,14 +162,20 @@
                 value = turn_ref[pl.ds(base + slot * SUB, SUB, stride=SUB), :]
                 field_ref[row, slot:slot + SUB, across] = value
     odd = lax.rem(lax.axis_index("lat"), 2)
-    near, far = (1 - odd) * (rows - HALO), odd * (rows - HALO)
+    near = (1 - odd) * (rows - HALO)
     for row in range(HALO):
         for place, there in message_parts(row, steps):
             swap_ref[place] = field_ref[near + row, there]
+
+
+def next_kernel(field_ref, next_ref, *, steps):
+    far = lax.rem(lax.axis_index("lat"), 2) * (field_ref.shape[0] - HALO)
+    for row in range(HALO):
+        for place, there in message_parts(row, steps):
             next_ref[place] = field_ref[far + row, there]
 
 
-def side_kernel(swap_ref, field_ref, next_ref, order_ref, whole_ref, pair_ref, beside_ref, *, steps):
+def side_kernel(next_ref, field_ref, swap_ref, order_ref, whole_ref, pair_ref, beside_ref, *, steps):
     rows, slots, cols = field_ref.shape
     place, count = lax.axis_index("lat"), lax.axis_size("lat")
     odd = lax.rem(place, 2)
@@ -496,9 +502,9 @@
     slots = slots_of(steps)
     turn = pltpu.VMEM((rows * (cols // LANE) * slots, LANE), jnp.float32)
 
-    field, to_swap, to_next = call(
+    field, to_swap = call(
         pack_kernel,
-        (f32(rows, slots, cols), f32(message_rows(steps), cols), f32(message_rows(steps), cols)),
+        (f32(rows, slots, cols), f32(message_rows(steps), cols)),
         [pltpu.with_memory_space_constraint(v, pltpu.HBM) for v in (gradient, land_mask, diffusivity)],
         specs=[HBM] * 3,
         scratch=[
@@ -507,8 +513,9 @@
         ],
         name="pack",
     )
+    to_next = call(functools.partial(next_kernel, steps=steps), f32(message_rows(steps), cols), (field,), name="next")
+    from_next = lax.ppermute(to_next, "lat", odd)
     from_swap = lax.ppermute(to_swap, "lat", even)
-    from_next = lax.ppermute(to_next, "lat", odd)
     pair_shape = jax.ShapeDtypeStruct(pair_steps.shape, jnp.bfloat16)
     cross, pair_steps, pair_grads = call(
         cross_kernel, (f32(NSYM, LANE), pair_shape, pair_shape),
@@ -526,7 +533,7 @@
     )
     side_shape = f32(slots, -(-tall // PER) * LANE)
     whole, to_pair, to_beside = call(
-        functools.partial(side_kernel, steps=steps), (f32(tall, slots, cols), side_shape, side_shape), (from_swap, field, from_next, cross), name="sides"
+        functools.partial(side_kernel, steps=steps), (f32(tall, slots, cols), side_shape, side_shape), (from_next, field, from_swap, cross), name="sides"
     )
     from_beside = lax.ppermute(to_beside, "lon", odds)
     from_pair = lax.ppermute(to_pair, "lon", evens)

time: 45.6 us -> 44.7 us (0.980)
  blocking collectives: 15.1 us -> 10.9 us
  starting transfers between devices: 9.93 us -> 12.6 us
  waiting for transfers between devices: 4.21 us -> 4.75 us
    all_to_all x1, blocking collectives: 15.1 us -> 10.9 us  [local(): lax.all_to_all(message, ('lat', 'lon', 'tm'), split_axis=0, concat_axis=0...]
    ppermute x1, starting transfers between devices: 3.09 us -> 5.9 us  [local(): from_swap = lax.ppermute(to_swap, 'lat', even)]
    pallas_call x16 -> x17, Pallas kernels: 16.1 us -> 16.1 us  [call(): pl.pallas_call(kernel, out_shape=outs, in_specs=specs or [VMEM] * len(arg...]
where the time goes in v12:
time: 44.7 us; the launch traced here: 44.4 us
  Pallas kernels  16.1 us (36%)
  starting transfers between devices  12.6 us (28%)
  blocking collectives  10.9 us (24%)
  waiting for transfers between devices  4.75 us (11%)
    pallas_call x17, Pallas kernels, call(): pl.pallas_call(kernel, out_shape=outs, in_specs=specs or [VMEM] * len(arg...  16.1 us
    all_to_all x1, blocking collectives, local(): lax.all_to_all(message, ('lat', 'lon', 'tm'), split_axis=0, concat_axis=0...  10.9 us
    ppermute x1, starting transfers between devices, local(): from_swap = lax.ppermute(to_swap, 'lat', even)  5.9 us
    ppermute x4, starting transfers between devices, local(): other.append(lax.ppermute(part, 'tm', pairs))  4.31 us
    ppermute x4, waiting for transfers between devices, local(): other.append(lax.ppermute(part, 'tm', pairs))  1.78 us
    ppermute x1, waiting for transfers between devices, local(): from_beside = lax.ppermute(to_beside, 'lon', odds)  1.77 us
    ppermute x1, starting transfers between devices, local(): from_beside = lax.ppermute(to_beside, 'lon', odds)  1.64 us
    ppermute x1, waiting for transfers between devices, local(): from_swap = lax.ppermute(to_swap, 'lat', even)  1.2 us
  transfers between devices with their start and end apart: 8, of which 4 were waited for; matrix products, arithmetic and copies ran while one was open for 0% of the time, Pallas kernels for 22%

profile of v12, /device:TPU:0, one launch (start us, length us, event | category | flops | bytes accessed | tf_op | source)
XLA Modules:
  0.0 44.4 jit_solution(17635315851172890523)
XLA Ops:
  0.0 1.2 %pack.1 = (f32[16,32,256]{2,1,0:T(8,128)S(1)}, f32[176,256]{1,0:T(8,128)S(1)}) custom-call(f32[28,16,256]{2,1,0:T(8,128)} %grad_hbm.1, s32[16,256]{1,0:T(8,128)} %mask_hbm.1, f32[16,256]{1,0:T(8,128)} %diff_hbm.1), custom_call_target="tpu_custom_call" | custom-call | tf_op jit(solution)/shard_map/pack/pallas_call | solution.py:34
  1.3 0.7 %collective-permute-start = (f32[176,256]{1,0:T(8,128)S(1)}, f32[176,256]{1,0:T(8,128)S(1)}, u32[]{:S(2)}, u32[]{:S(2)}) collective-permute-start(f32[176,256]{1,0:T(8,128)S(1)} %next.1), channel_id=1, source_target_pairs={{0,0},{8,16},{16,8},{24,24},{1,1},{9,17},{17,9},{25,25},{2,2},{10,... | collective-permute-start | bytes 540680 | tf_op jit(solution)/shard_map/ppermute | solution.py:517
  2.0 5.9 %collective-permute-start.1 = (f32[176,256]{1,0:T(8,128)S(1)}, f32[176,256]{1,0:T(8,128)S(1)}, u32[]{:S(2)}, u32[]{:S(2)}) collective-permute-start(f32[176,256]{1,0:T(8,128)S(1)} %get-tuple-element.28), channel_id=1, source_target_pairs={{0,8},{8,0},{16,24},{24,16},{1,9},{9,1},{17,25},{25,17},{2,10},{10... | collective-permute-start | bytes 540680 | tf_op jit(solution)/shard_map/ppermute | solution.py:518
  7.9 3.0 %cross.1 = (f32[36,128]{1,0:T(8,128)S(1)}, bf16[8,28,16,256]{3,2,1,0:T(8,128)(2,1)S(1)}, bf16[8,28,16,256]{3,2,1,0:T(8,128)(2,1)S(1)}) custom-call(bf16[8,28,16,256]{3,2,1,0:T(8,128)(2,1)} %steps_hbm.1, bf16[8,28,16,256]{3,2,1,0:T(8,128)(2,1)} %grads_hbm.1), custom_call_target="tpu_custom_call" | custom-call | tf_op jit(solution)/shard_map/cross/pallas_call | solution.py:34
  10.9 1.2 %collective-permute-done.1.swap_ref = f32[176,256]{1,0:T(8,128)S(1)} collective-permute-done((f32[176,256]{1,0:T(8,128)S(1)}, f32[176,256]{1,0:T(8,128)S(1)}, u32[]{:S(2)}, u32[]{:S(2)}) %collective-permute-start.1) | collective-permute-done | bytes 180256 | tf_op jit(solution)/shard_map/ppermute | solution.py:518
  12.1 0.3 sides.1
  12.6 1.6 %collective-permute-start.3 = (f32[32,256]{1,0:T(8,128)S(1)}, f32[32,256]{1,0:T(8,128)S(1)}, u32[]{:S(2)}, u32[]{:S(2)}) collective-permute-start(f32[32,256]{1,0:T(8,128)S(1)} %get-tuple-element.32), channel_id=1, source_target_pairs={{0,6},{2,4},{4,2},{6,0},{1,7},{3,5},{5,3},{7,1},{8,14},{10,12},{12... | collective-permute-start | bytes 98312 | tf_op jit(solution)/shard_map/ppermute | solution.py:538
  14.2 1.8 %collective-permute-done.3.beside_ref = f32[32,256]{1,0:T(8,128)S(1)} collective-permute-done((f32[32,256]{1,0:T(8,128)S(1)}, f32[32,256]{1,0:T(8,128)S(1)}, u32[]{:S(2)}, u32[]{:S(2)}) %collective-permute-start.3) | collective-permute-done | bytes 32800 | tf_op jit(solution)/shard_map/ppermute | solution.py:538
  16.0 0.3 weights.1
  16.3 1.3 %sweeps.4.refs_1_ = f32[16,8,256]{2,1,0:T(8,128)S(1)} custom-call(f32[28,32,256]{2,1,0:T(8,128)S(1)} %get-tuple-element.30.whole_ref, f32[32,256]{1,0:T(8,128)S(1)} %get-tuple-element.33.left_ref, f32[32,256]{1,0:T(8,128)S(1)} %get-tuple-element.34.right_ref, f32[29,8,384]{2,1,0:T(8,128)S(1)} %get-tuple-element.35.south_ref, ...), custom_call_target="tpu_custom_call" | custom-call | tf_op jit(solution)/shard_map/sweeps/pallas_call | solution.py:34
  17.7 1.6 %collective-permute-start.4 = (f32[16,8,256]{2,1,0:T(8,128)S(1)}, f32[16,8,256]{2,1,0:T(8,128)S(1)}, u32[]{:S(2)}, u32[]{:S(2)}) collective-permute-start(f32[16,8,256]{2,1,0:T(8,128)S(1)} %sweeps.4.refs_1_), channel_id=1, source_target_pairs={{0,1},{1,0},{2,3},{3,2},{4,5},{5,4},{6,7},{7,6},{8,9},{9,8},{10,11... | collective-permute-start | bytes 393224 | tf_op jit(solution)/shard_map/ppermute | solution.py:556
  19.2 1.3 %sweeps.5.refs_2_ = f32[16,8,256]{2,1,0:T(8,128)S(1)} custom-call(f32[28,32,256]{2,1,0:T(8,128)S(1)} %get-tuple-element.30.whole_ref, f32[32,256]{1,0:T(8,128)S(1)} %get-tuple-element.33.left_ref, f32[32,256]{1,0:T(8,128)S(1)} %get-tuple-element.34.right_ref, f32[29,8,384]{2,1,0:T(8,128)S(1)} %get-tuple-element.35.south_ref, ...), custom_call_target="tpu_custom_call" | custom-call | tf_op jit(solution)/shard_map/sweeps/pallas_call | solution.py:34
  20.6 0.6 %collective-permute-start.5 = (f32[16,8,256]{2,1,0:T(8,128)S(1)}, f32[16,8,256]{2,1,0:T(8,128)S(1)}, u32[]{:S(2)}, u32[]{:S(2)}) collective-permute-start(f32[16,8,256]{2,1,0:T(8,128)S(1)} %sweeps.5.refs_2_), channel_id=1, source_target_pairs={{0,1},{1,0},{2,3},{3,2},{4,5},{5,4},{6,7},{7,6},{8,9},{9,8},{10,11... | collective-permute-start | bytes 393224 | tf_op jit(solution)/shard_map/ppermute | solution.py:556
  21.2 1.3 %sweeps.6.refs_3_ = f32[16,8,256]{2,1,0:T(8,128)S(1)} custom-call(f32[28,32,256]{2,1,0:T(8,128)S(1)} %get-tuple-element.30.whole_ref, f32[32,256]{1,0:T(8,128)S(1)} %get-tuple-element.33.left_ref, f32[32,256]{1,0:T(8,128)S(1)} %get-tuple-element.34.right_ref, f32[29,8,384]{2,1,0:T(8,128)S(1)} %get-tuple-element.35.south_ref, ...), custom_call_target="tpu_custom_call" | custom-call | tf_op jit(solution)/shard_map/sweeps/pallas_call | solution.py:34
  22.5 1.6 %collective-permute-start.6 = (f32[16,8,256]{2,1,0:T(8,128)S(1)}, f32[16,8,256]{2,1,0:T(8,128)S(1)}, u32[]{:S(2)}, u32[]{:S(2)}) collective-permute-start(f32[16,8,256]{2,1,0:T(8,128)S(1)} %sweeps.6.refs_3_), channel_id=1, source_target_pairs={{0,1},{1,0},{2,3},{3,2},{4,5},{5,4},{6,7},{7,6},{8,9},{9,8},{10,11... | collective-permute-start | bytes 393224 | tf_op jit(solution)/shard_map/ppermute | solution.py:556
  24.1 1.3 %sweeps.7.refs_4_ = f32[16,4,256]{2,1,0:T(4,128)S(1)} custom-call(f32[28,32,256]{2,1,0:T(8,128)S(1)} %get-tuple-element.30.whole_ref, f32[32,256]{1,0:T(8,128)S(1)} %get-tuple-element.33.left_ref, f32[32,256]{1,0:T(8,128)S(1)} %get-tuple-element.34.right_ref, f32[29,8,384]{2,1,0:T(8,128)S(1)} %get-tuple-element.35.south_ref, ...), custom_call_target="tpu_custom_call" | custom-call | tf_op jit(solution)/shard_map/sweeps/pallas_call | solution.py:34
  25.5 0.6 %collective-permute-start.7 = (f32[16,4,256]{2,1,0:T(4,128)S(1)}, f32[16,4,256]{2,1,0:T(4,128)S(1)}, u32[]{:S(2)}, u32[]{:S(2)}) collective-permute-start(f32[16,4,256]{2,1,0:T(4,128)S(1)} %sweeps.7.refs_4_), channel_id=1, source_target_pairs={{0,1},{1,0},{2,3},{3,2},{4,5},{5,4},{6,7},{7,6},{8,9},{9,8},{10,11... | collective-permute-start | bytes 196616 | tf_op jit(solution)/shard_map/ppermute | solution.py:556
  26.2 0.4 mix_own.1.refs_0_.order_ref
  26.6 1.6 %square.1.square_ref = f32[36,128]{1,0:T(8,128)S(1)} custom-call(bf16[8,28,16,256]{3,2,1,0:T(8,128)(2,1)S(1)} %get-tuple-element.43.grads_ref, f32[16,28,256]{2,1,0:T(8,128)S(1)} %mix_own.1.refs_0_.order_ref), custom_call_target="tpu_custom_call" | custom-call | tf_op jit(solution)/shard_map/square/pallas_call | solution.py:34
  28.6 1.2 %collective-permute-done.6.refs_2_ = f32[16,8,256]{2,1,0:T(8,128)S(1)} collective-permute-done((f32[16,8,256]{2,1,0:T(8,128)S(1)}, f32[16,8,256]{2,1,0:T(8,128)S(1)}, u32[]{:S(2)}, u32[]{:S(2)}) %collective-permute-start.6) | collective-permute-done | bytes 131104 | tf_op jit(solution)/shard_map/ppermute | solution.py:556
  30.0 0.6 %collective-permute-done.7.field_ref = f32[16,4,256]{2,1,0:T(4,128)S(1)} collective-permute-done((f32[16,4,256]{2,1,0:T(4,128)S(1)}, f32[16,4,256]{2,1,0:T(4,128)S(1)}, u32[]{:S(2)}, u32[]{:S(2)}) %collective-permute-start.7) | collective-permute-done | bytes 65568 | tf_op jit(solution)/shard_map/ppermute | solution.py:556
  30.6 1.2 %mix_last.1 = (f32[28,16,256]{2,1,0:T(8,128)S(1)}, f32[32,1,128]{2,1,0:T(1,128)S(1)}) custom-call(f32[16,28,256]{2,1,0:T(8,128)S(1)} %mix_more.5.acc_ref, bf16[28,48]{1,0:T(8,128)(2,1)S(1)} %get-tuple-element.42.corr_ref, f32[16,4,256]{2,1,0:T(4,128)S(1)} %collective-permute-done.7.field_ref, f32[36,128]{1,0:T(8,128)S(1)} %get-tuple-element.29.order_ref.cross_ref, ...), custom_call_target="tpu_custom_call" | custom-call | tf_op jit(solution)/shard_map/mix_last/pallas_call | solution.py:34
  31.8 10.9 %all_to_all.5.inbox_ref = f32[32,1,128]{2,1,0:T(1,128)S(1)} all-to-all(f32[32,1,128]{2,1,0:T(1,128)S(1)} %get-tuple-element.45), channel_id=1, replica_groups={{31,30,29,28,27,26,25,24,23,22,21,20,19,18,17,16,15,14,13,12,11,10,9,8,..., dimensions={0} | all-to-all | bytes 32768 | tf_op jit(solution)/shard_map/all_to_all | solution.py:567
  42.7 1.7 %final.1 = f32[28,16,256]{2,1,0:T(8,128)} custom-call(f32[32,1,128]{2,1,0:T(1,128)S(1)} %all_to_all.5.inbox_ref, f32[28,16,256]{2,1,0:T(8,128)S(1)} %get-tuple-element.46.mixed_ref, f32[28,16,256]{2,1,0:T(8,128)S(1)} %copy-done, bf16[8,28,16,256]{3,2,1,0:T(8,128)(2,1)S(1)} %get-tuple-element.44.steps_ref, ...), custom_call_target="tpu_custom_call" | custom-call | tf_op jit(solution)/shard_map/final/pallas_call | solution.py:34
  (14 shorter events, 0.9 us)
Async XLA Ops:
  1.3 9.6 %collective-permute-start = (f32[176,256]{1,0:T(8,128)S(1)}, f32[176,256]{1,0:T(8,128)S(1)}, u32[]{:S(2)}, u32[]{:S(2)}) collective-permute-start(f32[176,256]{1,0:T(8,128)S(1)} %next.1), channel_id=1, source_target_pairs={{0,0},{8,16},{16,8},{24,24},{1,1},{9,17},{17,9},{25,25},{2,2},{10,... | collective-permute-start | bytes 540680 | tf_op jit(solution)/shard_map/ppermute | solution.py:517
  2.0 10.2 %collective-permute-start.1 = (f32[176,256]{1,0:T(8,128)S(1)}, f32[176,256]{1,0:T(8,128)S(1)}, u32[]{:S(2)}, u32[]{:S(2)}) collective-permute-start(f32[176,256]{1,0:T(8,128)S(1)} %get-tuple-element.28), channel_id=1, source_target_pairs={{0,8},{8,0},{16,24},{24,16},{1,9},{9,1},{17,25},{25,17},{2,10},{10... | collective-permute-start | bytes 540680 | tf_op jit(solution)/shard_map/ppermute | solution.py:518
  12.5 1.7 %collective-permute-start.2 = (f32[32,256]{1,0:T(8,128)S(1)}, f32[32,256]{1,0:T(8,128)S(1)}, u32[]{:S(2)}, u32[]{:S(2)}) collective-permute-start(f32[32,256]{1,0:T(8,128)S(1)} %get-tuple-element.31), channel_id=1, source_target_pairs={{0,2},{2,0},{4,6},{6,4},{1,3},{3,1},{5,7},{7,5},{8,10},{10,8},{12,... | collective-permute-start | bytes 98312 | tf_op jit(solution)/shard_map/ppermute | solution.py:539
  12.6 3.4 %collective-permute-start.3 = (f32[32,256]{1,0:T(8,128)S(1)}, f32[32,256]{1,0:T(8,128)S(1)}, u32[]{:S(2)}, u32[]{:S(2)}) collective-permute-start(f32[32,256]{1,0:T(8,128)S(1)} %get-tuple-element.32), channel_id=1, source_target_pairs={{0,6},{2,4},{4,2},{6,0},{1,7},{3,5},{5,3},{7,1},{8,14},{10,12},{12... | collective-permute-start | bytes 98312 | tf_op jit(solution)/shard_map/ppermute | solution.py:538
  17.7 10.5 %collective-permute-start.4 = (f32[16,8,256]{2,1,0:T(8,128)S(1)}, f32[16,8,256]{2,1,0:T(8,128)S(1)}, u32[]{:S(2)}, u32[]{:S(2)}) collective-permute-start(f32[16,8,256]{2,1,0:T(8,128)S(1)} %sweeps.4.refs_1_), channel_id=1, source_target_pairs={{0,1},{1,0},{2,3},{3,2},{4,5},{5,4},{6,7},{7,6},{8,9},{9,8},{10,11... | collective-permute-start | bytes 393224 | tf_op jit(solution)/shard_map/ppermute | solution.py:556
  20.6 7.8 %collective-permute-start.5 = (f32[16,8,256]{2,1,0:T(8,128)S(1)}, f32[16,8,256]{2,1,0:T(8,128)S(1)}, u32[]{:S(2)}, u32[]{:S(2)}) collective-permute-start(f32[16,8,256]{2,1,0:T(8,128)S(1)} %sweeps.5.refs_2_), channel_id=1, source_target_pairs={{0,1},{1,0},{2,3},{3,2},{4,5},{5,4},{6,7},{7,6},{8,9},{9,8},{10,11... | collective-permute-start | bytes 393224 | tf_op jit(solution)/shard_map/ppermute | solution.py:556
  22.5 3.5 %copy-start.1 = (f32[56,56]{1,0:T(8,128)S(1)}, f32[56,56]{1,0:T(8,128)}, u32[]{:S(2)}) copy-start(f32[56,56]{1,0:T(8,128)} %corr_ref.1) | copy-start | bytes 37636
  22.5 7.3 %collective-permute-start.6 = (f32[16,8,256]{2,1,0:T(8,128)S(1)}, f32[16,8,256]{2,1,0:T(8,128)S(1)}, u32[]{:S(2)}, u32[]{:S(2)}) collective-permute-start(f32[16,8,256]{2,1,0:T(8,128)S(1)} %sweeps.6.refs_3_), channel_id=1, source_target_pairs={{0,1},{1,0},{2,3},{3,2},{4,5},{5,4},{6,7},{7,6},{8,9},{9,8},{10,11... | collective-permute-start | bytes 393224 | tf_op jit(solution)/shard_map/ppermute | solution.py:556
  25.5 5.2 %collective-permute-start.7 = (f32[16,4,256]{2,1,0:T(4,128)S(1)}, f32[16,4,256]{2,1,0:T(4,128)S(1)}, u32[]{:S(2)}, u32[]{:S(2)}) collective-permute-start(f32[16,4,256]{2,1,0:T(4,128)S(1)} %sweeps.7.refs_4_), channel_id=1, source_target_pairs={{0,1},{1,0},{2,3},{3,2},{4,5},{5,4},{6,7},{7,6},{8,9},{9,8},{10,11... | collective-permute-start | bytes 196616 | tf_op jit(solution)/shard_map/ppermute | solution.py:556
  30.6 12.1 %copy-start = (f32[28,16,256]{2,1,0:T(8,128)S(1)}, f32[28,16,256]{2,1,0:T(8,128)}, u32[]{:S(2)}) copy-start(f32[28,16,256]{2,1,0:T(8,128)} %control_ref.1) | copy-start | bytes 1376260

commit v13 on v12

--- a/solution.py
+++ b/solution.py
@@ -408,7 +408,7 @@
                     sums[n] = sums[n] + (product[:SUB] + product[SUB:])
         return tuple(sums)
 
-    sums = lax.fori_loop(0, steps, body, (zero,) * NPROJ, unroll=2)
+    sums = lax.fori_loop(0, steps, body, (zero,) * NPROJ, unroll=2 if steps % 4 else 4)
     rows_ref[0:NSYM, :] = cross_ref[...]
     rows_ref[NSYM:NGRAM, :] = square_ref[...]
     for n in range(NPROJ):
@@ -477,7 +477,7 @@
 
     copies = []
     for n, (begin, count) in enumerate(groups_of(steps)):
-        lax.fori_loop(begin, begin + count, body, 0, unroll=2)
+        lax.fori_loop(begin, begin + count, body, 0, unroll=2 if count % 4 else 4)
         part = pl.ds(begin, count)
         copies.append(pltpu.make_async_copy(out_ref.at[part], out_hbm.at[part], sems.at[n]))
         copies[-1].start()

time: 44.7 us -> 44.5 us (level)
  no operation moved by 1% of the time
where the time goes in v13:
time: 44.5 us; the launch traced here: 44.3 us
  Pallas kernels  15.9 us (36%)
  starting transfers between devices  12.6 us (28%)
  blocking collectives  10.9 us (24%)
  waiting for transfers between devices  4.75 us (11%)
    pallas_call x17, Pallas kernels, call(): pl.pallas_call(kernel, out_shape=outs, in_specs=specs or [VMEM] * len(arg...  15.9 us
    all_to_all x1, blocking collectives, local(): lax.all_to_all(message, ('lat', 'lon', 'tm'), split_axis=0, concat_axis=0...  10.9 us
    ppermute x1, starting transfers between devices, local(): from_swap = lax.ppermute(to_swap, 'lat', even)  5.9 us
    ppermute x4, starting transfers between devices, local(): other.append(lax.ppermute(part, 'tm', pairs))  4.31 us
    ppermute x4, waiting for transfers between devices, local(): other.append(lax.ppermute(part, 'tm', pairs))  1.78 us
    ppermute x1, waiting for transfers between devices, local(): from_beside = lax.ppermute(to_beside, 'lon', odds)  1.77 us
    ppermute x1, starting transfers between devices, local(): from_beside = lax.ppermute(to_beside, 'lon', odds)  1.64 us
    ppermute x1, waiting for transfers between devices, local(): from_swap = lax.ppermute(to_swap, 'lat', even)  1.2 us
  transfers between devices with their start and end apart: 8, of which 4 were waited for; matrix products, arithmetic and copies ran while one was open for 0% of the time, Pallas kernels for 22%

profile of v13, /device:TPU:0, one launch (start us, length us, event | category | flops | bytes accessed | tf_op | source)
XLA Modules:
  0.0 44.3 jit_solution(11255913059369122748)
XLA Ops:
  0.0 1.2 %pack.1 = (f32[16,32,256]{2,1,0:T(8,128)S(1)}, f32[176,256]{1,0:T(8,128)S(1)}) custom-call(f32[28,16,256]{2,1,0:T(8,128)} %grad_hbm.1, s32[16,256]{1,0:T(8,128)} %mask_hbm.1, f32[16,256]{1,0:T(8,128)} %diff_hbm.1), custom_call_target="tpu_custom_call" | custom-call | tf_op jit(solution)/shard_map/pack/pallas_call | solution.py:34
  1.3 0.7 %collective-permute-start = (f32[176,256]{1,0:T(8,128)S(1)}, f32[176,256]{1,0:T(8,128)S(1)}, u32[]{:S(2)}, u32[]{:S(2)}) collective-permute-start(f32[176,256]{1,0:T(8,128)S(1)} %next.1), channel_id=1, source_target_pairs={{0,0},{8,16},{16,8},{24,24},{1,1},{9,17},{17,9},{25,25},{2,2},{10,... | collective-permute-start | bytes 540680 | tf_op jit(solution)/shard_map/ppermute | solution.py:517
  2.0 5.9 %collective-permute-start.1 = (f32[176,256]{1,0:T(8,128)S(1)}, f32[176,256]{1,0:T(8,128)S(1)}, u32[]{:S(2)}, u32[]{:S(2)}) collective-permute-start(f32[176,256]{1,0:T(8,128)S(1)} %get-tuple-element.28), channel_id=1, source_target_pairs={{0,8},{8,0},{16,24},{24,16},{1,9},{9,1},{17,25},{25,17},{2,10},{10... | collective-permute-start | bytes 540680 | tf_op jit(solution)/shard_map/ppermute | solution.py:518
  7.9 3.0 %cross.1 = (f32[36,128]{1,0:T(8,128)S(1)}, bf16[8,28,16,256]{3,2,1,0:T(8,128)(2,1)S(1)}, bf16[8,28,16,256]{3,2,1,0:T(8,128)(2,1)S(1)}) custom-call(bf16[8,28,16,256]{3,2,1,0:T(8,128)(2,1)} %steps_hbm.1, bf16[8,28,16,256]{3,2,1,0:T(8,128)(2,1)} %grads_hbm.1), custom_call_target="tpu_custom_call" | custom-call | tf_op jit(solution)/shard_map/cross/pallas_call | solution.py:34
  10.9 1.2 %collective-permute-done.1.swap_ref = f32[176,256]{1,0:T(8,128)S(1)} collective-permute-done((f32[176,256]{1,0:T(8,128)S(1)}, f32[176,256]{1,0:T(8,128)S(1)}, u32[]{:S(2)}, u32[]{:S(2)}) %collective-permute-start.1) | collective-permute-done | bytes 180256 | tf_op jit(solution)/shard_map/ppermute | solution.py:518
  12.1 0.3 sides.1
  12.6 1.6 %collective-permute-start.3 = (f32[32,256]{1,0:T(8,128)S(1)}, f32[32,256]{1,0:T(8,128)S(1)}, u32[]{:S(2)}, u32[]{:S(2)}) collective-permute-start(f32[32,256]{1,0:T(8,128)S(1)} %get-tuple-element.32), channel_id=1, source_target_pairs={{0,6},{2,4},{4,2},{6,0},{1,7},{3,5},{5,3},{7,1},{8,14},{10,12},{12... | collective-permute-start | bytes 98312 | tf_op jit(solution)/shard_map/ppermute | solution.py:538
  14.2 1.8 %collective-permute-done.3.beside_ref = f32[32,256]{1,0:T(8,128)S(1)} collective-permute-done((f32[32,256]{1,0:T(8,128)S(1)}, f32[32,256]{1,0:T(8,128)S(1)}, u32[]{:S(2)}, u32[]{:S(2)}) %collective-permute-start.3) | collective-permute-done | bytes 32800 | tf_op jit(solution)/shard_map/ppermute | solution.py:538
  16.0 0.3 weights.1
  16.3 1.3 %sweeps.4.refs_1_ = f32[16,8,256]{2,1,0:T(8,128)S(1)} custom-call(f32[28,32,256]{2,1,0:T(8,128)S(1)} %get-tuple-element.30.whole_ref, f32[32,256]{1,0:T(8,128)S(1)} %get-tuple-element.33.left_ref, f32[32,256]{1,0:T(8,128)S(1)} %get-tuple-element.34.right_ref, f32[29,8,384]{2,1,0:T(8,128)S(1)} %get-tuple-element.35.south_ref, ...), custom_call_target="tpu_custom_call" | custom-call | tf_op jit(solution)/shard_map/sweeps/pallas_call | solution.py:34
  17.7 1.6 %collective-permute-start.4 = (f32[16,8,256]{2,1,0:T(8,128)S(1)}, f32[16,8,256]{2,1,0:T(8,128)S(1)}, u32[]{:S(2)}, u32[]{:S(2)}) collective-permute-start(f32[16,8,256]{2,1,0:T(8,128)S(1)} %sweeps.4.refs_1_), channel_id=1, source_target_pairs={{0,1},{1,0},{2,3},{3,2},{4,5},{5,4},{6,7},{7,6},{8,9},{9,8},{10,11... | collective-permute-start | bytes 393224 | tf_op jit(solution)/shard_map/ppermute | solution.py:556
  19.2 1.3 %sweeps.5.refs_2_ = f32[16,8,256]{2,1,0:T(8,128)S(1)} custom-call(f32[28,32,256]{2,1,0:T(8,128)S(1)} %get-tuple-element.30.whole_ref, f32[32,256]{1,0:T(8,128)S(1)} %get-tuple-element.33.left_ref, f32[32,256]{1,0:T(8,128)S(1)} %get-tuple-element.34.right_ref, f32[29,8,384]{2,1,0:T(8,128)S(1)} %get-tuple-element.35.south_ref, ...), custom_call_target="tpu_custom_call" | custom-call | tf_op jit(solution)/shard_map/sweeps/pallas_call | solution.py:34
  20.6 0.6 %collective-permute-start.5 = (f32[16,8,256]{2,1,0:T(8,128)S(1)}, f32[16,8,256]{2,1,0:T(8,128)S(1)}, u32[]{:S(2)}, u32[]{:S(2)}) collective-permute-start(f32[16,8,256]{2,1,0:T(8,128)S(1)} %sweeps.5.refs_2_), channel_id=1, source_target_pairs={{0,1},{1,0},{2,3},{3,2},{4,5},{5,4},{6,7},{7,6},{8,9},{9,8},{10,11... | collective-permute-start | bytes 393224 | tf_op jit(solution)/shard_map/ppermute | solution.py:556
  21.2 1.3 %sweeps.6.refs_3_ = f32[16,8,256]{2,1,0:T(8,128)S(1)} custom-call(f32[28,32,256]{2,1,0:T(8,128)S(1)} %get-tuple-element.30.whole_ref, f32[32,256]{1,0:T(8,128)S(1)} %get-tuple-element.33.left_ref, f32[32,256]{1,0:T(8,128)S(1)} %get-tuple-element.34.right_ref, f32[29,8,384]{2,1,0:T(8,128)S(1)} %get-tuple-element.35.south_ref, ...), custom_call_target="tpu_custom_call" | custom-call | tf_op jit(solution)/shard_map/sweeps/pallas_call | solution.py:34
  22.5 1.6 %collective-permute-start.6 = (f32[16,8,256]{2,1,0:T(8,128)S(1)}, f32[16,8,256]{2,1,0:T(8,128)S(1)}, u32[]{:S(2)}, u32[]{:S(2)}) collective-permute-start(f32[16,8,256]{2,1,0:T(8,128)S(1)} %sweeps.6.refs_3_), channel_id=1, source_target_pairs={{0,1},{1,0},{2,3},{3,2},{4,5},{5,4},{6,7},{7,6},{8,9},{9,8},{10,11... | collective-permute-start | bytes 393224 | tf_op jit(solution)/shard_map/ppermute | solution.py:556
  24.1 1.3 %sweeps.7.refs_4_ = f32[16,4,256]{2,1,0:T(4,128)S(1)} custom-call(f32[28,32,256]{2,1,0:T(8,128)S(1)} %get-tuple-element.30.whole_ref, f32[32,256]{1,0:T(8,128)S(1)} %get-tuple-element.33.left_ref, f32[32,256]{1,0:T(8,128)S(1)} %get-tuple-element.34.right_ref, f32[29,8,384]{2,1,0:T(8,128)S(1)} %get-tuple-element.35.south_ref, ...), custom_call_target="tpu_custom_call" | custom-call | tf_op jit(solution)/shard_map/sweeps/pallas_call | solution.py:34
  25.5 0.6 %collective-permute-start.7 = (f32[16,4,256]{2,1,0:T(4,128)S(1)}, f32[16,4,256]{2,1,0:T(4,128)S(1)}, u32[]{:S(2)}, u32[]{:S(2)}) collective-permute-start(f32[16,4,256]{2,1,0:T(4,128)S(1)} %sweeps.7.refs_4_), channel_id=1, source_target_pairs={{0,1},{1,0},{2,3},{3,2},{4,5},{5,4},{6,7},{7,6},{8,9},{9,8},{10,11... | collective-permute-start | bytes 196616 | tf_op jit(solution)/shard_map/ppermute | solution.py:556
  26.2 0.4 mix_own.1.refs_0_.order_ref
  26.6 1.6 %square.1.square_ref = f32[36,128]{1,0:T(8,128)S(1)} custom-call(bf16[8,28,16,256]{3,2,1,0:T(8,128)(2,1)S(1)} %get-tuple-element.43.grads_ref, f32[16,28,256]{2,1,0:T(8,128)S(1)} %mix_own.1.refs_0_.order_ref), custom_call_target="tpu_custom_call" | custom-call | tf_op jit(solution)/shard_map/square/pallas_call | solution.py:34
  28.6 1.2 %collective-permute-done.6.refs_2_ = f32[16,8,256]{2,1,0:T(8,128)S(1)} collective-permute-done((f32[16,8,256]{2,1,0:T(8,128)S(1)}, f32[16,8,256]{2,1,0:T(8,128)S(1)}, u32[]{:S(2)}, u32[]{:S(2)}) %collective-permute-start.6) | collective-permute-done | bytes 131104 | tf_op jit(solution)/shard_map/ppermute | solution.py:556
  30.0 0.6 %collective-permute-done.7.field_ref = f32[16,4,256]{2,1,0:T(4,128)S(1)} collective-permute-done((f32[16,4,256]{2,1,0:T(4,128)S(1)}, f32[16,4,256]{2,1,0:T(4,128)S(1)}, u32[]{:S(2)}, u32[]{:S(2)}) %collective-permute-start.7) | collective-permute-done | bytes 65568 | tf_op jit(solution)/shard_map/ppermute | solution.py:556
  30.6 1.1 %mix_last.1 = (f32[28,16,256]{2,1,0:T(8,128)S(1)}, f32[32,1,128]{2,1,0:T(1,128)S(1)}) custom-call(f32[16,28,256]{2,1,0:T(8,128)S(1)} %mix_more.5.acc_ref, bf16[28,48]{1,0:T(8,128)(2,1)S(1)} %get-tuple-element.42.corr_ref, f32[16,4,256]{2,1,0:T(4,128)S(1)} %collective-permute-done.7.field_ref, f32[36,128]{1,0:T(8,128)S(1)} %get-tuple-element.29.order_ref.cross_ref, ...), custom_call_target="tpu_custom_call" | custom-call | tf_op jit(solution)/shard_map/mix_last/pallas_call | solution.py:34
  31.7 10.9 %all_to_all.5.inbox_ref = f32[32,1,128]{2,1,0:T(1,128)S(1)} all-to-all(f32[32,1,128]{2,1,0:T(1,128)S(1)} %get-tuple-element.45), channel_id=1, replica_groups={{31,30,29,28,27,26,25,24,23,22,21,20,19,18,17,16,15,14,13,12,11,10,9,8,..., dimensions={0} | all-to-all | bytes 32768 | tf_op jit(solution)/shard_map/all_to_all | solution.py:567
  42.6 1.7 %final.1 = f32[28,16,256]{2,1,0:T(8,128)} custom-call(f32[32,1,128]{2,1,0:T(1,128)S(1)} %all_to_all.5.inbox_ref, f32[28,16,256]{2,1,0:T(8,128)S(1)} %get-tuple-element.46.mixed_ref, f32[28,16,256]{2,1,0:T(8,128)S(1)} %copy-done, bf16[8,28,16,256]{3,2,1,0:T(8,128)(2,1)S(1)} %get-tuple-element.44.steps_ref, ...), custom_call_target="tpu_custom_call" | custom-call | tf_op jit(solution)/shard_map/final/pallas_call | solution.py:34
  (14 shorter events, 0.9 us)
Async XLA Ops:
  1.3 9.6 %collective-permute-start = (f32[176,256]{1,0:T(8,128)S(1)}, f32[176,256]{1,0:T(8,128)S(1)}, u32[]{:S(2)}, u32[]{:S(2)}) collective-permute-start(f32[176,256]{1,0:T(8,128)S(1)} %next.1), channel_id=1, source_target_pairs={{0,0},{8,16},{16,8},{24,24},{1,1},{9,17},{17,9},{25,25},{2,2},{10,... | collective-permute-start | bytes 540680 | tf_op jit(solution)/shard_map/ppermute | solution.py:517
  2.0 10.2 %collective-permute-start.1 = (f32[176,256]{1,0:T(8,128)S(1)}, f32[176,256]{1,0:T(8,128)S(1)}, u32[]{:S(2)}, u32[]{:S(2)}) collective-permute-start(f32[176,256]{1,0:T(8,128)S(1)} %get-tuple-element.28), channel_id=1, source_target_pairs={{0,8},{8,0},{16,24},{24,16},{1,9},{9,1},{17,25},{25,17},{2,10},{10... | collective-permute-start | bytes 540680 | tf_op jit(solution)/shard_map/ppermute | solution.py:518
  12.5 1.7 %collective-permute-start.2 = (f32[32,256]{1,0:T(8,128)S(1)}, f32[32,256]{1,0:T(8,128)S(1)}, u32[]{:S(2)}, u32[]{:S(2)}) collective-permute-start(f32[32,256]{1,0:T(8,128)S(1)} %get-tuple-element.31), channel_id=1, source_target_pairs={{0,2},{2,0},{4,6},{6,4},{1,3},{3,1},{5,7},{7,5},{8,10},{10,8},{12,... | collective-permute-start | bytes 98312 | tf_op jit(solution)/shard_map/ppermute | solution.py:539
  12.6 3.4 %collective-permute-start.3 = (f32[32,256]{1,0:T(8,128)S(1)}, f32[32,256]{1,0:T(8,128)S(1)}, u32[]{:S(2)}, u32[]{:S(2)}) collective-permute-start(f32[32,256]{1,0:T(8,128)S(1)} %get-tuple-element.32), channel_id=1, source_target_pairs={{0,6},{2,4},{4,2},{6,0},{1,7},{3,5},{5,3},{7,1},{8,14},{10,12},{12... | collective-permute-start | bytes 98312 | tf_op jit(solution)/shard_map/ppermute | solution.py:538
  17.7 10.5 %collective-permute-start.4 = (f32[16,8,256]{2,1,0:T(8,128)S(1)}, f32[16,8,256]{2,1,0:T(8,128)S(1)}, u32[]{:S(2)}, u32[]{:S(2)}) collective-permute-start(f32[16,8,256]{2,1,0:T(8,128)S(1)} %sweeps.4.refs_1_), channel_id=1, source_target_pairs={{0,1},{1,0},{2,3},{3,2},{4,5},{5,4},{6,7},{7,6},{8,9},{9,8},{10,11... | collective-permute-start | bytes 393224 | tf_op jit(solution)/shard_map/ppermute | solution.py:556
  20.6 7.8 %collective-permute-start.5 = (f32[16,8,256]{2,1,0:T(8,128)S(1)}, f32[16,8,256]{2,1,0:T(8,128)S(1)}, u32[]{:S(2)}, u32[]{:S(2)}) collective-permute-start(f32[16,8,256]{2,1,0:T(8,128)S(1)} %sweeps.5.refs_2_), channel_id=1, source_target_pairs={{0,1},{1,0},{2,3},{3,2},{4,5},{5,4},{6,7},{7,6},{8,9},{9,8},{10,11... | collective-permute-start | bytes 393224 | tf_op jit(solution)/shard_map/ppermute | solution.py:556
  22.5 3.5 %copy-start.1 = (f32[56,56]{1,0:T(8,128)S(1)}, f32[56,56]{1,0:T(8,128)}, u32[]{:S(2)}) copy-start(f32[56,56]{1,0:T(8,128)} %corr_ref.1) | copy-start | bytes 37636
  22.5 7.3 %collective-permute-start.6 = (f32[16,8,256]{2,1,0:T(8,128)S(1)}, f32[16,8,256]{2,1,0:T(8,128)S(1)}, u32[]{:S(2)}, u32[]{:S(2)}) collective-permute-start(f32[16,8,256]{2,1,0:T(8,128)S(1)} %sweeps.6.refs_3_), channel_id=1, source_target_pairs={{0,1},{1,0},{2,3},{3,2},{4,5},{5,4},{6,7},{7,6},{8,9},{9,8},{10,11... | collective-permute-start | bytes 393224 | tf_op jit(solution)/shard_map/ppermute | solution.py:556
  25.5 5.2 %collective-permute-start.7 = (f32[16,4,256]{2,1,0:T(4,128)S(1)}, f32[16,4,256]{2,1,0:T(4,128)S(1)}, u32[]{:S(2)}, u32[]{:S(2)}) collective-permute-start(f32[16,4,256]{2,1,0:T(4,128)S(1)} %sweeps.7.refs_4_), channel_id=1, source_target_pairs={{0,1},{1,0},{2,3},{3,2},{4,5},{5,4},{6,7},{7,6},{8,9},{9,8},{10,11... | collective-permute-start | bytes 196616 | tf_op jit(solution)/shard_map/ppermute | solution.py:556
  30.6 12.0 %copy-start = (f32[28,16,256]{2,1,0:T(8,128)S(1)}, f32[28,16,256]{2,1,0:T(8,128)}, u32[]{:S(2)}) copy-start(f32[28,16,256]{2,1,0:T(8,128)} %control_ref.1) | copy-start | bytes 1376260

commit v14 on v13

--- a/solution.py
+++ b/solution.py
@@ -175,7 +175,27 @@
             next_ref[place] = field_ref[far + row, there]
 
 
-def side_kernel(next_ref, field_ref, swap_ref, order_ref, whole_ref, pair_ref, beside_ref, *, steps):
+def own_side_kernel(field_ref, order_ref, west_ref, east_ref):
+    rows, slots, cols = field_ref.shape
+    lane = lane_index()
+    for slot in range(0, slots, SUB):
+        down = slice(slot, slot + SUB)
+        for base in range(0, rows + 2 * HALO, PER):
+            west = east = jnp.zeros((SUB, LANE), jnp.float32)
+            for row in range(max(base, HALO), min(base + PER, rows + HALO)):
+                begin = (row - base) * GROUP
+                here = (lane >= begin) & (lane < begin + GROUP)
+                left = field_ref[row - HALO, down, 0:LANE]
+                right = field_ref[row - HALO, down, cols - LANE:cols]
+                west = jnp.where(here, pltpu.roll(left, begin, 1) if begin else left, west)
+                turn = (begin + GROUP) % LANE
+                east = jnp.where(here, pltpu.roll(right, turn, 1) if turn else right, east)
+            across = slice(base // PER * LANE, (base // PER + 1) * LANE)
+            west_ref[down, across] = west
+            east_ref[down, across] = east
+
+
+def side_kernel(next_ref, field_ref, swap_ref, own_west_ref, own_east_ref, whole_ref, pair_ref, beside_ref, *, steps):
     rows, slots, cols = field_ref.shape
     place, count = lax.axis_index("lat"), lax.axis_size("lat")
     odd = lax.rem(place, 2)
@@ -197,8 +217,11 @@
     for slot in range(0, slots, SUB):
         down = slice(slot, slot + SUB)
         for base in range(0, rows + 2 * HALO, PER):
-            west = east = jnp.zeros((SUB, LANE), jnp.float32)
+            across = slice(base // PER * LANE, (base // PER + 1) * LANE)
+            west, east = own_west_ref[down, across], own_east_ref[down, across]
             for row in range(base, min(base + PER, rows + 2 * HALO)):
+                if HALO <= row < HALO + rows:
+                    continue
                 begin = (row - base) * GROUP
                 here = (lane >= begin) & (lane < begin + GROUP)
                 left = whole_ref[row, down, 0:LANE]
@@ -206,7 +229,6 @@
                 west = jnp.where(here, pltpu.roll(left, begin, 1) if begin else left, west)
                 turn = (begin + GROUP) % LANE
                 east = jnp.where(here, pltpu.roll(right, turn, 1) if turn else right, east)
-            across = slice(base // PER * LANE, (base // PER + 1) * LANE)
             pair_ref[down, across] = jnp.where(uneven, west, east)
             beside_ref[down, across] = jnp.where(uneven, east, west)
 
@@ -532,8 +554,9 @@
         (time_corr,), name="corr",
     )
     side_shape = f32(slots, -(-tall // PER) * LANE)
+    own_west, own_east = call(own_side_kernel, (side_shape, side_shape), (field, cross), name="own_sides")
     whole, to_pair, to_beside = call(
-        functools.partial(side_kernel, steps=steps), (f32(tall, slots, cols), side_shape, side_shape), (from_next, field, from_swap, cross), name="sides"
+        functools.partial(side_kernel, steps=steps), (f32(tall, slots, cols), side_shape, side_shape), (from_next, field, from_swap, own_west, own_east), name="sides"
     )
     from_beside = lax.ppermute(to_beside, "lon", odds)
     from_pair = lax.ppermute(to_pair, "lon", evens)

time: 44.5 us -> 44.4 us (level)
    pallas_call x17 -> x18, Pallas kernels: 15.9 us -> 16 us  [call(): pl.pallas_call(kernel, out_shape=outs, in_specs=specs or [VMEM] * len(arg...]
  transfers between devices with their start and end apart: 8 -> 8, of which waited for: 4 -> 4; matrix products, arithmetic and copies ran while one was open for 0% -> 0% of each run, Pallas kernels for 22% -> 23%
where the time goes in v14:
time: 44.4 us; the launch traced here: 44.2 us
  Pallas kernels  16 us (36%)
  starting transfers between devices  12.6 us (28%)
  blocking collectives  10.9 us (25%)
  waiting for transfers between devices  4.56 us (10%)
    pallas_call x18, Pallas kernels, call(): pl.pallas_call(kernel, out_shape=outs, in_specs=specs or [VMEM] * len(arg...  16 us
    all_to_all x1, blocking collectives, local(): lax.all_to_all(message, ('lat', 'lon', 'tm'), split_axis=0, concat_axis=0...  10.9 us
    ppermute x1, starting transfers between devices, local(): from_swap = lax.ppermute(to_swap, 'lat', even)  5.9 us
    ppermute x4, starting transfers between devices, local(): other.append(lax.ppermute(part, 'tm', pairs))  4.31 us
    ppermute x4, waiting for transfers between devices, local(): other.append(lax.ppermute(part, 'tm', pairs))  1.78 us
    ppermute x1, waiting for transfers between devices, local(): from_beside = lax.ppermute(to_beside, 'lon', odds)  1.77 us
    ppermute x1, starting transfers between devices, local(): from_beside = lax.ppermute(to_beside, 'lon', odds)  1.64 us
    ppermute x1, waiting for transfers between devices, local(): from_swap = lax.ppermute(to_swap, 'lat', even)  1.01 us
  transfers between devices with their start and end apart: 8, of which 4 were waited for; matrix products, arithmetic and copies ran while one was open for 0% of the time, Pallas kernels for 23%

profile of v14, /device:TPU:0, one launch (start us, length us, event | category | flops | bytes accessed | tf_op | source)
XLA Modules:
  0.0 44.2 jit_solution(3257185397485183596)
XLA Ops:
  0.0 1.2 %pack.1 = (f32[16,32,256]{2,1,0:T(8,128)S(1)}, f32[176,256]{1,0:T(8,128)S(1)}) custom-call(f32[28,16,256]{2,1,0:T(8,128)} %grad_hbm.1, s32[16,256]{1,0:T(8,128)} %mask_hbm.1, f32[16,256]{1,0:T(8,128)} %diff_hbm.1), custom_call_target="tpu_custom_call" | custom-call | tf_op jit(solution)/shard_map/pack/pallas_call | solution.py:34
  1.3 0.7 %collective-permute-start = (f32[176,256]{1,0:T(8,128)S(1)}, f32[176,256]{1,0:T(8,128)S(1)}, u32[]{:S(2)}, u32[]{:S(2)}) collective-permute-start(f32[176,256]{1,0:T(8,128)S(1)} %next.1), channel_id=1, source_target_pairs={{0,0},{8,16},{16,8},{24,24},{1,1},{9,17},{17,9},{25,25},{2,2},{10,... | collective-permute-start | bytes 540680 | tf_op jit(solution)/shard_map/ppermute | solution.py:539
  2.0 5.9 %collective-permute-start.1 = (f32[176,256]{1,0:T(8,128)S(1)}, f32[176,256]{1,0:T(8,128)S(1)}, u32[]{:S(2)}, u32[]{:S(2)}) collective-permute-start(f32[176,256]{1,0:T(8,128)S(1)} %get-tuple-element.30), channel_id=1, source_target_pairs={{0,8},{8,0},{16,24},{24,16},{1,9},{9,1},{17,25},{25,17},{2,10},{10... | collective-permute-start | bytes 540680 | tf_op jit(solution)/shard_map/ppermute | solution.py:540
  7.9 3.0 %cross.1 = (f32[36,128]{1,0:T(8,128)S(1)}, bf16[8,28,16,256]{3,2,1,0:T(8,128)(2,1)S(1)}, bf16[8,28,16,256]{3,2,1,0:T(8,128)(2,1)S(1)}) custom-call(bf16[8,28,16,256]{3,2,1,0:T(8,128)(2,1)} %steps_hbm.1, bf16[8,28,16,256]{3,2,1,0:T(8,128)(2,1)} %grads_hbm.1), custom_call_target="tpu_custom_call" | custom-call | tf_op jit(solution)/shard_map/cross/pallas_call | solution.py:34
  11.1 1.0 %collective-permute-done.1.swap_ref = f32[176,256]{1,0:T(8,128)S(1)} collective-permute-done((f32[176,256]{1,0:T(8,128)S(1)}, f32[176,256]{1,0:T(8,128)S(1)}, u32[]{:S(2)}, u32[]{:S(2)}) %collective-permute-start.1) | collective-permute-done | bytes 180256 | tf_op jit(solution)/shard_map/ppermute | solution.py:540
  12.1 0.3 sides.1
  12.5 1.6 %collective-permute-start.3 = (f32[32,256]{1,0:T(8,128)S(1)}, f32[32,256]{1,0:T(8,128)S(1)}, u32[]{:S(2)}, u32[]{:S(2)}) collective-permute-start(f32[32,256]{1,0:T(8,128)S(1)} %get-tuple-element.36), channel_id=1, source_target_pairs={{0,6},{2,4},{4,2},{6,0},{1,7},{3,5},{5,3},{7,1},{8,14},{10,12},{12... | collective-permute-start | bytes 98312 | tf_op jit(solution)/shard_map/ppermute | solution.py:561
  14.1 1.8 %collective-permute-done.3.beside_ref = f32[32,256]{1,0:T(8,128)S(1)} collective-permute-done((f32[32,256]{1,0:T(8,128)S(1)}, f32[32,256]{1,0:T(8,128)S(1)}, u32[]{:S(2)}, u32[]{:S(2)}) %collective-permute-start.3) | collective-permute-done | bytes 32800 | tf_op jit(solution)/shard_map/ppermute | solution.py:561
  15.9 0.3 weights.1
  16.2 1.3 %sweeps.4.refs_1_ = f32[16,8,256]{2,1,0:T(8,128)S(1)} custom-call(f32[28,32,256]{2,1,0:T(8,128)S(1)} %get-tuple-element.34.whole_ref, f32[32,256]{1,0:T(8,128)S(1)} %get-tuple-element.37.left_ref, f32[32,256]{1,0:T(8,128)S(1)} %get-tuple-element.38.right_ref, f32[29,8,384]{2,1,0:T(8,128)S(1)} %get-tuple-element.39.south_ref, ...), custom_call_target="tpu_custom_call" | custom-call | tf_op jit(solution)/shard_map/sweeps/pallas_call | solution.py:34
  17.6 1.6 %collective-permute-start.4 = (f32[16,8,256]{2,1,0:T(8,128)S(1)}, f32[16,8,256]{2,1,0:T(8,128)S(1)}, u32[]{:S(2)}, u32[]{:S(2)}) collective-permute-start(f32[16,8,256]{2,1,0:T(8,128)S(1)} %sweeps.4.refs_1_), channel_id=1, source_target_pairs={{0,1},{1,0},{2,3},{3,2},{4,5},{5,4},{6,7},{7,6},{8,9},{9,8},{10,11... | collective-permute-start | bytes 393224 | tf_op jit(solution)/shard_map/ppermute | solution.py:579
  19.1 1.3 %sweeps.5.refs_2_ = f32[16,8,256]{2,1,0:T(8,128)S(1)} custom-call(f32[28,32,256]{2,1,0:T(8,128)S(1)} %get-tuple-element.34.whole_ref, f32[32,256]{1,0:T(8,128)S(1)} %get-tuple-element.37.left_ref, f32[32,256]{1,0:T(8,128)S(1)} %get-tuple-element.38.right_ref, f32[29,8,384]{2,1,0:T(8,128)S(1)} %get-tuple-element.39.south_ref, ...), custom_call_target="tpu_custom_call" | custom-call | tf_op jit(solution)/shard_map/sweeps/pallas_call | solution.py:34
  20.5 0.6 %collective-permute-start.5 = (f32[16,8,256]{2,1,0:T(8,128)S(1)}, f32[16,8,256]{2,1,0:T(8,128)S(1)}, u32[]{:S(2)}, u32[]{:S(2)}) collective-permute-start(f32[16,8,256]{2,1,0:T(8,128)S(1)} %sweeps.5.refs_2_), channel_id=1, source_target_pairs={{0,1},{1,0},{2,3},{3,2},{4,5},{5,4},{6,7},{7,6},{8,9},{9,8},{10,11... | collective-permute-start | bytes 393224 | tf_op jit(solution)/shard_map/ppermute | solution.py:579
  21.1 1.3 %sweeps.6.refs_3_ = f32[16,8,256]{2,1,0:T(8,128)S(1)} custom-call(f32[28,32,256]{2,1,0:T(8,128)S(1)} %get-tuple-element.34.whole_ref, f32[32,256]{1,0:T(8,128)S(1)} %get-tuple-element.37.left_ref, f32[32,256]{1,0:T(8,128)S(1)} %get-tuple-element.38.right_ref, f32[29,8,384]{2,1,0:T(8,128)S(1)} %get-tuple-element.39.south_ref, ...), custom_call_target="tpu_custom_call" | custom-call | tf_op jit(solution)/shard_map/sweeps/pallas_call | solution.py:34
  22.5 1.6 %collective-permute-start.6 = (f32[16,8,256]{2,1,0:T(8,128)S(1)}, f32[16,8,256]{2,1,0:T(8,128)S(1)}, u32[]{:S(2)}, u32[]{:S(2)}) collective-permute-start(f32[16,8,256]{2,1,0:T(8,128)S(1)} %sweeps.6.refs_3_), channel_id=1, source_target_pairs={{0,1},{1,0},{2,3},{3,2},{4,5},{5,4},{6,7},{7,6},{8,9},{9,8},{10,11... | collective-permute-start | bytes 393224 | tf_op jit(solution)/shard_map/ppermute | solution.py:579
  24.0 1.3 %sweeps.7.refs_4_ = f32[16,4,256]{2,1,0:T(4,128)S(1)} custom-call(f32[28,32,256]{2,1,0:T(8,128)S(1)} %get-tuple-element.34.whole_ref, f32[32,256]{1,0:T(8,128)S(1)} %get-tuple-element.37.left_ref, f32[32,256]{1,0:T(8,128)S(1)} %get-tuple-element.38.right_ref, f32[29,8,384]{2,1,0:T(8,128)S(1)} %get-tuple-element.39.south_ref, ...), custom_call_target="tpu_custom_call" | custom-call | tf_op jit(solution)/shard_map/sweeps/pallas_call | solution.py:34
  25.4 0.6 %collective-permute-start.7 = (f32[16,4,256]{2,1,0:T(4,128)S(1)}, f32[16,4,256]{2,1,0:T(4,128)S(1)}, u32[]{:S(2)}, u32[]{:S(2)}) collective-permute-start(f32[16,4,256]{2,1,0:T(4,128)S(1)} %sweeps.7.refs_4_), channel_id=1, source_target_pairs={{0,1},{1,0},{2,3},{3,2},{4,5},{5,4},{6,7},{7,6},{8,9},{9,8},{10,11... | collective-permute-start | bytes 196616 | tf_op jit(solution)/shard_map/ppermute | solution.py:579
  26.1 0.4 mix_own.1.refs_0_.order_ref
  26.5 1.6 %square.1.square_ref = f32[36,128]{1,0:T(8,128)S(1)} custom-call(bf16[8,28,16,256]{3,2,1,0:T(8,128)(2,1)S(1)} %get-tuple-element.47.grads_ref, f32[16,28,256]{2,1,0:T(8,128)S(1)} %mix_own.1.refs_0_.order_ref), custom_call_target="tpu_custom_call" | custom-call | tf_op jit(solution)/shard_map/square/pallas_call | solution.py:34
  28.5 1.2 %collective-permute-done.6.refs_2_ = f32[16,8,256]{2,1,0:T(8,128)S(1)} collective-permute-done((f32[16,8,256]{2,1,0:T(8,128)S(1)}, f32[16,8,256]{2,1,0:T(8,128)S(1)}, u32[]{:S(2)}, u32[]{:S(2)}) %collective-permute-start.6) | collective-permute-done | bytes 131104 | tf_op jit(solution)/shard_map/ppermute | solution.py:579
  29.9 0.6 %collective-permute-done.7.field_ref = f32[16,4,256]{2,1,0:T(4,128)S(1)} collective-permute-done((f32[16,4,256]{2,1,0:T(4,128)S(1)}, f32[16,4,256]{2,1,0:T(4,128)S(1)}, u32[]{:S(2)}, u32[]{:S(2)}) %collective-permute-start.7) | collective-permute-done | bytes 65568 | tf_op jit(solution)/shard_map/ppermute | solution.py:579
  30.5 1.1 %mix_last.1 = (f32[28,16,256]{2,1,0:T(8,128)S(1)}, f32[32,1,128]{2,1,0:T(1,128)S(1)}) custom-call(f32[16,28,256]{2,1,0:T(8,128)S(1)} %mix_more.5.acc_ref, bf16[28,48]{1,0:T(8,128)(2,1)S(1)} %get-tuple-element.46.corr_ref, f32[16,4,256]{2,1,0:T(4,128)S(1)} %collective-permute-done.7.field_ref, f32[36,128]{1,0:T(8,128)S(1)} %get-tuple-element.31.order_ref.cross_ref, ...), custom_call_target="tpu_custom_call" | custom-call | tf_op jit(solution)/shard_map/mix_last/pallas_call | solution.py:34
  31.7 10.9 %all_to_all.5.inbox_ref = f32[32,1,128]{2,1,0:T(1,128)S(1)} all-to-all(f32[32,1,128]{2,1,0:T(1,128)S(1)} %get-tuple-element.49), channel_id=1, replica_groups={{31,30,29,28,27,26,25,24,23,22,21,20,19,18,17,16,15,14,13,12,11,10,9,8,..., dimensions={0} | all-to-all | bytes 32768 | tf_op jit(solution)/shard_map/all_to_all | solution.py:590
  42.5 1.7 %final.1 = f32[28,16,256]{2,1,0:T(8,128)} custom-call(f32[32,1,128]{2,1,0:T(1,128)S(1)} %all_to_all.5.inbox_ref, f32[28,16,256]{2,1,0:T(8,128)S(1)} %get-tuple-element.50.mixed_ref, f32[28,16,256]{2,1,0:T(8,128)S(1)} %copy-done, bf16[8,28,16,256]{3,2,1,0:T(8,128)(2,1)S(1)} %get-tuple-element.48.steps_ref, ...), custom_call_target="tpu_custom_call" | custom-call | tf_op jit(solution)/shard_map/final/pallas_call | solution.py:34
  (15 shorter events, 1.1 us)
Async XLA Ops:
  1.3 9.8 %collective-permute-start = (f32[176,256]{1,0:T(8,128)S(1)}, f32[176,256]{1,0:T(8,128)S(1)}, u32[]{:S(2)}, u32[]{:S(2)}) collective-permute-start(f32[176,256]{1,0:T(8,128)S(1)} %next.1), channel_id=1, source_target_pairs={{0,0},{8,16},{16,8},{24,24},{1,1},{9,17},{17,9},{25,25},{2,2},{10,... | collective-permute-start | bytes 540680 | tf_op jit(solution)/shard_map/ppermute | solution.py:539
  2.0 10.2 %collective-permute-start.1 = (f32[176,256]{1,0:T(8,128)S(1)}, f32[176,256]{1,0:T(8,128)S(1)}, u32[]{:S(2)}, u32[]{:S(2)}) collective-permute-start(f32[176,256]{1,0:T(8,128)S(1)} %get-tuple-element.30), channel_id=1, source_target_pairs={{0,8},{8,0},{16,24},{24,16},{1,9},{9,1},{17,25},{25,17},{2,10},{10... | collective-permute-start | bytes 540680 | tf_op jit(solution)/shard_map/ppermute | solution.py:540
  12.4 1.7 %collective-permute-start.2 = (f32[32,256]{1,0:T(8,128)S(1)}, f32[32,256]{1,0:T(8,128)S(1)}, u32[]{:S(2)}, u32[]{:S(2)}) collective-permute-start(f32[32,256]{1,0:T(8,128)S(1)} %get-tuple-element.35), channel_id=1, source_target_pairs={{0,2},{2,0},{4,6},{6,4},{1,3},{3,1},{5,7},{7,5},{8,10},{10,8},{12,... | collective-permute-start | bytes 98312 | tf_op jit(solution)/shard_map/ppermute | solution.py:562
  12.5 3.4 %collective-permute-start.3 = (f32[32,256]{1,0:T(8,128)S(1)}, f32[32,256]{1,0:T(8,128)S(1)}, u32[]{:S(2)}, u32[]{:S(2)}) collective-permute-start(f32[32,256]{1,0:T(8,128)S(1)} %get-tuple-element.36), channel_id=1, source_target_pairs={{0,6},{2,4},{4,2},{6,0},{1,7},{3,5},{5,3},{7,1},{8,14},{10,12},{12... | collective-permute-start | bytes 98312 | tf_op jit(solution)/shard_map/ppermute | solution.py:561
  17.6 10.5 %collective-permute-start.4 = (f32[16,8,256]{2,1,0:T(8,128)S(1)}, f32[16,8,256]{2,1,0:T(8,128)S(1)}, u32[]{:S(2)}, u32[]{:S(2)}) collective-permute-start(f32[16,8,256]{2,1,0:T(8,128)S(1)} %sweeps.4.refs_1_), channel_id=1, source_target_pairs={{0,1},{1,0},{2,3},{3,2},{4,5},{5,4},{6,7},{7,6},{8,9},{9,8},{10,11... | collective-permute-start | bytes 393224 | tf_op jit(solution)/shard_map/ppermute | solution.py:579
  20.5 7.8 %collective-permute-start.5 = (f32[16,8,256]{2,1,0:T(8,128)S(1)}, f32[16,8,256]{2,1,0:T(8,128)S(1)}, u32[]{:S(2)}, u32[]{:S(2)}) collective-permute-start(f32[16,8,256]{2,1,0:T(8,128)S(1)} %sweeps.5.refs_2_), channel_id=1, source_target_pairs={{0,1},{1,0},{2,3},{3,2},{4,5},{5,4},{6,7},{7,6},{8,9},{9,8},{10,11... | collective-permute-start | bytes 393224 | tf_op jit(solution)/shard_map/ppermute | solution.py:579
  22.4 3.5 %copy-start.1 = (f32[56,56]{1,0:T(8,128)S(1)}, f32[56,56]{1,0:T(8,128)}, u32[]{:S(2)}) copy-start(f32[56,56]{1,0:T(8,128)} %corr_ref.1) | copy-start | bytes 37636
  22.5 7.3 %collective-permute-start.6 = (f32[16,8,256]{2,1,0:T(8,128)S(1)}, f32[16,8,256]{2,1,0:T(8,128)S(1)}, u32[]{:S(2)}, u32[]{:S(2)}) collective-permute-start(f32[16,8,256]{2,1,0:T(8,128)S(1)} %sweeps.6.refs_3_), channel_id=1, source_target_pairs={{0,1},{1,0},{2,3},{3,2},{4,5},{5,4},{6,7},{7,6},{8,9},{9,8},{10,11... | collective-permute-start | bytes 393224 | tf_op jit(solution)/shard_map/ppermute | solution.py:579
  25.4 5.2 %collective-permute-start.7 = (f32[16,4,256]{2,1,0:T(4,128)S(1)}, f32[16,4,256]{2,1,0:T(4,128)S(1)}, u32[]{:S(2)}, u32[]{:S(2)}) collective-permute-start(f32[16,4,256]{2,1,0:T(4,128)S(1)} %sweeps.7.refs_4_), channel_id=1, source_target_pairs={{0,1},{1,0},{2,3},{3,2},{4,5},{5,4},{6,7},{7,6},{8,9},{9,8},{10,11... | collective-permute-start | bytes 196616 | tf_op jit(solution)/shard_map/ppermute | solution.py:579
  30.5 12.0 %copy-start = (f32[28,16,256]{2,1,0:T(8,128)S(1)}, f32[28,16,256]{2,1,0:T(8,128)}, u32[]{:S(2)}) copy-start(f32[28,16,256]{2,1,0:T(8,128)} %control_ref.1) | copy-start | bytes 1376260
